TPU v7x, 32 devices: a whole 2x2x4 slice. The times are simulated.
32 devices in a mesh: rep: 8 (over y, x, core), tp: 4 (over z).
Axes of the slice: x: 2, y: 2, z: 4, core: 2. Of those that a mesh axis runs over, the one named last changes fastest.
Arguments:
- hidden: bfloat16 [36864, 1024], P('rep', 'tp'), may hold values from -0.09375 to 0.09375
- out_grad: bfloat16 [36864, 512], P(('rep', 'tp')), may hold values from -6 to 6
- momentum: float32 [8, 1024, 512], P('rep', 'tp'), may hold values from -6 to 6
- band_rows: int32 [16, 8], P('tp'), may hold values from 0 to 48, as said below
- band_start_columns: int32 [16, 8], P('tp'), may hold values from 0 to 48, as said below
Outputs:
- momentum_out: float32 [8, 1024, 512], P('rep', 'tp')
- update: bfloat16 [1024, 512], P('tp')
Inputs may be any that keep to these rules, and one draw needn't show every extreme that they name: `band_rows`: multiples of 16, the same for every replica. `band_start_columns`: multiples of 16, the same for every replica.
All inputs are finite; a program needn't handle non-finite values.
Results may differ from a plain program's by a relative error of at most 0.001.
Values may be sent and summed in bfloat16 or wider, within the bound.
No kernel may reach another device: no remote copies, remote signals or barrier semaphores. Data moves between devices by JAX's collectives and lax.ppermute only.
A program may use at most 64 MiB of HBM per device.

v0:
```python
import functools

import jax
import jax.numpy as jnp
import numpy as np
from jax import lax
from jax.experimental import pallas as pl
from jax.experimental.pallas import tpu as pltpu
from jax.sharding import PartitionSpec as P

decay_rate = 0.9
order = 64
band = 16
steps = order // band


def basis_matrix():
    frequency = np.arange(order, dtype=np.float64)[:, None]
    sample_pos = np.arange(order, dtype=np.float64)[None, :]
    norm_scale = np.where(frequency == 0, np.sqrt(1.0 / order), np.sqrt(2.0 / order))
    return norm_scale * np.cos(np.pi * (sample_pos + 0.5) * frequency / order)


def halves_of(matrix):
    high = matrix.astype(jnp.bfloat16)
    low = (matrix - high.astype(matrix.dtype)).astype(jnp.bfloat16)
    return np.stack([high, low])


def diagonal_blocks(width):
    count = next(c for c in (4, 2, 1) if width % (c * order) == 0)
    return halves_of(np.kron(np.eye(count), basis_matrix()))


def fold_matrix(width):
    return np.kron(np.eye(width // order), np.kron(np.ones((steps, 1)), np.eye(band))).astype(jnp.bfloat16)


def split2(x):
    high = x.astype(jnp.bfloat16)
    return high, (x - high.astype(jnp.float32)).astype(jnp.bfloat16)


def split3(x):
    high, low = split2(x)
    rest = x - high.astype(jnp.float32) - low.astype(jnp.float32)
    return high, low, rest.astype(jnp.bfloat16)


def dot(a, b, dims=((1,), (0,))):
    return lax.dot_general(a, b, (dims, ((), ())), preferred_element_type=jnp.float32)


def dot3(a, b, dims=((1,), (0,))):
    return dot(a[0], b[0], dims) + (dot(a[0], b[1], dims) + dot(a[1], b[0], dims))


def on_rows(basis_ref, x, transposed):
    basis = basis_ref[0], basis_ref[1]
    side = basis[0].shape[0]
    dims = ((0,), (0,)) if transposed else ((1,), (0,))
    parts = [dot3(basis, split2(x[i : i + side]), dims) for i in range(0, x.shape[0], side)]
    return parts[0] if len(parts) == 1 else jnp.concatenate(parts, axis=0)


def on_columns(basis_ref, x, transposed):
    basis = basis_ref[0], basis_ref[1]
    side = basis[0].shape[0]
    dims = ((1,), (0,)) if transposed else ((1,), (1,))
    parts = [dot3(split2(x[:, i : i + side]), basis, dims) for i in range(0, x.shape[1], side)]
    return parts[0] if len(parts) == 1 else jnp.concatenate(parts, axis=1)


def column_mask(row, cols_ref, width):
    group = lax.rem(lax.broadcasted_iota(jnp.int32, (band, width), 1), order) // band
    return group == cols_ref[row : row + 1, :]


def lifted(folded, rows_ref, cols_ref, fold_ref, row_basis_ref, column_basis_ref):
    width = cols_ref.shape[1]
    spread = sum(dot(part, fold_ref[...], ((1,), (1,))) for part in split3(folded))
    pieces = []
    for row in range(rows_ref.shape[0]):
        inside = jnp.where(column_mask(row, cols_ref, width), spread[row * band : (row + 1) * band], 0.0)
        for step in range(steps):
            pieces.append(jnp.where(rows_ref[row : row + 1, :] == step, inside, 0.0))
    coefficients = jnp.concatenate(pieces, axis=0)
    return on_columns(column_basis_ref, on_rows(row_basis_ref, coefficients, True), True)


def bands_of(x, rows_ref, cols_ref, fold_ref, row_basis_ref, column_basis_ref):
    width = cols_ref.shape[1]
    coefficients = on_columns(column_basis_ref, on_rows(row_basis_ref, x, False), False)
    pieces = []
    for row in range(rows_ref.shape[0]):
        taken = jnp.zeros((band, width), jnp.float32)
        for step in range(steps):
            at = row * order + step * band
            taken = jnp.where(rows_ref[row : row + 1, :] == step, coefficients[at : at + band], taken)
        pieces.append(jnp.where(column_mask(row, cols_ref, width), taken, 0.0))
    taken = jnp.concatenate(pieces, axis=0)
    return sum(dot(part, fold_ref[...]) for part in split3(taken))


def bands_kernel(m_ref, *refs):
    *table_refs, bands_ref = refs
    bands_ref[...] = bands_of(m_ref[...], *table_refs)


def last_rows_kernel(m_ref, hidden_ref, grad_ref, *refs):
    *table_refs, out_ref, bands_ref = refs
    hidden = hidden_ref[hidden_ref.shape[0] - grad_ref.shape[0] :]
    out_ref[...] = m_ref[...] + dot(hidden, grad_ref[...], ((0,), (0,)))
    bands_ref[...] = bands_of(out_ref[...], *table_refs)


def remove_kernel(count, *refs):
    m_refs, band_refs, (*table_refs, out_ref) = refs[:count], refs[count : 2 * count], refs[2 * count :]
    bands = pair_sum([ref[...] for ref in band_refs])
    out_ref[...] = pair_sum([ref[...] for ref in m_refs]) - lifted(bands, *table_refs)


def update_kernel(*refs):
    *part_refs, rows_ref, cols_ref, fold_ref, row_basis_ref, column_basis_ref, out_ref = refs
    parts = [ref[...] for ref in part_refs]
    out_ref[...] = lifted(
        pair_sum(parts), rows_ref, cols_ref, fold_ref, row_basis_ref, column_basis_ref
    ).astype(out_ref.dtype)


def pair_sum(parts):
    while len(parts) > 1:
        parts = [sum(parts[i + 1 : i + 2], parts[i]) for i in range(0, len(parts), 2)]
    return parts[0]


def call(kernel, out_shapes, *operands):
    return pl.pallas_call(
        kernel,
        out_shape=out_shapes,
        compiler_params=pltpu.CompilerParams(vmem_limit_bytes=32 * 2**20),
        cost_estimate=pl.CostEstimate(flops=4 * 10**8, bytes_accessed=4 * 10**6, transcendentals=0),
    )(*operands)


def spread_sum(x, axis):
    size = lax.axis_size(axis)
    if size & (size - 1):
        return [lax.psum(x, axis)]
    stride, parts = 1, [x]
    while stride < size:
        count = min(8, size // stride)
        x = pair_sum(parts)
        parts = [x] + [
            lax.ppermute(x, axis, [(i, i ^ (stride * k)) for i in range(size)]) for k in range(1, count)
        ]
        stride *= count
    return parts


def product(hidden_rows, grad_rows):
    return dot(hidden_rows, grad_rows, ((0,), (0,)))


def after(x, *others):
    return lax.optimization_barrier((x, *others))[0]


def gathered(hidden, out_grad, carried, tables, make_tables, band_rows, band_start_columns):
    m = carried + product(hidden, lax.all_gather(out_grad, "tp", axis=0, tiled=True))
    folded = jax.ShapeDtypeStruct((m.shape[0] // steps, m.shape[1] // steps), jnp.float32)
    return [m], [call(bands_kernel, folded, m, *tables)]


def lined(hidden, out_grad, carried, tables, make_tables, band_rows, band_start_columns):
    tok = out_grad.shape[0]
    me = lax.axis_index("tp")
    left = me < 2
    cross = jnp.where(left, 2, 1)
    far = jnp.where(left, 3, 0)
    first = max(tok // 3 // 128 * 128, 16)
    handed = tok - first

    def rows_of(part, start=0, stop=tok):
        return lax.dynamic_slice_in_dim(hidden, part * tok + start, stop - start, 0)

    def send(x, perm):
        return lax.ppermute(x, "tp", perm)

    both_ways = [(0, 1), (1, 0), (2, 3), (3, 2)]
    across = [(1, 2), (2, 1)]
    outward = [(1, 0), (2, 3)]
    inward = [(0, 1), (3, 2)]

    cross_grad = send(out_grad, across)
    pair_head = send(out_grad[:first], both_ways)
    m = carried + product(rows_of(me), out_grad)
    pair_rest = send(after(out_grad, m)[first:], both_ways)

    far_head = send(pair_head, across)
    places = jnp.concatenate([band_rows, band_start_columns], axis=0)
    places = send(after(places, pair_head), inward)
    end_tables = make_tables(*(places[i * band_rows.shape[0] :][: band_rows.shape[0]] for i in range(2)))
    pair_rest = after(pair_rest, pair_head)
    far_rest = send(pair_rest, across)
    helped_hidden = jnp.concatenate([rows_of(cross, handed), rows_of(far)], axis=0)
    helped_hidden = send(after(helped_hidden, pair_rest), inward)
    cross_grad = after(cross_grad, pair_rest)
    passed_grad = send(cross_grad[:handed], outward)

    m = m + product(rows_of(me ^ 1, 0, first), pair_head) + product(rows_of(me ^ 1, first), pair_rest)
    m = m + product(rows_of(cross), cross_grad)
    m = m + product(rows_of(cross, 0, handed), passed_grad) + product(rows_of(far, 0, first), far_head)
    helped = product(helped_hidden[: tok - handed], cross_grad[handed:])
    helped = helped + product(helped_hidden[tok - handed :][:first], far_head)
    far_rest = after(far_rest, m, helped, tables, end_tables)

    full = jax.ShapeDtypeStruct(m.shape, jnp.float32)
    folded = jax.ShapeDtypeStruct((m.shape[0] // steps, m.shape[1] // steps), jnp.float32)
    helped, helped_bands = call(
        last_rows_kernel, (full, folded), helped, helped_hidden, far_rest, *end_tables
    )
    helped_bands = send(helped_bands, outward)
    m, bands = call(last_rows_kernel, (full, folded), m, rows_of(far, first), far_rest, *tables)
    helped_bands, bands = lax.optimization_barrier((helped_bands, bands))
    helped = send(after(helped, helped_bands), outward)
    return [m, helped], [bands, helped_bands]


def local(hidden, out_grad, momentum, band_rows, band_start_columns):
    row_count = hidden.shape[1]
    col_count = out_grad.shape[1]
    matrices = tuple(
        jnp.asarray(x) for x in (fold_matrix(col_count), diagonal_blocks(row_count), diagonal_blocks(col_count))
    )

    def make_tables(*places):
        return tuple(jnp.repeat(x.astype(jnp.int32) // band, order, axis=1) for x in places) + matrices

    tables = make_tables(band_rows, band_start_columns)
    form = lined if lax.axis_size("tp") == 4 else gathered
    m_parts, band_parts = form(
        hidden, out_grad, decay_rate * momentum[0], tables, make_tables, band_rows, band_start_columns
    )
    parts = spread_sum(pair_sum(band_parts), "rep")
    shape = (row_count, col_count)
    momentum_out = call(
        functools.partial(remove_kernel, len(m_parts)),
        jax.ShapeDtypeStruct(shape, jnp.float32),
        *m_parts,
        *band_parts,
        *tables,
    )
    update = call(update_kernel, jax.ShapeDtypeStruct(shape, jnp.bfloat16), *parts, *tables)
    return (momentum_out[None], update)


def solution(mesh):
    return jax.shard_map(
        local,
        mesh=mesh,
        in_specs=(
            P("rep", "tp"),
            P(("rep", "tp"), None),
            P("rep", "tp", None),
            P("tp", None),
            P("tp", None),
        ),
        out_specs=(P("rep", "tp", None), P("tp", None)),
        check_vma=False,
    )
```

profile of v0, /device:TPU:0, one launch (start us, length us, event | category | flops | bytes accessed | tf_op | source)
XLA Modules:
  0.0 113.3 jit_solution(10993380906814821330)
XLA Ops:
  0.7 1.8 %collective-permute-start.2 = (bf16[1152,512]{1,0:T(8,128)(2,1)}, bf16[1152,512]{1,0:T(8,128)(2,1)}, u32[]{:S(2)}, u32[]{:S(2)}) collective-permute-start(bf16[1152,512]{1,0:T(8,128)(2,1)} %param.9), channel_id=1, source_target_pairs={{1,2},{2,1},{5,6},{6,5},{9,10},{10,9},{13,14},{14,13},{17,18},{18,... | collective-permute-start | bytes 3538952 | tf_op jit(solution)/shard_map/ppermute | solution.py:188
  2.5 2.7 %convolution_add_fusion = f32[256,512]{1,0:T(8,128)} fusion(bf16[1152,512]{1,0:T(8,128)(2,1)} %param.9, bf16[4608,256]{1,0:T(8,128)(2,1)S(1)} %copy-done, s32[]{:T(128)S(6)} %select_n.44, f32[1,256,512]{2,1,0:T(8,128)} %param.10), kind=kOutput, calls=%fused_computation | convolution fusion | flops 302252032 | bytes 2818052 | tf_op jit(solution)/shard_map/dot_general | solution.py:51
  5.2 0.9 slice.27
  6.2 4.9 %collective-permute-start.1 = (bf16[768,512]{1,0:T(8,128)(2,1)}, bf16[768,512]{1,0:T(8,128)(2,1)}, u32[]{:S(2)}, u32[]{:S(2)}) collective-permute-start(bf16[768,512]{1,0:T(8,128)(2,1)} %slice.27), channel_id=1, source_target_pairs={{0,1},{1,0},{2,3},{3,2},{4,5},{5,4},{6,7},{7,6},{8,9},{9,8},{10,11... | collective-permute-start | bytes 2359304 | tf_op jit(solution)/shard_map/ppermute | solution.py:188
  11.1 0.8 slice.26
  12.1 0.9 pad_maximum_fusion
  13.0 24.1 %collective-permute-done = bf16[384,512]{1,0:T(8,128)(2,1)} collective-permute-done((bf16[384,512]{1,0:T(8,128)(2,1)}, bf16[384,512]{1,0:T(8,128)(2,1)}, u32[]{:S(2)}, u32[]{:S(2)}) %collective-permute-start) | collective-permute-done | bytes 393248 | tf_op jit(solution)/shard_map/ppermute | solution.py:188
  37.1 3.7 %collective-permute-start.6 = (bf16[1536,256]{1,0:T(8,128)(2,1)}, bf16[1536,256]{1,0:T(8,128)(2,1)S(1)}, u32[]{:S(2)}, u32[]{:S(2)}) collective-permute-start(bf16[1536,256]{1,0:T(8,128)(2,1)} %pad_maximum_fusion), channel_id=1, source_target_pairs={{0,1},{3,2},{4,5},{7,6},{8,9},{11,10},{12,13},{15,14},{16,17},{19,... | collective-permute-start | bytes 2359304 | tf_op jit(solution)/shard_map/ppermute | solution.py:188
  40.8 0.7 pad_add_fusion
  41.5 1.3 %collective-permute-start.7 = (s32[8,8]{1,0:T(8,128)S(1)}, s32[8,8]{1,0:T(8,128)S(1)}, u32[]{:S(2)}, u32[]{:S(2)}) collective-permute-start(s32[8,8]{1,0:T(8,128)S(1)} %pad_add_fusion), channel_id=1, source_target_pairs={{0,1},{3,2},{4,5},{7,6},{8,9},{11,10},{12,13},{15,14},{16,17},{19,... | collective-permute-start | bytes 776 | tf_op jit(solution)/shard_map/ppermute | solution.py:188
  42.8 0.7 broadcast_in_dim.15
  43.5 0.8 reshape.18.refs_0_.refs_4_.refs_8_
  44.3 1.4 %collective-permute-start.4 = (bf16[384,512]{1,0:T(8,128)(2,1)}, bf16[384,512]{1,0:T(8,128)(2,1)}, u32[]{:S(2)}, u32[]{:S(2)}) collective-permute-start(bf16[384,512]{1,0:T(8,128)(2,1)} %collective-permute-done), channel_id=1, source_target_pairs={{1,2},{2,1},{5,6},{6,5},{9,10},{10,9},{13,14},{14,13},{17,18},{18,... | collective-permute-start | bytes 1179656 | tf_op jit(solution)/shard_map/ppermute | solution.py:188
  45.7 11.0 %collective-permute-done.7 = s32[8,8]{1,0:T(8,128)S(1)} collective-permute-done((s32[8,8]{1,0:T(8,128)S(1)}, s32[8,8]{1,0:T(8,128)S(1)}, u32[]{:S(2)}, u32[]{:S(2)}) %collective-permute-start.7) | collective-permute-done | bytes 288 | tf_op jit(solution)/shard_map/ppermute | solution.py:188
  56.7 1.3 %add_select_fusion = (s32[4,8]{1,0:T(4,128)}, s32[4,8]{1,0:T(4,128)}, s32[4,8]{1,0:T(4,128)S(1)}) fusion(s32[8,8]{1,0:T(8,128)S(1)} %collective-permute-done.7, s32[4,8]{1,0:T(4,128)} %param.12), kind=kLoop, calls=%fused_computation.22 | loop fusion | flops 1440 | bytes 768 | tf_op jit(solution)/shard_map/jit(floor_divide)/jit(_where)/select_n | solution.py:238
  58.0 0.7 broadcast_in_dim.16
  58.7 0.8 reshape.19.refs_1_.refs_5_.refs_9_
  59.5 1.3 %broadcast_in_dim.17 = s32[4,8,64]{2,1,0:T(8,128)} broadcast(s32[4,8]{1,0:T(4,128)} %get-tuple-element.29), dimensions={0,1} | broadcast | bytes 8320 | tf_op jit(solution)/shard_map/broadcast_in_dim | solution.py:238
  60.8 1.4 %reshape.20.refs_0_ = s32[4,512]{1,0:T(4,128)} reshape(s32[4,8,64]{2,1,0:T(8,128)} %broadcast_in_dim.17) | data formatting | bytes 16384 | tf_op jit(solution)/shard_map/reshape | solution.py:238
  62.2 1.3 %broadcast_in_dim.18 = s32[4,8,64]{2,1,0:T(8,128)} broadcast(s32[4,8]{1,0:T(4,128)} %get-tuple-element.28), dimensions={0,1} | broadcast | bytes 8320 | tf_op jit(solution)/shard_map/broadcast_in_dim | solution.py:238
  63.5 1.4 %reshape.21.refs_1_ = s32[4,512]{1,0:T(4,128)} reshape(s32[4,8,64]{2,1,0:T(8,128)} %broadcast_in_dim.18) | data formatting | bytes 16384 | tf_op jit(solution)/shard_map/reshape | solution.py:238
  64.9 0.7 collective-permute-start.5
  65.6 1.2 %slice.28 = bf16[768,512]{1,0:T(8,128)(2,1)S(1)} slice(bf16[1152,512]{1,0:T(8,128)(2,1)} %collective-permute-done.2), slice={[0:768], [0:512]} | slice | bytes 1572864 | tf_op jit(solution)/shard_map/slice | solution.py:209
  66.8 1.3 %collective-permute-start.3 = (bf16[768,512]{1,0:T(8,128)(2,1)S(1)}, bf16[768,512]{1,0:T(8,128)(2,1)S(1)}, u32[]{:S(2)}, u32[]{:S(2)}) collective-permute-start(bf16[768,512]{1,0:T(8,128)(2,1)S(1)} %slice.28), channel_id=1, source_target_pairs={{1,0},{2,3},{5,4},{6,7},{9,8},{10,11},{13,12},{14,15},{17,16},{18,... | collective-permute-start | bytes 2359304 | tf_op jit(solution)/shard_map/ppermute | solution.py:188
  68.1 1.5 %fusion.10 = f32[256,512]{1,0:T(8,128)S(1)} fusion(bf16[768,512]{1,0:T(8,128)(2,1)} %collective-permute-done.1, bf16[4608,256]{1,0:T(8,128)(2,1)S(1)} %copy-done, s32[]{:T(128)S(6)} %select_n.46), kind=kOutput, calls=%fused_computation.15 | convolution fusion | flops 201326592 | bytes 1703940 | tf_op jit(solution)/shard_map/dot_general | solution.py:51
  69.6 1.8 %fusion.3 = f32[256,512]{1,0:T(8,128)S(1)} fusion(bf16[1152,512]{1,0:T(8,128)(2,1)} %collective-permute-done.2, bf16[4608,256]{1,0:T(8,128)(2,1)S(1)} %copy-done, s32[]{:T(128)S(6)} %select_n.48), kind=kOutput, calls=%fused_computation.8 | convolution fusion | flops 301989888 | bytes 2293764 | tf_op jit(solution)/shard_map/dot_general | solution.py:51
  71.5 1.4 %fusion.6 = f32[256,512]{1,0:T(8,128)S(1)} fusion(bf16[1152,512]{1,0:T(8,128)(2,1)} %collective-permute-done.2, bf16[1536,256]{1,0:T(8,128)(2,1)S(1)} %collective-permute-done.6.hidden_ref), kind=kOutput, calls=%fused_computation.11 | convolution fusion | flops 100663296 | bytes 1114112 | tf_op jit(solution)/shard_map/dot_general | solution.py:51
  72.8 1.3 %convolution_add_fusion.1.m_ref = f32[256,512]{1,0:T(8,128)S(1)} fusion(f32[256,512]{1,0:T(8,128)S(1)} %fusion.6, bf16[384,512]{1,0:T(8,128)(2,1)} %collective-permute-done.4, bf16[1536,256]{1,0:T(8,128)(2,1)S(1)} %collective-permute-done.6.hidden_ref), kind=kOutput, calls=%fused_computation.1 | convolution fusion | flops 100794368 | bytes 1638400 | tf_op jit(solution)/shard_map/dot_general | solution.py:51
  74.2 13.1 %collective-permute-done.3 = bf16[768,512]{1,0:T(8,128)(2,1)S(1)} collective-permute-done((bf16[768,512]{1,0:T(8,128)(2,1)S(1)}, bf16[768,512]{1,0:T(8,128)(2,1)S(1)}, u32[]{:S(2)}, u32[]{:S(2)}) %collective-permute-start.3) | collective-permute-done | bytes 786464 | tf_op jit(solution)/shard_map/ppermute | solution.py:188
  87.3 0.4 fusion.8
  87.8 1.4 %fusion.2 = f32[256,512]{1,0:T(8,128)S(1)} fusion(f32[256,512]{1,0:T(8,128)S(1)} %fusion.8, f32[256,512]{1,0:T(8,128)S(1)} %fusion.3, f32[256,512]{1,0:T(8,128)S(1)} %fusion.10, f32[256,512]{1,0:T(8,128)S(1)} %copy-done.6, bf16[384,512]{1,0:T(8,128)(2,1)} %collective-permute-done, bf16[4608,256]{1,0:T(8,128)(2,1)S(1)} %copy-done, s32[]{:T(128)S(6)} %select_n.45), kind=kOutput, calls=%fused_computation.6 | convolution fusion | flops 101187584 | bytes 3211268 | tf_op jit(solution)/shard_map/dot_general | solution.py:51
  89.2 1.3 %convolution_add_fusion.2.m_ref = f32[256,512]{1,0:T(8,128)S(1)} fusion(f32[256,512]{1,0:T(8,128)S(1)} %fusion.2, bf16[384,512]{1,0:T(8,128)(2,1)} %collective-permute-done.4, bf16[4608,256]{1,0:T(8,128)(2,1)S(1)} %copy-done, s32[]{:T(128)S(6)} %select_n.50), kind=kOutput, calls=%fused_computation.2 | convolution fusion | flops 100794368 | bytes 1638404 | tf_op jit(solution)/shard_map/dot_general | solution.py:51
  90.5 1.2 %shard_map.96 = (f32[256,512]{1,0:T(8,128)S(1)}, f32[64,128]{1,0:T(8,128)S(1)}) custom-call(f32[256,512]{1,0:T(8,128)S(1)} %convolution_add_fusion.1.m_ref, bf16[1536,256]{1,0:T(8,128)(2,1)S(1)} %collective-permute-done.6.hidden_ref, bf16[768,512]{1,0:T(8,128)(2,1)S(1)} %collective-permute-done.5.grad_ref, s32[4,512]{1,0:T(4,128)S(1)} %copy-done.3, ...), custom_call_target="tpu_custom_call" | custom-call | flops 400000000 | bytes 4000000 | tf_op jit(solution)/shard_map/pallas_call | solution.py:138
  91.7 1.3 %collective-permute-start.8 = (f32[64,128]{1,0:T(8,128)S(1)}, f32[64,128]{1,0:T(8,128)S(1)}, u32[]{:S(2)}, u32[]{:S(2)}) collective-permute-start(f32[64,128]{1,0:T(8,128)S(1)} %get-tuple-element.23), channel_id=1, source_target_pairs={{1,0},{2,3},{5,4},{6,7},{9,8},{10,11},{13,12},{14,15},{17,16},{18,... | collective-permute-start | bytes 98312 | tf_op jit(solution)/shard_map/ppermute | solution.py:188
  93.0 1.2 %shard_map.95 = (f32[256,512]{1,0:T(8,128)S(1)}, f32[64,128]{1,0:T(8,128)S(1)}) custom-call(f32[256,512]{1,0:T(8,128)S(1)} %convolution_add_fusion.2.m_ref, bf16[768,256]{1,0:T(8,128)(2,1)S(1)} %constant_dynamic-slice_fusion.2.hidden_ref, bf16[768,512]{1,0:T(8,128)(2,1)S(1)} %collective-permute-done.5.grad_ref, ...), custom_call_target="tpu_custom_call" | custom-call | flops 400000000 | bytes 4000000 | tf_op jit(solution)/shard_map/pallas_call | solution.py:138
  94.2 3.3 %collective-permute-done.8.refs_3_ = f32[64,128]{1,0:T(8,128)S(1)} collective-permute-done((f32[64,128]{1,0:T(8,128)S(1)}, f32[64,128]{1,0:T(8,128)S(1)}, u32[]{:S(2)}, u32[]{:S(2)}) %collective-permute-start.8) | collective-permute-done | bytes 32800 | tf_op jit(solution)/shard_map/ppermute | solution.py:188
  97.6 1.3 %collective-permute-start.9 = (f32[256,512]{1,0:T(8,128)S(1)}, f32[256,512]{1,0:T(8,128)S(1)}, u32[]{:S(2)}, u32[]{:S(2)}) collective-permute-start(f32[256,512]{1,0:T(8,128)S(1)} %get-tuple-element.26), channel_id=1, source_target_pairs={{1,0},{2,3},{5,4},{6,7},{9,8},{10,11},{13,12},{14,15},{17,16},{18,... | collective-permute-start | bytes 1572872 | tf_op jit(solution)/shard_map/ppermute | solution.py:188
  98.9 0.1 collective-permute-start.10
  98.9 1.6 %collective-permute-start.11 = (f32[64,128]{1,0:T(8,128)S(1)}, f32[64,128]{1,0:T(8,128)S(1)}, u32[]{:S(2)}, u32[]{:S(2)}) collective-permute-start(f32[64,128]{1,0:T(8,128)S(1)} %add.83.refs_0_), channel_id=1, source_target_pairs={{0,8},{4,12},{8,0},{12,4},{16,24},{20,28},{24,16},{28,20},{1,9},{5... | collective-permute-start | bytes 98312 | tf_op jit(solution)/shard_map/ppermute | solution.py:155
  100.5 0.3 collective-permute-start.12
  100.8 1.5 %collective-permute-start.13 = (f32[64,128]{1,0:T(8,128)S(1)}, f32[64,128]{1,0:T(8,128)S(1)}, u32[]{:S(2)}, u32[]{:S(2)}) collective-permute-start(f32[64,128]{1,0:T(8,128)S(1)} %add.83.refs_0_), channel_id=1, source_target_pairs={{0,16},{4,20},{8,24},{12,28},{16,0},{20,4},{24,8},{28,12},{1,17},{... | collective-permute-start | bytes 98312 | tf_op jit(solution)/shard_map/ppermute | solution.py:155
  102.3 0.2 collective-permute-start.14
  102.5 0.4 collective-permute-done.11.refs_2_
  102.9 2.7 %collective-permute-start.15 = (f32[64,128]{1,0:T(8,128)S(1)}, f32[64,128]{1,0:T(8,128)S(1)}, u32[]{:S(2)}, u32[]{:S(2)}) collective-permute-start(f32[64,128]{1,0:T(8,128)S(1)} %add.83.refs_0_), channel_id=1, source_target_pairs={{0,24},{4,28},{8,16},{12,20},{16,8},{20,12},{24,0},{28,4},{1,25},{... | collective-permute-start | bytes 98312 | tf_op jit(solution)/shard_map/ppermute | solution.py:155
  105.8 2.0 %collective-permute-done.15.refs_6_ = f32[64,128]{1,0:T(8,128)S(1)} collective-permute-done((f32[64,128]{1,0:T(8,128)S(1)}, f32[64,128]{1,0:T(8,128)S(1)}, u32[]{:S(2)}, u32[]{:S(2)}) %collective-permute-start.15) | collective-permute-done | bytes 32800 | tf_op jit(solution)/shard_map/ppermute | solution.py:155
  107.7 2.2 %collective-permute-done.16.refs_7_ = f32[64,128]{1,0:T(8,128)S(1)} collective-permute-done((f32[64,128]{1,0:T(8,128)S(1)}, f32[64,128]{1,0:T(8,128)S(1)}, u32[]{:S(2)}, u32[]{:S(2)}) %collective-permute-start.16) | collective-permute-done | bytes 32800 | tf_op jit(solution)/shard_map/ppermute | solution.py:155
  109.9 1.6 %shard_map.98 = bf16[256,512]{1,0:T(8,128)(2,1)} custom-call(f32[64,128]{1,0:T(8,128)S(1)} %add.83.refs_0_, f32[64,128]{1,0:T(8,128)S(1)} %collective-permute-done.10.refs_1_, f32[64,128]{1,0:T(8,128)S(1)} %collective-permute-done.11.refs_2_, f32[64,128]{1,0:T(8,128)S(1)} %collective-permute-done.12.refs_3_, f32[64,128]{1,0:T(8,128)S(1)} %collective-permute-done.13.refs_4_, ...), custom_call_target="tpu_custom_call" | custom-call | flops 400000000 | bytes 4000000 | tf_op jit(solution)/shard_map/pallas_call | solution.py:138
  111.6 1.7 %shard_map.97 = f32[256,512]{1,0:T(8,128)} custom-call(f32[256,512]{1,0:T(8,128)S(1)} %get-tuple-element.21.refs_0_, f32[256,512]{1,0:T(8,128)S(1)} %collective-permute-done.9.refs_1_, f32[64,128]{1,0:T(8,128)S(1)} %get-tuple-element.27.refs_2_, f32[64,128]{1,0:T(8,128)S(1)} %collective-permute-done.8.refs_3_, s32[4,512]{1,0:T(4,128)S(1)} %reshape.18.refs_0_.refs_4_.refs_8_, ...), custom_call_target="tpu_custom_call" | custom-call | flops 400000000 | bytes 4000000 | tf_op jit(solution)/shard_map/pallas_call | solution.py:138
  (33 shorter events, 0.3 us)
Async XLA Ops:
  0.6 1.9 %copy-start = (bf16[4608,256]{1,0:T(8,128)(2,1)S(1)}, bf16[4608,256]{1,0:T(8,128)(2,1)}, u32[]{:S(2)}) copy-start(bf16[4608,256]{1,0:T(8,128)(2,1)} %param.8) | copy-start | bytes 7077892
  0.6 4.6 %copy-start.5 = (bf16[1152,512]{1,0:T(8,128)(2,1)S(1)}, bf16[1152,512]{1,0:T(8,128)(2,1)}, u32[]{:S(2)}) copy-start(bf16[1152,512]{1,0:T(8,128)(2,1)} %param.9) | copy-start | bytes 3538948
  0.7 65.0 %collective-permute-start.2 = (bf16[1152,512]{1,0:T(8,128)(2,1)}, bf16[1152,512]{1,0:T(8,128)(2,1)}, u32[]{:S(2)}, u32[]{:S(2)}) collective-permute-start(bf16[1152,512]{1,0:T(8,128)(2,1)} %param.9), channel_id=1, source_target_pairs={{1,2},{2,1},{5,6},{6,5},{9,10},{10,9},{13,14},{14,13},{17,18},{18,... | collective-permute-start | bytes 3538952 | tf_op jit(solution)/shard_map/ppermute | solution.py:188
  2.5 9.4 %copy-start.7 = (s32[4,8]{1,0:T(4,128)S(1)}, s32[4,8]{1,0:T(4,128)}, u32[]{:S(2)}) copy-start(s32[4,8]{1,0:T(4,128)} %param.11) | copy-start | bytes 388
  6.2 30.9 %collective-permute-start.1 = (bf16[768,512]{1,0:T(8,128)(2,1)}, bf16[768,512]{1,0:T(8,128)(2,1)}, u32[]{:S(2)}, u32[]{:S(2)}) collective-permute-start(bf16[768,512]{1,0:T(8,128)(2,1)} %slice.27), channel_id=1, source_target_pairs={{0,1},{1,0},{2,3},{3,2},{4,5},{5,4},{6,7},{7,6},{8,9},{9,8},{10,11... | collective-permute-start | bytes 2359304 | tf_op jit(solution)/shard_map/ppermute | solution.py:188
  11.9 25.2 %collective-permute-start = (bf16[384,512]{1,0:T(8,128)(2,1)}, bf16[384,512]{1,0:T(8,128)(2,1)}, u32[]{:S(2)}, u32[]{:S(2)}) collective-permute-start(bf16[384,512]{1,0:T(8,128)(2,1)} %slice.26), channel_id=1, source_target_pairs={{0,1},{1,0},{2,3},{3,2},{4,5},{5,4},{6,7},{7,6},{8,9},{9,8},{10,11... | collective-permute-start | bytes 1179656 | tf_op jit(solution)/shard_map/ppermute | solution.py:188
  37.1 34.3 %collective-permute-start.6 = (bf16[1536,256]{1,0:T(8,128)(2,1)}, bf16[1536,256]{1,0:T(8,128)(2,1)S(1)}, u32[]{:S(2)}, u32[]{:S(2)}) collective-permute-start(bf16[1536,256]{1,0:T(8,128)(2,1)} %pad_maximum_fusion), channel_id=1, source_target_pairs={{0,1},{3,2},{4,5},{7,6},{8,9},{11,10},{12,13},{15,14},{16,17},{19,... | collective-permute-start | bytes 2359304 | tf_op jit(solution)/shard_map/ppermute | solution.py:188
  41.5 15.2 %collective-permute-start.7 = (s32[8,8]{1,0:T(8,128)S(1)}, s32[8,8]{1,0:T(8,128)S(1)}, u32[]{:S(2)}, u32[]{:S(2)}) collective-permute-start(s32[8,8]{1,0:T(8,128)S(1)} %pad_add_fusion), channel_id=1, source_target_pairs={{0,1},{3,2},{4,5},{7,6},{8,9},{11,10},{12,13},{15,14},{16,17},{19,... | collective-permute-start | bytes 776 | tf_op jit(solution)/shard_map/ppermute | solution.py:188
  44.3 28.6 %collective-permute-start.4 = (bf16[384,512]{1,0:T(8,128)(2,1)}, bf16[384,512]{1,0:T(8,128)(2,1)}, u32[]{:S(2)}, u32[]{:S(2)}) collective-permute-start(bf16[384,512]{1,0:T(8,128)(2,1)} %collective-permute-done), channel_id=1, source_target_pairs={{1,2},{2,1},{5,6},{6,5},{9,10},{10,9},{13,14},{14,13},{17,18},{18,... | collective-permute-start | bytes 1179656 | tf_op jit(solution)/shard_map/ppermute | solution.py:188
  64.9 25.6 %collective-permute-start.5 = (bf16[768,512]{1,0:T(8,128)(2,1)}, bf16[768,512]{1,0:T(8,128)(2,1)S(1)}, u32[]{:S(2)}, u32[]{:S(2)}) collective-permute-start(bf16[768,512]{1,0:T(8,128)(2,1)} %collective-permute-done.1), channel_id=1, source_target_pairs={{1,2},{2,1},{5,6},{6,5},{9,10},{10,9},{13,14},{14,13},{17,18},{18,... | collective-permute-start | bytes 2359304 | tf_op jit(solution)/shard_map/ppermute | solution.py:188
  66.8 20.5 %collective-permute-start.3 = (bf16[768,512]{1,0:T(8,128)(2,1)S(1)}, bf16[768,512]{1,0:T(8,128)(2,1)S(1)}, u32[]{:S(2)}, u32[]{:S(2)}) collective-permute-start(bf16[768,512]{1,0:T(8,128)(2,1)S(1)} %slice.28), channel_id=1, source_target_pairs={{1,0},{2,3},{5,4},{6,7},{9,8},{10,11},{13,12},{14,15},{17,16},{18,... | collective-permute-start | bytes 2359304 | tf_op jit(solution)/shard_map/ppermute | solution.py:188
  71.4 16.3 %copy-start.6 = (f32[256,512]{1,0:T(8,128)S(1)}, f32[256,512]{1,0:T(8,128)}, u32[]{:S(2)}) copy-start(f32[256,512]{1,0:T(8,128)} %convolution_add_fusion) | copy-start | bytes 1572868
  87.7 2.8 %copy-start.1 = (bf16[2,256,256]{2,1,0:T(8,128)(2,1)S(1)}, bf16[2,256,256]{2,1,0:T(8,128)(2,1)}, u32[]{:S(2)}) copy-start(bf16[2,256,256]{2,1,0:T(8,128)(2,1)} %constant.67.clone.refs_3_.refs_4_.refs_7_.refs_8_.refs_11_.refs_12_) | copy-start | bytes 786436
  87.7 2.8 %copy-start.2 = (bf16[512,128]{1,0:T(8,128)(2,1)S(1)}, bf16[512,128]{1,0:T(8,128)(2,1)}, u32[]{:S(2)}) copy-start(bf16[512,128]{1,0:T(8,128)(2,1)} %constant.66.clone.refs_2_.refs_6_.refs_10_) | copy-start | bytes 393220
  87.7 2.8 %copy-start.3 = (s32[4,512]{1,0:T(4,128)S(1)}, s32[4,512]{1,0:T(4,128)}, u32[]{:S(2)}) copy-start(s32[4,512]{1,0:T(4,128)} %reshape.20.refs_0_) | copy-start | bytes 24580
  87.7 2.8 %copy-start.4 = (s32[4,512]{1,0:T(4,128)S(1)}, s32[4,512]{1,0:T(4,128)}, u32[]{:S(2)}) copy-start(s32[4,512]{1,0:T(4,128)} %reshape.21.refs_1_) | copy-start | bytes 24580
  91.7 5.8 %collective-permute-start.8 = (f32[64,128]{1,0:T(8,128)S(1)}, f32[64,128]{1,0:T(8,128)S(1)}, u32[]{:S(2)}, u32[]{:S(2)}) collective-permute-start(f32[64,128]{1,0:T(8,128)S(1)} %get-tuple-element.23), channel_id=1, source_target_pairs={{1,0},{2,3},{5,4},{6,7},{9,8},{10,11},{13,12},{14,15},{17,16},{18,... | collective-permute-start | bytes 98312 | tf_op jit(solution)/shard_map/ppermute | solution.py:188
  97.6 14.0 %collective-permute-start.9 = (f32[256,512]{1,0:T(8,128)S(1)}, f32[256,512]{1,0:T(8,128)S(1)}, u32[]{:S(2)}, u32[]{:S(2)}) collective-permute-start(f32[256,512]{1,0:T(8,128)S(1)} %get-tuple-element.26), channel_id=1, source_target_pairs={{1,0},{2,3},{5,4},{6,7},{9,8},{10,11},{13,12},{14,15},{17,16},{18,... | collective-permute-start | bytes 1572872 | tf_op jit(solution)/shard_map/ppermute | solution.py:188
  98.9 3.5 %collective-permute-start.10 = (f32[64,128]{1,0:T(8,128)S(1)}, f32[64,128]{1,0:T(8,128)S(1)}, u32[]{:S(2)}, u32[]{:S(2)}) collective-permute-start(f32[64,128]{1,0:T(8,128)S(1)} %add.83.refs_0_), channel_id=1, source_target_pairs={{0,4},{4,0},{8,12},{12,8},{16,20},{20,16},{24,28},{28,24},{1,5},{5... | collective-permute-start | bytes 98312 | tf_op jit(solution)/shard_map/ppermute | solution.py:155
  98.9 4.0 %collective-permute-start.11 = (f32[64,128]{1,0:T(8,128)S(1)}, f32[64,128]{1,0:T(8,128)S(1)}, u32[]{:S(2)}, u32[]{:S(2)}) collective-permute-start(f32[64,128]{1,0:T(8,128)S(1)} %add.83.refs_0_), channel_id=1, source_target_pairs={{0,8},{4,12},{8,0},{12,4},{16,24},{20,28},{24,16},{28,20},{1,9},{5... | collective-permute-start | bytes 98312 | tf_op jit(solution)/shard_map/ppermute | solution.py:155
  100.5 5.2 %collective-permute-start.12 = (f32[64,128]{1,0:T(8,128)S(1)}, f32[64,128]{1,0:T(8,128)S(1)}, u32[]{:S(2)}, u32[]{:S(2)}) collective-permute-start(f32[64,128]{1,0:T(8,128)S(1)} %add.83.refs_0_), channel_id=1, source_target_pairs={{0,12},{4,8},{8,4},{12,0},{16,28},{20,24},{24,20},{28,16},{1,13},{... | collective-permute-start | bytes 98312 | tf_op jit(solution)/shard_map/ppermute | solution.py:155
  100.8 4.9 %collective-permute-start.13 = (f32[64,128]{1,0:T(8,128)S(1)}, f32[64,128]{1,0:T(8,128)S(1)}, u32[]{:S(2)}, u32[]{:S(2)}) collective-permute-start(f32[64,128]{1,0:T(8,128)S(1)} %add.83.refs_0_), channel_id=1, source_target_pairs={{0,16},{4,20},{8,24},{12,28},{16,0},{20,4},{24,8},{28,12},{1,17},{... | collective-permute-start | bytes 98312 | tf_op jit(solution)/shard_map/ppermute | solution.py:155
  102.3 3.4 %collective-permute-start.14 = (f32[64,128]{1,0:T(8,128)S(1)}, f32[64,128]{1,0:T(8,128)S(1)}, u32[]{:S(2)}, u32[]{:S(2)}) collective-permute-start(f32[64,128]{1,0:T(8,128)S(1)} %add.83.refs_0_), channel_id=1, source_target_pairs={{0,20},{4,16},{8,28},{12,24},{16,4},{20,0},{24,12},{28,8},{1,21},{... | collective-permute-start | bytes 98312 | tf_op jit(solution)/shard_map/ppermute | solution.py:155
  102.9 4.8 %collective-permute-start.15 = (f32[64,128]{1,0:T(8,128)S(1)}, f32[64,128]{1,0:T(8,128)S(1)}, u32[]{:S(2)}, u32[]{:S(2)}) collective-permute-start(f32[64,128]{1,0:T(8,128)S(1)} %add.83.refs_0_), channel_id=1, source_target_pairs={{0,24},{4,28},{8,16},{12,20},{16,8},{20,12},{24,0},{28,4},{1,25},{... | collective-permute-start | bytes 98312 | tf_op jit(solution)/shard_map/ppermute | solution.py:155
  105.7 4.2 %collective-permute-start.16 = (f32[64,128]{1,0:T(8,128)S(1)}, f32[64,128]{1,0:T(8,128)S(1)}, u32[]{:S(2)}, u32[]{:S(2)}) collective-permute-start(f32[64,128]{1,0:T(8,128)S(1)} %add.83.refs_0_), channel_id=1, source_target_pairs={{0,28},{4,24},{8,20},{12,16},{16,12},{20,8},{24,4},{28,0},{1,29},{... | collective-permute-start | bytes 98312 | tf_op jit(solution)/shard_map/ppermute | solution.py:155
where the time goes:
time: 114 us; the launch traced here: 113 us
  waiting for transfers between devices  56.2 us (49%)
  starting transfers between devices  24.2 us (21%)
  matrix products  11.8 us (10%)
  local copies, waits for them, and re-layouts  11.4 us (10%)
  Pallas kernels  5.77 us (5%)
  other arithmetic  2.94 us (3%)
    ppermute x10, waiting for transfers between devices, send(): return lax.ppermute(x, 'tp', perm)  51.6 us
    ppermute x10, starting transfers between devices, send(): return lax.ppermute(x, 'tp', perm)  17.7 us
    dot_general x8, matrix products, dot(): lax.dot_general(a, b, (dims, ((), ())), preferred_element_type=jnp.float32)  11.8 us
    ppermute x7, starting transfers between devices, spread_sum(): lax.ppermute(x, axis, [(i, i ^ stride * k) for i in range(size)])  6.45 us
    pallas_call x4, Pallas kernels, call(): pl.pallas_call(kernel, out_shape=out_shapes, compiler_params=pltpu.Compil...  5.77 us
    ppermute x7, waiting for transfers between devices, spread_sum(): lax.ppermute(x, axis, [(i, i ^ stride * k) for i in range(size)])  4.59 us
    reshape x4, local copies, waits for them, and re-layouts, make_tables(): jnp.repeat(x.astype(jnp.int32) // band, order, axis=1)  4.36 us
    broadcast_in_dim x4, local copies, waits for them, and re-layouts, make_tables(): jnp.repeat(x.astype(jnp.int32) // band, order, axis=1)  4.03 us
  transfers between devices with their start and end apart: 17, of which 7 were waited for; matrix products, arithmetic and copies ran while one was open for 23% of the time, Pallas kernels for 3%

commit v1 on v0

--- a/solution.py
+++ b/solution.py
@@ -71,33 +71,40 @@
     return parts[0] if len(parts) == 1 else jnp.concatenate(parts, axis=1)
 
 
-def column_mask(row, cols_ref, width):
-    group = lax.rem(lax.broadcasted_iota(jnp.int32, (band, width), 1), order) // band
-    return group == cols_ref[row : row + 1, :]
-
-
-def lifted(folded, rows_ref, cols_ref, fold_ref, row_basis_ref, column_basis_ref):
-    width = cols_ref.shape[1]
+def place_of_blocks(places_ref, row, width):
+    block = lax.broadcasted_iota(jnp.int32, (1, width), 1) // order
+    out = jnp.zeros((1, width), jnp.int32)
+    for column in range(width // order):
+        out = jnp.where(block == column, places_ref[row, column], out)
+    return out
+
+
+def masks_of(places_ref, width):
+    count = places_ref.shape[0] // 2
+    group = lax.rem(lax.broadcasted_iota(jnp.int32, (band, width), 1), order) // band * band
+    rows = [place_of_blocks(places_ref, row, width) for row in range(count)]
+    return [(at, group == place_of_blocks(places_ref, count + row, width)) for row, at in enumerate(rows)]
+
+
+def lifted(folded, places_ref, fold_ref, row_basis_ref, column_basis_ref):
     spread = sum(dot(part, fold_ref[...], ((1,), (1,))) for part in split3(folded))
     pieces = []
-    for row in range(rows_ref.shape[0]):
-        inside = jnp.where(column_mask(row, cols_ref, width), spread[row * band : (row + 1) * band], 0.0)
-        for step in range(steps):
-            pieces.append(jnp.where(rows_ref[row : row + 1, :] == step, inside, 0.0))
+    for row, (at, inside) in enumerate(masks_of(places_ref, fold_ref.shape[0])):
+        part = jnp.where(inside, spread[row * band : (row + 1) * band], 0.0)
+        pieces += [jnp.where(at == step * band, part, 0.0) for step in range(steps)]
     coefficients = jnp.concatenate(pieces, axis=0)
     return on_columns(column_basis_ref, on_rows(row_basis_ref, coefficients, True), True)
 
 
-def bands_of(x, rows_ref, cols_ref, fold_ref, row_basis_ref, column_basis_ref):
-    width = cols_ref.shape[1]
+def bands_of(x, places_ref, fold_ref, row_basis_ref, column_basis_ref):
     coefficients = on_columns(column_basis_ref, on_rows(row_basis_ref, x, False), False)
     pieces = []
-    for row in range(rows_ref.shape[0]):
-        taken = jnp.zeros((band, width), jnp.float32)
+    for row, (at, inside) in enumerate(masks_of(places_ref, fold_ref.shape[0])):
+        taken = jnp.zeros(inside.shape, jnp.float32)
         for step in range(steps):
-            at = row * order + step * band
-            taken = jnp.where(rows_ref[row : row + 1, :] == step, coefficients[at : at + band], taken)
-        pieces.append(jnp.where(column_mask(row, cols_ref, width), taken, 0.0))
+            start = row * order + step * band
+            taken = jnp.where(at == step * band, coefficients[start : start + band], taken)
+        pieces.append(jnp.where(inside, taken, 0.0))
     taken = jnp.concatenate(pieces, axis=0)
     return sum(dot(part, fold_ref[...]) for part in split3(taken))
 
@@ -121,11 +128,10 @@
 
 
 def update_kernel(*refs):
-    *part_refs, rows_ref, cols_ref, fold_ref, row_basis_ref, column_basis_ref, out_ref = refs
+    *part_refs, places_ref, fold_ref, row_basis_ref, column_basis_ref, out_ref = refs
     parts = [ref[...] for ref in part_refs]
-    out_ref[...] = lifted(
-        pair_sum(parts), rows_ref, cols_ref, fold_ref, row_basis_ref, column_basis_ref
-    ).astype(out_ref.dtype)
+    bands = pair_sum(parts)
+    out_ref[...] = lifted(bands, places_ref, fold_ref, row_basis_ref, column_basis_ref).astype(out_ref.dtype)
 
 
 def pair_sum(parts):
@@ -135,9 +141,11 @@
 
 
 def call(kernel, out_shapes, *operands):
+    spaces = [pltpu.SMEM if x.dtype == jnp.int32 else pltpu.VMEM for x in operands]
     return pl.pallas_call(
         kernel,
         out_shape=out_shapes,
+        in_specs=[pl.BlockSpec(memory_space=space) for space in spaces],
         compiler_params=pltpu.CompilerParams(vmem_limit_bytes=32 * 2**20),
         cost_estimate=pl.CostEstimate(flops=4 * 10**8, bytes_accessed=4 * 10**6, transcendentals=0),
     )(*operands)
@@ -149,7 +157,7 @@
         return [lax.psum(x, axis)]
     stride, parts = 1, [x]
     while stride < size:
-        count = min(8, size // stride)
+        count = min(4, size // stride)
         x = pair_sum(parts)
         parts = [x] + [
             lax.ppermute(x, axis, [(i, i ^ (stride * k)) for i in range(size)]) for k in range(1, count)
@@ -166,20 +174,20 @@
     return lax.optimization_barrier((x, *others))[0]
 
 
-def gathered(hidden, out_grad, carried, tables, make_tables, band_rows, band_start_columns):
+def gathered(hidden, out_grad, carried, places, matrices):
     m = carried + product(hidden, lax.all_gather(out_grad, "tp", axis=0, tiled=True))
     folded = jax.ShapeDtypeStruct((m.shape[0] // steps, m.shape[1] // steps), jnp.float32)
-    return [m], [call(bands_kernel, folded, m, *tables)]
-
-
-def lined(hidden, out_grad, carried, tables, make_tables, band_rows, band_start_columns):
+    return [m], [call(bands_kernel, folded, m, places, *matrices)]
+
+
+def lined(hidden, out_grad, carried, places, matrices):
     tok = out_grad.shape[0]
     me = lax.axis_index("tp")
     left = me < 2
     cross = jnp.where(left, 2, 1)
     far = jnp.where(left, 3, 0)
-    first = max(tok // 3 // 128 * 128, 16)
-    handed = tok - first
+    first = max(tok // 4 // 128 * 128, 16)
+    handed = tok - max(tok // 3 // 128 * 128, 16)
 
     def rows_of(part, start=0, stop=tok):
         return lax.dynamic_slice_in_dim(hidden, part * tok + start, stop - start, 0)
@@ -189,40 +197,39 @@
 
     both_ways = [(0, 1), (1, 0), (2, 3), (3, 2)]
     across = [(1, 2), (2, 1)]
+    over_one = [(0, 2), (3, 1)]
     outward = [(1, 0), (2, 3)]
     inward = [(0, 1), (3, 2)]
 
+    head, rest = out_grad[:first], out_grad[first:]
     cross_grad = send(out_grad, across)
-    pair_head = send(out_grad[:first], both_ways)
+    far_head = send(head, over_one)
+    pair_rest = send(rest, both_ways)
     m = carried + product(rows_of(me), out_grad)
-    pair_rest = send(after(out_grad, m)[first:], both_ways)
-
-    far_head = send(pair_head, across)
-    places = jnp.concatenate([band_rows, band_start_columns], axis=0)
-    places = send(after(places, pair_head), inward)
-    end_tables = make_tables(*(places[i * band_rows.shape[0] :][: band_rows.shape[0]] for i in range(2)))
-    pair_rest = after(pair_rest, pair_head)
+    helped_hidden = jnp.concatenate([rows_of(cross, handed), rows_of(far)], axis=0)
+    pair_rest, m, head, helped_hidden = lax.optimization_barrier((pair_rest, m, head, helped_hidden))
     far_rest = send(pair_rest, across)
-    helped_hidden = jnp.concatenate([rows_of(cross, handed), rows_of(far)], axis=0)
-    helped_hidden = send(after(helped_hidden, pair_rest), inward)
-    cross_grad = after(cross_grad, pair_rest)
+    pair_head = send(head, both_ways)
+    helped_hidden = send(helped_hidden, inward)
+    end_places = send(after(places, pair_head), inward)
     passed_grad = send(cross_grad[:handed], outward)
 
     m = m + product(rows_of(me ^ 1, 0, first), pair_head) + product(rows_of(me ^ 1, first), pair_rest)
-    m = m + product(rows_of(cross), cross_grad)
-    m = m + product(rows_of(cross, 0, handed), passed_grad) + product(rows_of(far, 0, first), far_head)
+    m = m + product(rows_of(cross), cross_grad) + product(rows_of(far, 0, first), far_head)
+    m = m + product(rows_of(cross, 0, handed), passed_grad)
     helped = product(helped_hidden[: tok - handed], cross_grad[handed:])
     helped = helped + product(helped_hidden[tok - handed :][:first], far_head)
-    far_rest = after(far_rest, m, helped, tables, end_tables)
+    far_rest = after(far_rest, m, helped)
 
     full = jax.ShapeDtypeStruct(m.shape, jnp.float32)
     folded = jax.ShapeDtypeStruct((m.shape[0] // steps, m.shape[1] // steps), jnp.float32)
     helped, helped_bands = call(
-        last_rows_kernel, (full, folded), helped, helped_hidden, far_rest, *end_tables
-    )
-    helped_bands = send(helped_bands, outward)
-    m, bands = call(last_rows_kernel, (full, folded), m, rows_of(far, first), far_rest, *tables)
-    helped_bands, bands = lax.optimization_barrier((helped_bands, bands))
+        last_rows_kernel, (full, folded), helped, helped_hidden, far_rest, end_places, *matrices
+    )
+    m, helped_bands = lax.optimization_barrier((m, helped_bands))
+    sent_bands = send(helped_bands, outward)
+    m, bands = call(last_rows_kernel, (full, folded), m, rows_of(far, first), far_rest, places, *matrices)
+    helped_bands, bands = lax.optimization_barrier((sent_bands, bands))
     helped = send(after(helped, helped_bands), outward)
     return [m, helped], [bands, helped_bands]
 
@@ -233,15 +240,9 @@
     matrices = tuple(
         jnp.asarray(x) for x in (fold_matrix(col_count), diagonal_blocks(row_count), diagonal_blocks(col_count))
     )
-
-    def make_tables(*places):
-        return tuple(jnp.repeat(x.astype(jnp.int32) // band, order, axis=1) for x in places) + matrices
-
-    tables = make_tables(band_rows, band_start_columns)
+    places = jnp.concatenate([band_rows, band_start_columns], axis=0).astype(jnp.int32)
     form = lined if lax.axis_size("tp") == 4 else gathered
-    m_parts, band_parts = form(
-        hidden, out_grad, decay_rate * momentum[0], tables, make_tables, band_rows, band_start_columns
-    )
+    m_parts, band_parts = form(hidden, out_grad, decay_rate * momentum[0], places, matrices)
     parts = spread_sum(pair_sum(band_parts), "rep")
     shape = (row_count, col_count)
     momentum_out = call(
@@ -249,9 +250,10 @@
         jax.ShapeDtypeStruct(shape, jnp.float32),
         *m_parts,
         *band_parts,
-        *tables,
-    )
-    update = call(update_kernel, jax.ShapeDtypeStruct(shape, jnp.bfloat16), *parts, *tables)
+        places,
+        *matrices,
+    )
+    update = call(update_kernel, jax.ShapeDtypeStruct(shape, jnp.bfloat16), *parts, places, *matrices)
     return (momentum_out[None], update)
 
 

time: 114 us -> 92 us (0.81)
  waiting for transfers between devices: 56.2 us -> 38.7 us
  local copies, waits for them, and re-layouts: 11.4 us -> 5.82 us
  Pallas kernels: 5.77 us -> 8.33 us
  other arithmetic: 2.94 us -> 1 us
  starting transfers between devices: 24.2 us -> 26.1 us
  matrix products: 11.8 us -> 10.5 us
    ppermute x10, waiting for transfers between devices: 51.6 us -> 34.2 us  [send(): return lax.ppermute(x, 'tp', perm)]
    ppermute x10, starting transfers between devices: 17.7 us -> 22.6 us  [send(): return lax.ppermute(x, 'tp', perm)]
    reshape x4 -> x0, local copies, waits for them, and re-layouts: 4.36 us -> none  [make_tables(): jnp.repeat(x.astype(jnp.int32) // band, order, axis=1)]
    broadcast_in_dim x4 -> x0, local copies, waits for them, and re-layouts: 4.03 us -> none  [make_tables(): jnp.repeat(x.astype(jnp.int32) // band, order, axis=1)]
    ppermute x7 -> x4, starting transfers between devices: 6.45 us -> 3.5 us  [spread_sum(): lax.ppermute(x, axis, [(i, i ^ stride * k) for i in range(size)])]
    pallas_call x4, Pallas kernels: 5.77 us -> 8.33 us  [call(): pl.pallas_call(kernel, out_shape=out_shapes, in_specs=[pl.BlockSpec(memor...]
    slice x2, local copies, waits for them, and re-layouts: 1.71 us -> 3.83 us  [lined(): head, rest = (out_grad[:first], out_grad[first:])]
    dot_general x8, matrix products: 11.8 us -> 10.5 us  [dot(): lax.dot_general(a, b, (dims, ((), ())), preferred_element_type=jnp.float32)]
  transfers between devices with their start and end apart: 17 -> 14, of which waited for: 7 -> 8; matrix products, arithmetic and copies ran while one was open for 23% -> 19% of each run, Pallas kernels for 3% -> 5%
where the time goes in v1:
time: 92 us; the launch traced here: 91.4 us
  waiting for transfers between devices  38.7 us (42%)
  starting transfers between devices  26.1 us (28%)
  matrix products  10.5 us (11%)
  Pallas kernels  8.33 us (9%)
  local copies, waits for them, and re-layouts  5.82 us (6%)
  other arithmetic  1 us (1%)
  between operations  0.92 us (1%)
    ppermute x10, waiting for transfers between devices, send(): return lax.ppermute(x, 'tp', perm)  34.2 us
    ppermute x10, starting transfers between devices, send(): return lax.ppermute(x, 'tp', perm)  22.6 us
    dot_general x8, matrix products, dot(): lax.dot_general(a, b, (dims, ((), ())), preferred_element_type=jnp.float32)  10.5 us
    pallas_call x4, Pallas kernels, call(): pl.pallas_call(kernel, out_shape=out_shapes, in_specs=[pl.BlockSpec(memor...  8.33 us
    ppermute x4, waiting for transfers between devices, spread_sum(): lax.ppermute(x, axis, [(i, i ^ stride * k) for i in range(size)])  4.58 us
    slice x2, local copies, waits for them, and re-layouts, lined(): head, rest = (out_grad[:first], out_grad[first:])  3.83 us
    ppermute x4, starting transfers between devices, spread_sum(): lax.ppermute(x, axis, [(i, i ^ stride * k) for i in range(size)])  3.5 us
  transfers between devices with their start and end apart: 14, of which 8 were waited for; matrix products, arithmetic and copies ran while one was open for 19% of the time, Pallas kernels for 5%

profile of v1, /device:TPU:0, one launch (start us, length us, event | category | flops | bytes accessed | tf_op | source)
XLA Modules:
  0.0 91.4 jit_solution(5595886776619112471)
XLA Ops:
  0.6 0.0 copy-start
  0.6 1.8 %collective-permute-start.2 = (bf16[1152,512]{1,0:T(8,128)(2,1)}, bf16[1152,512]{1,0:T(8,128)(2,1)}, u32[]{:S(2)}, u32[]{:S(2)}) collective-permute-start(bf16[1152,512]{1,0:T(8,128)(2,1)} %param.9), channel_id=1, source_target_pairs={{1,2},{2,1},{5,6},{6,5},{9,10},{10,9},{13,14},{14,13},{17,18},{18,... | collective-permute-start | bytes 3538952 | tf_op jit(solution)/shard_map/ppermute | solution.py:196
  2.5 1.7 %slice.21 = bf16[256,512]{1,0:T(8,128)(2,1)} slice(bf16[1152,512]{1,0:T(8,128)(2,1)} %param.9), slice={[0:256], [0:512]} | slice | bytes 524288 | tf_op jit(solution)/shard_map/slice | solution.py:204
  4.2 7.3 %collective-permute-start.3 = (bf16[256,512]{1,0:T(8,128)(2,1)}, bf16[256,512]{1,0:T(8,128)(2,1)}, u32[]{:S(2)}, u32[]{:S(2)}) collective-permute-start(bf16[256,512]{1,0:T(8,128)(2,1)} %slice.21), channel_id=1, source_target_pairs={{0,2},{3,1},{4,6},{7,5},{8,10},{11,9},{12,14},{15,13},{16,18},{19,... | collective-permute-start | bytes 786440 | tf_op jit(solution)/shard_map/ppermute | solution.py:196
  11.5 2.2 %slice.20 = bf16[896,512]{1,0:T(8,128)(2,1)} slice(bf16[1152,512]{1,0:T(8,128)(2,1)} %param.9), slice={[256:1152], [0:512]} | slice | bytes 1835008 | tf_op jit(solution)/shard_map/slice | solution.py:204
  13.6 0.0 collective-permute-start
  13.7 0.0 copy-start.4
  13.7 0.0 copy-start.5
  13.8 0.7 constant_dynamic-slice_fusion.2
  14.4 2.7 %convolution_add_fusion = f32[256,512]{1,0:T(8,128)} fusion(bf16[1152,512]{1,0:T(8,128)(2,1)} %param.9, bf16[4608,256]{1,0:T(8,128)(2,1)S(1)} %copy-done, s32[]{:T(128)S(6)} %select_n.30, f32[1,256,512]{2,1,0:T(8,128)} %param.10), kind=kOutput, calls=%fused_computation | convolution fusion | flops 302252032 | bytes 2818052 | tf_op jit(solution)/shard_map/dot_general | solution.py:51
  17.2 1.0 %pad_maximum_fusion = bf16[1536,256]{1,0:T(8,128)(2,1)S(1)} fusion(bf16[1152,256]{1,0:T(8,128)(2,1)S(1)} %constant_dynamic-slice_fusion.1, bf16[384,256]{1,0:T(8,128)(2,1)} %constant_dynamic-slice_fusion.2), kind=kLoop, calls=%fused_computation.2 | loop fusion | flops 1572864 | bytes 1572864 | tf_op jit(solution)/shard_map/concatenate | solution.py:209
  18.2 17.9 %collective-permute-done = bf16[896,512]{1,0:T(8,128)(2,1)} collective-permute-done((bf16[896,512]{1,0:T(8,128)(2,1)}, bf16[896,512]{1,0:T(8,128)(2,1)}, u32[]{:S(2)}, u32[]{:S(2)}) %collective-permute-start) | collective-permute-done | bytes 917536 | tf_op jit(solution)/shard_map/ppermute | solution.py:196
  36.1 2.5 %collective-permute-start.1 = (bf16[256,512]{1,0:T(8,128)(2,1)}, bf16[256,512]{1,0:T(8,128)(2,1)S(1)}, u32[]{:S(2)}, u32[]{:S(2)}) collective-permute-start(bf16[256,512]{1,0:T(8,128)(2,1)} %slice.21), channel_id=1, source_target_pairs={{0,1},{1,0},{2,3},{3,2},{4,5},{5,4},{6,7},{7,6},{8,9},{9,8},{10,11... | collective-permute-start | bytes 786440 | tf_op jit(solution)/shard_map/ppermute | solution.py:196
  38.5 1.9 %collective-permute-start.5 = (bf16[1536,256]{1,0:T(8,128)(2,1)S(1)}, bf16[1536,256]{1,0:T(8,128)(2,1)S(1)}, u32[]{:S(2)}, u32[]{:S(2)}) collective-permute-start(bf16[1536,256]{1,0:T(8,128)(2,1)S(1)} %pad_maximum_fusion), channel_id=1, source_target_pairs={{0,1},{3,2},{4,5},{7,6},{8,9},{11,10},{12,13},{15,14},{16,17},{19,... | collective-permute-start | bytes 2359304 | tf_op jit(solution)/shard_map/ppermute | solution.py:196
  40.5 0.0 collective-permute-done.3
  40.5 1.2 %fusion.13 = f32[256,512]{1,0:T(8,128)S(1)} fusion(bf16[256,512]{1,0:T(8,128)(2,1)} %collective-permute-done.3, bf16[4608,256]{1,0:T(8,128)(2,1)S(1)} %copy-done, s32[]{:T(128)S(6)} %select_n.34), kind=kOutput, calls=%fused_computation.15 | convolution fusion | flops 67108864 | bytes 917508 | tf_op jit(solution)/shard_map/dot_general | solution.py:51
  41.7 0.7 collective-permute-start.6
  42.4 1.6 %fusion.3 = f32[256,512]{1,0:T(8,128)S(1)} fusion(bf16[896,512]{1,0:T(8,128)(2,1)} %collective-permute-done, bf16[4608,256]{1,0:T(8,128)(2,1)S(1)} %copy-done, s32[]{:T(128)S(6)} %select_n.36), kind=kOutput, calls=%fused_computation.7 | convolution fusion | flops 234881024 | bytes 1900548 | tf_op jit(solution)/shard_map/dot_general | solution.py:51
  44.1 1.5 %collective-permute-done.1 = bf16[256,512]{1,0:T(8,128)(2,1)S(1)} collective-permute-done((bf16[256,512]{1,0:T(8,128)(2,1)}, bf16[256,512]{1,0:T(8,128)(2,1)S(1)}, u32[]{:S(2)}, u32[]{:S(2)}) %collective-permute-start.1) | collective-permute-done | bytes 262176 | tf_op jit(solution)/shard_map/ppermute | solution.py:196
  45.6 4.3 %collective-permute-start.7 = (s32[8,8]{1,0:T(8,128)S(1)}, s32[8,8]{1,0:T(8,128)S(1)}, u32[]{:S(2)}, u32[]{:S(2)}) collective-permute-start(s32[8,8]{1,0:T(8,128)S(1)} %pad_add_fusion.refs_0_.refs_4_.refs_2_), channel_id=1, source_target_pairs={{0,1},{3,2},{4,5},{7,6},{8,9},{11,10},{12,13},{15,14},{16,17},{19,... | collective-permute-start | bytes 776 | tf_op jit(solution)/shard_map/ppermute | solution.py:196
  49.9 0.0 collective-permute-done.2
  49.9 1.2 %slice.26 = bf16[768,512]{1,0:T(8,128)(2,1)S(1)} slice(bf16[1152,512]{1,0:T(8,128)(2,1)} %collective-permute-done.2), slice={[0:768], [0:512]} | slice | bytes 1572864 | tf_op jit(solution)/shard_map/slice | solution.py:215
  51.1 0.0 copy-start.3
  51.1 1.4 %collective-permute-start.4 = (bf16[768,512]{1,0:T(8,128)(2,1)S(1)}, bf16[768,512]{1,0:T(8,128)(2,1)S(1)}, u32[]{:S(2)}, u32[]{:S(2)}) collective-permute-start(bf16[768,512]{1,0:T(8,128)(2,1)S(1)} %slice.26), channel_id=1, source_target_pairs={{1,0},{2,3},{5,4},{6,7},{9,8},{10,11},{13,12},{14,15},{17,16},{18,... | collective-permute-start | bytes 2359304 | tf_op jit(solution)/shard_map/ppermute | solution.py:196
  52.5 1.8 %fusion = f32[256,512]{1,0:T(8,128)S(1)} fusion(bf16[1152,512]{1,0:T(8,128)(2,1)} %collective-permute-done.2, bf16[4608,256]{1,0:T(8,128)(2,1)S(1)} %copy-done, s32[]{:T(128)S(6)} %select_n.37), kind=kOutput, calls=%fused_computation.3 | convolution fusion | flops 301989888 | bytes 2293764 | tf_op jit(solution)/shard_map/dot_general | solution.py:51
  54.3 0.2 fusion.15
  54.6 5.5 %collective-permute-done.5.hidden_ref = bf16[1536,256]{1,0:T(8,128)(2,1)S(1)} collective-permute-done((bf16[1536,256]{1,0:T(8,128)(2,1)S(1)}, bf16[1536,256]{1,0:T(8,128)(2,1)S(1)}, u32[]{:S(2)}, u32[]{:S(2)}) %collective-permute-start.5) | collective-permute-done | bytes 786464 | tf_op jit(solution)/shard_map/ppermute | solution.py:196
  60.1 1.2 %fusion.11 = f32[256,512]{1,0:T(8,128)S(1)} fusion(bf16[256,512]{1,0:T(8,128)(2,1)} %collective-permute-done.3, bf16[1536,256]{1,0:T(8,128)(2,1)S(1)} %collective-permute-done.5.hidden_ref), kind=kOutput, calls=%fused_computation.13 | convolution fusion | flops 67108864 | bytes 917504 | tf_op jit(solution)/shard_map/dot_general | solution.py:51
  61.3 1.3 %convolution_add_fusion.1.m_ref = f32[256,512]{1,0:T(8,128)S(1)} fusion(f32[256,512]{1,0:T(8,128)S(1)} %fusion.11, bf16[1152,512]{1,0:T(8,128)(2,1)} %collective-permute-done.2, bf16[1536,256]{1,0:T(8,128)(2,1)S(1)} %collective-permute-done.5.hidden_ref), kind=kOutput, calls=%fused_computation.1 | convolution fusion | flops 100794368 | bytes 1638400 | tf_op jit(solution)/shard_map/dot_general | solution.py:51
  62.6 0.0 copy-start.1
  62.6 0.0 copy-start.2
  62.6 6.3 %collective-permute-done.4 = bf16[768,512]{1,0:T(8,128)(2,1)S(1)} collective-permute-done((bf16[768,512]{1,0:T(8,128)(2,1)S(1)}, bf16[768,512]{1,0:T(8,128)(2,1)S(1)}, u32[]{:S(2)}, u32[]{:S(2)}) %collective-permute-start.4) | collective-permute-done | bytes 786464 | tf_op jit(solution)/shard_map/ppermute | solution.py:196
  68.9 0.4 add_add_fusion.m_ref
  69.4 0.0 collective-permute-done.7.refs_0_
  69.4 1.9 %shard_map.95 = (f32[256,512]{1,0:T(8,128)S(1)}, f32[64,128]{1,0:T(8,128)S(1)}) custom-call(f32[256,512]{1,0:T(8,128)S(1)} %convolution_add_fusion.1.m_ref, bf16[1536,256]{1,0:T(8,128)(2,1)S(1)} %collective-permute-done.5.hidden_ref, bf16[896,512]{1,0:T(8,128)(2,1)S(1)} %collective-permute-done.6.grad_ref, s32[8,8]{1,0:T(8,128)S(1)} %collective-permute-done.7.refs_0_, ...), custom_call_target="tpu_custom_call" | custom-call | flops 400000000 | bytes 4000000 | tf_op jit(solution)/shard_map/pallas_call | solution.py:145
  71.3 1.3 %collective-permute-start.8 = (f32[64,128]{1,0:T(8,128)S(1)}, f32[64,128]{1,0:T(8,128)S(1)}, u32[]{:S(2)}, u32[]{:S(2)}) collective-permute-start(f32[64,128]{1,0:T(8,128)S(1)} %get-tuple-element.27), channel_id=1, source_target_pairs={{1,0},{2,3},{5,4},{6,7},{9,8},{10,11},{13,12},{14,15},{17,16},{18,... | collective-permute-start | bytes 98312 | tf_op jit(solution)/shard_map/ppermute | solution.py:196
  72.6 1.9 %shard_map.96 = (f32[256,512]{1,0:T(8,128)S(1)}, f32[64,128]{1,0:T(8,128)S(1)}) custom-call(f32[256,512]{1,0:T(8,128)S(1)} %add_add_fusion.m_ref, bf16[896,256]{1,0:T(8,128)(2,1)S(1)} %constant_dynamic-slice_fusion.hidden_ref, bf16[896,512]{1,0:T(8,128)(2,1)S(1)} %collective-permute-done.6.grad_ref, s32[8,8]{1,0:T(8,128)S(1)} %pad_add_fusion.refs_0_.refs_4_.refs_2_, ...), custom_call_target="tpu_custom_call" | custom-call | flops 400000000 | bytes 4000000 | tf_op jit(solution)/shard_map/pallas_call | solution.py:145
  74.5 2.9 %collective-permute-done.8.refs_3_ = f32[64,128]{1,0:T(8,128)S(1)} collective-permute-done((f32[64,128]{1,0:T(8,128)S(1)}, f32[64,128]{1,0:T(8,128)S(1)}, u32[]{:S(2)}, u32[]{:S(2)}) %collective-permute-start.8) | collective-permute-done | bytes 32800 | tf_op jit(solution)/shard_map/ppermute | solution.py:196
  77.4 1.3 %collective-permute-start.9 = (f32[256,512]{1,0:T(8,128)S(1)}, f32[256,512]{1,0:T(8,128)S(1)}, u32[]{:S(2)}, u32[]{:S(2)}) collective-permute-start(f32[256,512]{1,0:T(8,128)S(1)} %get-tuple-element.30), channel_id=1, source_target_pairs={{1,0},{2,3},{5,4},{6,7},{9,8},{10,11},{13,12},{14,15},{17,16},{18,... | collective-permute-start | bytes 1572872 | tf_op jit(solution)/shard_map/ppermute | solution.py:196
  78.7 0.1 collective-permute-start.12
  78.8 1.6 %collective-permute-start.11 = (f32[64,128]{1,0:T(8,128)S(1)}, f32[64,128]{1,0:T(8,128)S(1)}, u32[]{:S(2)}, u32[]{:S(2)}) collective-permute-start(f32[64,128]{1,0:T(8,128)S(1)} %add.88), channel_id=1, source_target_pairs={{0,8},{4,12},{8,0},{12,4},{16,24},{20,28},{24,16},{28,20},{1,9},{5... | collective-permute-start | bytes 98312 | tf_op jit(solution)/shard_map/ppermute | solution.py:163
  80.4 0.3 collective-permute-start.10
  80.7 1.8 %collective-permute-done.12 = f32[64,128]{1,0:T(8,128)S(1)} collective-permute-done((f32[64,128]{1,0:T(8,128)S(1)}, f32[64,128]{1,0:T(8,128)S(1)}, u32[]{:S(2)}, u32[]{:S(2)}) %collective-permute-start.12) | collective-permute-done | bytes 32800 | tf_op jit(solution)/shard_map/ppermute | solution.py:163
  82.4 0.4 collective-permute-done.11
  82.8 1.6 %collective-permute-start.13 = (f32[64,128]{1,0:T(8,128)S(1)}, f32[64,128]{1,0:T(8,128)S(1)}, u32[]{:S(2)}, u32[]{:S(2)}) collective-permute-start(f32[64,128]{1,0:T(8,128)S(1)} %add_add_fusion.1.refs_0_), channel_id=1, source_target_pairs={{0,16},{4,20},{8,24},{12,28},{16,0},{20,4},{24,8},{28,12},{1,17},{... | collective-permute-start | bytes 98312 | tf_op jit(solution)/shard_map/ppermute | solution.py:163
  84.4 2.4 %collective-permute-done.13.refs_1_ = f32[64,128]{1,0:T(8,128)S(1)} collective-permute-done((f32[64,128]{1,0:T(8,128)S(1)}, f32[64,128]{1,0:T(8,128)S(1)}, u32[]{:S(2)}, u32[]{:S(2)}) %collective-permute-start.13) | collective-permute-done | bytes 32800 | tf_op jit(solution)/shard_map/ppermute | solution.py:163
  86.8 2.2 %shard_map.98 = bf16[256,512]{1,0:T(8,128)(2,1)} custom-call(f32[64,128]{1,0:T(8,128)S(1)} %add_add_fusion.1.refs_0_, f32[64,128]{1,0:T(8,128)S(1)} %collective-permute-done.13.refs_1_, s32[8,8]{1,0:T(8,128)S(1)} %pad_add_fusion.refs_0_.refs_4_.refs_2_, bf16[512,128]{1,0:T(8,128)(2,1)S(1)} %copy-done.2, bf16[2,256,256]{2,1,0:T(8,128)(2,1)S(1)} %copy-done.1, ...), custom_call_target="tpu_custom_call" | custom-call | flops 400000000 | bytes 4000000 | tf_op jit(solution)/shard_map/pallas_call | solution.py:145
  89.1 2.3 %shard_map.97 = f32[256,512]{1,0:T(8,128)} custom-call(f32[256,512]{1,0:T(8,128)S(1)} %get-tuple-element.25.refs_0_, f32[256,512]{1,0:T(8,128)S(1)} %collective-permute-done.9.refs_1_, f32[64,128]{1,0:T(8,128)S(1)} %get-tuple-element.31.refs_2_, f32[64,128]{1,0:T(8,128)S(1)} %collective-permute-done.8.refs_3_, ...), custom_call_target="tpu_custom_call" | custom-call | flops 400000000 | bytes 4000000 | tf_op jit(solution)/shard_map/pallas_call | solution.py:145
  (14 shorter events, 0.1 us)
Async XLA Ops:
  0.6 13.0 %copy-start = (bf16[4608,256]{1,0:T(8,128)(2,1)S(1)}, bf16[4608,256]{1,0:T(8,128)(2,1)}, u32[]{:S(2)}) copy-start(bf16[4608,256]{1,0:T(8,128)(2,1)} %param.8) | copy-start | bytes 7077892
  0.6 49.2 %collective-permute-start.2 = (bf16[1152,512]{1,0:T(8,128)(2,1)}, bf16[1152,512]{1,0:T(8,128)(2,1)}, u32[]{:S(2)}, u32[]{:S(2)}) collective-permute-start(bf16[1152,512]{1,0:T(8,128)(2,1)} %param.9), channel_id=1, source_target_pairs={{1,2},{2,1},{5,6},{6,5},{9,10},{10,9},{13,14},{14,13},{17,18},{18,... | collective-permute-start | bytes 3538952 | tf_op jit(solution)/shard_map/ppermute | solution.py:196
  4.2 36.3 %collective-permute-start.3 = (bf16[256,512]{1,0:T(8,128)(2,1)}, bf16[256,512]{1,0:T(8,128)(2,1)}, u32[]{:S(2)}, u32[]{:S(2)}) collective-permute-start(bf16[256,512]{1,0:T(8,128)(2,1)} %slice.21), channel_id=1, source_target_pairs={{0,2},{3,1},{4,6},{7,5},{8,10},{11,9},{12,14},{15,13},{16,18},{19,... | collective-permute-start | bytes 786440 | tf_op jit(solution)/shard_map/ppermute | solution.py:196
  13.6 22.4 %collective-permute-start = (bf16[896,512]{1,0:T(8,128)(2,1)}, bf16[896,512]{1,0:T(8,128)(2,1)}, u32[]{:S(2)}, u32[]{:S(2)}) collective-permute-start(bf16[896,512]{1,0:T(8,128)(2,1)} %slice.20), channel_id=1, source_target_pairs={{0,1},{1,0},{2,3},{3,2},{4,5},{5,4},{6,7},{7,6},{8,9},{9,8},{10,11... | collective-permute-start | bytes 2752520 | tf_op jit(solution)/shard_map/ppermute | solution.py:196
  13.7 3.5 %copy-start.4 = (s32[4,8]{1,0:T(4,128)S(1)}, s32[4,8]{1,0:T(4,128)}, u32[]{:S(2)}) copy-start(s32[4,8]{1,0:T(4,128)} %param.12) | copy-start | bytes 388
  13.7 3.5 %copy-start.5 = (s32[4,8]{1,0:T(4,128)S(1)}, s32[4,8]{1,0:T(4,128)}, u32[]{:S(2)}) copy-start(s32[4,8]{1,0:T(4,128)} %param.11) | copy-start | bytes 388
  36.1 9.6 %collective-permute-start.1 = (bf16[256,512]{1,0:T(8,128)(2,1)}, bf16[256,512]{1,0:T(8,128)(2,1)S(1)}, u32[]{:S(2)}, u32[]{:S(2)}) collective-permute-start(bf16[256,512]{1,0:T(8,128)(2,1)} %slice.21), channel_id=1, source_target_pairs={{0,1},{1,0},{2,3},{3,2},{4,5},{5,4},{6,7},{7,6},{8,9},{9,8},{10,11... | collective-permute-start | bytes 786440 | tf_op jit(solution)/shard_map/ppermute | solution.py:196
  38.5 21.5 %collective-permute-start.5 = (bf16[1536,256]{1,0:T(8,128)(2,1)S(1)}, bf16[1536,256]{1,0:T(8,128)(2,1)S(1)}, u32[]{:S(2)}, u32[]{:S(2)}) collective-permute-start(bf16[1536,256]{1,0:T(8,128)(2,1)S(1)} %pad_maximum_fusion), channel_id=1, source_target_pairs={{0,1},{3,2},{4,5},{7,6},{8,9},{11,10},{12,13},{15,14},{16,17},{19,... | collective-permute-start | bytes 2359304 | tf_op jit(solution)/shard_map/ppermute | solution.py:196
  41.7 27.7 %collective-permute-start.6 = (bf16[896,512]{1,0:T(8,128)(2,1)}, bf16[896,512]{1,0:T(8,128)(2,1)S(1)}, u32[]{:S(2)}, u32[]{:S(2)}) collective-permute-start(bf16[896,512]{1,0:T(8,128)(2,1)} %collective-permute-done), channel_id=1, source_target_pairs={{1,2},{2,1},{5,6},{6,5},{9,10},{10,9},{13,14},{14,13},{17,18},{18,... | collective-permute-start | bytes 2752520 | tf_op jit(solution)/shard_map/ppermute | solution.py:196
  45.6 23.8 %collective-permute-start.7 = (s32[8,8]{1,0:T(8,128)S(1)}, s32[8,8]{1,0:T(8,128)S(1)}, u32[]{:S(2)}, u32[]{:S(2)}) collective-permute-start(s32[8,8]{1,0:T(8,128)S(1)} %pad_add_fusion.refs_0_.refs_4_.refs_2_), channel_id=1, source_target_pairs={{0,1},{3,2},{4,5},{7,6},{8,9},{11,10},{12,13},{15,14},{16,17},{19,... | collective-permute-start | bytes 776 | tf_op jit(solution)/shard_map/ppermute | solution.py:196
  51.1 17.8 %copy-start.3 = (f32[256,512]{1,0:T(8,128)S(1)}, f32[256,512]{1,0:T(8,128)}, u32[]{:S(2)}) copy-start(f32[256,512]{1,0:T(8,128)} %convolution_add_fusion) | copy-start | bytes 1572868
  51.1 17.8 %collective-permute-start.4 = (bf16[768,512]{1,0:T(8,128)(2,1)S(1)}, bf16[768,512]{1,0:T(8,128)(2,1)S(1)}, u32[]{:S(2)}, u32[]{:S(2)}) collective-permute-start(bf16[768,512]{1,0:T(8,128)(2,1)S(1)} %slice.26), channel_id=1, source_target_pairs={{1,0},{2,3},{5,4},{6,7},{9,8},{10,11},{13,12},{14,15},{17,16},{18,... | collective-permute-start | bytes 2359304 | tf_op jit(solution)/shard_map/ppermute | solution.py:196
  62.6 6.8 %copy-start.1 = (bf16[2,256,256]{2,1,0:T(8,128)(2,1)S(1)}, bf16[2,256,256]{2,1,0:T(8,128)(2,1)}, u32[]{:S(2)}) copy-start(bf16[2,256,256]{2,1,0:T(8,128)(2,1)} %constant.32.clone.refs_2_.refs_3_.refs_6_.refs_7_.refs_4_.refs_5_) | copy-start | bytes 786436
  62.6 6.8 %copy-start.2 = (bf16[512,128]{1,0:T(8,128)(2,1)S(1)}, bf16[512,128]{1,0:T(8,128)(2,1)}, u32[]{:S(2)}) copy-start(bf16[512,128]{1,0:T(8,128)(2,1)} %constant.31.clone.refs_1_.refs_5_.refs_3_) | copy-start | bytes 393220
  71.3 6.1 %collective-permute-start.8 = (f32[64,128]{1,0:T(8,128)S(1)}, f32[64,128]{1,0:T(8,128)S(1)}, u32[]{:S(2)}, u32[]{:S(2)}) collective-permute-start(f32[64,128]{1,0:T(8,128)S(1)} %get-tuple-element.27), channel_id=1, source_target_pairs={{1,0},{2,3},{5,4},{6,7},{9,8},{10,11},{13,12},{14,15},{17,16},{18,... | collective-permute-start | bytes 98312 | tf_op jit(solution)/shard_map/ppermute | solution.py:196
  77.4 11.7 %collective-permute-start.9 = (f32[256,512]{1,0:T(8,128)S(1)}, f32[256,512]{1,0:T(8,128)S(1)}, u32[]{:S(2)}, u32[]{:S(2)}) collective-permute-start(f32[256,512]{1,0:T(8,128)S(1)} %get-tuple-element.30), channel_id=1, source_target_pairs={{1,0},{2,3},{5,4},{6,7},{9,8},{10,11},{13,12},{14,15},{17,16},{18,... | collective-permute-start | bytes 1572872 | tf_op jit(solution)/shard_map/ppermute | solution.py:196
  78.7 3.7 %collective-permute-start.12 = (f32[64,128]{1,0:T(8,128)S(1)}, f32[64,128]{1,0:T(8,128)S(1)}, u32[]{:S(2)}, u32[]{:S(2)}) collective-permute-start(f32[64,128]{1,0:T(8,128)S(1)} %add.88), channel_id=1, source_target_pairs={{0,12},{4,8},{8,4},{12,0},{16,28},{20,24},{24,20},{28,16},{1,13},{... | collective-permute-start | bytes 98312 | tf_op jit(solution)/shard_map/ppermute | solution.py:163
  78.8 4.0 %collective-permute-start.11 = (f32[64,128]{1,0:T(8,128)S(1)}, f32[64,128]{1,0:T(8,128)S(1)}, u32[]{:S(2)}, u32[]{:S(2)}) collective-permute-start(f32[64,128]{1,0:T(8,128)S(1)} %add.88), channel_id=1, source_target_pairs={{0,8},{4,12},{8,0},{12,4},{16,24},{20,28},{24,16},{28,20},{1,9},{5... | collective-permute-start | bytes 98312 | tf_op jit(solution)/shard_map/ppermute | solution.py:163
  80.4 2.5 %collective-permute-start.10 = (f32[64,128]{1,0:T(8,128)S(1)}, f32[64,128]{1,0:T(8,128)S(1)}, u32[]{:S(2)}, u32[]{:S(2)}) collective-permute-start(f32[64,128]{1,0:T(8,128)S(1)} %add.88), channel_id=1, source_target_pairs={{0,4},{4,0},{8,12},{12,8},{16,20},{20,16},{24,28},{28,24},{1,5},{5... | collective-permute-start | bytes 98312 | tf_op jit(solution)/shard_map/ppermute | solution.py:163
  82.8 4.0 %collective-permute-start.13 = (f32[64,128]{1,0:T(8,128)S(1)}, f32[64,128]{1,0:T(8,128)S(1)}, u32[]{:S(2)}, u32[]{:S(2)}) collective-permute-start(f32[64,128]{1,0:T(8,128)S(1)} %add_add_fusion.1.refs_0_), channel_id=1, source_target_pairs={{0,16},{4,20},{8,24},{12,28},{16,0},{20,4},{24,8},{28,12},{1,17},{... | collective-permute-start | bytes 98312 | tf_op jit(solution)/shard_map/ppermute | solution.py:163

commit v2 on v1

--- a/solution.py
+++ b/solution.py
@@ -12,6 +12,7 @@
 order = 64
 band = 16
 steps = order // band
+place_rows = 16
 
 
 def basis_matrix():
@@ -71,35 +72,30 @@
     return parts[0] if len(parts) == 1 else jnp.concatenate(parts, axis=1)
 
 
-def place_of_blocks(places_ref, row, width):
-    block = lax.broadcasted_iota(jnp.int32, (1, width), 1) // order
-    out = jnp.zeros((1, width), jnp.int32)
-    for column in range(width // order):
-        out = jnp.where(block == column, places_ref[row, column], out)
-    return out
-
-
-def masks_of(places_ref, width):
-    count = places_ref.shape[0] // 2
-    group = lax.rem(lax.broadcasted_iota(jnp.int32, (band, width), 1), order) // band * band
-    rows = [place_of_blocks(places_ref, row, width) for row in range(count)]
-    return [(at, group == place_of_blocks(places_ref, count + row, width)) for row, at in enumerate(rows)]
-
-
-def lifted(folded, places_ref, fold_ref, row_basis_ref, column_basis_ref):
+def masks_of(places, count):
+    width = places.shape[1]
+    column = lax.rem(lax.broadcasted_iota(jnp.int32, (band, width), 1), order).astype(jnp.float32)
+    masks = []
+    for row in range(count):
+        start = places[count + row : count + row + 1, :]
+        masks.append((places[row : row + 1, :], (column >= start) & (column < start + band)))
+    return masks
+
+
+def lifted(folded, places, fold_ref, row_basis_ref, column_basis_ref):
     spread = sum(dot(part, fold_ref[...], ((1,), (1,))) for part in split3(folded))
     pieces = []
-    for row, (at, inside) in enumerate(masks_of(places_ref, fold_ref.shape[0])):
+    for row, (at, inside) in enumerate(masks_of(places, folded.shape[0] // band)):
         part = jnp.where(inside, spread[row * band : (row + 1) * band], 0.0)
         pieces += [jnp.where(at == step * band, part, 0.0) for step in range(steps)]
     coefficients = jnp.concatenate(pieces, axis=0)
     return on_columns(column_basis_ref, on_rows(row_basis_ref, coefficients, True), True)
 
 
-def bands_of(x, places_ref, fold_ref, row_basis_ref, column_basis_ref):
+def bands_of(x, places, fold_ref, row_basis_ref, column_basis_ref):
     coefficients = on_columns(column_basis_ref, on_rows(row_basis_ref, x, False), False)
     pieces = []
-    for row, (at, inside) in enumerate(masks_of(places_ref, fold_ref.shape[0])):
+    for row, (at, inside) in enumerate(masks_of(places, x.shape[0] // order)):
         taken = jnp.zeros(inside.shape, jnp.float32)
         for step in range(steps):
             start = row * order + step * band
@@ -109,29 +105,45 @@
     return sum(dot(part, fold_ref[...]) for part in split3(taken))
 
 
-def bands_kernel(m_ref, *refs):
-    *table_refs, bands_ref = refs
-    bands_ref[...] = bands_of(m_ref[...], *table_refs)
-
-
-def last_rows_kernel(m_ref, hidden_ref, grad_ref, *refs):
-    *table_refs, out_ref, bands_ref = refs
-    hidden = hidden_ref[hidden_ref.shape[0] - grad_ref.shape[0] :]
-    out_ref[...] = m_ref[...] + dot(hidden, grad_ref[...], ((0,), (0,)))
-    bands_ref[...] = bands_of(out_ref[...], *table_refs)
+def bands_kernel(m_ref, places_ref, *refs):
+    *matrix_refs, bands_ref = refs
+    bands_ref[...] = bands_of(m_ref[...], places_ref[...], *matrix_refs)
+
+
+def helped_kernel(swapped_ref, cross_ref, far_ref, *refs):
+    *matrix_refs, out_ref, bands_ref = refs
+    handed, side = swapped_ref.shape[0] - place_rows, out_ref.shape[0]
+    alone = cross_ref.shape[0] - handed
+    out_ref[...] = (
+        dot(swapped_ref[:alone, :side], cross_ref[handed:], ((0,), (0,)))
+        + dot(swapped_ref[alone:handed, :side], far_ref[: handed - alone], ((0,), (0,)))
+        + dot(swapped_ref[:handed, side:], far_ref[handed - alone :], ((0,), (0,)))
+    )
+    bands_ref[...] = bands_of(out_ref[...], swapped_ref[handed:].astype(jnp.float32), *matrix_refs)
+
+
+def last_rows_kernel(m_ref, far_hidden_ref, far_ref, cross_hidden_ref, swapped_ref, places_ref, *refs):
+    *matrix_refs, out_ref, bands_ref = refs
+    out_ref[...] = (
+        m_ref[...]
+        + dot(far_hidden_ref[...], far_ref[...], ((0,), (0,)))
+        + dot(cross_hidden_ref[...], swapped_ref[: cross_hidden_ref.shape[0]], ((0,), (0,)))
+    )
+    bands_ref[...] = bands_of(out_ref[...], places_ref[...], *matrix_refs)
 
 
 def remove_kernel(count, *refs):
-    m_refs, band_refs, (*table_refs, out_ref) = refs[:count], refs[count : 2 * count], refs[2 * count :]
+    m_refs, band_refs = refs[:count], refs[count : 2 * count]
+    places_ref, *matrix_refs, out_ref = refs[2 * count :]
     bands = pair_sum([ref[...] for ref in band_refs])
-    out_ref[...] = pair_sum([ref[...] for ref in m_refs]) - lifted(bands, *table_refs)
+    out_ref[...] = pair_sum([ref[...] for ref in m_refs]) - lifted(bands, places_ref[...], *matrix_refs)
 
 
 def update_kernel(*refs):
     *part_refs, places_ref, fold_ref, row_basis_ref, column_basis_ref, out_ref = refs
     parts = [ref[...] for ref in part_refs]
     bands = pair_sum(parts)
-    out_ref[...] = lifted(bands, places_ref, fold_ref, row_basis_ref, column_basis_ref).astype(out_ref.dtype)
+    out_ref[...] = lifted(bands, places_ref[...], fold_ref, row_basis_ref, column_basis_ref).astype(out_ref.dtype)
 
 
 def pair_sum(parts):
@@ -141,11 +153,9 @@
 
 
 def call(kernel, out_shapes, *operands):
-    spaces = [pltpu.SMEM if x.dtype == jnp.int32 else pltpu.VMEM for x in operands]
     return pl.pallas_call(
         kernel,
         out_shape=out_shapes,
-        in_specs=[pl.BlockSpec(memory_space=space) for space in spaces],
         compiler_params=pltpu.CompilerParams(vmem_limit_bytes=32 * 2**20),
         cost_estimate=pl.CostEstimate(flops=4 * 10**8, bytes_accessed=4 * 10**6, transcendentals=0),
     )(*operands)
@@ -184,10 +194,11 @@
     tok = out_grad.shape[0]
     me = lax.axis_index("tp")
     left = me < 2
+    end = (me == 0) | (me == 3)
     cross = jnp.where(left, 2, 1)
     far = jnp.where(left, 3, 0)
-    first = max(tok // 4 // 128 * 128, 16)
-    handed = tok - max(tok // 3 // 128 * 128, 16)
+    handed = tok * 2 // 3
+    alone = tok - handed
 
     def rows_of(part, start=0, stop=tok):
         return lax.dynamic_slice_in_dim(hidden, part * tok + start, stop - start, 0)
@@ -197,38 +208,39 @@
 
     both_ways = [(0, 1), (1, 0), (2, 3), (3, 2)]
     across = [(1, 2), (2, 1)]
-    over_one = [(0, 2), (3, 1)]
     outward = [(1, 0), (2, 3)]
-    inward = [(0, 1), (3, 2)]
-
-    head, rest = out_grad[:first], out_grad[first:]
+
+    pair_grad = send(out_grad, both_ways)
     cross_grad = send(out_grad, across)
-    far_head = send(head, over_one)
-    pair_rest = send(rest, both_ways)
     m = carried + product(rows_of(me), out_grad)
-    helped_hidden = jnp.concatenate([rows_of(cross, handed), rows_of(far)], axis=0)
-    pair_rest, m, head, helped_hidden = lax.optimization_barrier((pair_rest, m, head, helped_hidden))
-    far_rest = send(pair_rest, across)
-    pair_head = send(head, both_ways)
-    helped_hidden = send(helped_hidden, inward)
-    end_places = send(after(places, pair_head), inward)
-    passed_grad = send(cross_grad[:handed], outward)
-
-    m = m + product(rows_of(me ^ 1, 0, first), pair_head) + product(rows_of(me ^ 1, first), pair_rest)
-    m = m + product(rows_of(cross), cross_grad) + product(rows_of(far, 0, first), far_head)
-    m = m + product(rows_of(cross, 0, handed), passed_grad)
-    helped = product(helped_hidden[: tok - handed], cross_grad[handed:])
-    helped = helped + product(helped_hidden[tok - handed :][:first], far_head)
-    far_rest = after(far_rest, m, helped)
+    far_hidden = rows_of(far)
+    helped_hidden = jnp.concatenate(
+        [
+            jnp.concatenate([rows_of(cross, handed), far_hidden[: handed - alone]], axis=0),
+            far_hidden[handed - alone :],
+        ],
+        axis=1,
+    )
+    place_part = jnp.pad(places.astype(hidden.dtype), ((0, place_rows - places.shape[0]), (0, 0)))
+    helped_hidden = jnp.concatenate([helped_hidden, place_part], axis=0)
+    cross_hidden = jnp.where(end, rows_of(cross, 0, handed), 0)
+    helped_hidden, cross_hidden, m = lax.optimization_barrier((helped_hidden, cross_hidden, m))
+
+    far_grad = send(pair_grad, across)
+    cross_grad = after(cross_grad, pair_grad, m)
+    swapped = send(jnp.where(end, helped_hidden, cross_grad[: handed + place_rows]), both_ways)
+    m = m + product(rows_of(me ^ 1), pair_grad) + product(rows_of(cross), cross_grad)
+    far_grad = after(far_grad, m)
+    swapped = after(swapped, far_grad)
 
     full = jax.ShapeDtypeStruct(m.shape, jnp.float32)
     folded = jax.ShapeDtypeStruct((m.shape[0] // steps, m.shape[1] // steps), jnp.float32)
-    helped, helped_bands = call(
-        last_rows_kernel, (full, folded), helped, helped_hidden, far_rest, end_places, *matrices
-    )
+    helped, helped_bands = call(helped_kernel, (full, folded), swapped, cross_grad, far_grad, *matrices)
     m, helped_bands = lax.optimization_barrier((m, helped_bands))
     sent_bands = send(helped_bands, outward)
-    m, bands = call(last_rows_kernel, (full, folded), m, rows_of(far, first), far_rest, places, *matrices)
+    m, bands = call(
+        last_rows_kernel, (full, folded), m, far_hidden, far_grad, cross_hidden, swapped, places, *matrices
+    )
     helped_bands, bands = lax.optimization_barrier((sent_bands, bands))
     helped = send(after(helped, helped_bands), outward)
     return [m, helped], [bands, helped_bands]
@@ -237,11 +249,14 @@
 def local(hidden, out_grad, momentum, band_rows, band_start_columns):
     row_count = hidden.shape[1]
     col_count = out_grad.shape[1]
+    one_hot = jnp.asarray(np.kron(np.eye(col_count // order), np.ones((1, order))), jnp.float32)
     matrices = tuple(
         jnp.asarray(x) for x in (fold_matrix(col_count), diagonal_blocks(row_count), diagonal_blocks(col_count))
     )
-    places = jnp.concatenate([band_rows, band_start_columns], axis=0).astype(jnp.int32)
-    form = lined if lax.axis_size("tp") == 4 else gathered
+    places = jnp.concatenate([band_rows, band_start_columns], axis=0).astype(jnp.float32)
+    places = dot(places, one_hot)
+    fits = out_grad.shape[0] % 48 == 0 and 2 * row_count == col_count and places.shape[0] <= place_rows
+    form = lined if fits and lax.axis_size("tp") == 4 else gathered
     m_parts, band_parts = form(hidden, out_grad, decay_rate * momentum[0], places, matrices)
     parts = spread_sum(pair_sum(band_parts), "rep")
     shape = (row_count, col_count)

time: 92 us -> 80.3 us (0.87)
  starting transfers between devices: 26.1 us -> 14.2 us
  waiting for transfers between devices: 38.7 us -> 49.7 us
  matrix products: 10.5 us -> 4.1 us
  local copies, waits for them, and re-layouts: 5.82 us -> 1.19 us
  other arithmetic: 1 us -> 3.55 us
  Pallas kernels: 8.33 us -> 6.38 us
    ppermute x10 -> x6, starting transfers between devices: 22.6 us -> 10.4 us  [send(): return lax.ppermute(x, 'tp', perm)]
    ppermute x10 -> x6, waiting for transfers between devices: 34.2 us -> 44.7 us  [send(): return lax.ppermute(x, 'tp', perm)]
    dot_general x8 -> x4, matrix products: 10.5 us -> 4.1 us  [dot(): lax.dot_general(a, b, (dims, ((), ())), preferred_element_type=jnp.float32)]
    slice x3 -> x0, local copies, waits for them, and re-layouts: 5.01 us -> none  [the longest x2 3.83 us: lined(): head, rest = (out_grad[:first], out_grad[first:])]
    select_n x0 -> x2, other arithmetic: none -> 2.57 us  [the longest x1 1.38 us: lined(): jnp.where(end, helped_hidden, cross_grad[:handed + place_rows])]
    pallas_call x4, Pallas kernels: 8.33 us -> 6.38 us  [call(): pl.pallas_call(kernel, out_shape=out_shapes, compiler_params=pltpu.Compil...]
  transfers between devices with their start and end apart: 14 -> 10, of which waited for: 8 -> 7; matrix products, arithmetic and copies ran while one was open for 19% -> 11% of each run, Pallas kernels for 5% -> 4%
where the time goes in v2:
time: 80.3 us; the launch traced here: 80 us
  waiting for transfers between devices  49.7 us (62%)
  starting transfers between devices  14.2 us (18%)
  Pallas kernels  6.38 us (8%)
  matrix products  4.1 us (5%)
  other arithmetic  3.55 us (4%)
  local copies, waits for them, and re-layouts  1.19 us (1%)
  between operations  0.85 us (1%)
    ppermute x6, waiting for transfers between devices, send(): return lax.ppermute(x, 'tp', perm)  44.7 us
    ppermute x6, starting transfers between devices, send(): return lax.ppermute(x, 'tp', perm)  10.4 us
    pallas_call x4, Pallas kernels, call(): pl.pallas_call(kernel, out_shape=out_shapes, compiler_params=pltpu.Compil...  6.38 us
    ppermute x4, waiting for transfers between devices, spread_sum(): lax.ppermute(x, axis, [(i, i ^ stride * k) for i in range(size)])  5.08 us
    dot_general x4, matrix products, dot(): lax.dot_general(a, b, (dims, ((), ())), preferred_element_type=jnp.float32)  4.1 us
    ppermute x4, starting transfers between devices, spread_sum(): lax.ppermute(x, axis, [(i, i ^ stride * k) for i in range(size)])  3.8 us
  transfers between devices with their start and end apart: 10, of which 7 were waited for; matrix products, arithmetic and copies ran while one was open for 11% of the time, Pallas kernels for 4%

profile of v2, /device:TPU:0, one launch (start us, length us, event | category | flops | bytes accessed | tf_op | source)
XLA Modules:
  0.0 80.0 jit_solution(18300606706061719947)
XLA Ops:
  0.6 0.0 copy-start.5
  0.6 0.0 copy-start.3
  0.7 0.0 copy-start.6
  0.7 0.0 copy-start.7
  0.7 3.1 %collective-permute-start = (bf16[1152,512]{1,0:T(8,128)(2,1)}, bf16[1152,512]{1,0:T(8,128)(2,1)}, u32[]{:S(2)}, u32[]{:S(2)}) collective-permute-start(bf16[1152,512]{1,0:T(8,128)(2,1)} %param.10), channel_id=1, source_target_pairs={{0,1},{1,0},{2,3},{3,2},{4,5},{5,4},{6,7},{7,6},{8,9},{9,8},{10,11... | collective-permute-start | bytes 3538952 | tf_op jit(solution)/shard_map/ppermute | solution.py:207
  3.8 0.7 collective-permute-start.1
  4.5 0.0 copy-start.4
  4.5 1.1 %constant_dynamic-slice_fusion.3 = (bf16[384,256]{1,0:T(8,128)(2,1)S(1)}, bf16[384,256]{1,0:T(8,128)(2,1)S(1)}) fusion(bf16[4608,256]{1,0:T(8,128)(2,1)} %param.9, s32[]{:T(128)S(6)} %select_n.40, s32[]{:T(128)S(6)} %select_n.42), kind=kLoop, calls=%fused_computation.24 | loop fusion | bytes 786440 | tf_op jit(solution)/shard_map/dynamic_slice | solution.py:204
  5.6 1.2 %dynamic-slice_select_fusion = (bf16[768,256]{1,0:T(8,128)(2,1)S(1)}, bf16[768,256]{1,0:T(8,128)(2,1)S(1)}) fusion(bf16[4608,256]{1,0:T(8,128)(2,1)} %param.9, s32[]{:T(128)S(6)} %select_n.44, pred[]{:T(512)S(6)} %or.3, s32[]{:T(128)S(6)} %add.58), kind=kLoop, calls=%fused_computation.11 | loop fusion | flops 196608 | bytes 1572873 | tf_op jit(solution)/shard_map/jit(_where)/select_n | solution.py:226
  6.8 0.0 copy-done.5
  6.9 0.0 copy-done.6
  6.9 0.0 copy-done.7
  6.9 0.1 fusion.14
  7.0 0.0 copy-done.3
  7.0 0.0 copy-done.4
  7.0 1.6 %convolution_add_fusion.1 = f32[256,512]{1,0:T(8,128)S(1)} fusion(bf16[1152,512]{1,0:T(8,128)(2,1)S(1)} %copy-done.3, bf16[4608,256]{1,0:T(8,128)(2,1)} %param.9, s32[]{:T(128)S(6)} %select_n.46, f32[1,256,512]{2,1,0:T(8,128)S(1)} %copy-done.4), kind=kOutput, calls=%fused_computation.4 | convolution fusion | flops 302252032 | bytes 2818052 | tf_op jit(solution)/shard_map/dot_general | solution.py:52
  8.6 21.4 %collective-permute-done = bf16[1152,512]{1,0:T(8,128)(2,1)} collective-permute-done((bf16[1152,512]{1,0:T(8,128)(2,1)}, bf16[1152,512]{1,0:T(8,128)(2,1)}, u32[]{:S(2)}, u32[]{:S(2)}) %collective-permute-start) | collective-permute-done | bytes 1179680 | tf_op jit(solution)/shard_map/ppermute | solution.py:207
  30.0 0.7 collective-permute-start.3
  30.8 1.0 %fusion.2 = bf16[784,512]{1,0:T(8,128)(2,1)} fusion(bf16[8,512]{1,0:T(8,128)(2,1)S(1)} %get-tuple-element.36, bf16[768,256]{1,0:T(8,128)(2,1)S(1)} %get-tuple-element.33, bf16[384,256]{1,0:T(8,128)(2,1)S(1)} %get-tuple-element.35, bf16[384,256]{1,0:T(8,128)(2,1)S(1)} %get-tuple-element.34), kind=kLoop, calls=%fused_computation.5 | loop fusion | flops 4014080 | bytes 1597440 | tf_op jit(solution)/shard_map/concatenate | solution.py:225
  31.7 0.0 copy-start.2
  31.7 0.0 collective-permute-done.1.cross_ref
  31.7 1.4 %slice_select_fusion = bf16[784,512]{1,0:T(8,128)(2,1)S(1)} fusion(bf16[784,512]{1,0:T(8,128)(2,1)} %fusion.2, bf16[1152,512]{1,0:T(8,128)(2,1)S(1)} %collective-permute-done.1.cross_ref, pred[]{:T(512)S(6)} %or.3), kind=kLoop, calls=%fused_computation.6 | loop fusion | flops 401408 | bytes 2408449 | tf_op jit(solution)/shard_map/jit(_where)/select_n | solution.py:231
  33.1 3.3 %collective-permute-start.2 = (bf16[784,512]{1,0:T(8,128)(2,1)S(1)}, bf16[784,512]{1,0:T(8,128)(2,1)S(1)}, u32[]{:S(2)}, u32[]{:S(2)}) collective-permute-start(bf16[784,512]{1,0:T(8,128)(2,1)S(1)} %slice_select_fusion), channel_id=1, source_target_pairs={{0,1},{1,0},{2,3},{3,2},{4,5},{5,4},{6,7},{7,6},{8,9},{9,8},{10,11... | collective-permute-start | bytes 2408456 | tf_op jit(solution)/shard_map/ppermute | solution.py:207
  36.4 0.0 copy-done.2
  36.4 0.5 fusion.3
  37.0 0.0 copy-start
  37.0 0.0 copy-start.1
  37.0 1.8 %fusion.1.m_ref = f32[256,512]{1,0:T(8,128)S(1)} fusion(f32[256,512]{1,0:T(8,128)S(1)} %fusion.3, f32[256,512]{1,0:T(8,128)S(1)} %convolution_add_fusion.1, bf16[1152,512]{1,0:T(8,128)(2,1)} %collective-permute-done, bf16[4608,256]{1,0:T(8,128)(2,1)S(1)} %copy-done.2, s32[]{:T(128)S(6)} %select_n.47), kind=kOutput, calls=%fused_computation.3 | convolution fusion | flops 302252032 | bytes 3342340 | tf_op jit(solution)/shard_map/dot_general | solution.py:52
  38.9 0.0 collective-permute-done.3.far_ref
  38.9 14.3 %collective-permute-done.2.swapped_ref = bf16[784,512]{1,0:T(8,128)(2,1)S(1)} collective-permute-done((bf16[784,512]{1,0:T(8,128)(2,1)S(1)}, bf16[784,512]{1,0:T(8,128)(2,1)S(1)}, u32[]{:S(2)}, u32[]{:S(2)}) %collective-permute-start.2) | collective-permute-done | bytes 802848 | tf_op jit(solution)/shard_map/ppermute | solution.py:207
  53.1 0.0 copy-done
  53.1 0.0 copy-done.1
  53.1 1.5 %shard_map.104 = (f32[256,512]{1,0:T(8,128)S(1)}, f32[64,128]{1,0:T(8,128)S(1)}) custom-call(bf16[784,512]{1,0:T(8,128)(2,1)S(1)} %collective-permute-done.2.swapped_ref, bf16[1152,512]{1,0:T(8,128)(2,1)S(1)} %collective-permute-done.1.cross_ref, bf16[1152,512]{1,0:T(8,128)(2,1)S(1)} %collective-permute-done.3.far_ref, bf16[512,128]{1,0:T(8,128)(2,1)S(1)} %copy-done.1, ...), custom_call_target="tpu_custom_call" | custom-call | flops 400000000 | bytes 4000000 | tf_op jit(solution)/shard_map/pallas_call | solution.py:156
  54.6 1.3 %collective-permute-start.4 = (f32[64,128]{1,0:T(8,128)S(1)}, f32[64,128]{1,0:T(8,128)S(1)}, u32[]{:S(2)}, u32[]{:S(2)}) collective-permute-start(f32[64,128]{1,0:T(8,128)S(1)} %get-tuple-element.27), channel_id=1, source_target_pairs={{1,0},{2,3},{5,4},{6,7},{9,8},{10,11},{13,12},{14,15},{17,16},{18,... | collective-permute-start | bytes 98312 | tf_op jit(solution)/shard_map/ppermute | solution.py:207
  55.9 1.5 %shard_map.105 = (f32[256,512]{1,0:T(8,128)S(1)}, f32[64,128]{1,0:T(8,128)S(1)}) custom-call(f32[256,512]{1,0:T(8,128)S(1)} %fusion.1.m_ref, bf16[1152,256]{1,0:T(8,128)(2,1)S(1)} %constant_dynamic-slice_fusion.2.far_hidden_ref, bf16[1152,512]{1,0:T(8,128)(2,1)S(1)} %collective-permute-done.3.far_ref, ...), custom_call_target="tpu_custom_call" | custom-call | flops 400000000 | bytes 4000000 | tf_op jit(solution)/shard_map/pallas_call | solution.py:156
  57.4 7.9 %collective-permute-done.4.refs_3_ = f32[64,128]{1,0:T(8,128)S(1)} collective-permute-done((f32[64,128]{1,0:T(8,128)S(1)}, f32[64,128]{1,0:T(8,128)S(1)}, u32[]{:S(2)}, u32[]{:S(2)}) %collective-permute-start.4) | collective-permute-done | bytes 32800 | tf_op jit(solution)/shard_map/ppermute | solution.py:207
  65.4 1.3 %collective-permute-start.5 = (f32[256,512]{1,0:T(8,128)S(1)}, f32[256,512]{1,0:T(8,128)S(1)}, u32[]{:S(2)}, u32[]{:S(2)}) collective-permute-start(f32[256,512]{1,0:T(8,128)S(1)} %get-tuple-element.30), channel_id=1, source_target_pairs={{1,0},{2,3},{5,4},{6,7},{9,8},{10,11},{13,12},{14,15},{17,16},{18,... | collective-permute-start | bytes 1572872 | tf_op jit(solution)/shard_map/ppermute | solution.py:207
  66.7 1.6 %collective-permute-start.7 = (f32[64,128]{1,0:T(8,128)S(1)}, f32[64,128]{1,0:T(8,128)S(1)}, u32[]{:S(2)}, u32[]{:S(2)}) collective-permute-start(f32[64,128]{1,0:T(8,128)S(1)} %add.53), channel_id=1, source_target_pairs={{0,8},{4,12},{8,0},{12,4},{16,24},{20,28},{24,16},{28,20},{1,9},{5... | collective-permute-start | bytes 98312 | tf_op jit(solution)/shard_map/ppermute | solution.py:173
  68.2 0.0 collective-permute-start.8
  68.2 0.7 collective-permute-start.6
  68.9 1.8 %collective-permute-done.7 = f32[64,128]{1,0:T(8,128)S(1)} collective-permute-done((f32[64,128]{1,0:T(8,128)S(1)}, f32[64,128]{1,0:T(8,128)S(1)}, u32[]{:S(2)}, u32[]{:S(2)}) %collective-permute-start.7) | collective-permute-done | bytes 32800 | tf_op jit(solution)/shard_map/ppermute | solution.py:173
  70.6 0.9 %collective-permute-done.8 = f32[64,128]{1,0:T(8,128)S(1)} collective-permute-done((f32[64,128]{1,0:T(8,128)S(1)}, f32[64,128]{1,0:T(8,128)S(1)}, u32[]{:S(2)}, u32[]{:S(2)}) %collective-permute-start.8) | collective-permute-done | bytes 32800 | tf_op jit(solution)/shard_map/ppermute | solution.py:173
  71.5 0.0 collective-permute-done.6
  71.6 1.6 %collective-permute-start.9 = (f32[64,128]{1,0:T(8,128)S(1)}, f32[64,128]{1,0:T(8,128)S(1)}, u32[]{:S(2)}, u32[]{:S(2)}) collective-permute-start(f32[64,128]{1,0:T(8,128)S(1)} %add_add_fusion.refs_0_), channel_id=1, source_target_pairs={{0,16},{4,20},{8,24},{12,28},{16,0},{20,4},{24,8},{28,12},{1,17},{... | collective-permute-start | bytes 98312 | tf_op jit(solution)/shard_map/ppermute | solution.py:173
  73.2 2.4 %collective-permute-done.9.refs_1_ = f32[64,128]{1,0:T(8,128)S(1)} collective-permute-done((f32[64,128]{1,0:T(8,128)S(1)}, f32[64,128]{1,0:T(8,128)S(1)}, u32[]{:S(2)}, u32[]{:S(2)}) %collective-permute-start.9) | collective-permute-done | bytes 32800 | tf_op jit(solution)/shard_map/ppermute | solution.py:173
  75.5 1.6 %shard_map.107 = bf16[256,512]{1,0:T(8,128)(2,1)} custom-call(f32[64,128]{1,0:T(8,128)S(1)} %add_add_fusion.refs_0_, f32[64,128]{1,0:T(8,128)S(1)} %collective-permute-done.9.refs_1_, f32[8,512]{1,0:T(8,128)S(1)} %get-tuple-element.37.places_ref.refs_4_.refs_2_, bf16[512,128]{1,0:T(8,128)(2,1)S(1)} %copy-done.1, bf16[2,256,256]{2,1,0:T(8,128)(2,1)S(1)} %copy-done, ...), custom_call_target="tpu_custom_call" | custom-call | flops 400000000 | bytes 4000000 | tf_op jit(solution)/shard_map/pallas_call | solution.py:156
  77.2 1.0 %collective-permute-done.5.refs_1_ = f32[256,512]{1,0:T(8,128)S(1)} collective-permute-done((f32[256,512]{1,0:T(8,128)S(1)}, f32[256,512]{1,0:T(8,128)S(1)}, u32[]{:S(2)}, u32[]{:S(2)}) %collective-permute-start.5) | collective-permute-done | bytes 524320 | tf_op jit(solution)/shard_map/ppermute | solution.py:207
  78.2 1.7 %shard_map.106 = f32[256,512]{1,0:T(8,128)} custom-call(f32[256,512]{1,0:T(8,128)S(1)} %get-tuple-element.25.refs_0_, f32[256,512]{1,0:T(8,128)S(1)} %collective-permute-done.5.refs_1_, f32[64,128]{1,0:T(8,128)S(1)} %get-tuple-element.31.refs_2_, f32[64,128]{1,0:T(8,128)S(1)} %collective-permute-done.4.refs_3_, ...), custom_call_target="tpu_custom_call" | custom-call | flops 400000000 | bytes 4000000 | tf_op jit(solution)/shard_map/pallas_call | solution.py:156
  (3 shorter events, 0.1 us)
Async XLA Ops:
  0.6 6.2 %copy-start.5 = (bf16[8,512]{1,0:T(8,128)(2,1)S(1)}, bf16[8,512]{1,0:T(8,128)(2,1)}, u32[]{:S(2)}) copy-start(bf16[8,512]{1,0:T(8,128)(2,1)} %constant.51) | copy-start | bytes 24580
  0.6 6.4 %copy-start.3 = (bf16[1152,512]{1,0:T(8,128)(2,1)S(1)}, bf16[1152,512]{1,0:T(8,128)(2,1)}, u32[]{:S(2)}) copy-start(bf16[1152,512]{1,0:T(8,128)(2,1)} %param.10) | copy-start | bytes 3538948
  0.7 6.2 %copy-start.6 = (s32[4,8]{1,0:T(4,128)S(1)}, s32[4,8]{1,0:T(4,128)}, u32[]{:S(2)}) copy-start(s32[4,8]{1,0:T(4,128)} %param.13) | copy-start | bytes 388
  0.7 6.2 %copy-start.7 = (s32[4,8]{1,0:T(4,128)S(1)}, s32[4,8]{1,0:T(4,128)}, u32[]{:S(2)}) copy-start(s32[4,8]{1,0:T(4,128)} %param.12) | copy-start | bytes 388
  0.7 29.4 %collective-permute-start = (bf16[1152,512]{1,0:T(8,128)(2,1)}, bf16[1152,512]{1,0:T(8,128)(2,1)}, u32[]{:S(2)}, u32[]{:S(2)}) collective-permute-start(bf16[1152,512]{1,0:T(8,128)(2,1)} %param.10), channel_id=1, source_target_pairs={{0,1},{1,0},{2,3},{3,2},{4,5},{5,4},{6,7},{7,6},{8,9},{9,8},{10,11... | collective-permute-start | bytes 3538952 | tf_op jit(solution)/shard_map/ppermute | solution.py:207
  3.8 28.0 %collective-permute-start.1 = (bf16[1152,512]{1,0:T(8,128)(2,1)}, bf16[1152,512]{1,0:T(8,128)(2,1)S(1)}, u32[]{:S(2)}, u32[]{:S(2)}) collective-permute-start(bf16[1152,512]{1,0:T(8,128)(2,1)} %param.10), channel_id=1, source_target_pairs={{1,2},{2,1},{5,6},{6,5},{9,10},{10,9},{13,14},{14,13},{17,18},{18,... | collective-permute-start | bytes 3538952 | tf_op jit(solution)/shard_map/ppermute | solution.py:207
  4.5 2.5 %copy-start.4 = (f32[1,256,512]{2,1,0:T(8,128)S(1)}, f32[1,256,512]{2,1,0:T(8,128)}, u32[]{:S(2)}) copy-start(f32[1,256,512]{2,1,0:T(8,128)} %param.11) | copy-start | bytes 1572868
  30.0 8.8 %collective-permute-start.3 = (bf16[1152,512]{1,0:T(8,128)(2,1)}, bf16[1152,512]{1,0:T(8,128)(2,1)S(1)}, u32[]{:S(2)}, u32[]{:S(2)}) collective-permute-start(bf16[1152,512]{1,0:T(8,128)(2,1)} %collective-permute-done), channel_id=1, source_target_pairs={{1,2},{2,1},{5,6},{6,5},{9,10},{10,9},{13,14},{14,13},{17,18},{18,... | collective-permute-start | bytes 3538952 | tf_op jit(solution)/shard_map/ppermute | solution.py:207
  31.7 4.7 %copy-start.2 = (bf16[4608,256]{1,0:T(8,128)(2,1)S(1)}, bf16[4608,256]{1,0:T(8,128)(2,1)}, u32[]{:S(2)}) copy-start(bf16[4608,256]{1,0:T(8,128)(2,1)} %param.9) | copy-start | bytes 7077892
  33.1 20.0 %collective-permute-start.2 = (bf16[784,512]{1,0:T(8,128)(2,1)S(1)}, bf16[784,512]{1,0:T(8,128)(2,1)S(1)}, u32[]{:S(2)}, u32[]{:S(2)}) collective-permute-start(bf16[784,512]{1,0:T(8,128)(2,1)S(1)} %slice_select_fusion), channel_id=1, source_target_pairs={{0,1},{1,0},{2,3},{3,2},{4,5},{5,4},{6,7},{7,6},{8,9},{9,8},{10,11... | collective-permute-start | bytes 2408456 | tf_op jit(solution)/shard_map/ppermute | solution.py:207
  37.0 16.2 %copy-start = (bf16[2,256,256]{2,1,0:T(8,128)(2,1)S(1)}, bf16[2,256,256]{2,1,0:T(8,128)(2,1)}, u32[]{:S(2)}) copy-start(bf16[2,256,256]{2,1,0:T(8,128)(2,1)} %constant.32.clone.refs_1_.refs_2_.refs_6_.refs_7_.refs_4_.refs_5_) | copy-start | bytes 786436
  37.0 16.1 %copy-start.1 = (bf16[512,128]{1,0:T(8,128)(2,1)S(1)}, bf16[512,128]{1,0:T(8,128)(2,1)}, u32[]{:S(2)}) copy-start(bf16[512,128]{1,0:T(8,128)(2,1)} %constant.31.clone.refs_0_.refs_5_.refs_3_) | copy-start | bytes 393220
  54.6 10.8 %collective-permute-start.4 = (f32[64,128]{1,0:T(8,128)S(1)}, f32[64,128]{1,0:T(8,128)S(1)}, u32[]{:S(2)}, u32[]{:S(2)}) collective-permute-start(f32[64,128]{1,0:T(8,128)S(1)} %get-tuple-element.27), channel_id=1, source_target_pairs={{1,0},{2,3},{5,4},{6,7},{9,8},{10,11},{13,12},{14,15},{17,16},{18,... | collective-permute-start | bytes 98312 | tf_op jit(solution)/shard_map/ppermute | solution.py:207
  65.4 12.9 %collective-permute-start.5 = (f32[256,512]{1,0:T(8,128)S(1)}, f32[256,512]{1,0:T(8,128)S(1)}, u32[]{:S(2)}, u32[]{:S(2)}) collective-permute-start(f32[256,512]{1,0:T(8,128)S(1)} %get-tuple-element.30), channel_id=1, source_target_pairs={{1,0},{2,3},{5,4},{6,7},{9,8},{10,11},{13,12},{14,15},{17,16},{18,... | collective-permute-start | bytes 1572872 | tf_op jit(solution)/shard_map/ppermute | solution.py:207
  66.7 4.0 %collective-permute-start.7 = (f32[64,128]{1,0:T(8,128)S(1)}, f32[64,128]{1,0:T(8,128)S(1)}, u32[]{:S(2)}, u32[]{:S(2)}) collective-permute-start(f32[64,128]{1,0:T(8,128)S(1)} %add.53), channel_id=1, source_target_pairs={{0,8},{4,12},{8,0},{12,4},{16,24},{20,28},{24,16},{28,20},{1,9},{5... | collective-permute-start | bytes 98312 | tf_op jit(solution)/shard_map/ppermute | solution.py:173
  68.2 3.3 %collective-permute-start.8 = (f32[64,128]{1,0:T(8,128)S(1)}, f32[64,128]{1,0:T(8,128)S(1)}, u32[]{:S(2)}, u32[]{:S(2)}) collective-permute-start(f32[64,128]{1,0:T(8,128)S(1)} %add.53), channel_id=1, source_target_pairs={{0,12},{4,8},{8,4},{12,0},{16,28},{20,24},{24,20},{28,16},{1,13},{... | collective-permute-start | bytes 98312 | tf_op jit(solution)/shard_map/ppermute | solution.py:173
  68.2 3.3 %collective-permute-start.6 = (f32[64,128]{1,0:T(8,128)S(1)}, f32[64,128]{1,0:T(8,128)S(1)}, u32[]{:S(2)}, u32[]{:S(2)}) collective-permute-start(f32[64,128]{1,0:T(8,128)S(1)} %add.53), channel_id=1, source_target_pairs={{0,4},{4,0},{8,12},{12,8},{16,20},{20,16},{24,28},{28,24},{1,5},{5... | collective-permute-start | bytes 98312 | tf_op jit(solution)/shard_map/ppermute | solution.py:173
  71.6 4.0 %collective-permute-start.9 = (f32[64,128]{1,0:T(8,128)S(1)}, f32[64,128]{1,0:T(8,128)S(1)}, u32[]{:S(2)}, u32[]{:S(2)}) collective-permute-start(f32[64,128]{1,0:T(8,128)S(1)} %add_add_fusion.refs_0_), channel_id=1, source_target_pairs={{0,16},{4,20},{8,24},{12,28},{16,0},{20,4},{24,8},{28,12},{1,17},{... | collective-permute-start | bytes 98312 | tf_op jit(solution)/shard_map/ppermute | solution.py:173

commit v3 on v2

--- a/solution.py
+++ b/solution.py
@@ -13,6 +13,7 @@
 band = 16
 steps = order // band
 place_rows = 16
+code_rows = 16
 
 
 def basis_matrix():
@@ -82,68 +83,93 @@
     return masks
 
 
-def lifted(folded, places, fold_ref, row_basis_ref, column_basis_ref):
-    spread = sum(dot(part, fold_ref[...], ((1,), (1,))) for part in split3(folded))
+def selected(x, masks, row_basis_ref, column_basis_ref):
+    by_rows = on_rows(row_basis_ref, x, False)
     pieces = []
-    for row, (at, inside) in enumerate(masks_of(places, folded.shape[0] // band)):
-        part = jnp.where(inside, spread[row * band : (row + 1) * band], 0.0)
-        pieces += [jnp.where(at == step * band, part, 0.0) for step in range(steps)]
-    coefficients = jnp.concatenate(pieces, axis=0)
-    return on_columns(column_basis_ref, on_rows(row_basis_ref, coefficients, True), True)
-
-
-def bands_of(x, places, fold_ref, row_basis_ref, column_basis_ref):
-    coefficients = on_columns(column_basis_ref, on_rows(row_basis_ref, x, False), False)
-    pieces = []
-    for row, (at, inside) in enumerate(masks_of(places, x.shape[0] // order)):
-        taken = jnp.zeros(inside.shape, jnp.float32)
+    for row, (at, _) in enumerate(masks):
+        taken = jnp.zeros((band, x.shape[1]), jnp.float32)
         for step in range(steps):
             start = row * order + step * band
-            taken = jnp.where(at == step * band, coefficients[start : start + band], taken)
-        pieces.append(jnp.where(inside, taken, 0.0))
-    taken = jnp.concatenate(pieces, axis=0)
+            taken = jnp.where(at == step * band, by_rows[start : start + band], taken)
+        pieces.append(taken)
+    coefficients = on_columns(column_basis_ref, jnp.concatenate(pieces, axis=0), False)
+    return within(coefficients, masks)
+
+
+def within(x, masks):
+    return jnp.concatenate(
+        [jnp.where(inside, x[i * band : (i + 1) * band], 0.0) for i, (_, inside) in enumerate(masks)], axis=0
+    )
+
+
+def restored(x, masks, row_basis_ref, column_basis_ref):
+    by_columns = on_columns(column_basis_ref, x, True)
+    pieces = []
+    for row, (at, _) in enumerate(masks):
+        part = by_columns[row * band : (row + 1) * band]
+        pieces += [jnp.where(at == step * band, part, 0.0) for step in range(steps)]
+    return on_rows(row_basis_ref, jnp.concatenate(pieces, axis=0), True)
+
+
+def bands_of(x, places, fold_ref, *basis_refs):
+    taken = selected(x, masks_of(places, x.shape[0] // order), *basis_refs)
     return sum(dot(part, fold_ref[...]) for part in split3(taken))
 
 
-def bands_kernel(m_ref, places_ref, *refs):
-    *matrix_refs, bands_ref = refs
-    bands_ref[...] = bands_of(m_ref[...], places_ref[...], *matrix_refs)
-
-
-def helped_kernel(swapped_ref, cross_ref, far_ref, *refs):
-    *matrix_refs, out_ref, bands_ref = refs
+def bands_kernel(m_ref, places_ref, fold_ref, row_basis_ref, column_basis_ref, bands_ref):
+    bands_ref[...] = bands_of(m_ref[...], places_ref[...], fold_ref, row_basis_ref, column_basis_ref)
+
+
+def coded(x):
+    top = jnp.max(jnp.abs(x), axis=0, keepdims=True)
+    exponent = jnp.ceil(jnp.log2(jnp.maximum(top, 1e-30)) + 0.01)
+    scaled = x * jnp.exp2(15.0 - exponent)
+    values = jnp.clip(jnp.round(scaled), -32767.0, 32767.0).astype(jnp.int32).astype(jnp.int16)
+    row = jnp.broadcast_to(exponent, (code_rows, x.shape[1])).astype(jnp.int32).astype(jnp.int16)
+    return values, row
+
+
+def decoded(ref):
+    values = ref[: ref.shape[0] - code_rows].astype(jnp.int32).astype(jnp.float32)
+    row = ref[ref.shape[0] - code_rows :].astype(jnp.int32).astype(jnp.float32)
+    return values * jnp.exp2(row[:1] - 15.0)
+
+
+def last_rows_kernel(m_ref, far_hidden_ref, far_ref, cross_hidden_ref, cross_ref, swapped_ref, places_ref, *refs):
+    *matrix_refs, out_ref, code_ref, bands_ref = refs
     handed, side = swapped_ref.shape[0] - place_rows, out_ref.shape[0]
-    alone = cross_ref.shape[0] - handed
-    out_ref[...] = (
+    alone, count = cross_ref.shape[0] - handed, bands_ref.shape[0] // 2
+    helped = (
         dot(swapped_ref[:alone, :side], cross_ref[handed:], ((0,), (0,)))
         + dot(swapped_ref[alone:handed, :side], far_ref[: handed - alone], ((0,), (0,)))
         + dot(swapped_ref[:handed, side:], far_ref[handed - alone :], ((0,), (0,)))
     )
-    bands_ref[...] = bands_of(out_ref[...], swapped_ref[handed:].astype(jnp.float32), *matrix_refs)
-
-
-def last_rows_kernel(m_ref, far_hidden_ref, far_ref, cross_hidden_ref, swapped_ref, places_ref, *refs):
-    *matrix_refs, out_ref, bands_ref = refs
+    code_ref[:side], code_ref[side:] = coded(helped)
+    bands_ref[count:] = bands_of(helped, swapped_ref[handed:].astype(jnp.float32), *matrix_refs)
     out_ref[...] = (
         m_ref[...]
         + dot(far_hidden_ref[...], far_ref[...], ((0,), (0,)))
-        + dot(cross_hidden_ref[...], swapped_ref[: cross_hidden_ref.shape[0]], ((0,), (0,)))
-    )
-    bands_ref[...] = bands_of(out_ref[...], places_ref[...], *matrix_refs)
-
-
-def remove_kernel(count, *refs):
-    m_refs, band_refs = refs[:count], refs[count : 2 * count]
-    places_ref, *matrix_refs, out_ref = refs[2 * count :]
-    bands = pair_sum([ref[...] for ref in band_refs])
-    out_ref[...] = pair_sum([ref[...] for ref in m_refs]) - lifted(bands, places_ref[...], *matrix_refs)
+        + dot(cross_hidden_ref[...], swapped_ref[:handed], ((0,), (0,)))
+    )
+    bands_ref[:count] = bands_of(out_ref[...], places_ref[...], *matrix_refs)
+
+
+def remove_kernel(m_ref, *refs):
+    *code_refs, places_ref, row_basis_ref, column_basis_ref, out_ref = refs
+    m = m_ref[...]
+    for ref in code_refs:
+        m = m + decoded(ref)
+    masks = masks_of(places_ref[...], m.shape[0] // order)
+    taken = selected(m, masks, row_basis_ref, column_basis_ref)
+    out_ref[...] = m - restored(taken, masks, row_basis_ref, column_basis_ref)
 
 
 def update_kernel(*refs):
     *part_refs, places_ref, fold_ref, row_basis_ref, column_basis_ref, out_ref = refs
-    parts = [ref[...] for ref in part_refs]
-    bands = pair_sum(parts)
-    out_ref[...] = lifted(bands, places_ref[...], fold_ref, row_basis_ref, column_basis_ref).astype(out_ref.dtype)
+    folded = pair_sum([ref[...] for ref in part_refs])
+    masks = masks_of(places_ref[...], out_ref.shape[0] // order)
+    spread = sum(dot(part, fold_ref[...], ((1,), (1,))) for part in split3(folded))
+    out_ref[...] = restored(within(spread, masks), masks, row_basis_ref, column_basis_ref).astype(out_ref.dtype)
 
 
 def pair_sum(parts):
@@ -161,19 +187,27 @@
     )(*operands)
 
 
-def spread_sum(x, axis):
+def stages_of(axis):
+    size, stride, stages = lax.axis_size(axis), 1, []
+    while stride < size:
+        stages.append((stride, min(4, size // stride)))
+        stride *= stages[-1][1]
+    return stages
+
+
+def exchanged(x, axis, stride, count):
+    size = lax.axis_size(axis)
+    return [lax.ppermute(x, axis, [(i, i ^ (stride * k)) for i in range(size)]) for k in range(1, count)]
+
+
+def summed_but_last(x, axis, form):
     size = lax.axis_size(axis)
     if size & (size - 1):
-        return [lax.psum(x, axis)]
-    stride, parts = 1, [x]
-    while stride < size:
-        count = min(4, size // stride)
-        x = pair_sum(parts)
-        parts = [x] + [
-            lax.ppermute(x, axis, [(i, i ^ (stride * k)) for i in range(size)]) for k in range(1, count)
-        ]
-        stride *= count
-    return parts
+        return form(lax.psum(x, axis)), (1, 1)
+    *stages, last = stages_of(axis) or [(1, 1)]
+    for stride, count in stages:
+        x = pair_sum([x] + exchanged(x, axis, stride, count))
+    return form(x), last
 
 
 def product(hidden_rows, grad_rows):
@@ -187,7 +221,8 @@
 def gathered(hidden, out_grad, carried, places, matrices):
     m = carried + product(hidden, lax.all_gather(out_grad, "tp", axis=0, tiled=True))
     folded = jax.ShapeDtypeStruct((m.shape[0] // steps, m.shape[1] // steps), jnp.float32)
-    return [m], [call(bands_kernel, folded, m, places, *matrices)]
+    bands, last = summed_but_last(call(bands_kernel, folded, m, places, *matrices), "rep", lambda x: x)
+    return [m], [bands] + exchanged(bands, "rep", *last)
 
 
 def lined(hidden, out_grad, carried, places, matrices):
@@ -233,17 +268,32 @@
     far_grad = after(far_grad, m)
     swapped = after(swapped, far_grad)
 
-    full = jax.ShapeDtypeStruct(m.shape, jnp.float32)
-    folded = jax.ShapeDtypeStruct((m.shape[0] // steps, m.shape[1] // steps), jnp.float32)
-    helped, helped_bands = call(helped_kernel, (full, folded), swapped, cross_grad, far_grad, *matrices)
-    m, helped_bands = lax.optimization_barrier((m, helped_bands))
-    sent_bands = send(helped_bands, outward)
-    m, bands = call(
-        last_rows_kernel, (full, folded), m, far_hidden, far_grad, cross_hidden, swapped, places, *matrices
-    )
-    helped_bands, bands = lax.optimization_barrier((sent_bands, bands))
-    helped = send(after(helped, helped_bands), outward)
-    return [m, helped], [bands, helped_bands]
+    height, width = m.shape[0] // steps, m.shape[1] // steps
+    m, code, bands = call(
+        last_rows_kernel,
+        (
+            jax.ShapeDtypeStruct(m.shape, jnp.float32),
+            jax.ShapeDtypeStruct((m.shape[0] + code_rows, m.shape[1]), jnp.int16),
+            jax.ShapeDtypeStruct((2 * height, width), jnp.float32),
+        ),
+        m,
+        far_hidden,
+        far_grad,
+        cross_hidden,
+        cross_grad,
+        swapped,
+        places,
+        *matrices,
+    )
+    code = send(code, outward)
+    (bands, end_bands), (stride, count) = summed_but_last(bands, "rep", lambda x: (x[:height], x[height:]))
+    parts = [bands] + exchanged(bands, "rep", stride, count)
+    for k in range(count):
+        perm = [
+            (i * 4 + a, (i ^ (stride * k)) * 4 + b) for i in range(lax.axis_size("rep")) for a, b in outward
+        ]
+        parts.append(lax.ppermute(end_bands, ("rep", "tp"), perm))
+    return [m, code], parts
 
 
 def local(hidden, out_grad, momentum, band_rows, band_start_columns):
@@ -258,17 +308,11 @@
     fits = out_grad.shape[0] % 48 == 0 and 2 * row_count == col_count and places.shape[0] <= place_rows
     form = lined if fits and lax.axis_size("tp") == 4 else gathered
     m_parts, band_parts = form(hidden, out_grad, decay_rate * momentum[0], places, matrices)
-    parts = spread_sum(pair_sum(band_parts), "rep")
     shape = (row_count, col_count)
     momentum_out = call(
-        functools.partial(remove_kernel, len(m_parts)),
-        jax.ShapeDtypeStruct(shape, jnp.float32),
-        *m_parts,
-        *band_parts,
-        places,
-        *matrices,
-    )
-    update = call(update_kernel, jax.ShapeDtypeStruct(shape, jnp.bfloat16), *parts, places, *matrices)
+        remove_kernel, jax.ShapeDtypeStruct(shape, jnp.float32), *m_parts, places, *matrices[1:]
+    )
+    update = call(update_kernel, jax.ShapeDtypeStruct(shape, jnp.bfloat16), *band_parts, places, *matrices)
     return (momentum_out[None], update)
 
 

time: 80.3 us -> 79.9 us (level)
  waiting for transfers between devices: 49.7 us -> 48.2 us
  starting transfers between devices: 14.2 us -> 15.2 us
    ppermute x6 -> x5, waiting for transfers between devices: 44.7 us -> 35.7 us  [send(): return lax.ppermute(x, 'tp', perm)]
    ppermute x4 -> x6, waiting for transfers between devices: 5.08 us -> 12.5 us  [the longest x2 10.1 us: lined(): parts.append(lax.ppermute(end_bands, ('rep', 'tp'), perm))]
    ppermute x4 -> x6, starting transfers between devices: 3.8 us -> 6.09 us  [the longest x4 3.52 us: exchanged(): lax.ppermute(x, axis, [(i, i ^ stride * k) for i in range(size)])]
    ppermute x6 -> x5, starting transfers between devices: 10.4 us -> 9.08 us  [send(): return lax.ppermute(x, 'tp', perm)]
    pallas_call x4 -> x3, Pallas kernels: 6.38 us -> 6.45 us  [call(): pl.pallas_call(kernel, out_shape=out_shapes, compiler_params=pltpu.Compil...]
  transfers between devices with their start and end apart: 10 -> 11, of which waited for: 7 -> 5; matrix products, arithmetic and copies ran while one was open for 11% -> 11% of each run, Pallas kernels for 4% -> 2%
where the time goes in v3:
time: 79.9 us; the launch traced here: 79.6 us
  waiting for transfers between devices  48.2 us (60%)
  starting transfers between devices  15.2 us (19%)
  Pallas kernels  6.45 us (8%)
  matrix products  4.1 us (5%)
  other arithmetic  3.56 us (4%)
  local copies, waits for them, and re-layouts  1.2 us (2%)
  between operations  0.87 us (1%)
    ppermute x5, waiting for transfers between devices, send(): return lax.ppermute(x, 'tp', perm)  35.7 us
    ppermute x2, waiting for transfers between devices, lined(): parts.append(lax.ppermute(end_bands, ('rep', 'tp'), perm))  10.1 us
    ppermute x5, starting transfers between devices, send(): return lax.ppermute(x, 'tp', perm)  9.08 us
    pallas_call x3, Pallas kernels, call(): pl.pallas_call(kernel, out_shape=out_shapes, compiler_params=pltpu.Compil...  6.45 us
    dot_general x4, matrix products, dot(): lax.dot_general(a, b, (dims, ((), ())), preferred_element_type=jnp.float32)  4.1 us
    ppermute x4, starting transfers between devices, exchanged(): lax.ppermute(x, axis, [(i, i ^ stride * k) for i in range(size)])  3.52 us
    ppermute x2, starting transfers between devices, lined(): parts.append(lax.ppermute(end_bands, ('rep', 'tp'), perm))  2.57 us
    ppermute x4, waiting for transfers between devices, exchanged(): lax.ppermute(x, axis, [(i, i ^ stride * k) for i in range(size)])  2.45 us
  transfers between devices with their start and end apart: 11, of which 5 were waited for; matrix products, arithmetic and copies ran while one was open for 11% of the time, Pallas kernels for 2%

profile of v3, /device:TPU:0, one launch (start us, length us, event | category | flops | bytes accessed | tf_op | source)
XLA Modules:
  0.0 79.6 jit_solution(12246838459804930625)
XLA Ops:
  0.6 0.0 copy-start.5
  0.6 0.0 copy-start.3
  0.7 0.0 copy-start.7
  0.7 0.0 copy-start.6
  0.7 3.1 %collective-permute-start = (bf16[1152,512]{1,0:T(8,128)(2,1)}, bf16[1152,512]{1,0:T(8,128)(2,1)}, u32[]{:S(2)}, u32[]{:S(2)}) collective-permute-start(bf16[1152,512]{1,0:T(8,128)(2,1)} %param.10), channel_id=1, source_target_pairs={{0,1},{1,0},{2,3},{3,2},{4,5},{5,4},{6,7},{7,6},{8,9},{9,8},{10,11... | collective-permute-start | bytes 3538952 | tf_op jit(solution)/shard_map/ppermute | solution.py:242
  3.8 0.7 collective-permute-start.1
  4.5 0.0 copy-start.4
  4.5 1.1 %constant_dynamic-slice_fusion.3 = (bf16[384,256]{1,0:T(8,128)(2,1)S(1)}, bf16[384,256]{1,0:T(8,128)(2,1)S(1)}) fusion(bf16[4608,256]{1,0:T(8,128)(2,1)} %param.9, s32[]{:T(128)S(6)} %select_n.40, s32[]{:T(128)S(6)} %select_n.42), kind=kLoop, calls=%fused_computation.24 | loop fusion | bytes 786440 | tf_op jit(solution)/shard_map/dynamic_slice | solution.py:239
  5.6 1.2 %dynamic-slice_select_fusion = (bf16[768,256]{1,0:T(8,128)(2,1)S(1)}, bf16[768,256]{1,0:T(8,128)(2,1)S(1)}) fusion(bf16[4608,256]{1,0:T(8,128)(2,1)} %param.9, s32[]{:T(128)S(6)} %select_n.44, pred[]{:T(512)S(6)} %or.3, s32[]{:T(128)S(6)} %add.54), kind=kLoop, calls=%fused_computation.11 | loop fusion | flops 196608 | bytes 1572873 | tf_op jit(solution)/shard_map/jit(_where)/select_n | solution.py:261
  6.8 0.0 copy-done.5
  6.9 0.0 copy-done.7
  6.9 0.0 copy-done.6
  6.9 0.1 fusion.15
  7.0 0.0 copy-done.3
  7.0 0.0 copy-done.4
  7.0 1.6 %convolution_add_fusion.1 = f32[256,512]{1,0:T(8,128)S(1)} fusion(bf16[1152,512]{1,0:T(8,128)(2,1)S(1)} %copy-done.3, bf16[4608,256]{1,0:T(8,128)(2,1)} %param.9, s32[]{:T(128)S(6)} %select_n.46, f32[1,256,512]{2,1,0:T(8,128)S(1)} %copy-done.4), kind=kOutput, calls=%fused_computation.4 | convolution fusion | flops 302252032 | bytes 2818052 | tf_op jit(solution)/shard_map/dot_general | solution.py:53
  8.6 21.4 %collective-permute-done = bf16[1152,512]{1,0:T(8,128)(2,1)} collective-permute-done((bf16[1152,512]{1,0:T(8,128)(2,1)}, bf16[1152,512]{1,0:T(8,128)(2,1)}, u32[]{:S(2)}, u32[]{:S(2)}) %collective-permute-start) | collective-permute-done | bytes 1179680 | tf_op jit(solution)/shard_map/ppermute | solution.py:242
  30.0 0.7 collective-permute-start.2
  30.8 1.0 %fusion.2 = bf16[784,512]{1,0:T(8,128)(2,1)} fusion(bf16[8,512]{1,0:T(8,128)(2,1)S(1)} %get-tuple-element.26, bf16[768,256]{1,0:T(8,128)(2,1)S(1)} %get-tuple-element.21, bf16[384,256]{1,0:T(8,128)(2,1)S(1)} %get-tuple-element.23, bf16[384,256]{1,0:T(8,128)(2,1)S(1)} %get-tuple-element.22), kind=kLoop, calls=%fused_computation.5 | loop fusion | flops 4014080 | bytes 1597440 | tf_op jit(solution)/shard_map/concatenate | solution.py:260
  31.8 0.0 collective-permute-done.1.cross_ref
  31.8 1.4 %slice_select_fusion = bf16[784,512]{1,0:T(8,128)(2,1)S(1)} fusion(bf16[784,512]{1,0:T(8,128)(2,1)} %fusion.2, bf16[1152,512]{1,0:T(8,128)(2,1)S(1)} %collective-permute-done.1.cross_ref, pred[]{:T(512)S(6)} %or.3), kind=kLoop, calls=%fused_computation.6 | loop fusion | flops 401408 | bytes 2408449 | tf_op jit(solution)/shard_map/jit(_where)/select_n | solution.py:266
  33.1 3.3 %collective-permute-start.3 = (bf16[784,512]{1,0:T(8,128)(2,1)S(1)}, bf16[784,512]{1,0:T(8,128)(2,1)S(1)}, u32[]{:S(2)}, u32[]{:S(2)}) collective-permute-start(bf16[784,512]{1,0:T(8,128)(2,1)S(1)} %slice_select_fusion), channel_id=1, source_target_pairs={{0,1},{1,0},{2,3},{3,2},{4,5},{5,4},{6,7},{7,6},{8,9},{9,8},{10,11... | collective-permute-start | bytes 2408456 | tf_op jit(solution)/shard_map/ppermute | solution.py:242
  36.4 0.0 copy-done.2
  36.4 0.5 fusion.3
  37.0 0.0 copy-start
  37.0 0.0 copy-start.1
  37.0 1.8 %fusion.1.m_ref = f32[256,512]{1,0:T(8,128)S(1)} fusion(f32[256,512]{1,0:T(8,128)S(1)} %fusion.3, f32[256,512]{1,0:T(8,128)S(1)} %convolution_add_fusion.1, bf16[1152,512]{1,0:T(8,128)(2,1)} %collective-permute-done, bf16[4608,256]{1,0:T(8,128)(2,1)S(1)} %copy-done.2, s32[]{:T(128)S(6)} %select_n.47), kind=kOutput, calls=%fused_computation.3 | convolution fusion | flops 302252032 | bytes 3342340 | tf_op jit(solution)/shard_map/dot_general | solution.py:53
  38.9 0.0 collective-permute-done.2.far_ref
  38.9 14.3 %collective-permute-done.3.swapped_ref = bf16[784,512]{1,0:T(8,128)(2,1)S(1)} collective-permute-done((bf16[784,512]{1,0:T(8,128)(2,1)S(1)}, bf16[784,512]{1,0:T(8,128)(2,1)S(1)}, u32[]{:S(2)}, u32[]{:S(2)}) %collective-permute-start.3) | collective-permute-done | bytes 802848 | tf_op jit(solution)/shard_map/ppermute | solution.py:242
  53.1 0.0 copy-done
  53.1 0.0 copy-done.1
  53.1 2.8 %shard_map.104 = (f32[256,512]{1,0:T(8,128)S(1)}, s16[272,512]{1,0:T(8,128)(2,1)S(1)}, f32[128,128]{1,0:T(8,128)S(1)}) custom-call(f32[256,512]{1,0:T(8,128)S(1)} %fusion.1.m_ref, bf16[1152,256]{1,0:T(8,128)(2,1)S(1)} %constant_dynamic-slice_fusion.2.far_hidden_ref, bf16[1152,512]{1,0:T(8,128)(2,1)S(1)} %collective-permute-done.2.far_ref, ...), custom_call_target="tpu_custom_call" | custom-call | flops 400000000 | bytes 4000000 | tf_op jit(solution)/shard_map/pallas_call | solution.py:182
  55.9 0.1 collective-permute-start.5
  56.0 1.6 %collective-permute-start.6 = (f32[128,128]{1,0:T(8,128)S(1)}, f32[128,128]{1,0:T(8,128)S(1)}, u32[]{:S(2)}, u32[]{:S(2)}) collective-permute-start(f32[128,128]{1,0:T(8,128)S(1)} %get-tuple-element.19), channel_id=1, source_target_pairs={{0,8},{4,12},{8,0},{12,4},{16,24},{20,28},{24,16},{28,20},{1,9},{5... | collective-permute-start | bytes 196616 | tf_op jit(solution)/shard_map/ppermute | solution.py:200
  57.6 0.3 collective-permute-start.7
  57.9 1.3 %collective-permute-start.4 = (s16[272,512]{1,0:T(8,128)(2,1)S(1)}, s16[272,512]{1,0:T(8,128)(2,1)S(1)}, u32[]{:S(2)}, u32[]{:S(2)}) collective-permute-start(s16[272,512]{1,0:T(8,128)(2,1)S(1)} %get-tuple-element.18), channel_id=1, source_target_pairs={{1,0},{2,3},{5,4},{6,7},{9,8},{10,11},{13,12},{14,15},{17,16},{18,... | collective-permute-start | bytes 835592 | tf_op jit(solution)/shard_map/ppermute | solution.py:242
  59.2 0.0 collective-permute-done.5
  59.2 1.3 %collective-permute-done.6 = f32[128,128]{1,0:T(8,128)S(1)} collective-permute-done((f32[128,128]{1,0:T(8,128)S(1)}, f32[128,128]{1,0:T(8,128)S(1)}, u32[]{:S(2)}, u32[]{:S(2)}) %collective-permute-start.6) | collective-permute-done | bytes 65568 | tf_op jit(solution)/shard_map/ppermute | solution.py:200
  60.5 1.1 %collective-permute-done.7 = f32[128,128]{1,0:T(8,128)S(1)} collective-permute-done((f32[128,128]{1,0:T(8,128)S(1)}, f32[128,128]{1,0:T(8,128)S(1)}, u32[]{:S(2)}, u32[]{:S(2)}) %collective-permute-start.7) | collective-permute-done | bytes 65568 | tf_op jit(solution)/shard_map/ppermute | solution.py:200
  61.7 1.3 %collective-permute-start.10 = (f32[64,128]{1,0:T(8,128)S(1)}, f32[64,128]{1,0:T(8,128)S(1)}, u32[]{:S(2)}, u32[]{:S(2)}) collective-permute-start(f32[64,128]{1,0:T(8,128)S(1)} %get-tuple-element.24), channel_id=1, source_target_pairs={{1,16},{2,19},{5,20},{6,23},{9,24},{10,27},{13,28},{14,31},{17,0},... | collective-permute-start | bytes 98312 | tf_op jit(solution)/shard_map/ppermute | solution.py:295
  63.0 1.6 %collective-permute-start.8 = (f32[64,128]{1,0:T(8,128)S(1)}, f32[64,128]{1,0:T(8,128)S(1)}, u32[]{:S(2)}, u32[]{:S(2)}) collective-permute-start(f32[64,128]{1,0:T(8,128)S(1)} %get-tuple-element.25.refs_0_), channel_id=1, source_target_pairs={{0,16},{4,20},{8,24},{12,28},{16,0},{20,4},{24,8},{28,12},{1,17},{... | collective-permute-start | bytes 98312 | tf_op jit(solution)/shard_map/ppermute | solution.py:200
  64.6 1.3 %collective-permute-start.9 = (f32[64,128]{1,0:T(8,128)S(1)}, f32[64,128]{1,0:T(8,128)S(1)}, u32[]{:S(2)}, u32[]{:S(2)}) collective-permute-start(f32[64,128]{1,0:T(8,128)S(1)} %get-tuple-element.24), channel_id=1, source_target_pairs={{1,0},{2,3},{5,4},{6,7},{9,8},{10,11},{13,12},{14,15},{17,16},{18,... | collective-permute-start | bytes 98312 | tf_op jit(solution)/shard_map/ppermute | solution.py:295
  65.8 10.1 %collective-permute-done.10.refs_3_ = f32[64,128]{1,0:T(8,128)S(1)} collective-permute-done((f32[64,128]{1,0:T(8,128)S(1)}, f32[64,128]{1,0:T(8,128)S(1)}, u32[]{:S(2)}, u32[]{:S(2)}) %collective-permute-start.10) | collective-permute-done | bytes 32800 | tf_op jit(solution)/shard_map/ppermute | solution.py:295
  75.9 0.0 collective-permute-done.8.refs_1_
  75.9 0.0 collective-permute-done.9.refs_2_
  75.9 1.6 %shard_map.106 = bf16[256,512]{1,0:T(8,128)(2,1)} custom-call(f32[64,128]{1,0:T(8,128)S(1)} %get-tuple-element.25.refs_0_, f32[64,128]{1,0:T(8,128)S(1)} %collective-permute-done.8.refs_1_, f32[64,128]{1,0:T(8,128)S(1)} %collective-permute-done.9.refs_2_, f32[64,128]{1,0:T(8,128)S(1)} %collective-permute-done.10.refs_3_, ...), custom_call_target="tpu_custom_call" | custom-call | flops 400000000 | bytes 4000000 | tf_op jit(solution)/shard_map/pallas_call | solution.py:182
  77.5 0.0 collective-permute-done.4.refs_0_
  77.5 2.1 %shard_map.105 = f32[256,512]{1,0:T(8,128)} custom-call(f32[256,512]{1,0:T(8,128)S(1)} %get-tuple-element.17.m_ref, s16[272,512]{1,0:T(8,128)(2,1)S(1)} %collective-permute-done.4.refs_0_, f32[8,512]{1,0:T(8,128)S(1)} %get-tuple-element.27.places_ref.refs_1_.refs_4_, bf16[2,256,256]{2,1,0:T(8,128)(2,1)S(1)} %copy-done, bf16[2,256,256]{2,1,0:T(8,128)(2,1)S(1)} %copy-done), custom_call_target="tpu_custom_call" | custom-call | flops 400000000 | bytes 4000000 | tf_op jit(solution)/shard_map/pallas_call | solution.py:182
  (4 shorter events, 0.1 us)
Async XLA Ops:
  0.6 6.2 %copy-start.5 = (bf16[8,512]{1,0:T(8,128)(2,1)S(1)}, bf16[8,512]{1,0:T(8,128)(2,1)}, u32[]{:S(2)}) copy-start(bf16[8,512]{1,0:T(8,128)(2,1)} %constant.51) | copy-start | bytes 24580
  0.6 6.4 %copy-start.3 = (bf16[1152,512]{1,0:T(8,128)(2,1)S(1)}, bf16[1152,512]{1,0:T(8,128)(2,1)}, u32[]{:S(2)}) copy-start(bf16[1152,512]{1,0:T(8,128)(2,1)} %param.10) | copy-start | bytes 3538948
  0.7 6.2 %copy-start.7 = (s32[4,8]{1,0:T(4,128)S(1)}, s32[4,8]{1,0:T(4,128)}, u32[]{:S(2)}) copy-start(s32[4,8]{1,0:T(4,128)} %param.12) | copy-start | bytes 388
  0.7 6.2 %copy-start.6 = (s32[4,8]{1,0:T(4,128)S(1)}, s32[4,8]{1,0:T(4,128)}, u32[]{:S(2)}) copy-start(s32[4,8]{1,0:T(4,128)} %param.13) | copy-start | bytes 388
  0.7 29.4 %collective-permute-start = (bf16[1152,512]{1,0:T(8,128)(2,1)}, bf16[1152,512]{1,0:T(8,128)(2,1)}, u32[]{:S(2)}, u32[]{:S(2)}) collective-permute-start(bf16[1152,512]{1,0:T(8,128)(2,1)} %param.10), channel_id=1, source_target_pairs={{0,1},{1,0},{2,3},{3,2},{4,5},{5,4},{6,7},{7,6},{8,9},{9,8},{10,11... | collective-permute-start | bytes 3538952 | tf_op jit(solution)/shard_map/ppermute | solution.py:242
  3.8 28.0 %collective-permute-start.1 = (bf16[1152,512]{1,0:T(8,128)(2,1)}, bf16[1152,512]{1,0:T(8,128)(2,1)S(1)}, u32[]{:S(2)}, u32[]{:S(2)}) collective-permute-start(bf16[1152,512]{1,0:T(8,128)(2,1)} %param.10), channel_id=1, source_target_pairs={{1,2},{2,1},{5,6},{6,5},{9,10},{10,9},{13,14},{14,13},{17,18},{18,... | collective-permute-start | bytes 3538952 | tf_op jit(solution)/shard_map/ppermute | solution.py:242
  4.5 2.5 %copy-start.4 = (f32[1,256,512]{2,1,0:T(8,128)S(1)}, f32[1,256,512]{2,1,0:T(8,128)}, u32[]{:S(2)}) copy-start(f32[1,256,512]{2,1,0:T(8,128)} %param.11) | copy-start | bytes 1572868
  30.0 8.8 %collective-permute-start.2 = (bf16[1152,512]{1,0:T(8,128)(2,1)}, bf16[1152,512]{1,0:T(8,128)(2,1)S(1)}, u32[]{:S(2)}, u32[]{:S(2)}) collective-permute-start(bf16[1152,512]{1,0:T(8,128)(2,1)} %collective-permute-done), channel_id=1, source_target_pairs={{1,2},{2,1},{5,6},{6,5},{9,10},{10,9},{13,14},{14,13},{17,18},{18,... | collective-permute-start | bytes 3538952 | tf_op jit(solution)/shard_map/ppermute | solution.py:242
  31.8 4.7 %copy-start.2 = (bf16[4608,256]{1,0:T(8,128)(2,1)S(1)}, bf16[4608,256]{1,0:T(8,128)(2,1)}, u32[]{:S(2)}) copy-start(bf16[4608,256]{1,0:T(8,128)(2,1)} %param.9) | copy-start | bytes 7077892
  33.1 20.0 %collective-permute-start.3 = (bf16[784,512]{1,0:T(8,128)(2,1)S(1)}, bf16[784,512]{1,0:T(8,128)(2,1)S(1)}, u32[]{:S(2)}, u32[]{:S(2)}) collective-permute-start(bf16[784,512]{1,0:T(8,128)(2,1)S(1)} %slice_select_fusion), channel_id=1, source_target_pairs={{0,1},{1,0},{2,3},{3,2},{4,5},{5,4},{6,7},{7,6},{8,9},{9,8},{10,11... | collective-permute-start | bytes 2408456 | tf_op jit(solution)/shard_map/ppermute | solution.py:242
  37.0 16.2 %copy-start = (bf16[2,256,256]{2,1,0:T(8,128)(2,1)S(1)}, bf16[2,256,256]{2,1,0:T(8,128)(2,1)}, u32[]{:S(2)}) copy-start(bf16[2,256,256]{2,1,0:T(8,128)(2,1)} %constant.32.clone.refs_1_.refs_2_.refs_3_.refs_6_.refs_7_) | copy-start | bytes 786436
  37.0 16.1 %copy-start.1 = (bf16[512,128]{1,0:T(8,128)(2,1)S(1)}, bf16[512,128]{1,0:T(8,128)(2,1)}, u32[]{:S(2)}) copy-start(bf16[512,128]{1,0:T(8,128)(2,1)} %constant.31.clone.refs_0_.refs_5_) | copy-start | bytes 393220
  55.9 3.2 %collective-permute-start.5 = (f32[128,128]{1,0:T(8,128)S(1)}, f32[128,128]{1,0:T(8,128)S(1)}, u32[]{:S(2)}, u32[]{:S(2)}) collective-permute-start(f32[128,128]{1,0:T(8,128)S(1)} %get-tuple-element.19), channel_id=1, source_target_pairs={{0,4},{4,0},{8,12},{12,8},{16,20},{20,16},{24,28},{28,24},{1,5},{5... | collective-permute-start | bytes 196616 | tf_op jit(solution)/shard_map/ppermute | solution.py:200
  56.0 4.5 %collective-permute-start.6 = (f32[128,128]{1,0:T(8,128)S(1)}, f32[128,128]{1,0:T(8,128)S(1)}, u32[]{:S(2)}, u32[]{:S(2)}) collective-permute-start(f32[128,128]{1,0:T(8,128)S(1)} %get-tuple-element.19), channel_id=1, source_target_pairs={{0,8},{4,12},{8,0},{12,4},{16,24},{20,28},{24,16},{28,20},{1,9},{5... | collective-permute-start | bytes 196616 | tf_op jit(solution)/shard_map/ppermute | solution.py:200
  57.6 4.0 %collective-permute-start.7 = (f32[128,128]{1,0:T(8,128)S(1)}, f32[128,128]{1,0:T(8,128)S(1)}, u32[]{:S(2)}, u32[]{:S(2)}) collective-permute-start(f32[128,128]{1,0:T(8,128)S(1)} %get-tuple-element.19), channel_id=1, source_target_pairs={{0,12},{4,8},{8,4},{12,0},{16,28},{20,24},{24,20},{28,16},{1,13},{... | collective-permute-start | bytes 196616 | tf_op jit(solution)/shard_map/ppermute | solution.py:200
  57.9 19.6 %collective-permute-start.4 = (s16[272,512]{1,0:T(8,128)(2,1)S(1)}, s16[272,512]{1,0:T(8,128)(2,1)S(1)}, u32[]{:S(2)}, u32[]{:S(2)}) collective-permute-start(s16[272,512]{1,0:T(8,128)(2,1)S(1)} %get-tuple-element.18), channel_id=1, source_target_pairs={{1,0},{2,3},{5,4},{6,7},{9,8},{10,11},{13,12},{14,15},{17,16},{18,... | collective-permute-start | bytes 835592 | tf_op jit(solution)/shard_map/ppermute | solution.py:242
  61.7 14.2 %collective-permute-start.10 = (f32[64,128]{1,0:T(8,128)S(1)}, f32[64,128]{1,0:T(8,128)S(1)}, u32[]{:S(2)}, u32[]{:S(2)}) collective-permute-start(f32[64,128]{1,0:T(8,128)S(1)} %get-tuple-element.24), channel_id=1, source_target_pairs={{1,16},{2,19},{5,20},{6,23},{9,24},{10,27},{13,28},{14,31},{17,0},... | collective-permute-start | bytes 98312 | tf_op jit(solution)/shard_map/ppermute | solution.py:295
  63.0 12.9 %collective-permute-start.8 = (f32[64,128]{1,0:T(8,128)S(1)}, f32[64,128]{1,0:T(8,128)S(1)}, u32[]{:S(2)}, u32[]{:S(2)}) collective-permute-start(f32[64,128]{1,0:T(8,128)S(1)} %get-tuple-element.25.refs_0_), channel_id=1, source_target_pairs={{0,16},{4,20},{8,24},{12,28},{16,0},{20,4},{24,8},{28,12},{1,17},{... | collective-permute-start | bytes 98312 | tf_op jit(solution)/shard_map/ppermute | solution.py:200
  64.6 11.3 %collective-permute-start.9 = (f32[64,128]{1,0:T(8,128)S(1)}, f32[64,128]{1,0:T(8,128)S(1)}, u32[]{:S(2)}, u32[]{:S(2)}) collective-permute-start(f32[64,128]{1,0:T(8,128)S(1)} %get-tuple-element.24), channel_id=1, source_target_pairs={{1,0},{2,3},{5,4},{6,7},{9,8},{10,11},{13,12},{14,15},{17,16},{18,... | collective-permute-start | bytes 98312 | tf_op jit(solution)/shard_map/ppermute | solution.py:295

commit v4 on v3

--- a/solution.py
+++ b/solution.py
@@ -135,22 +135,29 @@
     return values * jnp.exp2(row[:1] - 15.0)
 
 
-def last_rows_kernel(m_ref, far_hidden_ref, far_ref, cross_hidden_ref, cross_ref, swapped_ref, places_ref, *refs):
-    *matrix_refs, out_ref, code_ref, bands_ref = refs
+def swapped_kernel(m_ref, far_hidden_ref, cross_hidden_ref, cross_ref, swapped_ref, *out_refs):
+    out_ref, helped_ref, own_turned_ref, end_turned_ref, end_places_ref = out_refs
     handed, side = swapped_ref.shape[0] - place_rows, out_ref.shape[0]
-    alone, count = cross_ref.shape[0] - handed, bands_ref.shape[0] // 2
-    helped = (
-        dot(swapped_ref[:alone, :side], cross_ref[handed:], ((0,), (0,)))
-        + dot(swapped_ref[alone:handed, :side], far_ref[: handed - alone], ((0,), (0,)))
-        + dot(swapped_ref[:handed, side:], far_ref[handed - alone :], ((0,), (0,)))
-    )
-    code_ref[:side], code_ref[side:] = coded(helped)
-    bands_ref[count:] = bands_of(helped, swapped_ref[handed:].astype(jnp.float32), *matrix_refs)
-    out_ref[...] = (
-        m_ref[...]
-        + dot(far_hidden_ref[...], far_ref[...], ((0,), (0,)))
-        + dot(cross_hidden_ref[...], swapped_ref[:handed], ((0,), (0,)))
-    )
+    alone = cross_ref.shape[0] - handed
+    out_ref[...] = m_ref[...] + dot(cross_hidden_ref[...], swapped_ref[:handed], ((0,), (0,)))
+    helped_ref[...] = dot(swapped_ref[:alone, :side], cross_ref[handed:], ((0,), (0,)))
+    own_turned_ref[...] = far_hidden_ref[...].T
+    end_turned_ref[:, : handed - alone] = swapped_ref[alone:handed, :side].T
+    end_turned_ref[:, handed - alone :] = swapped_ref[:handed, side:].T
+    end_places_ref[...] = swapped_ref[handed:].astype(jnp.float32)
+
+
+def helped_kernel(helped_ref, end_turned_ref, far_ref, out_ref, code_ref):
+    out_ref[...] = helped_ref[...] + dot(end_turned_ref[...], far_ref[...])
+    side = out_ref.shape[0]
+    code_ref[:side], code_ref[side:] = coded(out_ref[...])
+
+
+def last_rows_kernel(m_ref, own_turned_ref, far_ref, helped_ref, places_ref, end_places_ref, *refs):
+    *matrix_refs, out_ref, bands_ref = refs
+    count = bands_ref.shape[0] // 2
+    bands_ref[count:] = bands_of(helped_ref[...], end_places_ref[...], *matrix_refs)
+    out_ref[...] = m_ref[...] + dot(own_turned_ref[...], far_ref[...])
     bands_ref[:count] = bands_of(out_ref[...], places_ref[...], *matrix_refs)
 
 
@@ -265,27 +272,22 @@
     cross_grad = after(cross_grad, pair_grad, m)
     swapped = send(jnp.where(end, helped_hidden, cross_grad[: handed + place_rows]), both_ways)
     m = m + product(rows_of(me ^ 1), pair_grad) + product(rows_of(cross), cross_grad)
+
+    height, width = m.shape[0] // steps, m.shape[1] // steps
+    full = jax.ShapeDtypeStruct(m.shape, jnp.float32)
+    turned = jax.ShapeDtypeStruct((m.shape[0], tok), hidden.dtype)
+    table = jax.ShapeDtypeStruct((place_rows, m.shape[1]), jnp.float32)
+    m, helped, own_turned, end_turned, end_places = call(
+        swapped_kernel, (full, full, turned, turned, table), m, far_hidden, cross_hidden, cross_grad, swapped
+    )
     far_grad = after(far_grad, m)
-    swapped = after(swapped, far_grad)
-
-    height, width = m.shape[0] // steps, m.shape[1] // steps
-    m, code, bands = call(
-        last_rows_kernel,
-        (
-            jax.ShapeDtypeStruct(m.shape, jnp.float32),
-            jax.ShapeDtypeStruct((m.shape[0] + code_rows, m.shape[1]), jnp.int16),
-            jax.ShapeDtypeStruct((2 * height, width), jnp.float32),
-        ),
-        m,
-        far_hidden,
-        far_grad,
-        cross_hidden,
-        cross_grad,
-        swapped,
-        places,
-        *matrices,
-    )
+    code_shape = jax.ShapeDtypeStruct((m.shape[0] + code_rows, m.shape[1]), jnp.int16)
+    helped, code = call(helped_kernel, (full, code_shape), helped, end_turned, far_grad)
     code = send(code, outward)
+    folded = jax.ShapeDtypeStruct((2 * height, width), jnp.float32)
+    m, bands = call(
+        last_rows_kernel, (full, folded), m, own_turned, far_grad, helped, places, end_places, *matrices
+    )
     (bands, end_bands), (stride, count) = summed_but_last(bands, "rep", lambda x: (x[:height], x[height:]))
     parts = [bands] + exchanged(bands, "rep", stride, count)
     for k in range(count):
@@ -312,6 +314,7 @@
     momentum_out = call(
         remove_kernel, jax.ShapeDtypeStruct(shape, jnp.float32), *m_parts, places, *matrices[1:]
     )
+    *band_parts, momentum_out = lax.optimization_barrier((*band_parts, momentum_out))
     update = call(update_kernel, jax.ShapeDtypeStruct(shape, jnp.bfloat16), *band_parts, places, *matrices)
     return (momentum_out[None], update)
 

time: 79.9 us -> 77.9 us (0.975)
  waiting for transfers between devices: 48.2 us -> 45.7 us
    ppermute x2, waiting for transfers between devices: 10.1 us -> 0.01 us  [lined(): parts.append(lax.ppermute(end_bands, ('rep', 'tp'), perm))]
    ppermute x5, waiting for transfers between devices: 35.7 us -> 43 us  [send(): return lax.ppermute(x, 'tp', perm)]
    pallas_call x3 -> x5, Pallas kernels: 6.45 us -> 6.72 us  [call(): pl.pallas_call(kernel, out_shape=out_shapes, compiler_params=pltpu.Compil...]
  transfers between devices with their start and end apart: 11 -> 11, of which waited for: 5 -> 5; matrix products, arithmetic and copies ran while one was open for 11% -> 11% of each run, Pallas kernels for 2% -> 3%
where the time goes in v4:
time: 77.9 us; the launch traced here: 77.6 us
  waiting for transfers between devices  45.7 us (59%)
  starting transfers between devices  15.2 us (20%)
  Pallas kernels  6.72 us (9%)
  matrix products  4.05 us (5%)
  other arithmetic  3.55 us (5%)
  local copies, waits for them, and re-layouts  1.54 us (2%)
  between operations  0.87 us (1%)
    ppermute x5, waiting for transfers between devices, send(): return lax.ppermute(x, 'tp', perm)  43 us
    ppermute x5, starting transfers between devices, send(): return lax.ppermute(x, 'tp', perm)  9.08 us
    pallas_call x5, Pallas kernels, call(): pl.pallas_call(kernel, out_shape=out_shapes, compiler_params=pltpu.Compil...  6.72 us
    dot_general x4, matrix products, dot(): lax.dot_general(a, b, (dims, ((), ())), preferred_element_type=jnp.float32)  4.05 us
    ppermute x4, starting transfers between devices, exchanged(): lax.ppermute(x, axis, [(i, i ^ stride * k) for i in range(size)])  3.5 us
    ppermute x4, waiting for transfers between devices, exchanged(): lax.ppermute(x, axis, [(i, i ^ stride * k) for i in range(size)])  2.65 us
    ppermute x2, starting transfers between devices, lined(): parts.append(lax.ppermute(end_bands, ('rep', 'tp'), perm))  2.58 us
  transfers between devices with their start and end apart: 11, of which 5 were waited for; matrix products, arithmetic and copies ran while one was open for 11% of the time, Pallas kernels for 3%

profile of v4, /device:TPU:0, one launch (start us, length us, event | category | flops | bytes accessed | tf_op | source)
XLA Modules:
  0.0 77.6 jit_solution(17139856377496104591)
XLA Ops:
  0.6 0.0 copy-start.5
  0.6 0.0 copy-start.3
  0.7 0.0 copy-start.6
  0.7 0.0 copy-start.7
  0.7 3.1 %collective-permute-start = (bf16[1152,512]{1,0:T(8,128)(2,1)}, bf16[1152,512]{1,0:T(8,128)(2,1)}, u32[]{:S(2)}, u32[]{:S(2)}) collective-permute-start(bf16[1152,512]{1,0:T(8,128)(2,1)} %param.10), channel_id=1, source_target_pairs={{0,1},{1,0},{2,3},{3,2},{4,5},{5,4},{6,7},{7,6},{8,9},{9,8},{10,11... | collective-permute-start | bytes 3538952 | tf_op jit(solution)/shard_map/ppermute | solution.py:249
  3.8 0.7 collective-permute-start.1
  4.5 0.0 copy-start.4
  4.5 1.1 %constant_dynamic-slice_fusion.3 = (bf16[384,256]{1,0:T(8,128)(2,1)S(1)}, bf16[384,256]{1,0:T(8,128)(2,1)S(1)}) fusion(bf16[4608,256]{1,0:T(8,128)(2,1)} %param.9, s32[]{:T(128)S(6)} %select_n.40, s32[]{:T(128)S(6)} %select_n.42), kind=kLoop, calls=%fused_computation.24 | loop fusion | bytes 786440 | tf_op jit(solution)/shard_map/dynamic_slice | solution.py:246
  5.6 1.2 %dynamic-slice_select_fusion = (bf16[768,256]{1,0:T(8,128)(2,1)S(1)}, bf16[768,256]{1,0:T(8,128)(2,1)S(1)}) fusion(bf16[4608,256]{1,0:T(8,128)(2,1)} %param.9, s32[]{:T(128)S(6)} %select_n.44, pred[]{:T(512)S(6)} %or.3, s32[]{:T(128)S(6)} %add.54), kind=kLoop, calls=%fused_computation.11 | loop fusion | flops 196608 | bytes 1572873 | tf_op jit(solution)/shard_map/jit(_where)/select_n | solution.py:268
  6.8 0.0 copy-done.5
  6.8 0.0 copy-done.6
  6.9 0.0 copy-done.7
  6.9 0.1 fusion.15
  7.0 0.0 copy-done.3
  7.0 1.6 %convolution_add_fusion.1 = f32[256,512]{1,0:T(8,128)S(1)} fusion(bf16[1152,512]{1,0:T(8,128)(2,1)S(1)} %copy-done.3, bf16[4608,256]{1,0:T(8,128)(2,1)} %param.9, s32[]{:T(128)S(6)} %select_n.46, f32[1,256,512]{2,1,0:T(8,128)S(1)} %copy-done.4), kind=kOutput, calls=%fused_computation.4 | convolution fusion | flops 302252032 | bytes 2818052 | tf_op jit(solution)/shard_map/dot_general | solution.py:53
  8.6 21.5 %collective-permute-done = bf16[1152,512]{1,0:T(8,128)(2,1)} collective-permute-done((bf16[1152,512]{1,0:T(8,128)(2,1)}, bf16[1152,512]{1,0:T(8,128)(2,1)}, u32[]{:S(2)}, u32[]{:S(2)}) %collective-permute-start) | collective-permute-done | bytes 1179680 | tf_op jit(solution)/shard_map/ppermute | solution.py:249
  30.0 0.7 collective-permute-start.3
  30.8 1.0 %fusion.2 = bf16[784,512]{1,0:T(8,128)(2,1)} fusion(bf16[8,512]{1,0:T(8,128)(2,1)S(1)} %get-tuple-element.46, bf16[768,256]{1,0:T(8,128)(2,1)S(1)} %get-tuple-element.41, bf16[384,256]{1,0:T(8,128)(2,1)S(1)} %get-tuple-element.43, bf16[384,256]{1,0:T(8,128)(2,1)S(1)} %get-tuple-element.42), kind=kLoop, calls=%fused_computation.5 | loop fusion | flops 4014080 | bytes 1597440 | tf_op jit(solution)/shard_map/concatenate | solution.py:267
  31.7 0.0 collective-permute-done.1.cross_ref
  31.7 1.4 %slice_select_fusion = bf16[784,512]{1,0:T(8,128)(2,1)S(1)} fusion(bf16[784,512]{1,0:T(8,128)(2,1)} %fusion.2, bf16[1152,512]{1,0:T(8,128)(2,1)S(1)} %collective-permute-done.1.cross_ref, pred[]{:T(512)S(6)} %or.3), kind=kLoop, calls=%fused_computation.6 | loop fusion | flops 401408 | bytes 2408449 | tf_op jit(solution)/shard_map/jit(_where)/select_n | solution.py:273
  33.1 3.3 %collective-permute-start.2 = (bf16[784,512]{1,0:T(8,128)(2,1)S(1)}, bf16[784,512]{1,0:T(8,128)(2,1)S(1)}, u32[]{:S(2)}, u32[]{:S(2)}) collective-permute-start(bf16[784,512]{1,0:T(8,128)(2,1)S(1)} %slice_select_fusion), channel_id=1, source_target_pairs={{0,1},{1,0},{2,3},{3,2},{4,5},{5,4},{6,7},{7,6},{8,9},{9,8},{10,11... | collective-permute-start | bytes 2408456 | tf_op jit(solution)/shard_map/ppermute | solution.py:249
  36.4 0.5 fusion.3
  37.0 1.8 %fusion.1.m_ref = f32[256,512]{1,0:T(8,128)S(1)} fusion(f32[256,512]{1,0:T(8,128)S(1)} %fusion.3, f32[256,512]{1,0:T(8,128)S(1)} %convolution_add_fusion.1, bf16[1152,512]{1,0:T(8,128)(2,1)} %collective-permute-done, bf16[4608,256]{1,0:T(8,128)(2,1)S(1)} %copy-done.2, s32[]{:T(128)S(6)} %select_n.47), kind=kOutput, calls=%fused_computation.3 | convolution fusion | flops 302252032 | bytes 3342340 | tf_op jit(solution)/shard_map/dot_general | solution.py:53
  38.8 14.3 %collective-permute-done.2.swapped_ref = bf16[784,512]{1,0:T(8,128)(2,1)S(1)} collective-permute-done((bf16[784,512]{1,0:T(8,128)(2,1)S(1)}, bf16[784,512]{1,0:T(8,128)(2,1)S(1)}, u32[]{:S(2)}, u32[]{:S(2)}) %collective-permute-start.2) | collective-permute-done | bytes 802848 | tf_op jit(solution)/shard_map/ppermute | solution.py:249
  53.1 0.5 shard_map.104
  53.7 0.0 copy-start
  53.7 0.0 copy-start.1
  53.7 0.0 collective-permute-done.3.far_ref
  53.7 0.6 shard_map.105
  54.3 0.3 copy-done
  54.6 0.0 copy-done.1
  54.7 1.9 %shard_map.106 = (f32[256,512]{1,0:T(8,128)S(1)}, f32[128,128]{1,0:T(8,128)S(1)}) custom-call(f32[256,512]{1,0:T(8,128)S(1)} %get-tuple-element.25.m_ref, bf16[256,1152]{1,0:T(8,128)(2,1)S(1)} %get-tuple-element.26.own_turned_ref, bf16[1152,512]{1,0:T(8,128)(2,1)S(1)} %collective-permute-done.3.far_ref, f32[256,512]{1,0:T(8,128)S(1)} %get-tuple-element.30.helped_ref, ...), custom_call_target="tpu_custom_call" | custom-call | flops 400000000 | bytes 4000000 | tf_op jit(solution)/shard_map/pallas_call | solution.py:189
  56.6 0.1 collective-permute-start.6
  56.7 1.6 %collective-permute-start.5 = (f32[128,128]{1,0:T(8,128)S(1)}, f32[128,128]{1,0:T(8,128)S(1)}, u32[]{:S(2)}, u32[]{:S(2)}) collective-permute-start(f32[128,128]{1,0:T(8,128)S(1)} %get-tuple-element.32), channel_id=1, source_target_pairs={{0,8},{4,12},{8,0},{12,4},{16,24},{20,28},{24,16},{28,20},{1,9},{5... | collective-permute-start | bytes 196616 | tf_op jit(solution)/shard_map/ppermute | solution.py:207
  58.2 0.3 collective-permute-start.4
  58.5 1.3 %collective-permute-start.10 = (s16[272,512]{1,0:T(8,128)(2,1)S(1)}, s16[272,512]{1,0:T(8,128)(2,1)S(1)}, u32[]{:S(2)}, u32[]{:S(2)}) collective-permute-start(s16[272,512]{1,0:T(8,128)(2,1)S(1)} %get-tuple-element.34), channel_id=1, source_target_pairs={{1,0},{2,3},{5,4},{6,7},{9,8},{10,11},{13,12},{14,15},{17,16},{18,... | collective-permute-start | bytes 835592 | tf_op jit(solution)/shard_map/ppermute | solution.py:249
  59.8 1.2 %collective-permute-done.6 = f32[128,128]{1,0:T(8,128)S(1)} collective-permute-done((f32[128,128]{1,0:T(8,128)S(1)}, f32[128,128]{1,0:T(8,128)S(1)}, u32[]{:S(2)}, u32[]{:S(2)}) %collective-permute-start.6) | collective-permute-done | bytes 65568 | tf_op jit(solution)/shard_map/ppermute | solution.py:207
  61.0 1.4 %collective-permute-done.5 = f32[128,128]{1,0:T(8,128)S(1)} collective-permute-done((f32[128,128]{1,0:T(8,128)S(1)}, f32[128,128]{1,0:T(8,128)S(1)}, u32[]{:S(2)}, u32[]{:S(2)}) %collective-permute-start.5) | collective-permute-done | bytes 65568 | tf_op jit(solution)/shard_map/ppermute | solution.py:207
  62.5 0.0 collective-permute-done.4
  62.5 1.3 %collective-permute-start.9 = (f32[64,128]{1,0:T(8,128)S(1)}, f32[64,128]{1,0:T(8,128)S(1)}, u32[]{:S(2)}, u32[]{:S(2)}) collective-permute-start(f32[64,128]{1,0:T(8,128)S(1)} %get-tuple-element.44), channel_id=1, source_target_pairs={{1,16},{2,19},{5,20},{6,23},{9,24},{10,27},{13,28},{14,31},{17,0},... | collective-permute-start | bytes 98312 | tf_op jit(solution)/shard_map/ppermute | solution.py:297
  63.8 1.3 %collective-permute-start.8 = (f32[64,128]{1,0:T(8,128)S(1)}, f32[64,128]{1,0:T(8,128)S(1)}, u32[]{:S(2)}, u32[]{:S(2)}) collective-permute-start(f32[64,128]{1,0:T(8,128)S(1)} %get-tuple-element.44), channel_id=1, source_target_pairs={{1,0},{2,3},{5,4},{6,7},{9,8},{10,11},{13,12},{14,15},{17,16},{18,... | collective-permute-start | bytes 98312 | tf_op jit(solution)/shard_map/ppermute | solution.py:297
  65.1 1.6 %collective-permute-start.7 = (f32[64,128]{1,0:T(8,128)S(1)}, f32[64,128]{1,0:T(8,128)S(1)}, u32[]{:S(2)}, u32[]{:S(2)}) collective-permute-start(f32[64,128]{1,0:T(8,128)S(1)} %get-tuple-element.36.refs_0_), channel_id=1, source_target_pairs={{0,16},{4,20},{8,24},{12,28},{16,0},{20,4},{24,8},{28,12},{1,17},{... | collective-permute-start | bytes 98312 | tf_op jit(solution)/shard_map/ppermute | solution.py:207
  66.7 7.2 %collective-permute-done.10.refs_0_ = s16[272,512]{1,0:T(8,128)(2,1)S(1)} collective-permute-done((s16[272,512]{1,0:T(8,128)(2,1)S(1)}, s16[272,512]{1,0:T(8,128)(2,1)S(1)}, u32[]{:S(2)}, u32[]{:S(2)}) %collective-permute-start.10) | collective-permute-done | bytes 278560 | tf_op jit(solution)/shard_map/ppermute | solution.py:249
  73.9 2.1 %shard_map.107 = f32[256,512]{1,0:T(8,128)} custom-call(f32[256,512]{1,0:T(8,128)S(1)} %get-tuple-element.33.m_ref, s16[272,512]{1,0:T(8,128)(2,1)S(1)} %collective-permute-done.10.refs_0_, f32[8,512]{1,0:T(8,128)S(1)} %get-tuple-element.47.places_ref.refs_1_.refs_4_, bf16[2,256,256]{2,1,0:T(8,128)(2,1)S(1)} %copy-done, bf16[2,256,256]{2,1,0:T(8,128)(2,1)S(1)} %copy-done), custom_call_target="tpu_custom_call" | custom-call | flops 400000000 | bytes 4000000 | tf_op jit(solution)/shard_map/pallas_call | solution.py:189
  76.0 0.0 collective-permute-done.9.refs_3_
  76.0 0.0 collective-permute-done.8.refs_2_
  76.0 0.0 collective-permute-done.7.refs_1_
  76.0 1.6 %shard_map.108 = bf16[256,512]{1,0:T(8,128)(2,1)} custom-call(f32[64,128]{1,0:T(8,128)S(1)} %get-tuple-element.36.refs_0_, f32[64,128]{1,0:T(8,128)S(1)} %collective-permute-done.7.refs_1_, f32[64,128]{1,0:T(8,128)S(1)} %collective-permute-done.8.refs_2_, f32[64,128]{1,0:T(8,128)S(1)} %collective-permute-done.9.refs_3_, ...), custom_call_target="tpu_custom_call" | custom-call | flops 400000000 | bytes 4000000 | tf_op jit(solution)/shard_map/pallas_call | solution.py:189
  (6 shorter events, 0.1 us)
Async XLA Ops:
  0.6 6.2 %copy-start.5 = (bf16[8,512]{1,0:T(8,128)(2,1)S(1)}, bf16[8,512]{1,0:T(8,128)(2,1)}, u32[]{:S(2)}) copy-start(bf16[8,512]{1,0:T(8,128)(2,1)} %constant.51) | copy-start | bytes 24580
  0.6 6.4 %copy-start.3 = (bf16[1152,512]{1,0:T(8,128)(2,1)S(1)}, bf16[1152,512]{1,0:T(8,128)(2,1)}, u32[]{:S(2)}) copy-start(bf16[1152,512]{1,0:T(8,128)(2,1)} %param.10) | copy-start | bytes 3538948
  0.7 6.2 %copy-start.6 = (s32[4,8]{1,0:T(4,128)S(1)}, s32[4,8]{1,0:T(4,128)}, u32[]{:S(2)}) copy-start(s32[4,8]{1,0:T(4,128)} %param.13) | copy-start | bytes 388
  0.7 6.2 %copy-start.7 = (s32[4,8]{1,0:T(4,128)S(1)}, s32[4,8]{1,0:T(4,128)}, u32[]{:S(2)}) copy-start(s32[4,8]{1,0:T(4,128)} %param.12) | copy-start | bytes 388
  0.7 29.4 %collective-permute-start = (bf16[1152,512]{1,0:T(8,128)(2,1)}, bf16[1152,512]{1,0:T(8,128)(2,1)}, u32[]{:S(2)}, u32[]{:S(2)}) collective-permute-start(bf16[1152,512]{1,0:T(8,128)(2,1)} %param.10), channel_id=1, source_target_pairs={{0,1},{1,0},{2,3},{3,2},{4,5},{5,4},{6,7},{7,6},{8,9},{9,8},{10,11... | collective-permute-start | bytes 3538952 | tf_op jit(solution)/shard_map/ppermute | solution.py:249
  3.8 28.0 %collective-permute-start.1 = (bf16[1152,512]{1,0:T(8,128)(2,1)}, bf16[1152,512]{1,0:T(8,128)(2,1)S(1)}, u32[]{:S(2)}, u32[]{:S(2)}) collective-permute-start(bf16[1152,512]{1,0:T(8,128)(2,1)} %param.10), channel_id=1, source_target_pairs={{1,2},{2,1},{5,6},{6,5},{9,10},{10,9},{13,14},{14,13},{17,18},{18,... | collective-permute-start | bytes 3538952 | tf_op jit(solution)/shard_map/ppermute | solution.py:249
  4.5 2.5 %copy-start.4 = (f32[1,256,512]{2,1,0:T(8,128)S(1)}, f32[1,256,512]{2,1,0:T(8,128)}, u32[]{:S(2)}) copy-start(f32[1,256,512]{2,1,0:T(8,128)} %param.11) | copy-start | bytes 1572868
  30.0 23.7 %collective-permute-start.3 = (bf16[1152,512]{1,0:T(8,128)(2,1)}, bf16[1152,512]{1,0:T(8,128)(2,1)S(1)}, u32[]{:S(2)}, u32[]{:S(2)}) collective-permute-start(bf16[1152,512]{1,0:T(8,128)(2,1)} %collective-permute-done), channel_id=1, source_target_pairs={{1,2},{2,1},{5,6},{6,5},{9,10},{10,9},{13,14},{14,13},{17,18},{18,... | collective-permute-start | bytes 3538952 | tf_op jit(solution)/shard_map/ppermute | solution.py:249
  31.7 4.7 %copy-start.2 = (bf16[4608,256]{1,0:T(8,128)(2,1)S(1)}, bf16[4608,256]{1,0:T(8,128)(2,1)}, u32[]{:S(2)}) copy-start(bf16[4608,256]{1,0:T(8,128)(2,1)} %param.9) | copy-start | bytes 7077892
  33.1 20.0 %collective-permute-start.2 = (bf16[784,512]{1,0:T(8,128)(2,1)S(1)}, bf16[784,512]{1,0:T(8,128)(2,1)S(1)}, u32[]{:S(2)}, u32[]{:S(2)}) collective-permute-start(bf16[784,512]{1,0:T(8,128)(2,1)S(1)} %slice_select_fusion), channel_id=1, source_target_pairs={{0,1},{1,0},{2,3},{3,2},{4,5},{5,4},{6,7},{7,6},{8,9},{9,8},{10,11... | collective-permute-start | bytes 2408456 | tf_op jit(solution)/shard_map/ppermute | solution.py:249
  53.7 1.0 %copy-start = (bf16[2,256,256]{2,1,0:T(8,128)(2,1)S(1)}, bf16[2,256,256]{2,1,0:T(8,128)(2,1)}, u32[]{:S(2)}) copy-start(bf16[2,256,256]{2,1,0:T(8,128)(2,1)} %constant.32.clone.refs_1_.refs_2_.refs_3_.refs_6_.refs_7_) | copy-start | bytes 786436
  53.7 1.0 %copy-start.1 = (bf16[512,128]{1,0:T(8,128)(2,1)S(1)}, bf16[512,128]{1,0:T(8,128)(2,1)}, u32[]{:S(2)}) copy-start(bf16[512,128]{1,0:T(8,128)(2,1)} %constant.31.clone.refs_0_.refs_5_) | copy-start | bytes 393220
  56.6 4.4 %collective-permute-start.6 = (f32[128,128]{1,0:T(8,128)S(1)}, f32[128,128]{1,0:T(8,128)S(1)}, u32[]{:S(2)}, u32[]{:S(2)}) collective-permute-start(f32[128,128]{1,0:T(8,128)S(1)} %get-tuple-element.32), channel_id=1, source_target_pairs={{0,12},{4,8},{8,4},{12,0},{16,28},{20,24},{24,20},{28,16},{1,13},{... | collective-permute-start | bytes 196616 | tf_op jit(solution)/shard_map/ppermute | solution.py:207
  56.7 5.8 %collective-permute-start.5 = (f32[128,128]{1,0:T(8,128)S(1)}, f32[128,128]{1,0:T(8,128)S(1)}, u32[]{:S(2)}, u32[]{:S(2)}) collective-permute-start(f32[128,128]{1,0:T(8,128)S(1)} %get-tuple-element.32), channel_id=1, source_target_pairs={{0,8},{4,12},{8,0},{12,4},{16,24},{20,28},{24,16},{28,20},{1,9},{5... | collective-permute-start | bytes 196616 | tf_op jit(solution)/shard_map/ppermute | solution.py:207
  58.2 4.2 %collective-permute-start.4 = (f32[128,128]{1,0:T(8,128)S(1)}, f32[128,128]{1,0:T(8,128)S(1)}, u32[]{:S(2)}, u32[]{:S(2)}) collective-permute-start(f32[128,128]{1,0:T(8,128)S(1)} %get-tuple-element.32), channel_id=1, source_target_pairs={{0,4},{4,0},{8,12},{12,8},{16,20},{20,16},{24,28},{28,24},{1,5},{5... | collective-permute-start | bytes 196616 | tf_op jit(solution)/shard_map/ppermute | solution.py:207
  58.5 15.4 %collective-permute-start.10 = (s16[272,512]{1,0:T(8,128)(2,1)S(1)}, s16[272,512]{1,0:T(8,128)(2,1)S(1)}, u32[]{:S(2)}, u32[]{:S(2)}) collective-permute-start(s16[272,512]{1,0:T(8,128)(2,1)S(1)} %get-tuple-element.34), channel_id=1, source_target_pairs={{1,0},{2,3},{5,4},{6,7},{9,8},{10,11},{13,12},{14,15},{17,16},{18,... | collective-permute-start | bytes 835592 | tf_op jit(solution)/shard_map/ppermute | solution.py:249
  62.5 13.5 %collective-permute-start.9 = (f32[64,128]{1,0:T(8,128)S(1)}, f32[64,128]{1,0:T(8,128)S(1)}, u32[]{:S(2)}, u32[]{:S(2)}) collective-permute-start(f32[64,128]{1,0:T(8,128)S(1)} %get-tuple-element.44), channel_id=1, source_target_pairs={{1,16},{2,19},{5,20},{6,23},{9,24},{10,27},{13,28},{14,31},{17,0},... | collective-permute-start | bytes 98312 | tf_op jit(solution)/shard_map/ppermute | solution.py:297
  63.8 12.2 %collective-permute-start.8 = (f32[64,128]{1,0:T(8,128)S(1)}, f32[64,128]{1,0:T(8,128)S(1)}, u32[]{:S(2)}, u32[]{:S(2)}) collective-permute-start(f32[64,128]{1,0:T(8,128)S(1)} %get-tuple-element.44), channel_id=1, source_target_pairs={{1,0},{2,3},{5,4},{6,7},{9,8},{10,11},{13,12},{14,15},{17,16},{18,... | collective-permute-start | bytes 98312 | tf_op jit(solution)/shard_map/ppermute | solution.py:297
  65.1 10.9 %collective-permute-start.7 = (f32[64,128]{1,0:T(8,128)S(1)}, f32[64,128]{1,0:T(8,128)S(1)}, u32[]{:S(2)}, u32[]{:S(2)}) collective-permute-start(f32[64,128]{1,0:T(8,128)S(1)} %get-tuple-element.36.refs_0_), channel_id=1, source_target_pairs={{0,16},{4,20},{8,24},{12,28},{16,0},{20,4},{24,8},{28,12},{1,17},{... | collective-permute-start | bytes 98312 | tf_op jit(solution)/shard_map/ppermute | solution.py:207

commit v5 on v4

--- a/solution.py
+++ b/solution.py
@@ -23,15 +23,9 @@
     return norm_scale * np.cos(np.pi * (sample_pos + 0.5) * frequency / order)
 
 
-def halves_of(matrix):
-    high = matrix.astype(jnp.bfloat16)
-    low = (matrix - high.astype(matrix.dtype)).astype(jnp.bfloat16)
-    return np.stack([high, low])
-
-
 def diagonal_blocks(width):
     count = next(c for c in (4, 2, 1) if width % (c * order) == 0)
-    return halves_of(np.kron(np.eye(count), basis_matrix()))
+    return np.kron(np.eye(count), basis_matrix()).astype(np.float32)
 
 
 def fold_matrix(width):
@@ -58,16 +52,14 @@
 
 
 def on_rows(basis_ref, x, transposed):
-    basis = basis_ref[0], basis_ref[1]
-    side = basis[0].shape[0]
+    basis, side = split2(basis_ref[...]), basis_ref.shape[0]
     dims = ((0,), (0,)) if transposed else ((1,), (0,))
     parts = [dot3(basis, split2(x[i : i + side]), dims) for i in range(0, x.shape[0], side)]
     return parts[0] if len(parts) == 1 else jnp.concatenate(parts, axis=0)
 
 
 def on_columns(basis_ref, x, transposed):
-    basis = basis_ref[0], basis_ref[1]
-    side = basis[0].shape[0]
+    basis, side = split2(basis_ref[...]), basis_ref.shape[0]
     dims = ((1,), (0,)) if transposed else ((1,), (1,))
     parts = [dot3(split2(x[:, i : i + side]), basis, dims) for i in range(0, x.shape[1], side)]
     return parts[0] if len(parts) == 1 else jnp.concatenate(parts, axis=1)
@@ -83,8 +75,8 @@
     return masks
 
 
-def selected(x, masks, row_basis_ref, column_basis_ref):
-    by_rows = on_rows(row_basis_ref, x, False)
+def selected(x, masks, *basis_refs):
+    by_rows = on_rows(basis_refs[0], x, False)
     pieces = []
     for row, (at, _) in enumerate(masks):
         taken = jnp.zeros((band, x.shape[1]), jnp.float32)
@@ -92,7 +84,7 @@
             start = row * order + step * band
             taken = jnp.where(at == step * band, by_rows[start : start + band], taken)
         pieces.append(taken)
-    coefficients = on_columns(column_basis_ref, jnp.concatenate(pieces, axis=0), False)
+    coefficients = on_columns(basis_refs[-1], jnp.concatenate(pieces, axis=0), False)
     return within(coefficients, masks)
 
 
@@ -102,13 +94,13 @@
     )
 
 
-def restored(x, masks, row_basis_ref, column_basis_ref):
-    by_columns = on_columns(column_basis_ref, x, True)
+def restored(x, masks, *basis_refs):
+    by_columns = on_columns(basis_refs[-1], x, True)
     pieces = []
     for row, (at, _) in enumerate(masks):
         part = by_columns[row * band : (row + 1) * band]
         pieces += [jnp.where(at == step * band, part, 0.0) for step in range(steps)]
-    return on_rows(row_basis_ref, jnp.concatenate(pieces, axis=0), True)
+    return on_rows(basis_refs[0], jnp.concatenate(pieces, axis=0), True)
 
 
 def bands_of(x, places, fold_ref, *basis_refs):
@@ -116,8 +108,9 @@
     return sum(dot(part, fold_ref[...]) for part in split3(taken))
 
 
-def bands_kernel(m_ref, places_ref, fold_ref, row_basis_ref, column_basis_ref, bands_ref):
-    bands_ref[...] = bands_of(m_ref[...], places_ref[...], fold_ref, row_basis_ref, column_basis_ref)
+def bands_kernel(m_ref, places_ref, *refs):
+    *matrix_refs, bands_ref = refs
+    bands_ref[...] = bands_of(m_ref[...], places_ref[...], *matrix_refs)
 
 
 def coded(x):
@@ -129,26 +122,32 @@
     return values, row
 
 
-def decoded(ref):
-    values = ref[: ref.shape[0] - code_rows].astype(jnp.int32).astype(jnp.float32)
-    row = ref[ref.shape[0] - code_rows :].astype(jnp.int32).astype(jnp.float32)
-    return values * jnp.exp2(row[:1] - 15.0)
-
-
-def swapped_kernel(m_ref, far_hidden_ref, cross_hidden_ref, cross_ref, swapped_ref, *out_refs):
+def decoded(code_ref, exponents_ref):
+    values = code_ref[: code_ref.shape[0] - code_rows].astype(jnp.int32).astype(jnp.float32)
+    exponents = exponents_ref[...].astype(jnp.int32).astype(jnp.float32)
+    return values * jnp.exp2(exponents[:1] - 15.0)
+
+
+def swapped_kernel(m_ref, far_hidden_ref, cross_hidden_ref, head_ref, cross_ref, swapped_ref, *out_refs):
     out_ref, helped_ref, own_turned_ref, end_turned_ref, end_places_ref = out_refs
     handed, side = swapped_ref.shape[0] - place_rows, out_ref.shape[0]
-    alone = cross_ref.shape[0] - handed
-    out_ref[...] = m_ref[...] + dot(cross_hidden_ref[...], swapped_ref[:handed], ((0,), (0,)))
-    helped_ref[...] = dot(swapped_ref[:alone, :side], cross_ref[handed:], ((0,), (0,)))
+    alone, first = cross_ref.shape[0] - handed, head_ref.shape[0]
     own_turned_ref[...] = far_hidden_ref[...].T
     end_turned_ref[:, : handed - alone] = swapped_ref[alone:handed, :side].T
     end_turned_ref[:, handed - alone :] = swapped_ref[:handed, side:].T
+    out_ref[...] = (
+        m_ref[...]
+        + dot(cross_hidden_ref[...], swapped_ref[:handed], ((0,), (0,)))
+        + dot(own_turned_ref[:, :first], head_ref[...])
+    )
+    helped_ref[...] = dot(swapped_ref[:alone, :side], cross_ref[handed:], ((0,), (0,))) + dot(
+        end_turned_ref[:, :first], head_ref[...]
+    )
     end_places_ref[...] = swapped_ref[handed:].astype(jnp.float32)
 
 
 def helped_kernel(helped_ref, end_turned_ref, far_ref, out_ref, code_ref):
-    out_ref[...] = helped_ref[...] + dot(end_turned_ref[...], far_ref[...])
+    out_ref[...] = helped_ref[...] + dot(end_turned_ref[:, -far_ref.shape[0] :], far_ref[...])
     side = out_ref.shape[0]
     code_ref[:side], code_ref[side:] = coded(out_ref[...])
 
@@ -157,26 +156,25 @@
     *matrix_refs, out_ref, bands_ref = refs
     count = bands_ref.shape[0] // 2
     bands_ref[count:] = bands_of(helped_ref[...], end_places_ref[...], *matrix_refs)
-    out_ref[...] = m_ref[...] + dot(own_turned_ref[...], far_ref[...])
+    out_ref[...] = m_ref[...] + dot(own_turned_ref[:, -far_ref.shape[0] :], far_ref[...])
     bands_ref[:count] = bands_of(out_ref[...], places_ref[...], *matrix_refs)
 
 
-def remove_kernel(m_ref, *refs):
-    *code_refs, places_ref, row_basis_ref, column_basis_ref, out_ref = refs
+def remove_kernel(count, *refs):
+    (m_ref, *code_refs), (places_ref, *basis_refs, out_ref) = refs[:count], refs[count:]
     m = m_ref[...]
-    for ref in code_refs:
-        m = m + decoded(ref)
+    if code_refs:
+        m = m + decoded(*code_refs)
     masks = masks_of(places_ref[...], m.shape[0] // order)
-    taken = selected(m, masks, row_basis_ref, column_basis_ref)
-    out_ref[...] = m - restored(taken, masks, row_basis_ref, column_basis_ref)
-
-
-def update_kernel(*refs):
-    *part_refs, places_ref, fold_ref, row_basis_ref, column_basis_ref, out_ref = refs
+    out_ref[...] = m - restored(selected(m, masks, *basis_refs), masks, *basis_refs)
+
+
+def update_kernel(count, *refs):
+    part_refs, (places_ref, fold_ref, *basis_refs, out_ref) = refs[:count], refs[count:]
     folded = pair_sum([ref[...] for ref in part_refs])
     masks = masks_of(places_ref[...], out_ref.shape[0] // order)
     spread = sum(dot(part, fold_ref[...], ((1,), (1,))) for part in split3(folded))
-    out_ref[...] = restored(within(spread, masks), masks, row_basis_ref, column_basis_ref).astype(out_ref.dtype)
+    out_ref[...] = restored(within(spread, masks), masks, *basis_refs).astype(out_ref.dtype)
 
 
 def pair_sum(parts):
@@ -207,13 +205,13 @@
     return [lax.ppermute(x, axis, [(i, i ^ (stride * k)) for i in range(size)]) for k in range(1, count)]
 
 
-def summed_but_last(x, axis, form):
+def summed_but_last(x, axis, form, then=lambda x: x):
     size = lax.axis_size(axis)
     if size & (size - 1):
         return form(lax.psum(x, axis)), (1, 1)
     *stages, last = stages_of(axis) or [(1, 1)]
     for stride, count in stages:
-        x = pair_sum([x] + exchanged(x, axis, stride, count))
+        x = pair_sum([x] + then(exchanged(x, axis, stride, count)))
     return form(x), last
 
 
@@ -229,7 +227,7 @@
     m = carried + product(hidden, lax.all_gather(out_grad, "tp", axis=0, tiled=True))
     folded = jax.ShapeDtypeStruct((m.shape[0] // steps, m.shape[1] // steps), jnp.float32)
     bands, last = summed_but_last(call(bands_kernel, folded, m, places, *matrices), "rep", lambda x: x)
-    return [m], [bands] + exchanged(bands, "rep", *last)
+    return [m], [bands] + exchanged(bands, "rep", *last), places, matrices
 
 
 def lined(hidden, out_grad, carried, places, matrices):
@@ -241,6 +239,7 @@
     far = jnp.where(left, 3, 0)
     handed = tok * 2 // 3
     alone = tok - handed
+    first = tok // 4 // 128 * 128
 
     def rows_of(part, start=0, stop=tok):
         return lax.dynamic_slice_in_dim(hidden, part * tok + start, stop - start, 0)
@@ -251,6 +250,7 @@
     both_ways = [(0, 1), (1, 0), (2, 3), (3, 2)]
     across = [(1, 2), (2, 1)]
     outward = [(1, 0), (2, 3)]
+    over_one = [(0, 2), (3, 1)]
 
     pair_grad = send(out_grad, both_ways)
     cross_grad = send(out_grad, across)
@@ -268,8 +268,9 @@
     cross_hidden = jnp.where(end, rows_of(cross, 0, handed), 0)
     helped_hidden, cross_hidden, m = lax.optimization_barrier((helped_hidden, cross_hidden, m))
 
-    far_grad = send(pair_grad, across)
-    cross_grad = after(cross_grad, pair_grad, m)
+    far_head = send(out_grad[:first], over_one)
+    far_grad = send(pair_grad[first:], across)
+    cross_grad, matrices, places = after((cross_grad, matrices, places), pair_grad, far_head, m)
     swapped = send(jnp.where(end, helped_hidden, cross_grad[: handed + place_rows]), both_ways)
     m = m + product(rows_of(me ^ 1), pair_grad) + product(rows_of(cross), cross_grad)
 
@@ -278,7 +279,7 @@
     turned = jax.ShapeDtypeStruct((m.shape[0], tok), hidden.dtype)
     table = jax.ShapeDtypeStruct((place_rows, m.shape[1]), jnp.float32)
     m, helped, own_turned, end_turned, end_places = call(
-        swapped_kernel, (full, full, turned, turned, table), m, far_hidden, cross_hidden, cross_grad, swapped
+        swapped_kernel, (full, full, turned, turned, table), m, far_hidden, cross_hidden, far_head, cross_grad, swapped
     )
     far_grad = after(far_grad, m)
     code_shape = jax.ShapeDtypeStruct((m.shape[0] + code_rows, m.shape[1]), jnp.int16)
@@ -288,34 +289,54 @@
     m, bands = call(
         last_rows_kernel, (full, folded), m, own_turned, far_grad, helped, places, end_places, *matrices
     )
-    (bands, end_bands), (stride, count) = summed_but_last(bands, "rep", lambda x: (x[:height], x[height:]))
+    exponents = code[m.shape[0] :]
+
+    def behind_code(x):
+        nonlocal exponents
+        x, exponents = lax.optimization_barrier((x, exponents))
+        return x
+
+    (bands, end_bands), (stride, count) = summed_but_last(
+        bands, "rep", lambda x: (x[:height], x[height:]), behind_code
+    )
     parts = [bands] + exchanged(bands, "rep", stride, count)
     for k in range(count):
         perm = [
             (i * 4 + a, (i ^ (stride * k)) * 4 + b) for i in range(lax.axis_size("rep")) for a, b in outward
         ]
         parts.append(lax.ppermute(end_bands, ("rep", "tp"), perm))
-    return [m, code], parts
+    return [m, code, exponents], parts, places, matrices
 
 
 def local(hidden, out_grad, momentum, band_rows, band_start_columns):
     row_count = hidden.shape[1]
     col_count = out_grad.shape[1]
     one_hot = jnp.asarray(np.kron(np.eye(col_count // order), np.ones((1, order))), jnp.float32)
-    matrices = tuple(
-        jnp.asarray(x) for x in (fold_matrix(col_count), diagonal_blocks(row_count), diagonal_blocks(col_count))
-    )
+    bases = [diagonal_blocks(row_count), diagonal_blocks(col_count)]
+    if bases[0].shape == bases[1].shape:
+        bases = bases[:1]
+    matrices = tuple(jnp.asarray(x) for x in (fold_matrix(col_count), *bases))
     places = jnp.concatenate([band_rows, band_start_columns], axis=0).astype(jnp.float32)
     places = dot(places, one_hot)
-    fits = out_grad.shape[0] % 48 == 0 and 2 * row_count == col_count and places.shape[0] <= place_rows
+    fits = out_grad.shape[0] % 384 == 0 and out_grad.shape[0] >= 768 and 2 * row_count == col_count and places.shape[0] <= place_rows
     form = lined if fits and lax.axis_size("tp") == 4 else gathered
-    m_parts, band_parts = form(hidden, out_grad, decay_rate * momentum[0], places, matrices)
+    m_parts, band_parts, places, matrices = form(hidden, out_grad, decay_rate * momentum[0], places, matrices)
     shape = (row_count, col_count)
     momentum_out = call(
-        remove_kernel, jax.ShapeDtypeStruct(shape, jnp.float32), *m_parts, places, *matrices[1:]
+        functools.partial(remove_kernel, len(m_parts)),
+        jax.ShapeDtypeStruct(shape, jnp.float32),
+        *m_parts,
+        places,
+        *matrices[1:],
     )
     *band_parts, momentum_out = lax.optimization_barrier((*band_parts, momentum_out))
-    update = call(update_kernel, jax.ShapeDtypeStruct(shape, jnp.bfloat16), *band_parts, places, *matrices)
+    update = call(
+        functools.partial(update_kernel, len(band_parts)),
+        jax.ShapeDtypeStruct(shape, jnp.bfloat16),
+        *band_parts,
+        places,
+        *matrices,
+    )
     return (momentum_out[None], update)
 
 

time: 77.9 us -> 77.9 us (level)
  starting transfers between devices: 15.2 us -> 24.3 us
  waiting for transfers between devices: 45.7 us -> 37.5 us
  local copies, waits for them, and re-layouts: 1.54 us -> 2.88 us
  matrix products: 4.05 us -> 2.79 us
  other arithmetic: 3.55 us -> 2.38 us
    ppermute x5 -> x6, starting transfers between devices: 9.08 us -> 18.2 us  [send(): return lax.ppermute(x, 'tp', perm)]
    ppermute x5 -> x6, waiting for transfers between devices: 43 us -> 35.4 us  [send(): return lax.ppermute(x, 'tp', perm)]
    ppermute x4, waiting for transfers between devices: 2.65 us -> 0.24 us  [exchanged(): lax.ppermute(x, axis, [(i, i ^ stride * k) for i in range(size)])]
    ppermute x2, waiting for transfers between devices: 0.01 us -> 1.81 us  [lined(): parts.append(lax.ppermute(end_bands, ('rep', 'tp'), perm))]
    slice x0 -> x3, local copies, waits for them, and re-layouts: none -> 1.73 us  [the longest x1 1.67 us: lined(): far_head = send(out_grad[:first], over_one)]
    select_n x1, other arithmetic: 1.38 us -> 0.08 us  [lined(): jnp.where(end, helped_hidden, cross_grad[:handed + place_rows])]
    dot_general x4, matrix products: 4.05 us -> 2.79 us  [dot(): lax.dot_general(a, b, (dims, ((), ())), preferred_element_type=jnp.float32)]
  transfers between devices with their start and end apart: 11 -> 12, of which waited for: 5 -> 7; matrix products, arithmetic and copies ran while one was open for 11% -> 10% of each run, Pallas kernels for 3% -> 6%
where the time goes in v5:
time: 77.9 us; the launch traced here: 77.5 us
  waiting for transfers between devices  37.5 us (48%)
  starting transfers between devices  24.3 us (31%)
  Pallas kernels  6.75 us (9%)
  local copies, waits for them, and re-layouts  2.88 us (4%)
  matrix products  2.79 us (4%)
  other arithmetic  2.38 us (3%)
  between operations  0.92 us (1%)
    ppermute x6, waiting for transfers between devices, send(): return lax.ppermute(x, 'tp', perm)  35.4 us
    ppermute x6, starting transfers between devices, send(): return lax.ppermute(x, 'tp', perm)  18.2 us
    pallas_call x5, Pallas kernels, call(): pl.pallas_call(kernel, out_shape=out_shapes, compiler_params=pltpu.Compil...  6.75 us
    ppermute x4, starting transfers between devices, exchanged(): lax.ppermute(x, axis, [(i, i ^ stride * k) for i in range(size)])  3.5 us
    dot_general x4, matrix products, dot(): lax.dot_general(a, b, (dims, ((), ())), preferred_element_type=jnp.float32)  2.79 us
    ppermute x2, starting transfers between devices, lined(): parts.append(lax.ppermute(end_bands, ('rep', 'tp'), perm))  2.58 us
    ppermute x2, waiting for transfers between devices, lined(): parts.append(lax.ppermute(end_bands, ('rep', 'tp'), perm))  1.81 us
    slice x1, local copies, waits for them, and re-layouts, lined(): far_head = send(out_grad[:first], over_one)  1.67 us
  transfers between devices with their start and end apart: 12, of which 7 were waited for; matrix products, arithmetic and copies ran while one was open for 10% of the time, Pallas kernels for 6%

profile of v5, /device:TPU:0, one launch (start us, length us, event | category | flops | bytes accessed | tf_op | source)
XLA Modules:
  0.0 77.5 jit_solution(1861952020677493071)
XLA Ops:
  0.6 0.0 copy-start.6
  0.6 0.0 copy-start.7
  0.7 0.0 copy-start.8
  0.7 3.1 %collective-permute-start = (bf16[1152,512]{1,0:T(8,128)(2,1)}, bf16[1152,512]{1,0:T(8,128)(2,1)S(1)}, u32[]{:S(2)}, u32[]{:S(2)}) collective-permute-start(bf16[1152,512]{1,0:T(8,128)(2,1)} %param.9), channel_id=1, source_target_pairs={{0,1},{1,0},{2,3},{3,2},{4,5},{5,4},{6,7},{7,6},{8,9},{9,8},{10,11... | collective-permute-start | bytes 3538952 | tf_op jit(solution)/shard_map/ppermute | solution.py:248
  3.8 0.7 collective-permute-start.1
  4.5 1.7 %slice.26 = bf16[256,512]{1,0:T(8,128)(2,1)} slice(bf16[1152,512]{1,0:T(8,128)(2,1)} %param.9), slice={[0:256], [0:512]} | slice | bytes 524288 | tf_op jit(solution)/shard_map/slice | solution.py:271
  6.2 5.7 %collective-permute-start.2 = (bf16[256,512]{1,0:T(8,128)(2,1)}, bf16[256,512]{1,0:T(8,128)(2,1)S(1)}, u32[]{:S(2)}, u32[]{:S(2)}) collective-permute-start(bf16[256,512]{1,0:T(8,128)(2,1)} %slice.26), channel_id=1, source_target_pairs={{0,2},{3,1},{4,6},{7,5},{8,10},{11,9},{12,14},{15,13},{16,18},{19,... | collective-permute-start | bytes 786440 | tf_op jit(solution)/shard_map/ppermute | solution.py:248
  11.9 1.1 %constant_dynamic-slice_fusion.3 = (bf16[384,256]{1,0:T(8,128)(2,1)S(1)}, bf16[384,256]{1,0:T(8,128)(2,1)S(1)}) fusion(bf16[4608,256]{1,0:T(8,128)(2,1)} %param.8, s32[]{:T(128)S(6)} %select_n.40, s32[]{:T(128)S(6)} %select_n.42), kind=kLoop, calls=%fused_computation.24 | loop fusion | bytes 786440 | tf_op jit(solution)/shard_map/dynamic_slice | solution.py:245
  12.9 0.0 copy-start.4
  12.9 0.0 copy-start.5
  13.0 1.3 %dynamic-slice_select_fusion = (bf16[768,256]{1,0:T(8,128)(2,1)S(1)}, bf16[768,256]{1,0:T(8,128)(2,1)S(1)}) fusion(bf16[4608,256]{1,0:T(8,128)(2,1)} %param.8, s32[]{:T(128)S(6)} %select_n.44, pred[]{:T(512)S(6)} %or.3, s32[]{:T(128)S(6)} %add.54), kind=kLoop, calls=%fused_computation.11 | loop fusion | flops 196608 | bytes 1572873 | tf_op jit(solution)/shard_map/jit(_where)/select_n | solution.py:268
  14.3 0.1 fusion.15
  14.4 1.0 %fusion.2 = bf16[784,512]{1,0:T(8,128)(2,1)} fusion(bf16[8,512]{1,0:T(8,128)(2,1)S(1)} %get-tuple-element.60, bf16[768,256]{1,0:T(8,128)(2,1)S(1)} %get-tuple-element.55, bf16[384,256]{1,0:T(8,128)(2,1)S(1)} %get-tuple-element.57, bf16[384,256]{1,0:T(8,128)(2,1)S(1)} %get-tuple-element.56), kind=kLoop, calls=%fused_computation.5 | loop fusion | flops 4014080 | bytes 1597440 | tf_op jit(solution)/shard_map/concatenate | solution.py:267
  15.4 0.0 copy-done.5
  15.4 1.6 %convolution_add_fusion.1 = f32[256,512]{1,0:T(8,128)S(1)} fusion(bf16[1152,512]{1,0:T(8,128)(2,1)S(1)} %copy-done.4, bf16[4608,256]{1,0:T(8,128)(2,1)} %param.8, s32[]{:T(128)S(6)} %select_n.46, f32[1,256,512]{2,1,0:T(8,128)S(1)} %copy-done.5), kind=kOutput, calls=%fused_computation.4 | convolution fusion | flops 302252032 | bytes 2818052 | tf_op jit(solution)/shard_map/dot_general | solution.py:47
  17.0 13.4 %collective-permute-done = bf16[1152,512]{1,0:T(8,128)(2,1)S(1)} collective-permute-done((bf16[1152,512]{1,0:T(8,128)(2,1)}, bf16[1152,512]{1,0:T(8,128)(2,1)S(1)}, u32[]{:S(2)}, u32[]{:S(2)}) %collective-permute-start) | collective-permute-done | bytes 1179680 | tf_op jit(solution)/shard_map/ppermute | solution.py:248
  30.4 0.1 slice.32
  30.5 0.0 copy-start.2
  30.5 0.9 %collective-permute-start.4 = (bf16[896,512]{1,0:T(8,128)(2,1)S(1)}, bf16[896,512]{1,0:T(8,128)(2,1)S(1)}, u32[]{:S(2)}, u32[]{:S(2)}) collective-permute-start(bf16[896,512]{1,0:T(8,128)(2,1)S(1)} %slice.32), channel_id=1, source_target_pairs={{1,2},{2,1},{5,6},{6,5},{9,10},{10,9},{13,14},{14,13},{17,18},{18,... | collective-permute-start | bytes 2752520 | tf_op jit(solution)/shard_map/ppermute | solution.py:248
  31.4 3.6 %collective-permute-done.2.head_ref = bf16[256,512]{1,0:T(8,128)(2,1)S(1)} collective-permute-done((bf16[256,512]{1,0:T(8,128)(2,1)}, bf16[256,512]{1,0:T(8,128)(2,1)S(1)}, u32[]{:S(2)}, u32[]{:S(2)}) %collective-permute-start.2) | collective-permute-done | bytes 262176 | tf_op jit(solution)/shard_map/ppermute | solution.py:248
  35.0 0.0 collective-permute-done.1.cross_ref
  35.0 0.1 slice_select_fusion
  35.1 6.6 %collective-permute-start.3 = (bf16[784,512]{1,0:T(8,128)(2,1)S(1)}, bf16[784,512]{1,0:T(8,128)(2,1)S(1)}, u32[]{:S(2)}, u32[]{:S(2)}) collective-permute-start(bf16[784,512]{1,0:T(8,128)(2,1)S(1)} %slice_select_fusion), channel_id=1, source_target_pairs={{0,1},{1,0},{2,3},{3,2},{4,5},{5,4},{6,7},{7,6},{8,9},{9,8},{10,11... | collective-permute-start | bytes 2408456 | tf_op jit(solution)/shard_map/ppermute | solution.py:248
  41.7 0.5 fusion.3
  42.2 0.5 fusion.1.m_ref
  42.8 14.7 %collective-permute-done.3.swapped_ref = bf16[784,512]{1,0:T(8,128)(2,1)S(1)} collective-permute-done((bf16[784,512]{1,0:T(8,128)(2,1)S(1)}, bf16[784,512]{1,0:T(8,128)(2,1)S(1)}, u32[]{:S(2)}, u32[]{:S(2)}) %collective-permute-start.3) | collective-permute-done | bytes 802848 | tf_op jit(solution)/shard_map/ppermute | solution.py:248
  57.5 0.7 shard_map.95
  58.2 0.0 copy-start
  58.2 0.0 copy-start.1
  58.2 0.0 collective-permute-done.4.far_ref
  58.2 0.5 shard_map.96
  58.7 1.3 %collective-permute-start.8 = (s16[272,512]{1,0:T(8,128)(2,1)S(1)}, s16[272,512]{1,0:T(8,128)(2,1)S(1)}, u32[]{:S(2)}, u32[]{:S(2)}) collective-permute-start(s16[272,512]{1,0:T(8,128)(2,1)S(1)} %get-tuple-element.43), channel_id=1, source_target_pairs={{1,0},{2,3},{5,4},{6,7},{9,8},{10,11},{13,12},{14,15},{17,16},{18,... | collective-permute-start | bytes 835592 | tf_op jit(solution)/shard_map/ppermute | solution.py:248
  60.0 1.9 %shard_map.97 = (f32[256,512]{1,0:T(8,128)S(1)}, f32[128,128]{1,0:T(8,128)S(1)}) custom-call(f32[256,512]{1,0:T(8,128)S(1)} %get-tuple-element.32.m_ref, bf16[256,1152]{1,0:T(8,128)(2,1)S(1)} %get-tuple-element.33.own_turned_ref, bf16[896,512]{1,0:T(8,128)(2,1)S(1)} %collective-permute-done.4.far_ref, f32[256,512]{1,0:T(8,128)S(1)} %get-tuple-element.37.helped_ref, ...), custom_call_target="tpu_custom_call" | custom-call | flops 400000000 | bytes 4000000 | tf_op jit(solution)/shard_map/pallas_call | solution.py:187
  61.9 0.1 collective-permute-start.7
  62.0 1.6 %collective-permute-start.6 = (f32[128,128]{1,0:T(8,128)S(1)}, f32[128,128]{1,0:T(8,128)S(1)}, u32[]{:S(2)}, u32[]{:S(2)}) collective-permute-start(f32[128,128]{1,0:T(8,128)S(1)} %get-tuple-element.42), channel_id=1, source_target_pairs={{0,8},{4,12},{8,0},{12,4},{16,24},{20,28},{24,16},{28,20},{1,9},{5... | collective-permute-start | bytes 196616 | tf_op jit(solution)/shard_map/ppermute | solution.py:205
  63.6 0.3 collective-permute-start.5
  63.9 3.7 %collective-permute-done.8.refs_1_ = s16[272,512]{1,0:T(8,128)(2,1)S(1)} collective-permute-done((s16[272,512]{1,0:T(8,128)(2,1)S(1)}, s16[272,512]{1,0:T(8,128)(2,1)S(1)}, u32[]{:S(2)}, u32[]{:S(2)}) %collective-permute-start.8) | collective-permute-done | bytes 278560 | tf_op jit(solution)/shard_map/ppermute | solution.py:248
  67.6 0.0 collective-permute-done.7
  67.6 0.2 collective-permute-done.6
  67.8 0.0 collective-permute-done.5
  67.8 1.3 %collective-permute-start.11 = (f32[64,128]{1,0:T(8,128)S(1)}, f32[64,128]{1,0:T(8,128)S(1)}, u32[]{:S(2)}, u32[]{:S(2)}) collective-permute-start(f32[64,128]{1,0:T(8,128)S(1)} %get-tuple-element.58), channel_id=1, source_target_pairs={{1,16},{2,19},{5,20},{6,23},{9,24},{10,27},{13,28},{14,31},{17,0},... | collective-permute-start | bytes 98312 | tf_op jit(solution)/shard_map/ppermute | solution.py:307
  69.1 1.3 %collective-permute-start.10 = (f32[64,128]{1,0:T(8,128)S(1)}, f32[64,128]{1,0:T(8,128)S(1)}, u32[]{:S(2)}, u32[]{:S(2)}) collective-permute-start(f32[64,128]{1,0:T(8,128)S(1)} %get-tuple-element.58), channel_id=1, source_target_pairs={{1,0},{2,3},{5,4},{6,7},{9,8},{10,11},{13,12},{14,15},{17,16},{18,... | collective-permute-start | bytes 98312 | tf_op jit(solution)/shard_map/ppermute | solution.py:307
  70.4 1.6 %collective-permute-start.9 = (f32[64,128]{1,0:T(8,128)S(1)}, f32[64,128]{1,0:T(8,128)S(1)}, u32[]{:S(2)}, u32[]{:S(2)}) collective-permute-start(f32[64,128]{1,0:T(8,128)S(1)} %get-tuple-element.50.refs_0_), channel_id=1, source_target_pairs={{0,16},{4,20},{8,24},{12,28},{16,0},{20,4},{24,8},{28,12},{1,17},{... | collective-permute-start | bytes 98312 | tf_op jit(solution)/shard_map/ppermute | solution.py:205
  72.0 2.1 %shard_map.98 = f32[256,512]{1,0:T(8,128)} custom-call(f32[256,512]{1,0:T(8,128)S(1)} %get-tuple-element.47.refs_0_, s16[272,512]{1,0:T(8,128)(2,1)S(1)} %collective-permute-done.8.refs_1_, s16[16,512]{1,0:T(8,128)(2,1)S(1)} %slice.33.refs_2_, f32[8,512]{1,0:T(8,128)S(1)} %get-tuple-element.38.places_ref.refs_3_.refs_4_, f32[256,256]{1,0:T(8,128)S(1)} %copy-done), custom_call_target="tpu_custom_call" | custom-call | flops 400000000 | bytes 4000000 | tf_op jit(solution)/shard_map/pallas_call | solution.py:187
  74.1 0.6 collective-permute-done.11.refs_3_
  74.7 1.2 %collective-permute-done.10.refs_2_ = f32[64,128]{1,0:T(8,128)S(1)} collective-permute-done((f32[64,128]{1,0:T(8,128)S(1)}, f32[64,128]{1,0:T(8,128)S(1)}, u32[]{:S(2)}, u32[]{:S(2)}) %collective-permute-start.10) | collective-permute-done | bytes 32800 | tf_op jit(solution)/shard_map/ppermute | solution.py:307
  75.9 0.0 collective-permute-done.9.refs_1_
  75.9 1.6 %shard_map.99 = bf16[256,512]{1,0:T(8,128)(2,1)} custom-call(f32[64,128]{1,0:T(8,128)S(1)} %get-tuple-element.50.refs_0_, f32[64,128]{1,0:T(8,128)S(1)} %collective-permute-done.9.refs_1_, f32[64,128]{1,0:T(8,128)S(1)} %collective-permute-done.10.refs_2_, f32[64,128]{1,0:T(8,128)S(1)} %collective-permute-done.11.refs_3_, ...), custom_call_target="tpu_custom_call" | custom-call | flops 400000000 | bytes 4000000 | tf_op jit(solution)/shard_map/pallas_call | solution.py:187
  (13 shorter events, 0.1 us)
Async XLA Ops:
  0.6 13.7 %copy-start.6 = (bf16[8,512]{1,0:T(8,128)(2,1)S(1)}, bf16[8,512]{1,0:T(8,128)(2,1)}, u32[]{:S(2)}) copy-start(bf16[8,512]{1,0:T(8,128)(2,1)} %constant.51) | copy-start | bytes 24580
  0.6 13.7 %copy-start.7 = (s32[4,8]{1,0:T(4,128)S(1)}, s32[4,8]{1,0:T(4,128)}, u32[]{:S(2)}) copy-start(s32[4,8]{1,0:T(4,128)} %param.12) | copy-start | bytes 388
  0.7 13.7 %copy-start.8 = (s32[4,8]{1,0:T(4,128)S(1)}, s32[4,8]{1,0:T(4,128)}, u32[]{:S(2)}) copy-start(s32[4,8]{1,0:T(4,128)} %param.11) | copy-start | bytes 388
  0.7 29.8 %collective-permute-start = (bf16[1152,512]{1,0:T(8,128)(2,1)}, bf16[1152,512]{1,0:T(8,128)(2,1)S(1)}, u32[]{:S(2)}, u32[]{:S(2)}) collective-permute-start(bf16[1152,512]{1,0:T(8,128)(2,1)} %param.9), channel_id=1, source_target_pairs={{0,1},{1,0},{2,3},{3,2},{4,5},{5,4},{6,7},{7,6},{8,9},{9,8},{10,11... | collective-permute-start | bytes 3538952 | tf_op jit(solution)/shard_map/ppermute | solution.py:248
  3.8 31.2 %collective-permute-start.1 = (bf16[1152,512]{1,0:T(8,128)(2,1)}, bf16[1152,512]{1,0:T(8,128)(2,1)S(1)}, u32[]{:S(2)}, u32[]{:S(2)}) collective-permute-start(bf16[1152,512]{1,0:T(8,128)(2,1)} %param.9), channel_id=1, source_target_pairs={{1,2},{2,1},{5,6},{6,5},{9,10},{10,9},{13,14},{14,13},{17,18},{18,... | collective-permute-start | bytes 3538952 | tf_op jit(solution)/shard_map/ppermute | solution.py:248
  6.2 28.8 %collective-permute-start.2 = (bf16[256,512]{1,0:T(8,128)(2,1)}, bf16[256,512]{1,0:T(8,128)(2,1)S(1)}, u32[]{:S(2)}, u32[]{:S(2)}) collective-permute-start(bf16[256,512]{1,0:T(8,128)(2,1)} %slice.26), channel_id=1, source_target_pairs={{0,2},{3,1},{4,6},{7,5},{8,10},{11,9},{12,14},{15,13},{16,18},{19,... | collective-permute-start | bytes 786440 | tf_op jit(solution)/shard_map/ppermute | solution.py:248
  12.9 2.5 %copy-start.4 = (bf16[1152,512]{1,0:T(8,128)(2,1)S(1)}, bf16[1152,512]{1,0:T(8,128)(2,1)}, u32[]{:S(2)}) copy-start(bf16[1152,512]{1,0:T(8,128)(2,1)} %param.9) | copy-start | bytes 3538948
  12.9 2.5 %copy-start.5 = (f32[1,256,512]{2,1,0:T(8,128)S(1)}, f32[1,256,512]{2,1,0:T(8,128)}, u32[]{:S(2)}) copy-start(f32[1,256,512]{2,1,0:T(8,128)} %param.10) | copy-start | bytes 1572868
  17.0 18.0 %copy-start.3 = (bf16[784,512]{1,0:T(8,128)(2,1)S(1)}, bf16[784,512]{1,0:T(8,128)(2,1)}, u32[]{:S(2)}) copy-start(bf16[784,512]{1,0:T(8,128)(2,1)} %fusion.2) | copy-start | bytes 2408452
  30.5 11.1 %copy-start.2 = (bf16[4608,256]{1,0:T(8,128)(2,1)S(1)}, bf16[4608,256]{1,0:T(8,128)(2,1)}, u32[]{:S(2)}) copy-start(bf16[4608,256]{1,0:T(8,128)(2,1)} %param.8) | copy-start | bytes 7077892
  30.5 27.7 %collective-permute-start.4 = (bf16[896,512]{1,0:T(8,128)(2,1)S(1)}, bf16[896,512]{1,0:T(8,128)(2,1)S(1)}, u32[]{:S(2)}, u32[]{:S(2)}) collective-permute-start(bf16[896,512]{1,0:T(8,128)(2,1)S(1)} %slice.32), channel_id=1, source_target_pairs={{1,2},{2,1},{5,6},{6,5},{9,10},{10,9},{13,14},{14,13},{17,18},{18,... | collective-permute-start | bytes 2752520 | tf_op jit(solution)/shard_map/ppermute | solution.py:248
  35.1 22.4 %collective-permute-start.3 = (bf16[784,512]{1,0:T(8,128)(2,1)S(1)}, bf16[784,512]{1,0:T(8,128)(2,1)S(1)}, u32[]{:S(2)}, u32[]{:S(2)}) collective-permute-start(bf16[784,512]{1,0:T(8,128)(2,1)S(1)} %slice_select_fusion), channel_id=1, source_target_pairs={{0,1},{1,0},{2,3},{3,2},{4,5},{5,4},{6,7},{7,6},{8,9},{9,8},{10,11... | collective-permute-start | bytes 2408456 | tf_op jit(solution)/shard_map/ppermute | solution.py:248
  58.2 1.9 %copy-start = (f32[256,256]{1,0:T(8,128)S(1)}, f32[256,256]{1,0:T(8,128)}, u32[]{:S(2)}) copy-start(f32[256,256]{1,0:T(8,128)} %constant.32.clone.refs_1_.refs_4_.refs_6_) | copy-start | bytes 786436
  58.2 1.9 %copy-start.1 = (bf16[512,128]{1,0:T(8,128)(2,1)S(1)}, bf16[512,128]{1,0:T(8,128)(2,1)}, u32[]{:S(2)}) copy-start(bf16[512,128]{1,0:T(8,128)(2,1)} %constant.31.clone.refs_0_.refs_5_) | copy-start | bytes 393220
  58.7 8.8 %collective-permute-start.8 = (s16[272,512]{1,0:T(8,128)(2,1)S(1)}, s16[272,512]{1,0:T(8,128)(2,1)S(1)}, u32[]{:S(2)}, u32[]{:S(2)}) collective-permute-start(s16[272,512]{1,0:T(8,128)(2,1)S(1)} %get-tuple-element.43), channel_id=1, source_target_pairs={{1,0},{2,3},{5,4},{6,7},{9,8},{10,11},{13,12},{14,15},{17,16},{18,... | collective-permute-start | bytes 835592 | tf_op jit(solution)/shard_map/ppermute | solution.py:248
  61.9 5.6 %collective-permute-start.7 = (f32[128,128]{1,0:T(8,128)S(1)}, f32[128,128]{1,0:T(8,128)S(1)}, u32[]{:S(2)}, u32[]{:S(2)}) collective-permute-start(f32[128,128]{1,0:T(8,128)S(1)} %get-tuple-element.42), channel_id=1, source_target_pairs={{0,12},{4,8},{8,4},{12,0},{16,28},{20,24},{24,20},{28,16},{1,13},{... | collective-permute-start | bytes 196616 | tf_op jit(solution)/shard_map/ppermute | solution.py:205
  62.0 5.8 %collective-permute-start.6 = (f32[128,128]{1,0:T(8,128)S(1)}, f32[128,128]{1,0:T(8,128)S(1)}, u32[]{:S(2)}, u32[]{:S(2)}) collective-permute-start(f32[128,128]{1,0:T(8,128)S(1)} %get-tuple-element.42), channel_id=1, source_target_pairs={{0,8},{4,12},{8,0},{12,4},{16,24},{20,28},{24,16},{28,20},{1,9},{5... | collective-permute-start | bytes 196616 | tf_op jit(solution)/shard_map/ppermute | solution.py:205
  63.6 4.2 %collective-permute-start.5 = (f32[128,128]{1,0:T(8,128)S(1)}, f32[128,128]{1,0:T(8,128)S(1)}, u32[]{:S(2)}, u32[]{:S(2)}) collective-permute-start(f32[128,128]{1,0:T(8,128)S(1)} %get-tuple-element.42), channel_id=1, source_target_pairs={{0,4},{4,0},{8,12},{12,8},{16,20},{20,16},{24,28},{28,24},{1,5},{5... | collective-permute-start | bytes 196616 | tf_op jit(solution)/shard_map/ppermute | solution.py:205
  67.8 6.9 %collective-permute-start.11 = (f32[64,128]{1,0:T(8,128)S(1)}, f32[64,128]{1,0:T(8,128)S(1)}, u32[]{:S(2)}, u32[]{:S(2)}) collective-permute-start(f32[64,128]{1,0:T(8,128)S(1)} %get-tuple-element.58), channel_id=1, source_target_pairs={{1,16},{2,19},{5,20},{6,23},{9,24},{10,27},{13,28},{14,31},{17,0},... | collective-permute-start | bytes 98312 | tf_op jit(solution)/shard_map/ppermute | solution.py:307
  69.1 6.8 %collective-permute-start.10 = (f32[64,128]{1,0:T(8,128)S(1)}, f32[64,128]{1,0:T(8,128)S(1)}, u32[]{:S(2)}, u32[]{:S(2)}) collective-permute-start(f32[64,128]{1,0:T(8,128)S(1)} %get-tuple-element.58), channel_id=1, source_target_pairs={{1,0},{2,3},{5,4},{6,7},{9,8},{10,11},{13,12},{14,15},{17,16},{18,... | collective-permute-start | bytes 98312 | tf_op jit(solution)/shard_map/ppermute | solution.py:307
  70.4 5.5 %collective-permute-start.9 = (f32[64,128]{1,0:T(8,128)S(1)}, f32[64,128]{1,0:T(8,128)S(1)}, u32[]{:S(2)}, u32[]{:S(2)}) collective-permute-start(f32[64,128]{1,0:T(8,128)S(1)} %get-tuple-element.50.refs_0_), channel_id=1, source_target_pairs={{0,16},{4,20},{8,24},{12,28},{16,0},{20,4},{24,8},{28,12},{1,17},{... | collective-permute-start | bytes 98312 | tf_op jit(solution)/shard_map/ppermute | solution.py:205

commit v6 on v5

--- a/solution.py
+++ b/solution.py
@@ -48,7 +48,10 @@
 
 
 def dot3(a, b, dims=((1,), (0,))):
-    return dot(a[0], b[0], dims) + (dot(a[0], b[1], dims) + dot(a[1], b[0], dims))
+    (a_high, a_low), (b_high, b_low) = a, b
+    left = jnp.concatenate([a_high, a_low, a_high], axis=dims[0][0])
+    right = jnp.concatenate([b_high, b_high, b_low], axis=dims[1][0])
+    return dot(left, right, dims)
 
 
 def on_rows(basis_ref, x, transposed):
@@ -75,17 +78,20 @@
     return masks
 
 
-def selected(x, masks, *basis_refs):
-    by_rows = on_rows(basis_refs[0], x, False)
+def rows_taken(x, masks):
     pieces = []
     for row, (at, _) in enumerate(masks):
         taken = jnp.zeros((band, x.shape[1]), jnp.float32)
         for step in range(steps):
             start = row * order + step * band
-            taken = jnp.where(at == step * band, by_rows[start : start + band], taken)
+            taken = jnp.where(at == step * band, x[start : start + band], taken)
         pieces.append(taken)
-    coefficients = on_columns(basis_refs[-1], jnp.concatenate(pieces, axis=0), False)
-    return within(coefficients, masks)
+    return jnp.concatenate(pieces, axis=0)
+
+
+def selected(x, masks, *basis_refs):
+    taken = rows_taken(on_rows(basis_refs[0], x, False), masks)
+    return within(on_columns(basis_refs[-1], taken, False), masks)
 
 
 def within(x, masks):
@@ -104,8 +110,15 @@
 
 
 def bands_of(x, places, fold_ref, *basis_refs):
-    taken = selected(x, masks_of(places, x.shape[0] // order), *basis_refs)
-    return sum(dot(part, fold_ref[...]) for part in split3(taken))
+    return folded(selected(x, masks_of(places, x.shape[0] // order), *basis_refs), fold_ref[...])
+
+
+def folded(x, fold):
+    return dot(jnp.concatenate(split3(x), axis=1), jnp.concatenate([fold] * 3, axis=0))
+
+
+def spread(x, fold):
+    return dot(jnp.concatenate(split3(x), axis=1), jnp.concatenate([fold] * 3, axis=1), ((1,), (1,)))
 
 
 def bands_kernel(m_ref, places_ref, *refs):
@@ -153,28 +166,34 @@
 
 
 def last_rows_kernel(m_ref, own_turned_ref, far_ref, helped_ref, places_ref, end_places_ref, *refs):
-    *matrix_refs, out_ref, bands_ref = refs
-    count = bands_ref.shape[0] // 2
-    bands_ref[count:] = bands_of(helped_ref[...], end_places_ref[...], *matrix_refs)
+    fold_ref, *basis_refs, out_ref, bands_ref = refs
     out_ref[...] = m_ref[...] + dot(own_turned_ref[:, -far_ref.shape[0] :], far_ref[...])
-    bands_ref[:count] = bands_of(out_ref[...], places_ref[...], *matrix_refs)
+    rows, width = out_ref.shape
+    by_rows = on_rows(basis_refs[0], jnp.concatenate([out_ref[...], helped_ref[...]], axis=1), False)
+    masks = [masks_of(places[...], rows // order) for places in (places_ref, end_places_ref)]
+    taken = [rows_taken(by_rows[:, i * width :][:, :width], masks[i]) for i in range(2)]
+    coefficients = on_columns(basis_refs[-1], jnp.concatenate(taken, axis=0), False)
+    bands_ref[...] = folded(within(coefficients, masks[0] + masks[1]), fold_ref[...])
 
 
 def remove_kernel(count, *refs):
-    (m_ref, *code_refs), (places_ref, *basis_refs, out_ref) = refs[:count], refs[count:]
+    (m_ref, *code_refs), (end_ref, places_ref, *basis_refs, out_ref) = refs[:count], refs[count:]
     m = m_ref[...]
     if code_refs:
-        m = m + decoded(*code_refs)
+        m = m + jnp.where(end_ref[:1, :] > 0, decoded(*code_refs), 0.0)
     masks = masks_of(places_ref[...], m.shape[0] // order)
     out_ref[...] = m - restored(selected(m, masks, *basis_refs), masks, *basis_refs)
 
 
-def update_kernel(count, *refs):
-    part_refs, (places_ref, fold_ref, *basis_refs, out_ref) = refs[:count], refs[count:]
-    folded = pair_sum([ref[...] for ref in part_refs])
+def update_kernel(own_count, count, *refs):
+    part_refs, (end_ref, places_ref, fold_ref, *basis_refs, out_ref) = refs[:count], refs[count:]
+    parts = [ref[...] for ref in part_refs]
+    bands = pair_sum(parts[:own_count])
+    if own_count < count:
+        bands = bands + jnp.where(end_ref[:1, : bands.shape[1]] > 0, pair_sum(parts[own_count:]), 0.0)
     masks = masks_of(places_ref[...], out_ref.shape[0] // order)
-    spread = sum(dot(part, fold_ref[...], ((1,), (1,))) for part in split3(folded))
-    out_ref[...] = restored(within(spread, masks), masks, *basis_refs).astype(out_ref.dtype)
+    coefficients = within(spread(bands, fold_ref[...]), masks)
+    out_ref[...] = restored(coefficients, masks, *basis_refs).astype(out_ref.dtype)
 
 
 def pair_sum(parts):
@@ -227,7 +246,8 @@
     m = carried + product(hidden, lax.all_gather(out_grad, "tp", axis=0, tiled=True))
     folded = jax.ShapeDtypeStruct((m.shape[0] // steps, m.shape[1] // steps), jnp.float32)
     bands, last = summed_but_last(call(bands_kernel, folded, m, places, *matrices), "rep", lambda x: x)
-    return [m], [bands] + exchanged(bands, "rep", *last), places, matrices
+    parts = [bands] + exchanged(bands, "rep", *last)
+    return [m], parts, len(parts), jnp.zeros((8, m.shape[1]), jnp.float32), places, matrices
 
 
 def lined(hidden, out_grad, carried, places, matrices):
@@ -249,7 +269,6 @@
 
     both_ways = [(0, 1), (1, 0), (2, 3), (3, 2)]
     across = [(1, 2), (2, 1)]
-    outward = [(1, 0), (2, 3)]
     over_one = [(0, 2), (3, 1)]
 
     pair_grad = send(out_grad, both_ways)
@@ -269,9 +288,12 @@
     helped_hidden, cross_hidden, m = lax.optimization_barrier((helped_hidden, cross_hidden, m))
 
     far_head = send(out_grad[:first], over_one)
+    cross_grad, matrices, places = after((cross_grad, matrices, places), m)
+    to_swap = jnp.where(end, helped_hidden, cross_grad[: handed + place_rows])
+    pair_grad, to_swap = lax.optimization_barrier((pair_grad, to_swap))
     far_grad = send(pair_grad[first:], across)
-    cross_grad, matrices, places = after((cross_grad, matrices, places), pair_grad, far_head, m)
-    swapped = send(jnp.where(end, helped_hidden, cross_grad[: handed + place_rows]), both_ways)
+    far_head, to_swap = lax.optimization_barrier((far_head, to_swap))
+    swapped = send(to_swap, both_ways)
     m = m + product(rows_of(me ^ 1), pair_grad) + product(rows_of(cross), cross_grad)
 
     height, width = m.shape[0] // steps, m.shape[1] // steps
@@ -284,7 +306,7 @@
     far_grad = after(far_grad, m)
     code_shape = jax.ShapeDtypeStruct((m.shape[0] + code_rows, m.shape[1]), jnp.int16)
     helped, code = call(helped_kernel, (full, code_shape), helped, end_turned, far_grad)
-    code = send(code, outward)
+    code = send(code, both_ways)
     folded = jax.ShapeDtypeStruct((2 * height, width), jnp.float32)
     m, bands = call(
         last_rows_kernel, (full, folded), m, own_turned, far_grad, helped, places, end_places, *matrices
@@ -300,12 +322,13 @@
         bands, "rep", lambda x: (x[:height], x[height:]), behind_code
     )
     parts = [bands] + exchanged(bands, "rep", stride, count)
+    end_flag = jnp.full((8, m.shape[1]), end, jnp.float32)
     for k in range(count):
         perm = [
-            (i * 4 + a, (i ^ (stride * k)) * 4 + b) for i in range(lax.axis_size("rep")) for a, b in outward
+            (i * 4 + a, (i ^ (stride * k)) * 4 + b) for i in range(lax.axis_size("rep")) for a, b in both_ways
         ]
         parts.append(lax.ppermute(end_bands, ("rep", "tp"), perm))
-    return [m, code, exponents], parts, places, matrices
+    return [m, code, exponents], parts, count, end_flag, places, matrices
 
 
 def local(hidden, out_grad, momentum, band_rows, band_start_columns):
@@ -320,20 +343,24 @@
     places = dot(places, one_hot)
     fits = out_grad.shape[0] % 384 == 0 and out_grad.shape[0] >= 768 and 2 * row_count == col_count and places.shape[0] <= place_rows
     form = lined if fits and lax.axis_size("tp") == 4 else gathered
-    m_parts, band_parts, places, matrices = form(hidden, out_grad, decay_rate * momentum[0], places, matrices)
+    m_parts, band_parts, own_count, end_flag, places, matrices = form(
+        hidden, out_grad, decay_rate * momentum[0], places, matrices
+    )
     shape = (row_count, col_count)
     momentum_out = call(
         functools.partial(remove_kernel, len(m_parts)),
         jax.ShapeDtypeStruct(shape, jnp.float32),
         *m_parts,
+        end_flag,
         places,
         *matrices[1:],
     )
     *band_parts, momentum_out = lax.optimization_barrier((*band_parts, momentum_out))
     update = call(
-        functools.partial(update_kernel, len(band_parts)),
+        functools.partial(update_kernel, own_count, len(band_parts)),
         jax.ShapeDtypeStruct(shape, jnp.bfloat16),
         *band_parts,
+        end_flag,
         places,
         *matrices,
     )

time: 77.9 us -> 77.1 us (0.990)
  starting transfers between devices: 24.3 us -> 19.5 us
  local copies, waits for them, and re-layouts: 2.88 us -> 5.99 us
  matrix products: 2.79 us -> 4.89 us
    ppermute x6, starting transfers between devices: 18.2 us -> 14 us  [send(): return lax.ppermute(x, 'tp', perm)]
    ppermute x4, waiting for transfers between devices: 0.24 us -> 4.13 us  [exchanged(): lax.ppermute(x, axis, [(i, i ^ stride * k) for i in range(size)])]
    ppermute x6, waiting for transfers between devices: 35.4 us -> 32.6 us  [send(): return lax.ppermute(x, 'tp', perm)]
    dot_general x4, matrix products: 2.79 us -> 4.89 us  [dot(): lax.dot_general(a, b, (dims, ((), ())), preferred_element_type=jnp.float32)]
    ppermute x2, waiting for transfers between devices: 1.81 us -> 0.01 us  [lined(): parts.append(lax.ppermute(end_bands, ('rep', 'tp'), perm))]
    unnamed x18, local copies, waits for them, and re-layouts: 0.05 us -> 1.15 us
    ppermute x4, starting transfers between devices: 3.5 us -> 2.42 us  [exchanged(): lax.ppermute(x, axis, [(i, i ^ stride * k) for i in range(size)])]
    dynamic_slice x2, local copies, waits for them, and re-layouts: 1.09 us -> 2.16 us  [rows_of(): return lax.dynamic_slice_in_dim(hidden, part * tok + start, stop - start, 0)]
  transfers between devices with their start and end apart: 12 -> 12, of which waited for: 7 -> 7; matrix products, arithmetic and copies ran while one was open for 10% -> 16% of each run, Pallas kernels for 6% -> 5%
where the time goes in v6:
time: 77.1 us; the launch traced here: 76.7 us
  waiting for transfers between devices  36.8 us (48%)
  starting transfers between devices  19.5 us (25%)
  Pallas kernels  6.27 us (8%)
  local copies, waits for them, and re-layouts  5.99 us (8%)
  matrix products  4.89 us (6%)
  other arithmetic  2.37 us (3%)
  between operations  0.89 us (1%)
    ppermute x6, waiting for transfers between devices, send(): return lax.ppermute(x, 'tp', perm)  32.6 us
    ppermute x6, starting transfers between devices, send(): return lax.ppermute(x, 'tp', perm)  14 us
    pallas_call x5, Pallas kernels, call(): pl.pallas_call(kernel, out_shape=out_shapes, compiler_params=pltpu.Compil...  6.27 us
    dot_general x4, matrix products, dot(): lax.dot_general(a, b, (dims, ((), ())), preferred_element_type=jnp.float32)  4.89 us
    ppermute x4, waiting for transfers between devices, exchanged(): lax.ppermute(x, axis, [(i, i ^ stride * k) for i in range(size)])  4.13 us
    ppermute x2, starting transfers between devices, lined(): parts.append(lax.ppermute(end_bands, ('rep', 'tp'), perm))  3.05 us
    ppermute x4, starting transfers between devices, exchanged(): lax.ppermute(x, axis, [(i, i ^ stride * k) for i in range(size)])  2.42 us
    dynamic_slice x2, local copies, waits for them, and re-layouts, rows_of(): return lax.dynamic_slice_in_dim(hidden, part * tok + start, stop - start, 0)  2.16 us
  transfers between devices with their start and end apart: 12, of which 7 were waited for; matrix products, arithmetic and copies ran while one was open for 16% of the time, Pallas kernels for 5%

profile of v6, /device:TPU:0, one launch (start us, length us, event | category | flops | bytes accessed | tf_op | source)
XLA Modules:
  0.0 76.7 jit_solution(15311848702663517812)
XLA Ops:
  0.6 0.0 copy-start.6
  0.7 0.9 %collective-permute-start.1 = (bf16[1152,512]{1,0:T(8,128)(2,1)}, bf16[1152,512]{1,0:T(8,128)(2,1)S(1)}, u32[]{:S(2)}, u32[]{:S(2)}) collective-permute-start(bf16[1152,512]{1,0:T(8,128)(2,1)} %param.9), channel_id=1, source_target_pairs={{1,2},{2,1},{5,6},{6,5},{9,10},{10,9},{13,14},{14,13},{17,18},{18,... | collective-permute-start | bytes 3538952 | tf_op jit(solution)/shard_map/ppermute | solution.py:268
  1.5 5.8 %collective-permute-start = (bf16[1152,512]{1,0:T(8,128)(2,1)}, bf16[1152,512]{1,0:T(8,128)(2,1)S(1)}, u32[]{:S(2)}, u32[]{:S(2)}) collective-permute-start(bf16[1152,512]{1,0:T(8,128)(2,1)} %param.9), channel_id=1, source_target_pairs={{0,1},{1,0},{2,3},{3,2},{4,5},{5,4},{6,7},{7,6},{8,9},{9,8},{10,11... | collective-permute-start | bytes 3538952 | tf_op jit(solution)/shard_map/ppermute | solution.py:268
  7.4 1.7 %slice.27 = bf16[256,512]{1,0:T(8,128)(2,1)} slice(bf16[1152,512]{1,0:T(8,128)(2,1)} %param.9), slice={[0:256], [0:512]} | slice | bytes 524288 | tf_op jit(solution)/shard_map/slice | solution.py:290
  9.1 1.8 %collective-permute-start.2 = (bf16[256,512]{1,0:T(8,128)(2,1)}, bf16[256,512]{1,0:T(8,128)(2,1)S(1)}, u32[]{:S(2)}, u32[]{:S(2)}) collective-permute-start(bf16[256,512]{1,0:T(8,128)(2,1)} %slice.27), channel_id=1, source_target_pairs={{0,2},{3,1},{4,6},{7,5},{8,10},{11,9},{12,14},{15,13},{16,18},{19,... | collective-permute-start | bytes 786440 | tf_op jit(solution)/shard_map/ppermute | solution.py:268
  10.9 1.1 %constant_dynamic-slice_fusion.3 = (bf16[384,256]{1,0:T(8,128)(2,1)S(1)}, bf16[384,256]{1,0:T(8,128)(2,1)S(1)}) fusion(bf16[4608,256]{1,0:T(8,128)(2,1)} %param.8, s32[]{:T(128)S(6)} %select_n.40, s32[]{:T(128)S(6)} %select_n.42), kind=kLoop, calls=%fused_computation.24 | loop fusion | bytes 786440 | tf_op jit(solution)/shard_map/dynamic_slice | solution.py:265
  12.0 0.0 copy-start.4
  12.0 0.0 copy-start.5
  12.0 1.3 %dynamic-slice_select_fusion = (bf16[768,256]{1,0:T(8,128)(2,1)S(1)}, bf16[768,256]{1,0:T(8,128)(2,1)S(1)}) fusion(bf16[4608,256]{1,0:T(8,128)(2,1)} %param.8, s32[]{:T(128)S(6)} %select_n.44, pred[]{:T(512)S(6)} %or.3, s32[]{:T(128)S(6)} %add.54), kind=kLoop, calls=%fused_computation.11 | loop fusion | flops 196608 | bytes 1572873 | tf_op jit(solution)/shard_map/jit(_where)/select_n | solution.py:287
  13.3 0.1 fusion.15
  13.5 0.1 fusion.2
  13.5 0.1 copy-done.5
  13.6 1.6 %convolution_add_fusion.1 = f32[256,512]{1,0:T(8,128)S(1)} fusion(bf16[1152,512]{1,0:T(8,128)(2,1)S(1)} %copy-done.4, bf16[4608,256]{1,0:T(8,128)(2,1)} %param.8, s32[]{:T(128)S(6)} %select_n.46, f32[1,256,512]{2,1,0:T(8,128)S(1)} %copy-done.5), kind=kOutput, calls=%fused_computation.4 | convolution fusion | flops 302252032 | bytes 2818052 | tf_op jit(solution)/shard_map/dot_general | solution.py:47
  15.2 0.0 collective-permute-done.1.cross_ref
  15.2 1.0 %slice_select_fusion = bf16[784,512]{1,0:T(8,128)(2,1)} fusion(bf16[784,512]{1,0:T(8,128)(2,1)S(1)} %fusion.2, bf16[1152,512]{1,0:T(8,128)(2,1)S(1)} %collective-permute-done.1.cross_ref, pred[]{:T(512)S(6)} %or.3), kind=kLoop, calls=%fused_computation.6 | loop fusion | flops 401408 | bytes 2408449 | tf_op jit(solution)/shard_map/jit(_where)/select_n | solution.py:292
  16.2 17.9 %collective-permute-done = bf16[1152,512]{1,0:T(8,128)(2,1)S(1)} collective-permute-done((bf16[1152,512]{1,0:T(8,128)(2,1)}, bf16[1152,512]{1,0:T(8,128)(2,1)S(1)}, u32[]{:S(2)}, u32[]{:S(2)}) %collective-permute-start) | collective-permute-done | bytes 1179680 | tf_op jit(solution)/shard_map/ppermute | solution.py:268
  34.1 1.0 %copy-done.2 = bf16[1152,512]{1,0:T(8,128)(2,1)} copy-done((bf16[1152,512]{1,0:T(8,128)(2,1)}, bf16[1152,512]{1,0:T(8,128)(2,1)S(1)}, u32[]{:S(2)}) %copy-start.2) | copy-done | bytes 1179672
  35.2 1.0 %slice.28 = bf16[896,512]{1,0:T(8,128)(2,1)} slice(bf16[1152,512]{1,0:T(8,128)(2,1)S(1)} %collective-permute-done), slice={[256:1152], [0:512]} | slice | bytes 1835008 | tf_op jit(solution)/shard_map/slice | solution.py:294
  36.1 0.7 collective-permute-start.4
  36.9 1.4 %collective-permute-done.2.head_ref = bf16[256,512]{1,0:T(8,128)(2,1)S(1)} collective-permute-done((bf16[256,512]{1,0:T(8,128)(2,1)}, bf16[256,512]{1,0:T(8,128)(2,1)S(1)}, u32[]{:S(2)}, u32[]{:S(2)}) %collective-permute-start.2) | collective-permute-done | bytes 262176 | tf_op jit(solution)/shard_map/ppermute | solution.py:268
  38.3 2.7 %collective-permute-start.3 = (bf16[784,512]{1,0:T(8,128)(2,1)}, bf16[784,512]{1,0:T(8,128)(2,1)S(1)}, u32[]{:S(2)}, u32[]{:S(2)}) collective-permute-start(bf16[784,512]{1,0:T(8,128)(2,1)} %slice_select_fusion), channel_id=1, source_target_pairs={{0,1},{1,0},{2,3},{3,2},{4,5},{5,4},{6,7},{7,6},{8,9},{9,8},{10,11... | collective-permute-start | bytes 2408456 | tf_op jit(solution)/shard_map/ppermute | solution.py:268
  40.9 1.1 %constant_dynamic-slice_fusion.2.far_hidden_ref = bf16[1152,256]{1,0:T(8,128)(2,1)S(1)} fusion(bf16[4608,256]{1,0:T(8,128)(2,1)} %param.8, s32[]{:T(128)S(6)} %select_n.42), kind=kLoop, calls=%fused_computation.23 | loop fusion | bytes 1179652 | tf_op jit(solution)/shard_map/dynamic_slice | solution.py:265
  42.1 1.6 %fusion.3 = f32[256,512]{1,0:T(8,128)S(1)} fusion(bf16[1152,512]{1,0:T(8,128)(2,1)S(1)} %collective-permute-done.1.cross_ref, bf16[4608,256]{1,0:T(8,128)(2,1)} %param.8, s32[]{:T(128)S(6)} %select_n.44), kind=kOutput, calls=%fused_computation.7 | convolution fusion | flops 301989888 | bytes 2293764 | tf_op jit(solution)/shard_map/dot_general | solution.py:47
  43.7 1.6 %fusion.1.m_ref = f32[256,512]{1,0:T(8,128)S(1)} fusion(f32[256,512]{1,0:T(8,128)S(1)} %fusion.3, f32[256,512]{1,0:T(8,128)S(1)} %convolution_add_fusion.1, bf16[1152,512]{1,0:T(8,128)(2,1)S(1)} %copy-done.3, bf16[4608,256]{1,0:T(8,128)(2,1)} %param.8, s32[]{:T(128)S(6)} %select_n.47), kind=kOutput, calls=%fused_computation.3 | convolution fusion | flops 302252032 | bytes 3342340 | tf_op jit(solution)/shard_map/dot_general | solution.py:47
  45.3 12.2 %collective-permute-done.3.swapped_ref = bf16[784,512]{1,0:T(8,128)(2,1)S(1)} collective-permute-done((bf16[784,512]{1,0:T(8,128)(2,1)}, bf16[784,512]{1,0:T(8,128)(2,1)S(1)}, u32[]{:S(2)}, u32[]{:S(2)}) %collective-permute-start.3) | collective-permute-done | bytes 802848 | tf_op jit(solution)/shard_map/ppermute | solution.py:268
  57.4 0.7 shard_map.95
  58.1 0.0 copy-start
  58.1 0.0 copy-start.1
  58.1 0.0 collective-permute-done.4.far_ref
  58.1 0.5 shard_map.96
  58.7 2.1 %collective-permute-start.8 = (s16[272,512]{1,0:T(8,128)(2,1)S(1)}, s16[272,512]{1,0:T(8,128)(2,1)S(1)}, u32[]{:S(2)}, u32[]{:S(2)}) collective-permute-start(s16[272,512]{1,0:T(8,128)(2,1)S(1)} %get-tuple-element.51), channel_id=1, source_target_pairs={{0,1},{1,0},{2,3},{3,2},{4,5},{5,4},{6,7},{7,6},{8,9},{9,8},{10,11... | collective-permute-start | bytes 835592 | tf_op jit(solution)/shard_map/ppermute | solution.py:268
  60.8 0.0 copy-done.1
  60.8 1.5 %shard_map.97 = (f32[256,512]{1,0:T(8,128)S(1)}, f32[128,128]{1,0:T(8,128)S(1)}) custom-call(f32[256,512]{1,0:T(8,128)S(1)} %get-tuple-element.40.m_ref, bf16[256,1152]{1,0:T(8,128)(2,1)S(1)} %get-tuple-element.41.own_turned_ref, bf16[896,512]{1,0:T(8,128)(2,1)S(1)} %collective-permute-done.4.far_ref, f32[256,512]{1,0:T(8,128)S(1)} %get-tuple-element.45.helped_ref, ...), custom_call_target="tpu_custom_call" | custom-call | flops 400000000 | bytes 4000000 | tf_op jit(solution)/shard_map/pallas_call | solution.py:206
  62.2 0.1 collective-permute-start.7
  62.3 1.6 %collective-permute-start.6 = (f32[128,128]{1,0:T(8,128)S(1)}, f32[128,128]{1,0:T(8,128)S(1)}, u32[]{:S(2)}, u32[]{:S(2)}) collective-permute-start(f32[128,128]{1,0:T(8,128)S(1)} %get-tuple-element.50), channel_id=1, source_target_pairs={{0,8},{4,12},{8,0},{12,4},{16,24},{20,28},{24,16},{28,20},{1,9},{5... | collective-permute-start | bytes 196616 | tf_op jit(solution)/shard_map/ppermute | solution.py:224
  63.9 0.3 collective-permute-start.5
  64.2 1.1 %collective-permute-done.8.refs_1_ = s16[272,512]{1,0:T(8,128)(2,1)S(1)} collective-permute-done((s16[272,512]{1,0:T(8,128)(2,1)S(1)}, s16[272,512]{1,0:T(8,128)(2,1)S(1)}, u32[]{:S(2)}, u32[]{:S(2)}) %collective-permute-start.8) | collective-permute-done | bytes 278560 | tf_op jit(solution)/shard_map/ppermute | solution.py:268
  65.3 1.3 %collective-permute-done.7 = f32[128,128]{1,0:T(8,128)S(1)} collective-permute-done((f32[128,128]{1,0:T(8,128)S(1)}, f32[128,128]{1,0:T(8,128)S(1)}, u32[]{:S(2)}, u32[]{:S(2)}) %collective-permute-start.7) | collective-permute-done | bytes 65568 | tf_op jit(solution)/shard_map/ppermute | solution.py:224
  66.7 1.5 %collective-permute-done.6 = f32[128,128]{1,0:T(8,128)S(1)} collective-permute-done((f32[128,128]{1,0:T(8,128)S(1)}, f32[128,128]{1,0:T(8,128)S(1)}, u32[]{:S(2)}, u32[]{:S(2)}) %collective-permute-start.6) | collective-permute-done | bytes 65568 | tf_op jit(solution)/shard_map/ppermute | solution.py:224
  68.1 0.0 collective-permute-done.5
  68.1 1.1 %collective-permute-start.11 = (f32[64,128]{1,0:T(8,128)S(1)}, f32[64,128]{1,0:T(8,128)S(1)}, u32[]{:S(2)}, u32[]{:S(2)}) collective-permute-start(f32[64,128]{1,0:T(8,128)S(1)} %get-tuple-element.66), channel_id=1, source_target_pairs={{0,17},{1,16},{2,19},{3,18},{4,21},{5,20},{6,23},{7,22},{8,25},{9,... | collective-permute-start | bytes 98312 | tf_op jit(solution)/shard_map/ppermute | solution.py:330
  69.2 2.0 %collective-permute-start.10 = (f32[64,128]{1,0:T(8,128)S(1)}, f32[64,128]{1,0:T(8,128)S(1)}, u32[]{:S(2)}, u32[]{:S(2)}) collective-permute-start(f32[64,128]{1,0:T(8,128)S(1)} %get-tuple-element.66), channel_id=1, source_target_pairs={{0,1},{1,0},{2,3},{3,2},{4,5},{5,4},{6,7},{7,6},{8,9},{9,8},{10,11... | collective-permute-start | bytes 98312 | tf_op jit(solution)/shard_map/ppermute | solution.py:330
  71.2 0.5 collective-permute-start.9
  71.7 2.1 %shard_map.98 = f32[256,512]{1,0:T(8,128)} custom-call(f32[256,512]{1,0:T(8,128)S(1)} %get-tuple-element.55.refs_0_, s16[272,512]{1,0:T(8,128)(2,1)S(1)} %collective-permute-done.8.refs_1_, s16[16,512]{1,0:T(8,128)(2,1)S(1)} %slice.32.refs_2_, f32[8,512]{1,0:T(8,128)S(1)} %broadcast_in_dim.11.refs_3_.refs_4_, ...), custom_call_target="tpu_custom_call" | custom-call | flops 400000000 | bytes 4000000 | tf_op jit(solution)/shard_map/pallas_call | solution.py:206
  73.8 0.0 collective-permute-done.11.refs_3_
  73.8 0.0 collective-permute-done.10.refs_2_
  73.8 1.3 %collective-permute-done.9.refs_1_ = f32[64,128]{1,0:T(8,128)S(1)} collective-permute-done((f32[64,128]{1,0:T(8,128)S(1)}, f32[64,128]{1,0:T(8,128)S(1)}, u32[]{:S(2)}, u32[]{:S(2)}) %collective-permute-start.9) | collective-permute-done | bytes 32800 | tf_op jit(solution)/shard_map/ppermute | solution.py:224
  75.1 1.6 %shard_map.99 = bf16[256,512]{1,0:T(8,128)(2,1)} custom-call(f32[64,128]{1,0:T(8,128)S(1)} %get-tuple-element.58.refs_0_, f32[64,128]{1,0:T(8,128)S(1)} %collective-permute-done.9.refs_1_, f32[64,128]{1,0:T(8,128)S(1)} %collective-permute-done.10.refs_2_, f32[64,128]{1,0:T(8,128)S(1)} %collective-permute-done.11.refs_3_, ...), custom_call_target="tpu_custom_call" | custom-call | flops 400000000 | bytes 4000000 | tf_op jit(solution)/shard_map/pallas_call | solution.py:206
  (14 shorter events, 0.0 us)
Async XLA Ops:
  0.6 12.7 %copy-start.6 = (bf16[8,512]{1,0:T(8,128)(2,1)S(1)}, bf16[8,512]{1,0:T(8,128)(2,1)}, u32[]{:S(2)}) copy-start(bf16[8,512]{1,0:T(8,128)(2,1)} %constant.51) | copy-start | bytes 24580
  0.6 12.7 %copy-start.7 = (s32[4,8]{1,0:T(4,128)S(1)}, s32[4,8]{1,0:T(4,128)}, u32[]{:S(2)}) copy-start(s32[4,8]{1,0:T(4,128)} %param.12) | copy-start | bytes 388
  0.7 12.7 %copy-start.8 = (s32[4,8]{1,0:T(4,128)S(1)}, s32[4,8]{1,0:T(4,128)}, u32[]{:S(2)}) copy-start(s32[4,8]{1,0:T(4,128)} %param.11) | copy-start | bytes 388
  0.7 14.5 %collective-permute-start.1 = (bf16[1152,512]{1,0:T(8,128)(2,1)}, bf16[1152,512]{1,0:T(8,128)(2,1)S(1)}, u32[]{:S(2)}, u32[]{:S(2)}) collective-permute-start(bf16[1152,512]{1,0:T(8,128)(2,1)} %param.9), channel_id=1, source_target_pairs={{1,2},{2,1},{5,6},{6,5},{9,10},{10,9},{13,14},{14,13},{17,18},{18,... | collective-permute-start | bytes 3538952 | tf_op jit(solution)/shard_map/ppermute | solution.py:268
  1.5 32.6 %collective-permute-start = (bf16[1152,512]{1,0:T(8,128)(2,1)}, bf16[1152,512]{1,0:T(8,128)(2,1)S(1)}, u32[]{:S(2)}, u32[]{:S(2)}) collective-permute-start(bf16[1152,512]{1,0:T(8,128)(2,1)} %param.9), channel_id=1, source_target_pairs={{0,1},{1,0},{2,3},{3,2},{4,5},{5,4},{6,7},{7,6},{8,9},{9,8},{10,11... | collective-permute-start | bytes 3538952 | tf_op jit(solution)/shard_map/ppermute | solution.py:268
  9.1 29.2 %collective-permute-start.2 = (bf16[256,512]{1,0:T(8,128)(2,1)}, bf16[256,512]{1,0:T(8,128)(2,1)S(1)}, u32[]{:S(2)}, u32[]{:S(2)}) collective-permute-start(bf16[256,512]{1,0:T(8,128)(2,1)} %slice.27), channel_id=1, source_target_pairs={{0,2},{3,1},{4,6},{7,5},{8,10},{11,9},{12,14},{15,13},{16,18},{19,... | collective-permute-start | bytes 786440 | tf_op jit(solution)/shard_map/ppermute | solution.py:268
  12.0 1.6 %copy-start.4 = (bf16[1152,512]{1,0:T(8,128)(2,1)S(1)}, bf16[1152,512]{1,0:T(8,128)(2,1)}, u32[]{:S(2)}) copy-start(bf16[1152,512]{1,0:T(8,128)(2,1)} %param.9) | copy-start | bytes 3538948
  12.0 1.6 %copy-start.5 = (f32[1,256,512]{2,1,0:T(8,128)S(1)}, f32[1,256,512]{2,1,0:T(8,128)}, u32[]{:S(2)}) copy-start(f32[1,256,512]{2,1,0:T(8,128)} %param.10) | copy-start | bytes 1572868
  34.1 1.0 %copy-start.2 = (bf16[1152,512]{1,0:T(8,128)(2,1)}, bf16[1152,512]{1,0:T(8,128)(2,1)S(1)}, u32[]{:S(2)}) copy-start(bf16[1152,512]{1,0:T(8,128)(2,1)S(1)} %collective-permute-done) | copy-start | bytes 3538948
  36.1 22.0 %collective-permute-start.4 = (bf16[896,512]{1,0:T(8,128)(2,1)}, bf16[896,512]{1,0:T(8,128)(2,1)S(1)}, u32[]{:S(2)}, u32[]{:S(2)}) collective-permute-start(bf16[896,512]{1,0:T(8,128)(2,1)} %slice.28), channel_id=1, source_target_pairs={{1,2},{2,1},{5,6},{6,5},{9,10},{10,9},{13,14},{14,13},{17,18},{18,... | collective-permute-start | bytes 2752520 | tf_op jit(solution)/shard_map/ppermute | solution.py:268
  36.8 6.8 %copy-start.3 = (bf16[1152,512]{1,0:T(8,128)(2,1)S(1)}, bf16[1152,512]{1,0:T(8,128)(2,1)}, u32[]{:S(2)}) copy-start(bf16[1152,512]{1,0:T(8,128)(2,1)} %copy-done.2) | copy-start | bytes 3538948
  38.3 19.2 %collective-permute-start.3 = (bf16[784,512]{1,0:T(8,128)(2,1)}, bf16[784,512]{1,0:T(8,128)(2,1)S(1)}, u32[]{:S(2)}, u32[]{:S(2)}) collective-permute-start(bf16[784,512]{1,0:T(8,128)(2,1)} %slice_select_fusion), channel_id=1, source_target_pairs={{0,1},{1,0},{2,3},{3,2},{4,5},{5,4},{6,7},{7,6},{8,9},{9,8},{10,11... | collective-permute-start | bytes 2408456 | tf_op jit(solution)/shard_map/ppermute | solution.py:268
  58.1 2.7 %copy-start = (f32[256,256]{1,0:T(8,128)S(1)}, f32[256,256]{1,0:T(8,128)}, u32[]{:S(2)}) copy-start(f32[256,256]{1,0:T(8,128)} %constant.32.clone.refs_1_.refs_5_.refs_7_) | copy-start | bytes 786436
  58.1 2.7 %copy-start.1 = (bf16[512,128]{1,0:T(8,128)(2,1)S(1)}, bf16[512,128]{1,0:T(8,128)(2,1)}, u32[]{:S(2)}) copy-start(bf16[512,128]{1,0:T(8,128)(2,1)} %constant.31.clone.refs_0_.refs_6_) | copy-start | bytes 393220
  58.7 6.6 %collective-permute-start.8 = (s16[272,512]{1,0:T(8,128)(2,1)S(1)}, s16[272,512]{1,0:T(8,128)(2,1)S(1)}, u32[]{:S(2)}, u32[]{:S(2)}) collective-permute-start(s16[272,512]{1,0:T(8,128)(2,1)S(1)} %get-tuple-element.51), channel_id=1, source_target_pairs={{0,1},{1,0},{2,3},{3,2},{4,5},{5,4},{6,7},{7,6},{8,9},{9,8},{10,11... | collective-permute-start | bytes 835592 | tf_op jit(solution)/shard_map/ppermute | solution.py:268
  62.2 4.4 %collective-permute-start.7 = (f32[128,128]{1,0:T(8,128)S(1)}, f32[128,128]{1,0:T(8,128)S(1)}, u32[]{:S(2)}, u32[]{:S(2)}) collective-permute-start(f32[128,128]{1,0:T(8,128)S(1)} %get-tuple-element.50), channel_id=1, source_target_pairs={{0,12},{4,8},{8,4},{12,0},{16,28},{20,24},{24,20},{28,16},{1,13},{... | collective-permute-start | bytes 196616 | tf_op jit(solution)/shard_map/ppermute | solution.py:224
  62.3 5.8 %collective-permute-start.6 = (f32[128,128]{1,0:T(8,128)S(1)}, f32[128,128]{1,0:T(8,128)S(1)}, u32[]{:S(2)}, u32[]{:S(2)}) collective-permute-start(f32[128,128]{1,0:T(8,128)S(1)} %get-tuple-element.50), channel_id=1, source_target_pairs={{0,8},{4,12},{8,0},{12,4},{16,24},{20,28},{24,16},{28,20},{1,9},{5... | collective-permute-start | bytes 196616 | tf_op jit(solution)/shard_map/ppermute | solution.py:224
  63.9 4.2 %collective-permute-start.5 = (f32[128,128]{1,0:T(8,128)S(1)}, f32[128,128]{1,0:T(8,128)S(1)}, u32[]{:S(2)}, u32[]{:S(2)}) collective-permute-start(f32[128,128]{1,0:T(8,128)S(1)} %get-tuple-element.50), channel_id=1, source_target_pairs={{0,4},{4,0},{8,12},{12,8},{16,20},{20,16},{24,28},{28,24},{1,5},{5... | collective-permute-start | bytes 196616 | tf_op jit(solution)/shard_map/ppermute | solution.py:224
  68.1 5.6 %collective-permute-start.11 = (f32[64,128]{1,0:T(8,128)S(1)}, f32[64,128]{1,0:T(8,128)S(1)}, u32[]{:S(2)}, u32[]{:S(2)}) collective-permute-start(f32[64,128]{1,0:T(8,128)S(1)} %get-tuple-element.66), channel_id=1, source_target_pairs={{0,17},{1,16},{2,19},{3,18},{4,21},{5,20},{6,23},{7,22},{8,25},{9,... | collective-permute-start | bytes 98312 | tf_op jit(solution)/shard_map/ppermute | solution.py:330
  69.2 4.6 %collective-permute-start.10 = (f32[64,128]{1,0:T(8,128)S(1)}, f32[64,128]{1,0:T(8,128)S(1)}, u32[]{:S(2)}, u32[]{:S(2)}) collective-permute-start(f32[64,128]{1,0:T(8,128)S(1)} %get-tuple-element.66), channel_id=1, source_target_pairs={{0,1},{1,0},{2,3},{3,2},{4,5},{5,4},{6,7},{7,6},{8,9},{9,8},{10,11... | collective-permute-start | bytes 98312 | tf_op jit(solution)/shard_map/ppermute | solution.py:330
  71.2 3.9 %collective-permute-start.9 = (f32[64,128]{1,0:T(8,128)S(1)}, f32[64,128]{1,0:T(8,128)S(1)}, u32[]{:S(2)}, u32[]{:S(2)}) collective-permute-start(f32[64,128]{1,0:T(8,128)S(1)} %get-tuple-element.58.refs_0_), channel_id=1, source_target_pairs={{0,16},{4,20},{8,24},{12,28},{16,0},{20,4},{24,8},{28,12},{1,17},{... | collective-permute-start | bytes 98312 | tf_op jit(solution)/shard_map/ppermute | solution.py:224

commit v7 on v6

--- a/solution.py
+++ b/solution.py
@@ -141,33 +141,27 @@
     return values * jnp.exp2(exponents[:1] - 15.0)
 
 
-def swapped_kernel(m_ref, far_hidden_ref, cross_hidden_ref, head_ref, cross_ref, swapped_ref, *out_refs):
+def swapped_kernel(m_ref, far_hidden_ref, cross_hidden_ref, cross_ref, swapped_ref, *out_refs):
     out_ref, helped_ref, own_turned_ref, end_turned_ref, end_places_ref = out_refs
     handed, side = swapped_ref.shape[0] - place_rows, out_ref.shape[0]
-    alone, first = cross_ref.shape[0] - handed, head_ref.shape[0]
+    alone = cross_ref.shape[0] - handed
+    out_ref[...] = m_ref[...] + dot(cross_hidden_ref[...], swapped_ref[:handed], ((0,), (0,)))
+    helped_ref[...] = dot(swapped_ref[:alone, :side], cross_ref[handed:], ((0,), (0,)))
     own_turned_ref[...] = far_hidden_ref[...].T
     end_turned_ref[:, : handed - alone] = swapped_ref[alone:handed, :side].T
     end_turned_ref[:, handed - alone :] = swapped_ref[:handed, side:].T
-    out_ref[...] = (
-        m_ref[...]
-        + dot(cross_hidden_ref[...], swapped_ref[:handed], ((0,), (0,)))
-        + dot(own_turned_ref[:, :first], head_ref[...])
-    )
-    helped_ref[...] = dot(swapped_ref[:alone, :side], cross_ref[handed:], ((0,), (0,))) + dot(
-        end_turned_ref[:, :first], head_ref[...]
-    )
     end_places_ref[...] = swapped_ref[handed:].astype(jnp.float32)
 
 
 def helped_kernel(helped_ref, end_turned_ref, far_ref, out_ref, code_ref):
-    out_ref[...] = helped_ref[...] + dot(end_turned_ref[:, -far_ref.shape[0] :], far_ref[...])
+    out_ref[...] = helped_ref[...] + dot(end_turned_ref[...], far_ref[...])
     side = out_ref.shape[0]
     code_ref[:side], code_ref[side:] = coded(out_ref[...])
 
 
 def last_rows_kernel(m_ref, own_turned_ref, far_ref, helped_ref, places_ref, end_places_ref, *refs):
     fold_ref, *basis_refs, out_ref, bands_ref = refs
-    out_ref[...] = m_ref[...] + dot(own_turned_ref[:, -far_ref.shape[0] :], far_ref[...])
+    out_ref[...] = m_ref[...] + dot(own_turned_ref[...], far_ref[...])
     rows, width = out_ref.shape
     by_rows = on_rows(basis_refs[0], jnp.concatenate([out_ref[...], helped_ref[...]], axis=1), False)
     masks = [masks_of(places[...], rows // order) for places in (places_ref, end_places_ref)]
@@ -259,7 +253,6 @@
     far = jnp.where(left, 3, 0)
     handed = tok * 2 // 3
     alone = tok - handed
-    first = tok // 4 // 128 * 128
 
     def rows_of(part, start=0, stop=tok):
         return lax.dynamic_slice_in_dim(hidden, part * tok + start, stop - start, 0)
@@ -269,7 +262,6 @@
 
     both_ways = [(0, 1), (1, 0), (2, 3), (3, 2)]
     across = [(1, 2), (2, 1)]
-    over_one = [(0, 2), (3, 1)]
 
     pair_grad = send(out_grad, both_ways)
     cross_grad = send(out_grad, across)
@@ -287,13 +279,9 @@
     cross_hidden = jnp.where(end, rows_of(cross, 0, handed), 0)
     helped_hidden, cross_hidden, m = lax.optimization_barrier((helped_hidden, cross_hidden, m))
 
-    far_head = send(out_grad[:first], over_one)
-    cross_grad, matrices, places = after((cross_grad, matrices, places), m)
-    to_swap = jnp.where(end, helped_hidden, cross_grad[: handed + place_rows])
-    pair_grad, to_swap = lax.optimization_barrier((pair_grad, to_swap))
-    far_grad = send(pair_grad[first:], across)
-    far_head, to_swap = lax.optimization_barrier((far_head, to_swap))
-    swapped = send(to_swap, both_ways)
+    far_grad = send(pair_grad, across)
+    cross_grad, matrices, places = after((cross_grad, matrices, places), pair_grad, m)
+    swapped = send(jnp.where(end, helped_hidden, cross_grad[: handed + place_rows]), both_ways)
     m = m + product(rows_of(me ^ 1), pair_grad) + product(rows_of(cross), cross_grad)
 
     height, width = m.shape[0] // steps, m.shape[1] // steps
@@ -301,7 +289,7 @@
     turned = jax.ShapeDtypeStruct((m.shape[0], tok), hidden.dtype)
     table = jax.ShapeDtypeStruct((place_rows, m.shape[1]), jnp.float32)
     m, helped, own_turned, end_turned, end_places = call(
-        swapped_kernel, (full, full, turned, turned, table), m, far_hidden, cross_hidden, far_head, cross_grad, swapped
+        swapped_kernel, (full, full, turned, turned, table), m, far_hidden, cross_hidden, cross_grad, swapped
     )
     far_grad = after(far_grad, m)
     code_shape = jax.ShapeDtypeStruct((m.shape[0] + code_rows, m.shape[1]), jnp.int16)
@@ -341,7 +329,7 @@
     matrices = tuple(jnp.asarray(x) for x in (fold_matrix(col_count), *bases))
     places = jnp.concatenate([band_rows, band_start_columns], axis=0).astype(jnp.float32)
     places = dot(places, one_hot)
-    fits = out_grad.shape[0] % 384 == 0 and out_grad.shape[0] >= 768 and 2 * row_count == col_count and places.shape[0] <= place_rows
+    fits = out_grad.shape[0] % 384 == 0 and 2 * row_count == col_count and places.shape[0] <= place_rows
     form = lined if fits and lax.axis_size("tp") == 4 else gathered
     m_parts, band_parts, own_count, end_flag, places, matrices = form(
         hidden, out_grad, decay_rate * momentum[0], places, matrices

time: 77.1 us -> 77.5 us (level)
  local copies, waits for them, and re-layouts: 5.99 us -> 1.2 us
  waiting for transfers between devices: 36.8 us -> 40.9 us
  other arithmetic: 2.37 us -> 3.55 us
  starting transfers between devices: 19.5 us -> 20.4 us
  matrix products: 4.89 us -> 4.05 us
    ppermute x6 -> x5, waiting for transfers between devices: 32.6 us -> 37.2 us  [send(): return lax.ppermute(x, 'tp', perm)]
    slice x2 -> x0, local copies, waits for them, and re-layouts: 2.67 us -> none  [the longest x1 1.7 us: lined(): far_head = send(out_grad[:first], over_one)]
    unnamed x18 -> x16, local copies, waits for them, and re-layouts: 1.15 us -> 0.04 us
    dynamic_slice x2, local copies, waits for them, and re-layouts: 2.16 us -> 1.15 us  [rows_of(): return lax.dynamic_slice_in_dim(hidden, part * tok + start, stop - start, 0)]
    concatenate x1, other arithmetic: 0.06 us -> 0.96 us  [lined(): helped_hidden = jnp.concatenate([helped_hidden, place_part], axis=0)]
    ppermute x6 -> x5, starting transfers between devices: 14 us -> 14.9 us  [send(): return lax.ppermute(x, 'tp', perm)]
    dot_general x4, matrix products: 4.89 us -> 4.05 us  [dot(): lax.dot_general(a, b, (dims, ((), ())), preferred_element_type=jnp.float32)]
  transfers between devices with their start and end apart: 12 -> 11, of which waited for: 7 -> 6; matrix products, arithmetic and copies ran while one was open for 16% -> 11% of each run, Pallas kernels for 5% -> 5%
where the time goes in v7:
time: 77.5 us; the launch traced here: 77.2 us
  waiting for transfers between devices  40.9 us (53%)
  starting transfers between devices  20.4 us (26%)
  Pallas kernels  6.28 us (8%)
  matrix products  4.05 us (5%)
  other arithmetic  3.55 us (5%)
  local copies, waits for them, and re-layouts  1.2 us (2%)
  between operations  0.85 us (1%)
    ppermute x5, waiting for transfers between devices, send(): return lax.ppermute(x, 'tp', perm)  37.2 us
    ppermute x5, starting transfers between devices, send(): return lax.ppermute(x, 'tp', perm)  14.9 us
    pallas_call x5, Pallas kernels, call(): pl.pallas_call(kernel, out_shape=out_shapes, compiler_params=pltpu.Compil...  6.28 us
    dot_general x4, matrix products, dot(): lax.dot_general(a, b, (dims, ((), ())), preferred_element_type=jnp.float32)  4.05 us
    ppermute x4, waiting for transfers between devices, exchanged(): lax.ppermute(x, axis, [(i, i ^ stride * k) for i in range(size)])  3.69 us
    ppermute x2, starting transfers between devices, lined(): parts.append(lax.ppermute(end_bands, ('rep', 'tp'), perm))  3.05 us
    ppermute x4, starting transfers between devices, exchanged(): lax.ppermute(x, axis, [(i, i ^ stride * k) for i in range(size)])  2.43 us
  transfers between devices with their start and end apart: 11, of which 6 were waited for; matrix products, arithmetic and copies ran while one was open for 11% of the time, Pallas kernels for 5%

profile of v7, /device:TPU:0, one launch (start us, length us, event | category | flops | bytes accessed | tf_op | source)
XLA Modules:
  0.0 77.2 jit_solution(8082239047302979984)
XLA Ops:
  0.6 0.0 copy-start.5
  0.6 0.0 copy-start.3
  0.7 0.0 copy-start.7
  0.7 0.0 copy-start.6
  0.7 3.1 %collective-permute-start = (bf16[1152,512]{1,0:T(8,128)(2,1)}, bf16[1152,512]{1,0:T(8,128)(2,1)}, u32[]{:S(2)}, u32[]{:S(2)}) collective-permute-start(bf16[1152,512]{1,0:T(8,128)(2,1)} %param.9), channel_id=1, source_target_pairs={{0,1},{1,0},{2,3},{3,2},{4,5},{5,4},{6,7},{7,6},{8,9},{9,8},{10,11... | collective-permute-start | bytes 3538952 | tf_op jit(solution)/shard_map/ppermute | solution.py:261
  3.8 0.7 collective-permute-start.1
  4.5 0.0 copy-start.4
  4.5 1.1 %constant_dynamic-slice_fusion.3 = (bf16[384,256]{1,0:T(8,128)(2,1)S(1)}, bf16[384,256]{1,0:T(8,128)(2,1)S(1)}) fusion(bf16[4608,256]{1,0:T(8,128)(2,1)} %param.8, s32[]{:T(128)S(6)} %select_n.40, s32[]{:T(128)S(6)} %select_n.42), kind=kLoop, calls=%fused_computation.24 | loop fusion | bytes 786440 | tf_op jit(solution)/shard_map/dynamic_slice | solution.py:258
  5.6 1.2 %dynamic-slice_select_fusion = (bf16[768,256]{1,0:T(8,128)(2,1)S(1)}, bf16[768,256]{1,0:T(8,128)(2,1)S(1)}) fusion(bf16[4608,256]{1,0:T(8,128)(2,1)} %param.8, s32[]{:T(128)S(6)} %select_n.44, pred[]{:T(512)S(6)} %or.3, s32[]{:T(128)S(6)} %add.54), kind=kLoop, calls=%fused_computation.11 | loop fusion | flops 196608 | bytes 1572873 | tf_op jit(solution)/shard_map/jit(_where)/select_n | solution.py:279
  6.8 0.0 copy-done.5
  6.9 0.0 copy-done.7
  6.9 0.0 copy-done.6
  6.9 0.1 fusion.15
  7.0 0.0 copy-done.3
  7.0 0.0 copy-done.4
  7.0 1.6 %convolution_add_fusion.1 = f32[256,512]{1,0:T(8,128)S(1)} fusion(bf16[1152,512]{1,0:T(8,128)(2,1)S(1)} %copy-done.3, bf16[4608,256]{1,0:T(8,128)(2,1)} %param.8, s32[]{:T(128)S(6)} %select_n.46, f32[1,256,512]{2,1,0:T(8,128)S(1)} %copy-done.4), kind=kOutput, calls=%fused_computation.4 | convolution fusion | flops 302252032 | bytes 2818052 | tf_op jit(solution)/shard_map/dot_general | solution.py:47
  8.6 21.5 %collective-permute-done = bf16[1152,512]{1,0:T(8,128)(2,1)} collective-permute-done((bf16[1152,512]{1,0:T(8,128)(2,1)}, bf16[1152,512]{1,0:T(8,128)(2,1)}, u32[]{:S(2)}, u32[]{:S(2)}) %collective-permute-start) | collective-permute-done | bytes 1179680 | tf_op jit(solution)/shard_map/ppermute | solution.py:261
  30.0 0.7 collective-permute-start.3
  30.8 1.0 %fusion.2 = bf16[784,512]{1,0:T(8,128)(2,1)} fusion(bf16[8,512]{1,0:T(8,128)(2,1)S(1)} %get-tuple-element.60, bf16[768,256]{1,0:T(8,128)(2,1)S(1)} %get-tuple-element.55, bf16[384,256]{1,0:T(8,128)(2,1)S(1)} %get-tuple-element.57, bf16[384,256]{1,0:T(8,128)(2,1)S(1)} %get-tuple-element.56), kind=kLoop, calls=%fused_computation.5 | loop fusion | flops 4014080 | bytes 1597440 | tf_op jit(solution)/shard_map/concatenate | solution.py:278
  31.7 0.0 collective-permute-done.1.cross_ref
  31.7 1.4 %slice_select_fusion = bf16[784,512]{1,0:T(8,128)(2,1)S(1)} fusion(bf16[784,512]{1,0:T(8,128)(2,1)} %fusion.2, bf16[1152,512]{1,0:T(8,128)(2,1)S(1)} %collective-permute-done.1.cross_ref, pred[]{:T(512)S(6)} %or.3), kind=kLoop, calls=%fused_computation.6 | loop fusion | flops 401408 | bytes 2408449 | tf_op jit(solution)/shard_map/jit(_where)/select_n | solution.py:284
  33.1 3.3 %collective-permute-start.2 = (bf16[784,512]{1,0:T(8,128)(2,1)S(1)}, bf16[784,512]{1,0:T(8,128)(2,1)S(1)}, u32[]{:S(2)}, u32[]{:S(2)}) collective-permute-start(bf16[784,512]{1,0:T(8,128)(2,1)S(1)} %slice_select_fusion), channel_id=1, source_target_pairs={{0,1},{1,0},{2,3},{3,2},{4,5},{5,4},{6,7},{7,6},{8,9},{9,8},{10,11... | collective-permute-start | bytes 2408456 | tf_op jit(solution)/shard_map/ppermute | solution.py:261
  36.4 0.5 fusion.3
  37.0 1.8 %fusion.1.m_ref = f32[256,512]{1,0:T(8,128)S(1)} fusion(f32[256,512]{1,0:T(8,128)S(1)} %fusion.3, f32[256,512]{1,0:T(8,128)S(1)} %convolution_add_fusion.1, bf16[1152,512]{1,0:T(8,128)(2,1)} %collective-permute-done, bf16[4608,256]{1,0:T(8,128)(2,1)S(1)} %copy-done.2, s32[]{:T(128)S(6)} %select_n.47), kind=kOutput, calls=%fused_computation.3 | convolution fusion | flops 302252032 | bytes 3342340 | tf_op jit(solution)/shard_map/dot_general | solution.py:47
  38.8 14.3 %collective-permute-done.2.swapped_ref = bf16[784,512]{1,0:T(8,128)(2,1)S(1)} collective-permute-done((bf16[784,512]{1,0:T(8,128)(2,1)S(1)}, bf16[784,512]{1,0:T(8,128)(2,1)S(1)}, u32[]{:S(2)}, u32[]{:S(2)}) %collective-permute-start.2) | collective-permute-done | bytes 802848 | tf_op jit(solution)/shard_map/ppermute | solution.py:261
  53.1 0.5 shard_map.95
  53.7 0.0 copy-start
  53.7 0.0 copy-start.1
  53.7 0.0 collective-permute-done.3.far_ref
  53.7 0.6 shard_map.96
  54.3 7.1 %collective-permute-start.7 = (s16[272,512]{1,0:T(8,128)(2,1)S(1)}, s16[272,512]{1,0:T(8,128)(2,1)S(1)}, u32[]{:S(2)}, u32[]{:S(2)}) collective-permute-start(s16[272,512]{1,0:T(8,128)(2,1)S(1)} %get-tuple-element.43), channel_id=1, source_target_pairs={{0,1},{1,0},{2,3},{3,2},{4,5},{5,4},{6,7},{7,6},{8,9},{9,8},{10,11... | collective-permute-start | bytes 835592 | tf_op jit(solution)/shard_map/ppermute | solution.py:261
  61.4 0.0 copy-done
  61.4 1.5 %shard_map.97 = (f32[256,512]{1,0:T(8,128)S(1)}, f32[128,128]{1,0:T(8,128)S(1)}) custom-call(f32[256,512]{1,0:T(8,128)S(1)} %get-tuple-element.32.m_ref, bf16[256,1152]{1,0:T(8,128)(2,1)S(1)} %get-tuple-element.33.own_turned_ref, bf16[1152,512]{1,0:T(8,128)(2,1)S(1)} %collective-permute-done.3.far_ref, f32[256,512]{1,0:T(8,128)S(1)} %get-tuple-element.37.helped_ref, ...), custom_call_target="tpu_custom_call" | custom-call | flops 400000000 | bytes 4000000 | tf_op jit(solution)/shard_map/pallas_call | solution.py:200
  62.9 0.1 collective-permute-start.4
  63.0 1.5 %collective-permute-start.5 = (f32[128,128]{1,0:T(8,128)S(1)}, f32[128,128]{1,0:T(8,128)S(1)}, u32[]{:S(2)}, u32[]{:S(2)}) collective-permute-start(f32[128,128]{1,0:T(8,128)S(1)} %get-tuple-element.42), channel_id=1, source_target_pairs={{0,8},{4,12},{8,0},{12,4},{16,24},{20,28},{24,16},{28,20},{1,9},{5... | collective-permute-start | bytes 196616 | tf_op jit(solution)/shard_map/ppermute | solution.py:218
  64.5 0.3 collective-permute-start.6
  64.9 1.4 %collective-permute-done.7.refs_1_ = s16[272,512]{1,0:T(8,128)(2,1)S(1)} collective-permute-done((s16[272,512]{1,0:T(8,128)(2,1)S(1)}, s16[272,512]{1,0:T(8,128)(2,1)S(1)}, u32[]{:S(2)}, u32[]{:S(2)}) %collective-permute-start.7) | collective-permute-done | bytes 278560 | tf_op jit(solution)/shard_map/ppermute | solution.py:261
  66.2 0.0 collective-permute-done.4
  66.3 1.3 %collective-permute-done.5 = f32[128,128]{1,0:T(8,128)S(1)} collective-permute-done((f32[128,128]{1,0:T(8,128)S(1)}, f32[128,128]{1,0:T(8,128)S(1)}, u32[]{:S(2)}, u32[]{:S(2)}) %collective-permute-start.5) | collective-permute-done | bytes 65568 | tf_op jit(solution)/shard_map/ppermute | solution.py:218
  67.5 1.1 %collective-permute-done.6 = f32[128,128]{1,0:T(8,128)S(1)} collective-permute-done((f32[128,128]{1,0:T(8,128)S(1)}, f32[128,128]{1,0:T(8,128)S(1)}, u32[]{:S(2)}, u32[]{:S(2)}) %collective-permute-start.6) | collective-permute-done | bytes 65568 | tf_op jit(solution)/shard_map/ppermute | solution.py:218
  68.6 1.1 %collective-permute-start.10 = (f32[64,128]{1,0:T(8,128)S(1)}, f32[64,128]{1,0:T(8,128)S(1)}, u32[]{:S(2)}, u32[]{:S(2)}) collective-permute-start(f32[64,128]{1,0:T(8,128)S(1)} %get-tuple-element.58), channel_id=1, source_target_pairs={{0,17},{1,16},{2,19},{3,18},{4,21},{5,20},{6,23},{7,22},{8,25},{9,... | collective-permute-start | bytes 98312 | tf_op jit(solution)/shard_map/ppermute | solution.py:318
  69.7 2.0 %collective-permute-start.9 = (f32[64,128]{1,0:T(8,128)S(1)}, f32[64,128]{1,0:T(8,128)S(1)}, u32[]{:S(2)}, u32[]{:S(2)}) collective-permute-start(f32[64,128]{1,0:T(8,128)S(1)} %get-tuple-element.58), channel_id=1, source_target_pairs={{0,1},{1,0},{2,3},{3,2},{4,5},{5,4},{6,7},{7,6},{8,9},{9,8},{10,11... | collective-permute-start | bytes 98312 | tf_op jit(solution)/shard_map/ppermute | solution.py:318
  71.7 0.5 collective-permute-start.8
  72.2 2.1 %shard_map.98 = f32[256,512]{1,0:T(8,128)} custom-call(f32[256,512]{1,0:T(8,128)S(1)} %get-tuple-element.47.refs_0_, s16[272,512]{1,0:T(8,128)(2,1)S(1)} %collective-permute-done.7.refs_1_, s16[16,512]{1,0:T(8,128)(2,1)S(1)} %slice.24.refs_2_, f32[8,512]{1,0:T(8,128)S(1)} %broadcast_in_dim.11.refs_3_.refs_4_, ...), custom_call_target="tpu_custom_call" | custom-call | flops 400000000 | bytes 4000000 | tf_op jit(solution)/shard_map/pallas_call | solution.py:200
  74.3 0.0 collective-permute-done.10.refs_3_
  74.3 1.3 %collective-permute-done.8.refs_1_ = f32[64,128]{1,0:T(8,128)S(1)} collective-permute-done((f32[64,128]{1,0:T(8,128)S(1)}, f32[64,128]{1,0:T(8,128)S(1)}, u32[]{:S(2)}, u32[]{:S(2)}) %collective-permute-start.8) | collective-permute-done | bytes 32800 | tf_op jit(solution)/shard_map/ppermute | solution.py:218
  75.6 0.0 collective-permute-done.9.refs_2_
  75.6 1.6 %shard_map.99 = bf16[256,512]{1,0:T(8,128)(2,1)} custom-call(f32[64,128]{1,0:T(8,128)S(1)} %get-tuple-element.50.refs_0_, f32[64,128]{1,0:T(8,128)S(1)} %collective-permute-done.8.refs_1_, f32[64,128]{1,0:T(8,128)S(1)} %collective-permute-done.9.refs_2_, f32[64,128]{1,0:T(8,128)S(1)} %collective-permute-done.10.refs_3_, ...), custom_call_target="tpu_custom_call" | custom-call | flops 400000000 | bytes 4000000 | tf_op jit(solution)/shard_map/pallas_call | solution.py:200
  (8 shorter events, 0.1 us)
Async XLA Ops:
  0.6 6.2 %copy-start.5 = (bf16[8,512]{1,0:T(8,128)(2,1)S(1)}, bf16[8,512]{1,0:T(8,128)(2,1)}, u32[]{:S(2)}) copy-start(bf16[8,512]{1,0:T(8,128)(2,1)} %constant.51) | copy-start | bytes 24580
  0.6 6.4 %copy-start.3 = (bf16[1152,512]{1,0:T(8,128)(2,1)S(1)}, bf16[1152,512]{1,0:T(8,128)(2,1)}, u32[]{:S(2)}) copy-start(bf16[1152,512]{1,0:T(8,128)(2,1)} %param.9) | copy-start | bytes 3538948
  0.7 6.2 %copy-start.7 = (s32[4,8]{1,0:T(4,128)S(1)}, s32[4,8]{1,0:T(4,128)}, u32[]{:S(2)}) copy-start(s32[4,8]{1,0:T(4,128)} %param.11) | copy-start | bytes 388
  0.7 6.2 %copy-start.6 = (s32[4,8]{1,0:T(4,128)S(1)}, s32[4,8]{1,0:T(4,128)}, u32[]{:S(2)}) copy-start(s32[4,8]{1,0:T(4,128)} %param.12) | copy-start | bytes 388
  0.7 29.4 %collective-permute-start = (bf16[1152,512]{1,0:T(8,128)(2,1)}, bf16[1152,512]{1,0:T(8,128)(2,1)}, u32[]{:S(2)}, u32[]{:S(2)}) collective-permute-start(bf16[1152,512]{1,0:T(8,128)(2,1)} %param.9), channel_id=1, source_target_pairs={{0,1},{1,0},{2,3},{3,2},{4,5},{5,4},{6,7},{7,6},{8,9},{9,8},{10,11... | collective-permute-start | bytes 3538952 | tf_op jit(solution)/shard_map/ppermute | solution.py:261
  3.8 28.0 %collective-permute-start.1 = (bf16[1152,512]{1,0:T(8,128)(2,1)}, bf16[1152,512]{1,0:T(8,128)(2,1)S(1)}, u32[]{:S(2)}, u32[]{:S(2)}) collective-permute-start(bf16[1152,512]{1,0:T(8,128)(2,1)} %param.9), channel_id=1, source_target_pairs={{1,2},{2,1},{5,6},{6,5},{9,10},{10,9},{13,14},{14,13},{17,18},{18,... | collective-permute-start | bytes 3538952 | tf_op jit(solution)/shard_map/ppermute | solution.py:261
  4.5 2.5 %copy-start.4 = (f32[1,256,512]{2,1,0:T(8,128)S(1)}, f32[1,256,512]{2,1,0:T(8,128)}, u32[]{:S(2)}) copy-start(f32[1,256,512]{2,1,0:T(8,128)} %param.10) | copy-start | bytes 1572868
  30.0 23.7 %collective-permute-start.3 = (bf16[1152,512]{1,0:T(8,128)(2,1)}, bf16[1152,512]{1,0:T(8,128)(2,1)S(1)}, u32[]{:S(2)}, u32[]{:S(2)}) collective-permute-start(bf16[1152,512]{1,0:T(8,128)(2,1)} %collective-permute-done), channel_id=1, source_target_pairs={{1,2},{2,1},{5,6},{6,5},{9,10},{10,9},{13,14},{14,13},{17,18},{18,... | collective-permute-start | bytes 3538952 | tf_op jit(solution)/shard_map/ppermute | solution.py:261
  31.7 4.7 %copy-start.2 = (bf16[4608,256]{1,0:T(8,128)(2,1)S(1)}, bf16[4608,256]{1,0:T(8,128)(2,1)}, u32[]{:S(2)}) copy-start(bf16[4608,256]{1,0:T(8,128)(2,1)} %param.8) | copy-start | bytes 7077892
  33.1 20.0 %collective-permute-start.2 = (bf16[784,512]{1,0:T(8,128)(2,1)S(1)}, bf16[784,512]{1,0:T(8,128)(2,1)S(1)}, u32[]{:S(2)}, u32[]{:S(2)}) collective-permute-start(bf16[784,512]{1,0:T(8,128)(2,1)S(1)} %slice_select_fusion), channel_id=1, source_target_pairs={{0,1},{1,0},{2,3},{3,2},{4,5},{5,4},{6,7},{7,6},{8,9},{9,8},{10,11... | collective-permute-start | bytes 2408456 | tf_op jit(solution)/shard_map/ppermute | solution.py:261
  53.7 7.7 %copy-start = (f32[256,256]{1,0:T(8,128)S(1)}, f32[256,256]{1,0:T(8,128)}, u32[]{:S(2)}) copy-start(f32[256,256]{1,0:T(8,128)} %constant.32.clone.refs_1_.refs_5_.refs_7_) | copy-start | bytes 786436
  53.7 7.7 %copy-start.1 = (bf16[512,128]{1,0:T(8,128)(2,1)S(1)}, bf16[512,128]{1,0:T(8,128)(2,1)}, u32[]{:S(2)}) copy-start(bf16[512,128]{1,0:T(8,128)(2,1)} %constant.31.clone.refs_0_.refs_6_) | copy-start | bytes 393220
  54.3 11.9 %collective-permute-start.7 = (s16[272,512]{1,0:T(8,128)(2,1)S(1)}, s16[272,512]{1,0:T(8,128)(2,1)S(1)}, u32[]{:S(2)}, u32[]{:S(2)}) collective-permute-start(s16[272,512]{1,0:T(8,128)(2,1)S(1)} %get-tuple-element.43), channel_id=1, source_target_pairs={{0,1},{1,0},{2,3},{3,2},{4,5},{5,4},{6,7},{7,6},{8,9},{9,8},{10,11... | collective-permute-start | bytes 835592 | tf_op jit(solution)/shard_map/ppermute | solution.py:261
  62.9 3.3 %collective-permute-start.4 = (f32[128,128]{1,0:T(8,128)S(1)}, f32[128,128]{1,0:T(8,128)S(1)}, u32[]{:S(2)}, u32[]{:S(2)}) collective-permute-start(f32[128,128]{1,0:T(8,128)S(1)} %get-tuple-element.42), channel_id=1, source_target_pairs={{0,4},{4,0},{8,12},{12,8},{16,20},{20,16},{24,28},{28,24},{1,5},{5... | collective-permute-start | bytes 196616 | tf_op jit(solution)/shard_map/ppermute | solution.py:218
  63.0 4.5 %collective-permute-start.5 = (f32[128,128]{1,0:T(8,128)S(1)}, f32[128,128]{1,0:T(8,128)S(1)}, u32[]{:S(2)}, u32[]{:S(2)}) collective-permute-start(f32[128,128]{1,0:T(8,128)S(1)} %get-tuple-element.42), channel_id=1, source_target_pairs={{0,8},{4,12},{8,0},{12,4},{16,24},{20,28},{24,16},{28,20},{1,9},{5... | collective-permute-start | bytes 196616 | tf_op jit(solution)/shard_map/ppermute | solution.py:218
  64.5 4.0 %collective-permute-start.6 = (f32[128,128]{1,0:T(8,128)S(1)}, f32[128,128]{1,0:T(8,128)S(1)}, u32[]{:S(2)}, u32[]{:S(2)}) collective-permute-start(f32[128,128]{1,0:T(8,128)S(1)} %get-tuple-element.42), channel_id=1, source_target_pairs={{0,12},{4,8},{8,4},{12,0},{16,28},{20,24},{24,20},{28,16},{1,13},{... | collective-permute-start | bytes 196616 | tf_op jit(solution)/shard_map/ppermute | solution.py:218
  68.6 5.6 %collective-permute-start.10 = (f32[64,128]{1,0:T(8,128)S(1)}, f32[64,128]{1,0:T(8,128)S(1)}, u32[]{:S(2)}, u32[]{:S(2)}) collective-permute-start(f32[64,128]{1,0:T(8,128)S(1)} %get-tuple-element.58), channel_id=1, source_target_pairs={{0,17},{1,16},{2,19},{3,18},{4,21},{5,20},{6,23},{7,22},{8,25},{9,... | collective-permute-start | bytes 98312 | tf_op jit(solution)/shard_map/ppermute | solution.py:318
  69.7 5.9 %collective-permute-start.9 = (f32[64,128]{1,0:T(8,128)S(1)}, f32[64,128]{1,0:T(8,128)S(1)}, u32[]{:S(2)}, u32[]{:S(2)}) collective-permute-start(f32[64,128]{1,0:T(8,128)S(1)} %get-tuple-element.58), channel_id=1, source_target_pairs={{0,1},{1,0},{2,3},{3,2},{4,5},{5,4},{6,7},{7,6},{8,9},{9,8},{10,11... | collective-permute-start | bytes 98312 | tf_op jit(solution)/shard_map/ppermute | solution.py:318
  71.7 3.9 %collective-permute-start.8 = (f32[64,128]{1,0:T(8,128)S(1)}, f32[64,128]{1,0:T(8,128)S(1)}, u32[]{:S(2)}, u32[]{:S(2)}) collective-permute-start(f32[64,128]{1,0:T(8,128)S(1)} %get-tuple-element.50.refs_0_), channel_id=1, source_target_pairs={{0,16},{4,20},{8,24},{12,28},{16,0},{20,4},{24,8},{28,12},{1,17},{... | collective-permute-start | bytes 98312 | tf_op jit(solution)/shard_map/ppermute | solution.py:218

commit v8 on v7

--- a/solution.py
+++ b/solution.py
@@ -141,8 +141,8 @@
     return values * jnp.exp2(exponents[:1] - 15.0)
 
 
-def swapped_kernel(m_ref, far_hidden_ref, cross_hidden_ref, cross_ref, swapped_ref, *out_refs):
-    out_ref, helped_ref, own_turned_ref, end_turned_ref, end_places_ref = out_refs
+def swapped_kernel(m_ref, far_hidden_ref, cross_hidden_ref, cross_ref, swapped_ref, places_ref, *refs):
+    *matrix_refs, out_ref, helped_ref, own_turned_ref, end_turned_ref, end_places_ref, bands_ref = refs
     handed, side = swapped_ref.shape[0] - place_rows, out_ref.shape[0]
     alone = cross_ref.shape[0] - handed
     out_ref[...] = m_ref[...] + dot(cross_hidden_ref[...], swapped_ref[:handed], ((0,), (0,)))
@@ -151,6 +151,7 @@
     end_turned_ref[:, : handed - alone] = swapped_ref[alone:handed, :side].T
     end_turned_ref[:, handed - alone :] = swapped_ref[:handed, side:].T
     end_places_ref[...] = swapped_ref[handed:].astype(jnp.float32)
+    bands_ref[...] = bands_of(out_ref[...], places_ref[...], *matrix_refs)
 
 
 def helped_kernel(helped_ref, end_turned_ref, far_ref, out_ref, code_ref):
@@ -159,15 +160,26 @@
     code_ref[:side], code_ref[side:] = coded(out_ref[...])
 
 
-def last_rows_kernel(m_ref, own_turned_ref, far_ref, helped_ref, places_ref, end_places_ref, *refs):
-    fold_ref, *basis_refs, out_ref, bands_ref = refs
-    out_ref[...] = m_ref[...] + dot(own_turned_ref[...], far_ref[...])
+def last_rows_kernel(end_ref, m_ref, own_bands_ref, own_turned_ref, far_ref, helped_ref, *refs):
+    places_ref, end_places_ref, fold_ref, *basis_refs, out_ref, bands_ref = refs
     rows, width = out_ref.shape
-    by_rows = on_rows(basis_refs[0], jnp.concatenate([out_ref[...], helped_ref[...]], axis=1), False)
-    masks = [masks_of(places[...], rows // order) for places in (places_ref, end_places_ref)]
-    taken = [rows_taken(by_rows[:, i * width :][:, :width], masks[i]) for i in range(2)]
-    coefficients = on_columns(basis_refs[-1], jnp.concatenate(taken, axis=0), False)
-    bands_ref[...] = folded(within(coefficients, masks[0] + masks[1]), fold_ref[...])
+    count = own_bands_ref.shape[0]
+
+    @pl.when(end_ref[0] == 1)
+    def _():
+        out_ref[...] = m_ref[...]
+        bands_ref[:count] = own_bands_ref[...]
+        bands_ref[count:] = jnp.zeros_like(own_bands_ref)
+
+    @pl.when(end_ref[0] == 0)
+    def _():
+        out_ref[...] = m_ref[...] + dot(own_turned_ref[...], far_ref[...])
+        both = jnp.concatenate([out_ref[...], helped_ref[...]], axis=1)
+        by_rows = on_rows(basis_refs[0], both, False)
+        masks = [masks_of(places[...], rows // order) for places in (places_ref, end_places_ref)]
+        taken = [rows_taken(by_rows[:, i * width :][:, :width], masks[i]) for i in range(2)]
+        coefficients = on_columns(basis_refs[-1], jnp.concatenate(taken, axis=0), False)
+        bands_ref[...] = folded(within(coefficients, masks[0] + masks[1]), fold_ref[...])
 
 
 def remove_kernel(count, *refs):
@@ -197,9 +209,11 @@
 
 
 def call(kernel, out_shapes, *operands):
+    spaces = [pltpu.SMEM if x.dtype == jnp.int32 else pltpu.VMEM for x in operands]
     return pl.pallas_call(
         kernel,
         out_shape=out_shapes,
+        in_specs=[pl.BlockSpec(memory_space=space) for space in spaces],
         compiler_params=pltpu.CompilerParams(vmem_limit_bytes=32 * 2**20),
         cost_estimate=pl.CostEstimate(flops=4 * 10**8, bytes_accessed=4 * 10**6, transcendentals=0),
     )(*operands)
@@ -288,16 +302,34 @@
     full = jax.ShapeDtypeStruct(m.shape, jnp.float32)
     turned = jax.ShapeDtypeStruct((m.shape[0], tok), hidden.dtype)
     table = jax.ShapeDtypeStruct((place_rows, m.shape[1]), jnp.float32)
-    m, helped, own_turned, end_turned, end_places = call(
-        swapped_kernel, (full, full, turned, turned, table), m, far_hidden, cross_hidden, cross_grad, swapped
+    own_bands = jax.ShapeDtypeStruct((height, width), jnp.float32)
+    m, helped, own_turned, end_turned, end_places, own_bands = call(
+        swapped_kernel,
+        (full, full, turned, turned, table, own_bands),
+        m,
+        far_hidden,
+        cross_hidden,
+        cross_grad,
+        swapped,
+        places,
+        *matrices,
     )
     far_grad = after(far_grad, m)
     code_shape = jax.ShapeDtypeStruct((m.shape[0] + code_rows, m.shape[1]), jnp.int16)
     helped, code = call(helped_kernel, (full, code_shape), helped, end_turned, far_grad)
     code = send(code, both_ways)
-    folded = jax.ShapeDtypeStruct((2 * height, width), jnp.float32)
     m, bands = call(
-        last_rows_kernel, (full, folded), m, own_turned, far_grad, helped, places, end_places, *matrices
+        last_rows_kernel,
+        (full, jax.ShapeDtypeStruct((2 * height, width), jnp.float32)),
+        end.astype(jnp.int32).reshape(1),
+        m,
+        own_bands,
+        own_turned,
+        far_grad,
+        helped,
+        places,
+        end_places,
+        *matrices,
     )
     exponents = code[m.shape[0] :]
 
@@ -307,16 +339,18 @@
         return x
 
     (bands, end_bands), (stride, count) = summed_but_last(
-        bands, "rep", lambda x: (x[:height], x[height:]), behind_code
-    )
-    parts = [bands] + exchanged(bands, "rep", stride, count)
-    end_flag = jnp.full((8, m.shape[1]), end, jnp.float32)
+        bands, "rep", lambda x: lax.optimization_barrier((x[:height], x[height:])), behind_code
+    )
+    own_sum = pair_sum([bands] + exchanged(bands, "rep", stride, count))
+    to_ends = []
     for k in range(count):
         perm = [
             (i * 4 + a, (i ^ (stride * k)) * 4 + b) for i in range(lax.axis_size("rep")) for a, b in both_ways
         ]
-        parts.append(lax.ppermute(end_bands, ("rep", "tp"), perm))
-    return [m, code, exponents], parts, count, end_flag, places, matrices
+        to_ends.append(lax.ppermute(end_bands, ("rep", "tp"), perm))
+    m, own_sum = lax.optimization_barrier((m, own_sum))
+    end_flag = jnp.full((8, m.shape[1]), end, jnp.float32)
+    return [m, code, exponents], [own_sum] + to_ends, 1, end_flag, places, matrices
 
 
 def local(hidden, out_grad, momentum, band_rows, band_start_columns):

time: 77.5 us -> 79.4 us (1.025)
  local copies, waits for them, and re-layouts: 1.2 us -> 3.81 us
  waiting for transfers between devices: 40.9 us -> 40 us
  matrix products: 4.05 us -> 4.89 us
    unnamed x16 -> x32, local copies, waits for them, and re-layouts: 0.04 us -> 2.65 us
    ppermute x5, waiting for transfers between devices: 37.2 us -> 35.4 us  [send(): return lax.ppermute(x, 'tp', perm)]
    ppermute x2, starting transfers between devices: 3.05 us -> 1.97 us  [lined(): to_ends.append(lax.ppermute(end_bands, ('rep', 'tp'), perm))]
    ppermute x4, starting transfers between devices: 2.43 us -> 3.52 us  [exchanged(): lax.ppermute(x, axis, [(i, i ^ stride * k) for i in range(size)])]
    ppermute x2, waiting for transfers between devices: 0.01 us -> 0.88 us  [lined(): to_ends.append(lax.ppermute(end_bands, ('rep', 'tp'), perm))]
    dot_general x4, matrix products: 4.05 us -> 4.89 us  [dot(): lax.dot_general(a, b, (dims, ((), ())), preferred_element_type=jnp.float32)]
  transfers between devices with their start and end apart: 11 -> 11, of which waited for: 6 -> 8; matrix products, arithmetic and copies ran while one was open for 11% -> 12% of each run, Pallas kernels for 5% -> 4%
where the time goes in v8:
time: 79.4 us; the launch traced here: 79 us
  waiting for transfers between devices  40 us (50%)
  starting transfers between devices  19.7 us (25%)
  Pallas kernels  6.14 us (8%)
  matrix products  4.89 us (6%)
  local copies, waits for them, and re-layouts  3.81 us (5%)
  other arithmetic  3.53 us (4%)
  between operations  0.89 us (1%)
    ppermute x5, waiting for transfers between devices, send(): return lax.ppermute(x, 'tp', perm)  35.4 us
    ppermute x5, starting transfers between devices, send(): return lax.ppermute(x, 'tp', perm)  14.2 us
    pallas_call x5, Pallas kernels, call(): pl.pallas_call(kernel, out_shape=out_shapes, in_specs=[pl.BlockSpec(memor...  6.14 us
    dot_general x4, matrix products, dot(): lax.dot_general(a, b, (dims, ((), ())), preferred_element_type=jnp.float32)  4.89 us
    ppermute x4, waiting for transfers between devices, exchanged(): lax.ppermute(x, axis, [(i, i ^ stride * k) for i in range(size)])  3.67 us
    ppermute x4, starting transfers between devices, exchanged(): lax.ppermute(x, axis, [(i, i ^ stride * k) for i in range(size)])  3.52 us
    unnamed x32, local copies, waits for them, and re-layouts  2.65 us
    ppermute x2, starting transfers between devices, lined(): to_ends.append(lax.ppermute(end_bands, ('rep', 'tp'), perm))  1.97 us
  transfers between devices with their start and end apart: 11, of which 8 were waited for; matrix products, arithmetic and copies ran while one was open for 12% of the time, Pallas kernels for 4%

profile of v8, /device:TPU:0, one launch (start us, length us, event | category | flops | bytes accessed | tf_op | source)
XLA Modules:
  0.0 79.0 jit_solution(5757836306230657115)
XLA Ops:
  0.6 0.0 copy-start.13
  0.6 0.0 copy-start.11
  0.7 0.0 copy-start.15
  0.7 0.0 copy-start.14
  0.7 3.1 %collective-permute-start = (bf16[1152,512]{1,0:T(8,128)(2,1)}, bf16[1152,512]{1,0:T(8,128)(2,1)}, u32[]{:S(2)}, u32[]{:S(2)}) collective-permute-start(bf16[1152,512]{1,0:T(8,128)(2,1)} %param.9), channel_id=1, source_target_pairs={{0,1},{1,0},{2,3},{3,2},{4,5},{5,4},{6,7},{7,6},{8,9},{9,8},{10,11... | collective-permute-start | bytes 3538952 | tf_op jit(solution)/shard_map/ppermute | solution.py:275
  3.8 0.7 collective-permute-start.1
  4.5 1.1 %constant_dynamic-slice_fusion.3 = (bf16[384,256]{1,0:T(8,128)(2,1)S(1)}, bf16[384,256]{1,0:T(8,128)(2,1)S(1)}) fusion(bf16[4608,256]{1,0:T(8,128)(2,1)} %param.8, s32[]{:T(128)S(6)} %select_n.40, s32[]{:T(128)S(6)} %select_n.42), kind=kLoop, calls=%fused_computation.24 | loop fusion | bytes 786440 | tf_op jit(solution)/shard_map/dynamic_slice | solution.py:272
  5.6 1.2 %dynamic-slice_select_fusion = (bf16[768,256]{1,0:T(8,128)(2,1)S(1)}, bf16[768,256]{1,0:T(8,128)(2,1)S(1)}) fusion(bf16[4608,256]{1,0:T(8,128)(2,1)} %param.8, s32[]{:T(128)S(6)} %select_n.44, pred[]{:T(512)S(6)} %or.3, s32[]{:T(128)S(6)} %add.58), kind=kLoop, calls=%fused_computation.11 | loop fusion | flops 196608 | bytes 1572873 | tf_op jit(solution)/shard_map/jit(_where)/select_n | solution.py:293
  6.9 0.1 fusion.15
  7.0 2.4 %convolution_add_fusion.1 = f32[256,512]{1,0:T(8,128)} fusion(bf16[1152,512]{1,0:T(8,128)(2,1)S(1)} %copy-done.11, bf16[4608,256]{1,0:T(8,128)(2,1)} %param.8, s32[]{:T(128)S(6)} %select_n.46, f32[1,256,512]{2,1,0:T(8,128)S(1)} %copy-done.12), kind=kOutput, calls=%fused_computation.4 | convolution fusion | flops 302252032 | bytes 2818052 | tf_op jit(solution)/shard_map/dot_general | solution.py:47
  9.4 20.7 %collective-permute-done = bf16[1152,512]{1,0:T(8,128)(2,1)} collective-permute-done((bf16[1152,512]{1,0:T(8,128)(2,1)}, bf16[1152,512]{1,0:T(8,128)(2,1)}, u32[]{:S(2)}, u32[]{:S(2)}) %collective-permute-start) | collective-permute-done | bytes 1179680 | tf_op jit(solution)/shard_map/ppermute | solution.py:275
  30.0 0.7 collective-permute-start.3
  30.8 0.9 %fusion.2 = bf16[784,512]{1,0:T(8,128)(2,1)} fusion(bf16[8,512]{1,0:T(8,128)(2,1)S(1)} %get-tuple-element.68, bf16[768,256]{1,0:T(8,128)(2,1)S(1)} %get-tuple-element.63, bf16[384,256]{1,0:T(8,128)(2,1)S(1)} %get-tuple-element.65, bf16[384,256]{1,0:T(8,128)(2,1)S(1)} %get-tuple-element.64), kind=kLoop, calls=%fused_computation.5 | loop fusion | flops 4014080 | bytes 1597440 | tf_op jit(solution)/shard_map/concatenate | solution.py:292
  31.7 0.0 collective-permute-done.1.cross_ref
  31.7 1.4 %slice_select_fusion = bf16[784,512]{1,0:T(8,128)(2,1)S(1)} fusion(bf16[784,512]{1,0:T(8,128)(2,1)} %fusion.2, bf16[1152,512]{1,0:T(8,128)(2,1)S(1)} %collective-permute-done.1.cross_ref, pred[]{:T(512)S(6)} %or.3), kind=kLoop, calls=%fused_computation.6 | loop fusion | flops 401408 | bytes 2408449 | tf_op jit(solution)/shard_map/jit(_where)/select_n | solution.py:298
  33.1 0.0 copy-start.10
  33.1 3.3 %collective-permute-start.2 = (bf16[784,512]{1,0:T(8,128)(2,1)S(1)}, bf16[784,512]{1,0:T(8,128)(2,1)S(1)}, u32[]{:S(2)}, u32[]{:S(2)}) collective-permute-start(bf16[784,512]{1,0:T(8,128)(2,1)S(1)} %slice_select_fusion), channel_id=1, source_target_pairs={{0,1},{1,0},{2,3},{3,2},{4,5},{5,4},{6,7},{7,6},{8,9},{9,8},{10,11... | collective-permute-start | bytes 2408456 | tf_op jit(solution)/shard_map/ppermute | solution.py:275
  36.4 0.5 fusion.3
  37.0 0.0 copy-done.10
  37.0 0.0 copy-start
  37.0 0.0 copy-start.3
  37.0 1.8 %fusion.1.m_ref = f32[256,512]{1,0:T(8,128)S(1)} fusion(f32[256,512]{1,0:T(8,128)S(1)} %fusion.3, f32[256,512]{1,0:T(8,128)S(1)} %copy-done.10, bf16[1152,512]{1,0:T(8,128)(2,1)} %collective-permute-done, bf16[4608,256]{1,0:T(8,128)(2,1)S(1)} %copy-done.9, s32[]{:T(128)S(6)} %select_n.47), kind=kOutput, calls=%fused_computation.3 | convolution fusion | flops 302252032 | bytes 3342340 | tf_op jit(solution)/shard_map/dot_general | solution.py:47
  38.9 14.3 %collective-permute-done.2.swapped_ref = bf16[784,512]{1,0:T(8,128)(2,1)S(1)} collective-permute-done((bf16[784,512]{1,0:T(8,128)(2,1)S(1)}, bf16[784,512]{1,0:T(8,128)(2,1)S(1)}, u32[]{:S(2)}, u32[]{:S(2)}) %collective-permute-start.2) | collective-permute-done | bytes 802848 | tf_op jit(solution)/shard_map/ppermute | solution.py:275
  53.1 1.1 %shard_map.95 = (f32[256,512]{1,0:T(8,128)S(1)}, f32[256,512]{1,0:T(8,128)S(1)}, bf16[256,1152]{1,0:T(8,128)(2,1)S(1)}, bf16[256,1152]{1,0:T(8,128)(2,1)S(1)}, f...) custom-call(f32[256,512]{1,0:T(8,128)S(1)} %fusion.1.m_ref, ...), custom_call_target="tpu_custom_call" | custom-call | flops 400000000 | bytes 4000000 | tf_op jit(solution)/shard_map/pallas_call | solution.py:213
  54.3 0.0 copy-start.7
  54.3 0.0 copy-start.4
  54.3 0.0 collective-permute-done.3.far_ref
  54.3 1.3 %shard_map.96 = (f32[256,512]{1,0:T(8,128)S(1)}, s16[272,512]{1,0:T(8,128)(2,1)}) custom-call(f32[256,512]{1,0:T(8,128)S(1)} %get-tuple-element.43.helped_ref, bf16[256,1152]{1,0:T(8,128)(2,1)S(1)} %get-tuple-element.44.end_turned_ref, bf16[1152,512]{1,0:T(8,128)(2,1)S(1)} %collective-permute-done.3.far_ref), custom_call_target="tpu_custom_call" | custom-call | flops 400000000 | bytes 4000000 | tf_op jit(solution)/shard_map/pallas_call | solution.py:213
  55.7 0.0 copy-done.1
  55.7 6.4 %collective-permute-start.7 = (s16[272,512]{1,0:T(8,128)(2,1)}, s16[272,512]{1,0:T(8,128)(2,1)S(1)}, u32[]{:S(2)}, u32[]{:S(2)}) collective-permute-start(s16[272,512]{1,0:T(8,128)(2,1)} %get-tuple-element.49), channel_id=1, source_target_pairs={{0,1},{1,0},{2,3},{3,2},{4,5},{5,4},{6,7},{7,6},{8,9},{9,8},{10,11... | collective-permute-start | bytes 835592 | tf_op jit(solution)/shard_map/ppermute | solution.py:275
  62.1 1.1 %copy-done.2 = bf16[256,1152]{1,0:T(8,128)(2,1)S(1)} copy-done((bf16[256,1152]{1,0:T(8,128)(2,1)S(1)}, bf16[256,1152]{1,0:T(8,128)(2,1)}, u32[]{:S(2)}) %copy-start.2) | copy-done | bytes 589848
  63.2 0.8 copy-done.6
  63.9 0.8 copy-done.8
  64.7 0.1 collective-permute-start.4
  64.8 1.6 %collective-permute-start.5 = (f32[128,128]{1,0:T(8,128)S(1)}, f32[128,128]{1,0:T(8,128)S(1)}, u32[]{:S(2)}, u32[]{:S(2)}) collective-permute-start(f32[128,128]{1,0:T(8,128)S(1)} %get-tuple-element.48), channel_id=1, source_target_pairs={{0,8},{4,12},{8,0},{12,4},{16,24},{20,28},{24,16},{28,20},{1,9},{5... | collective-permute-start | bytes 196616 | tf_op jit(solution)/shard_map/ppermute | solution.py:232
  66.4 0.3 collective-permute-start.6
  66.7 0.5 collective-permute-done.7.refs_1_
  67.2 0.0 collective-permute-done.4
  67.2 2.1 %collective-permute-done.5 = f32[128,128]{1,0:T(8,128)S(1)} collective-permute-done((f32[128,128]{1,0:T(8,128)S(1)}, f32[128,128]{1,0:T(8,128)S(1)}, u32[]{:S(2)}, u32[]{:S(2)}) %collective-permute-start.5) | collective-permute-done | bytes 65568 | tf_op jit(solution)/shard_map/ppermute | solution.py:232
  69.3 1.1 %collective-permute-done.6 = f32[128,128]{1,0:T(8,128)S(1)} collective-permute-done((f32[128,128]{1,0:T(8,128)S(1)}, f32[128,128]{1,0:T(8,128)S(1)}, u32[]{:S(2)}, u32[]{:S(2)}) %collective-permute-start.6) | collective-permute-done | bytes 65568 | tf_op jit(solution)/shard_map/ppermute | solution.py:232
  70.5 1.6 %collective-permute-start.8 = (f32[64,128]{1,0:T(8,128)S(1)}, f32[64,128]{1,0:T(8,128)S(1)}, u32[]{:S(2)}, u32[]{:S(2)}) collective-permute-start(f32[64,128]{1,0:T(8,128)S(1)} %get-tuple-element.53), channel_id=1, source_target_pairs={{0,16},{4,20},{8,24},{12,28},{16,0},{20,4},{24,8},{28,12},{1,17},{... | collective-permute-start | bytes 98312 | tf_op jit(solution)/shard_map/ppermute | solution.py:232
  72.0 1.4 %collective-permute-start.10 = (f32[64,128]{1,0:T(8,128)S(1)}, f32[64,128]{1,0:T(8,128)S(1)}, u32[]{:S(2)}, u32[]{:S(2)}) collective-permute-start(f32[64,128]{1,0:T(8,128)S(1)} %get-tuple-element.55), channel_id=1, source_target_pairs={{0,17},{1,16},{2,19},{3,18},{4,21},{5,20},{6,23},{7,22},{8,25},{9,... | collective-permute-start | bytes 98312 | tf_op jit(solution)/shard_map/ppermute | solution.py:350
  73.5 0.5 collective-permute-start.9
  74.0 0.4 collective-permute-done.8
  74.5 2.1 %shard_map.98 = f32[256,512]{1,0:T(8,128)} custom-call(f32[256,512]{1,0:T(8,128)S(1)} %get-tuple-element.56.refs_0_, s16[272,512]{1,0:T(8,128)(2,1)S(1)} %collective-permute-done.7.refs_1_, s16[16,512]{1,0:T(8,128)(2,1)S(1)} %slice.24.refs_2_, f32[8,512]{1,0:T(8,128)S(1)} %broadcast_in_dim.11.refs_3_, ...), custom_call_target="tpu_custom_call" | custom-call | flops 400000000 | bytes 4000000 | tf_op jit(solution)/shard_map/pallas_call | solution.py:213
  76.5 0.5 collective-permute-done.10.refs_2_
  77.1 0.3 collective-permute-done.9.refs_1_
  77.4 1.6 %shard_map.99 = bf16[256,512]{1,0:T(8,128)(2,1)} custom-call(f32[64,128]{1,0:T(8,128)S(1)} %add.56.refs_0_, f32[64,128]{1,0:T(8,128)S(1)} %collective-permute-done.9.refs_1_, f32[64,128]{1,0:T(8,128)S(1)} %collective-permute-done.10.refs_2_, f32[8,512]{1,0:T(8,128)S(1)} %broadcast_in_dim.11.refs_3_, ...), custom_call_target="tpu_custom_call" | custom-call | flops 400000000 | bytes 4000000 | tf_op jit(solution)/shard_map/pallas_call | solution.py:213
  (25 shorter events, 0.1 us)
Async XLA Ops:
  0.6 6.2 %copy-start.13 = (bf16[8,512]{1,0:T(8,128)(2,1)S(1)}, bf16[8,512]{1,0:T(8,128)(2,1)}, u32[]{:S(2)}) copy-start(bf16[8,512]{1,0:T(8,128)(2,1)} %constant.51) | copy-start | bytes 24580
  0.6 6.4 %copy-start.11 = (bf16[1152,512]{1,0:T(8,128)(2,1)S(1)}, bf16[1152,512]{1,0:T(8,128)(2,1)}, u32[]{:S(2)}) copy-start(bf16[1152,512]{1,0:T(8,128)(2,1)} %param.9) | copy-start | bytes 3538948
  0.7 6.2 %copy-start.15 = (s32[4,8]{1,0:T(4,128)S(1)}, s32[4,8]{1,0:T(4,128)}, u32[]{:S(2)}) copy-start(s32[4,8]{1,0:T(4,128)} %param.11) | copy-start | bytes 388
  0.7 6.2 %copy-start.14 = (s32[4,8]{1,0:T(4,128)S(1)}, s32[4,8]{1,0:T(4,128)}, u32[]{:S(2)}) copy-start(s32[4,8]{1,0:T(4,128)} %param.12) | copy-start | bytes 388
  0.7 29.4 %collective-permute-start = (bf16[1152,512]{1,0:T(8,128)(2,1)}, bf16[1152,512]{1,0:T(8,128)(2,1)}, u32[]{:S(2)}, u32[]{:S(2)}) collective-permute-start(bf16[1152,512]{1,0:T(8,128)(2,1)} %param.9), channel_id=1, source_target_pairs={{0,1},{1,0},{2,3},{3,2},{4,5},{5,4},{6,7},{7,6},{8,9},{9,8},{10,11... | collective-permute-start | bytes 3538952 | tf_op jit(solution)/shard_map/ppermute | solution.py:275
  3.8 28.0 %collective-permute-start.1 = (bf16[1152,512]{1,0:T(8,128)(2,1)}, bf16[1152,512]{1,0:T(8,128)(2,1)S(1)}, u32[]{:S(2)}, u32[]{:S(2)}) collective-permute-start(bf16[1152,512]{1,0:T(8,128)(2,1)} %param.9), channel_id=1, source_target_pairs={{1,2},{2,1},{5,6},{6,5},{9,10},{10,9},{13,14},{14,13},{17,18},{18,... | collective-permute-start | bytes 3538952 | tf_op jit(solution)/shard_map/ppermute | solution.py:275
  4.5 2.5 %copy-start.12 = (f32[1,256,512]{2,1,0:T(8,128)S(1)}, f32[1,256,512]{2,1,0:T(8,128)}, u32[]{:S(2)}) copy-start(f32[1,256,512]{2,1,0:T(8,128)} %param.10) | copy-start | bytes 1572868
  30.0 24.3 %collective-permute-start.3 = (bf16[1152,512]{1,0:T(8,128)(2,1)}, bf16[1152,512]{1,0:T(8,128)(2,1)S(1)}, u32[]{:S(2)}, u32[]{:S(2)}) collective-permute-start(bf16[1152,512]{1,0:T(8,128)(2,1)} %collective-permute-done), channel_id=1, source_target_pairs={{1,2},{2,1},{5,6},{6,5},{9,10},{10,9},{13,14},{14,13},{17,18},{18,... | collective-permute-start | bytes 3538952 | tf_op jit(solution)/shard_map/ppermute | solution.py:275
  31.7 4.7 %copy-start.9 = (bf16[4608,256]{1,0:T(8,128)(2,1)S(1)}, bf16[4608,256]{1,0:T(8,128)(2,1)}, u32[]{:S(2)}) copy-start(bf16[4608,256]{1,0:T(8,128)(2,1)} %param.8) | copy-start | bytes 7077892
  33.1 3.9 %copy-start.10 = (f32[256,512]{1,0:T(8,128)S(1)}, f32[256,512]{1,0:T(8,128)}, u32[]{:S(2)}) copy-start(f32[256,512]{1,0:T(8,128)} %convolution_add_fusion.1) | copy-start | bytes 1572868
  33.1 20.0 %collective-permute-start.2 = (bf16[784,512]{1,0:T(8,128)(2,1)S(1)}, bf16[784,512]{1,0:T(8,128)(2,1)S(1)}, u32[]{:S(2)}, u32[]{:S(2)}) collective-permute-start(bf16[784,512]{1,0:T(8,128)(2,1)S(1)} %slice_select_fusion), channel_id=1, source_target_pairs={{0,1},{1,0},{2,3},{3,2},{4,5},{5,4},{6,7},{7,6},{8,9},{9,8},{10,11... | collective-permute-start | bytes 2408456 | tf_op jit(solution)/shard_map/ppermute | solution.py:275
  37.0 16.1 %copy-start = (f32[256,256]{1,0:T(8,128)S(1)}, f32[256,256]{1,0:T(8,128)}, u32[]{:S(2)}) copy-start(f32[256,256]{1,0:T(8,128)} %constant.32.clone.refs_1_.refs_3_.refs_5_.refs_6_) | copy-start | bytes 786436
  37.0 16.1 %copy-start.3 = (bf16[512,128]{1,0:T(8,128)(2,1)S(1)}, bf16[512,128]{1,0:T(8,128)(2,1)}, u32[]{:S(2)}) copy-start(bf16[512,128]{1,0:T(8,128)(2,1)} %constant.31.clone.refs_0_.refs_2_.refs_5_) | copy-start | bytes 393220
  54.3 1.4 %copy-start.1 = (bf16[256,1152]{1,0:T(8,128)(2,1)}, bf16[256,1152]{1,0:T(8,128)(2,1)S(1)}, u32[]{:S(2)}) copy-start(bf16[256,1152]{1,0:T(8,128)(2,1)S(1)} %get-tuple-element.41.own_turned_ref) | copy-start | bytes 1769476
  54.3 1.4 %copy-start.5 = (f32[16,512]{1,0:T(8,128)}, f32[16,512]{1,0:T(8,128)S(1)}, u32[]{:S(2)}) copy-start(f32[16,512]{1,0:T(8,128)S(1)} %get-tuple-element.46.refs_1_) | copy-start | bytes 98308
  54.3 1.4 %copy-start.7 = (f32[64,128]{1,0:T(8,128)}, f32[64,128]{1,0:T(8,128)S(1)}, u32[]{:S(2)}) copy-start(f32[64,128]{1,0:T(8,128)S(1)} %get-tuple-element.40.own_bands_ref) | copy-start | bytes 98308
  54.3 7.8 %copy-start.4 = (bf16[512,128]{1,0:T(8,128)(2,1)S(1)}, bf16[512,128]{1,0:T(8,128)(2,1)}, u32[]{:S(2)}) copy-start(bf16[512,128]{1,0:T(8,128)(2,1)} %constant.31.clone.refs_0_.refs_2_.refs_5_) | copy-start | bytes 393220
  55.7 11.5 %collective-permute-start.7 = (s16[272,512]{1,0:T(8,128)(2,1)}, s16[272,512]{1,0:T(8,128)(2,1)S(1)}, u32[]{:S(2)}, u32[]{:S(2)}) collective-permute-start(s16[272,512]{1,0:T(8,128)(2,1)} %get-tuple-element.49), channel_id=1, source_target_pairs={{0,1},{1,0},{2,3},{3,2},{4,5},{5,4},{6,7},{7,6},{8,9},{9,8},{10,11... | collective-permute-start | bytes 835592 | tf_op jit(solution)/shard_map/ppermute | solution.py:275
  62.1 1.1 %copy-start.2 = (bf16[256,1152]{1,0:T(8,128)(2,1)S(1)}, bf16[256,1152]{1,0:T(8,128)(2,1)}, u32[]{:S(2)}) copy-start(bf16[256,1152]{1,0:T(8,128)(2,1)} %copy-done.1) | copy-start | bytes 1769476
  63.2 0.8 copy-start.6
  63.9 0.8 copy-start.8
  64.7 2.4 %collective-permute-start.4 = (f32[128,128]{1,0:T(8,128)S(1)}, f32[128,128]{1,0:T(8,128)S(1)}, u32[]{:S(2)}, u32[]{:S(2)}) collective-permute-start(f32[128,128]{1,0:T(8,128)S(1)} %get-tuple-element.48), channel_id=1, source_target_pairs={{0,4},{4,0},{8,12},{12,8},{16,20},{20,16},{24,28},{28,24},{1,5},{5... | collective-permute-start | bytes 196616 | tf_op jit(solution)/shard_map/ppermute | solution.py:232
  64.8 4.5 %collective-permute-start.5 = (f32[128,128]{1,0:T(8,128)S(1)}, f32[128,128]{1,0:T(8,128)S(1)}, u32[]{:S(2)}, u32[]{:S(2)}) collective-permute-start(f32[128,128]{1,0:T(8,128)S(1)} %get-tuple-element.48), channel_id=1, source_target_pairs={{0,8},{4,12},{8,0},{12,4},{16,24},{20,28},{24,16},{28,20},{1,9},{5... | collective-permute-start | bytes 196616 | tf_op jit(solution)/shard_map/ppermute | solution.py:232
  66.4 4.0 %collective-permute-start.6 = (f32[128,128]{1,0:T(8,128)S(1)}, f32[128,128]{1,0:T(8,128)S(1)}, u32[]{:S(2)}, u32[]{:S(2)}) collective-permute-start(f32[128,128]{1,0:T(8,128)S(1)} %get-tuple-element.48), channel_id=1, source_target_pairs={{0,12},{4,8},{8,4},{12,0},{16,28},{20,24},{24,20},{28,16},{1,13},{... | collective-permute-start | bytes 196616 | tf_op jit(solution)/shard_map/ppermute | solution.py:232
  70.5 4.0 %collective-permute-start.8 = (f32[64,128]{1,0:T(8,128)S(1)}, f32[64,128]{1,0:T(8,128)S(1)}, u32[]{:S(2)}, u32[]{:S(2)}) collective-permute-start(f32[64,128]{1,0:T(8,128)S(1)} %get-tuple-element.53), channel_id=1, source_target_pairs={{0,16},{4,20},{8,24},{12,28},{16,0},{20,4},{24,8},{28,12},{1,17},{... | collective-permute-start | bytes 98312 | tf_op jit(solution)/shard_map/ppermute | solution.py:232
  72.0 5.0 %collective-permute-start.10 = (f32[64,128]{1,0:T(8,128)S(1)}, f32[64,128]{1,0:T(8,128)S(1)}, u32[]{:S(2)}, u32[]{:S(2)}) collective-permute-start(f32[64,128]{1,0:T(8,128)S(1)} %get-tuple-element.55), channel_id=1, source_target_pairs={{0,17},{1,16},{2,19},{3,18},{4,21},{5,20},{6,23},{7,22},{8,25},{9,... | collective-permute-start | bytes 98312 | tf_op jit(solution)/shard_map/ppermute | solution.py:350
  73.5 3.9 %collective-permute-start.9 = (f32[64,128]{1,0:T(8,128)S(1)}, f32[64,128]{1,0:T(8,128)S(1)}, u32[]{:S(2)}, u32[]{:S(2)}) collective-permute-start(f32[64,128]{1,0:T(8,128)S(1)} %get-tuple-element.55), channel_id=1, source_target_pairs={{0,1},{1,0},{2,3},{3,2},{4,5},{5,4},{6,7},{7,6},{8,9},{9,8},{10,11... | collective-permute-start | bytes 98312 | tf_op jit(solution)/shard_map/ppermute | solution.py:350

commit v9 on v7

--- a/solution.py
+++ b/solution.py
@@ -200,17 +200,17 @@
     return pl.pallas_call(
         kernel,
         out_shape=out_shapes,
-        compiler_params=pltpu.CompilerParams(vmem_limit_bytes=32 * 2**20),
+        compiler_params=pltpu.CompilerParams(vmem_limit_bytes=16 * 2**20),
         cost_estimate=pl.CostEstimate(flops=4 * 10**8, bytes_accessed=4 * 10**6, transcendentals=0),
     )(*operands)
 
 
 def stages_of(axis):
-    size, stride, stages = lax.axis_size(axis), 1, []
+    size, stride, stages = lax.axis_size(axis), 2, []
     while stride < size:
         stages.append((stride, min(4, size // stride)))
         stride *= stages[-1][1]
-    return stages
+    return stages + [(1, min(2, size))]
 
 
 def exchanged(x, axis, stride, count):
@@ -222,7 +222,7 @@
     size = lax.axis_size(axis)
     if size & (size - 1):
         return form(lax.psum(x, axis)), (1, 1)
-    *stages, last = stages_of(axis) or [(1, 1)]
+    *stages, last = stages_of(axis)
     for stride, count in stages:
         x = pair_sum([x] + then(exchanged(x, axis, stride, count)))
     return form(x), last
@@ -262,6 +262,7 @@
 
     both_ways = [(0, 1), (1, 0), (2, 3), (3, 2)]
     across = [(1, 2), (2, 1)]
+    outward = [(1, 0), (2, 3)]
 
     pair_grad = send(out_grad, both_ways)
     cross_grad = send(out_grad, across)
@@ -294,7 +295,7 @@
     far_grad = after(far_grad, m)
     code_shape = jax.ShapeDtypeStruct((m.shape[0] + code_rows, m.shape[1]), jnp.int16)
     helped, code = call(helped_kernel, (full, code_shape), helped, end_turned, far_grad)
-    code = send(code, both_ways)
+    code = send(code, outward)
     folded = jax.ShapeDtypeStruct((2 * height, width), jnp.float32)
     m, bands = call(
         last_rows_kernel, (full, folded), m, own_turned, far_grad, helped, places, end_places, *matrices
@@ -307,16 +308,18 @@
         return x
 
     (bands, end_bands), (stride, count) = summed_but_last(
-        bands, "rep", lambda x: (x[:height], x[height:]), behind_code
-    )
-    parts = [bands] + exchanged(bands, "rep", stride, count)
-    end_flag = jnp.full((8, m.shape[1]), end, jnp.float32)
+        bands, "rep", lambda x: lax.optimization_barrier((x[:height], x[height:])), behind_code
+    )
+    own_sum = pair_sum([bands] + exchanged(bands, "rep", stride, count))
+    to_ends = []
     for k in range(count):
         perm = [
             (i * 4 + a, (i ^ (stride * k)) * 4 + b) for i in range(lax.axis_size("rep")) for a, b in both_ways
         ]
-        parts.append(lax.ppermute(end_bands, ("rep", "tp"), perm))
-    return [m, code, exponents], parts, count, end_flag, places, matrices
+        to_ends.append(lax.ppermute(end_bands, ("rep", "tp"), perm))
+    m, own_sum = lax.optimization_barrier((m, own_sum))
+    end_flag = jnp.full((8, m.shape[1]), end, jnp.float32)
+    return [m, code, exponents], [own_sum] + to_ends, 1, end_flag, places, matrices
 
 
 def local(hidden, out_grad, momentum, band_rows, band_start_columns):

time: 77.5 us -> 78.4 us (1.012)
  waiting for transfers between devices: 40.9 us -> 44.3 us
  starting transfers between devices: 20.4 us -> 17.8 us
    ppermute x5, starting transfers between devices: 14.9 us -> 9.1 us  [send(): return lax.ppermute(x, 'tp', perm)]
    ppermute x5, waiting for transfers between devices: 37.2 us -> 42.5 us  [send(): return lax.ppermute(x, 'tp', perm)]
    ppermute x4, waiting for transfers between devices: 3.69 us -> 0.01 us  [exchanged(): lax.ppermute(x, axis, [(i, i ^ stride * k) for i in range(size)])]
    ppermute x2, starting transfers between devices: 3.05 us -> 5.1 us  [lined(): to_ends.append(lax.ppermute(end_bands, ('rep', 'tp'), perm))]
    ppermute x2, waiting for transfers between devices: 0.01 us -> 1.78 us  [lined(): to_ends.append(lax.ppermute(end_bands, ('rep', 'tp'), perm))]
    ppermute x4, starting transfers between devices: 2.43 us -> 3.62 us  [exchanged(): lax.ppermute(x, axis, [(i, i ^ stride * k) for i in range(size)])]
  transfers between devices with their start and end apart: 11 -> 11, of which waited for: 6 -> 4; matrix products, arithmetic and copies ran while one was open for 11% -> 11% of each run, Pallas kernels for 5% -> 5%
where the time goes in v9:
time: 78.4 us; the launch traced here: 78.1 us
  waiting for transfers between devices  44.3 us (57%)
  starting transfers between devices  17.8 us (23%)
  Pallas kernels  6.29 us (8%)
  matrix products  4.05 us (5%)
  other arithmetic  3.56 us (5%)
  local copies, waits for them, and re-layouts  1.2 us (2%)
  between operations  0.9 us (1%)
    ppermute x5, waiting for transfers between devices, send(): return lax.ppermute(x, 'tp', perm)  42.5 us
    ppermute x5, starting transfers between devices, send(): return lax.ppermute(x, 'tp', perm)  9.1 us
    pallas_call x5, Pallas kernels, call(): pl.pallas_call(kernel, out_shape=out_shapes, compiler_params=pltpu.Compil...  6.29 us
    ppermute x2, starting transfers between devices, lined(): to_ends.append(lax.ppermute(end_bands, ('rep', 'tp'), perm))  5.1 us
    dot_general x4, matrix products, dot(): lax.dot_general(a, b, (dims, ((), ())), preferred_element_type=jnp.float32)  4.05 us
    ppermute x4, starting transfers between devices, exchanged(): lax.ppermute(x, axis, [(i, i ^ stride * k) for i in range(size)])  3.62 us
    ppermute x2, waiting for transfers between devices, lined(): to_ends.append(lax.ppermute(end_bands, ('rep', 'tp'), perm))  1.78 us
  transfers between devices with their start and end apart: 11, of which 4 were waited for; matrix products, arithmetic and copies ran while one was open for 11% of the time, Pallas kernels for 5%

profile of v9, /device:TPU:0, one launch (start us, length us, event | category | flops | bytes accessed | tf_op | source)
XLA Modules:
  0.0 78.1 jit_solution(11792699546274970047)
XLA Ops:
  0.6 0.0 copy-start.5
  0.6 0.0 copy-start.3
  0.7 0.0 copy-start.7
  0.7 0.0 copy-start.6
  0.7 3.1 %collective-permute-start = (bf16[1152,512]{1,0:T(8,128)(2,1)}, bf16[1152,512]{1,0:T(8,128)(2,1)}, u32[]{:S(2)}, u32[]{:S(2)}) collective-permute-start(bf16[1152,512]{1,0:T(8,128)(2,1)} %param.9), channel_id=1, source_target_pairs={{0,1},{1,0},{2,3},{3,2},{4,5},{5,4},{6,7},{7,6},{8,9},{9,8},{10,11... | collective-permute-start | bytes 3538952 | tf_op jit(solution)/shard_map/ppermute | solution.py:261
  3.8 0.7 collective-permute-start.1
  4.5 0.0 copy-start.4
  4.5 1.1 %constant_dynamic-slice_fusion.3 = (bf16[384,256]{1,0:T(8,128)(2,1)S(1)}, bf16[384,256]{1,0:T(8,128)(2,1)S(1)}) fusion(bf16[4608,256]{1,0:T(8,128)(2,1)} %param.8, s32[]{:T(128)S(6)} %select_n.40, s32[]{:T(128)S(6)} %select_n.42), kind=kLoop, calls=%fused_computation.24 | loop fusion | bytes 786440 | tf_op jit(solution)/shard_map/dynamic_slice | solution.py:258
  5.6 1.2 %dynamic-slice_select_fusion = (bf16[768,256]{1,0:T(8,128)(2,1)S(1)}, bf16[768,256]{1,0:T(8,128)(2,1)S(1)}) fusion(bf16[4608,256]{1,0:T(8,128)(2,1)} %param.8, s32[]{:T(128)S(6)} %select_n.44, pred[]{:T(512)S(6)} %or.3, s32[]{:T(128)S(6)} %add.58), kind=kLoop, calls=%fused_computation.11 | loop fusion | flops 196608 | bytes 1572873 | tf_op jit(solution)/shard_map/jit(_where)/select_n | solution.py:280
  6.8 0.0 copy-done.5
  6.9 0.0 copy-done.7
  6.9 0.0 copy-done.6
  6.9 0.1 fusion.15
  7.0 0.0 copy-done.3
  7.0 1.6 %convolution_add_fusion.1 = f32[256,512]{1,0:T(8,128)S(1)} fusion(bf16[1152,512]{1,0:T(8,128)(2,1)S(1)} %copy-done.3, bf16[4608,256]{1,0:T(8,128)(2,1)} %param.8, s32[]{:T(128)S(6)} %select_n.46, f32[1,256,512]{2,1,0:T(8,128)S(1)} %copy-done.4), kind=kOutput, calls=%fused_computation.4 | convolution fusion | flops 302252032 | bytes 2818052 | tf_op jit(solution)/shard_map/dot_general | solution.py:47
  8.6 21.5 %collective-permute-done = bf16[1152,512]{1,0:T(8,128)(2,1)} collective-permute-done((bf16[1152,512]{1,0:T(8,128)(2,1)}, bf16[1152,512]{1,0:T(8,128)(2,1)}, u32[]{:S(2)}, u32[]{:S(2)}) %collective-permute-start) | collective-permute-done | bytes 1179680 | tf_op jit(solution)/shard_map/ppermute | solution.py:261
  30.0 0.7 collective-permute-start.3
  30.8 1.0 %fusion.2 = bf16[784,512]{1,0:T(8,128)(2,1)} fusion(bf16[8,512]{1,0:T(8,128)(2,1)S(1)} %get-tuple-element.66, bf16[768,256]{1,0:T(8,128)(2,1)S(1)} %get-tuple-element.61, bf16[384,256]{1,0:T(8,128)(2,1)S(1)} %get-tuple-element.63, bf16[384,256]{1,0:T(8,128)(2,1)S(1)} %get-tuple-element.62), kind=kLoop, calls=%fused_computation.5 | loop fusion | flops 4014080 | bytes 1597440 | tf_op jit(solution)/shard_map/concatenate | solution.py:279
  31.7 0.0 collective-permute-done.1.cross_ref
  31.7 1.4 %slice_select_fusion = bf16[784,512]{1,0:T(8,128)(2,1)S(1)} fusion(bf16[784,512]{1,0:T(8,128)(2,1)} %fusion.2, bf16[1152,512]{1,0:T(8,128)(2,1)S(1)} %collective-permute-done.1.cross_ref, pred[]{:T(512)S(6)} %or.3), kind=kLoop, calls=%fused_computation.6 | loop fusion | flops 401408 | bytes 2408449 | tf_op jit(solution)/shard_map/jit(_where)/select_n | solution.py:285
  33.1 3.3 %collective-permute-start.2 = (bf16[784,512]{1,0:T(8,128)(2,1)S(1)}, bf16[784,512]{1,0:T(8,128)(2,1)S(1)}, u32[]{:S(2)}, u32[]{:S(2)}) collective-permute-start(bf16[784,512]{1,0:T(8,128)(2,1)S(1)} %slice_select_fusion), channel_id=1, source_target_pairs={{0,1},{1,0},{2,3},{3,2},{4,5},{5,4},{6,7},{7,6},{8,9},{9,8},{10,11... | collective-permute-start | bytes 2408456 | tf_op jit(solution)/shard_map/ppermute | solution.py:261
  36.4 0.5 fusion.3
  37.0 1.8 %fusion.1.m_ref = f32[256,512]{1,0:T(8,128)S(1)} fusion(f32[256,512]{1,0:T(8,128)S(1)} %fusion.3, f32[256,512]{1,0:T(8,128)S(1)} %convolution_add_fusion.1, bf16[1152,512]{1,0:T(8,128)(2,1)} %collective-permute-done, bf16[4608,256]{1,0:T(8,128)(2,1)S(1)} %copy-done.2, s32[]{:T(128)S(6)} %select_n.47), kind=kOutput, calls=%fused_computation.3 | convolution fusion | flops 302252032 | bytes 3342340 | tf_op jit(solution)/shard_map/dot_general | solution.py:47
  38.8 14.3 %collective-permute-done.2.swapped_ref = bf16[784,512]{1,0:T(8,128)(2,1)S(1)} collective-permute-done((bf16[784,512]{1,0:T(8,128)(2,1)S(1)}, bf16[784,512]{1,0:T(8,128)(2,1)S(1)}, u32[]{:S(2)}, u32[]{:S(2)}) %collective-permute-start.2) | collective-permute-done | bytes 802848 | tf_op jit(solution)/shard_map/ppermute | solution.py:261
  53.1 0.5 shard_map.95
  53.7 0.0 copy-start
  53.7 0.0 copy-start.1
  53.7 0.0 collective-permute-done.3.far_ref
  53.7 0.6 shard_map.96
  54.3 1.3 %collective-permute-start.7 = (s16[272,512]{1,0:T(8,128)(2,1)S(1)}, s16[272,512]{1,0:T(8,128)(2,1)S(1)}, u32[]{:S(2)}, u32[]{:S(2)}) collective-permute-start(s16[272,512]{1,0:T(8,128)(2,1)S(1)} %get-tuple-element.47), channel_id=1, source_target_pairs={{1,0},{2,3},{5,4},{6,7},{9,8},{10,11},{13,12},{14,15},{17,16},{18,... | collective-permute-start | bytes 835592 | tf_op jit(solution)/shard_map/ppermute | solution.py:261
  55.6 0.0 copy-done
  55.6 0.0 copy-done.1
  55.6 1.5 %shard_map.97 = (f32[256,512]{1,0:T(8,128)S(1)}, f32[128,128]{1,0:T(8,128)S(1)}) custom-call(f32[256,512]{1,0:T(8,128)S(1)} %get-tuple-element.35.m_ref, bf16[256,1152]{1,0:T(8,128)(2,1)S(1)} %get-tuple-element.36.own_turned_ref, bf16[1152,512]{1,0:T(8,128)(2,1)S(1)} %collective-permute-done.3.far_ref, f32[256,512]{1,0:T(8,128)S(1)} %get-tuple-element.40.helped_ref, ...), custom_call_target="tpu_custom_call" | custom-call | flops 400000000 | bytes 4000000 | tf_op jit(solution)/shard_map/pallas_call | solution.py:200
  57.2 1.6 %collective-permute-start.4 = (f32[128,128]{1,0:T(8,128)S(1)}, f32[128,128]{1,0:T(8,128)S(1)}, u32[]{:S(2)}, u32[]{:S(2)}) collective-permute-start(f32[128,128]{1,0:T(8,128)S(1)} %get-tuple-element.46), channel_id=1, source_target_pairs={{0,8},{4,12},{8,0},{12,4},{16,24},{20,28},{24,16},{28,20},{1,9},{5... | collective-permute-start | bytes 196616 | tf_op jit(solution)/shard_map/ppermute | solution.py:218
  58.7 1.5 %collective-permute-start.5 = (f32[128,128]{1,0:T(8,128)S(1)}, f32[128,128]{1,0:T(8,128)S(1)}, u32[]{:S(2)}, u32[]{:S(2)}) collective-permute-start(f32[128,128]{1,0:T(8,128)S(1)} %get-tuple-element.46), channel_id=1, source_target_pairs={{0,16},{4,20},{8,24},{12,28},{16,0},{20,4},{24,8},{28,12},{1,17},{... | collective-permute-start | bytes 196616 | tf_op jit(solution)/shard_map/ppermute | solution.py:218
  60.3 0.5 collective-permute-start.6
  60.7 6.7 %collective-permute-done.7.refs_1_ = s16[272,512]{1,0:T(8,128)(2,1)S(1)} collective-permute-done((s16[272,512]{1,0:T(8,128)(2,1)S(1)}, s16[272,512]{1,0:T(8,128)(2,1)S(1)}, u32[]{:S(2)}, u32[]{:S(2)}) %collective-permute-start.7) | collective-permute-done | bytes 278560 | tf_op jit(solution)/shard_map/ppermute | solution.py:261
  67.5 0.0 collective-permute-done.4
  67.5 0.0 collective-permute-done.5
  67.5 0.0 collective-permute-done.6
  67.5 0.1 collective-permute-start.8
  67.6 5.1 %collective-permute-start.10 = (f32[64,128]{1,0:T(8,128)S(1)}, f32[64,128]{1,0:T(8,128)S(1)}, u32[]{:S(2)}, u32[]{:S(2)}) collective-permute-start(f32[64,128]{1,0:T(8,128)S(1)} %get-tuple-element.53), channel_id=1, source_target_pairs={{0,5},{1,4},{2,7},{3,6},{4,1},{5,0},{6,3},{7,2},{8,13},{9,12},{10,... | collective-permute-start | bytes 98312 | tf_op jit(solution)/shard_map/ppermute | solution.py:319
  72.7 0.0 collective-permute-start.9
  72.7 0.0 collective-permute-done.8
  72.7 2.1 %shard_map.98 = f32[256,512]{1,0:T(8,128)} custom-call(f32[256,512]{1,0:T(8,128)S(1)} %get-tuple-element.54.refs_0_, s16[272,512]{1,0:T(8,128)(2,1)S(1)} %collective-permute-done.7.refs_1_, s16[16,512]{1,0:T(8,128)(2,1)S(1)} %slice.24.refs_2_, f32[8,512]{1,0:T(8,128)S(1)} %broadcast_in_dim.11.refs_3_, f32[8,512]{1,0:T(8,128)S(1)} %get-tuple-element.41.places_ref.refs_4_, ...), custom_call_target="tpu_custom_call" | custom-call | flops 400000000 | bytes 4000000 | tf_op jit(solution)/shard_map/pallas_call | solution.py:200
  74.8 0.0 collective-permute-done.10.refs_2_
  74.8 1.8 %collective-permute-done.9.refs_1_ = f32[64,128]{1,0:T(8,128)S(1)} collective-permute-done((f32[64,128]{1,0:T(8,128)S(1)}, f32[64,128]{1,0:T(8,128)S(1)}, u32[]{:S(2)}, u32[]{:S(2)}) %collective-permute-start.9) | collective-permute-done | bytes 32800 | tf_op jit(solution)/shard_map/ppermute | solution.py:319
  76.6 1.6 %shard_map.99 = bf16[256,512]{1,0:T(8,128)(2,1)} custom-call(f32[64,128]{1,0:T(8,128)S(1)} %add.56.refs_0_, f32[64,128]{1,0:T(8,128)S(1)} %collective-permute-done.9.refs_1_, f32[64,128]{1,0:T(8,128)S(1)} %collective-permute-done.10.refs_2_, f32[8,512]{1,0:T(8,128)S(1)} %broadcast_in_dim.11.refs_3_, f32[8,512]{1,0:T(8,128)S(1)} %get-tuple-element.41.places_ref.refs_4_, ...), custom_call_target="tpu_custom_call" | custom-call | flops 400000000 | bytes 4000000 | tf_op jit(solution)/shard_map/pallas_call | solution.py:200
  (9 shorter events, 0.1 us)
Async XLA Ops:
  0.6 6.2 %copy-start.5 = (bf16[8,512]{1,0:T(8,128)(2,1)S(1)}, bf16[8,512]{1,0:T(8,128)(2,1)}, u32[]{:S(2)}) copy-start(bf16[8,512]{1,0:T(8,128)(2,1)} %constant.51) | copy-start | bytes 24580
  0.6 6.4 %copy-start.3 = (bf16[1152,512]{1,0:T(8,128)(2,1)S(1)}, bf16[1152,512]{1,0:T(8,128)(2,1)}, u32[]{:S(2)}) copy-start(bf16[1152,512]{1,0:T(8,128)(2,1)} %param.9) | copy-start | bytes 3538948
  0.7 6.2 %copy-start.7 = (s32[4,8]{1,0:T(4,128)S(1)}, s32[4,8]{1,0:T(4,128)}, u32[]{:S(2)}) copy-start(s32[4,8]{1,0:T(4,128)} %param.11) | copy-start | bytes 388
  0.7 6.2 %copy-start.6 = (s32[4,8]{1,0:T(4,128)S(1)}, s32[4,8]{1,0:T(4,128)}, u32[]{:S(2)}) copy-start(s32[4,8]{1,0:T(4,128)} %param.12) | copy-start | bytes 388
  0.7 29.4 %collective-permute-start = (bf16[1152,512]{1,0:T(8,128)(2,1)}, bf16[1152,512]{1,0:T(8,128)(2,1)}, u32[]{:S(2)}, u32[]{:S(2)}) collective-permute-start(bf16[1152,512]{1,0:T(8,128)(2,1)} %param.9), channel_id=1, source_target_pairs={{0,1},{1,0},{2,3},{3,2},{4,5},{5,4},{6,7},{7,6},{8,9},{9,8},{10,11... | collective-permute-start | bytes 3538952 | tf_op jit(solution)/shard_map/ppermute | solution.py:261
  3.8 28.0 %collective-permute-start.1 = (bf16[1152,512]{1,0:T(8,128)(2,1)}, bf16[1152,512]{1,0:T(8,128)(2,1)S(1)}, u32[]{:S(2)}, u32[]{:S(2)}) collective-permute-start(bf16[1152,512]{1,0:T(8,128)(2,1)} %param.9), channel_id=1, source_target_pairs={{1,2},{2,1},{5,6},{6,5},{9,10},{10,9},{13,14},{14,13},{17,18},{18,... | collective-permute-start | bytes 3538952 | tf_op jit(solution)/shard_map/ppermute | solution.py:261
  4.5 2.5 %copy-start.4 = (f32[1,256,512]{2,1,0:T(8,128)S(1)}, f32[1,256,512]{2,1,0:T(8,128)}, u32[]{:S(2)}) copy-start(f32[1,256,512]{2,1,0:T(8,128)} %param.10) | copy-start | bytes 1572868
  30.0 23.7 %collective-permute-start.3 = (bf16[1152,512]{1,0:T(8,128)(2,1)}, bf16[1152,512]{1,0:T(8,128)(2,1)S(1)}, u32[]{:S(2)}, u32[]{:S(2)}) collective-permute-start(bf16[1152,512]{1,0:T(8,128)(2,1)} %collective-permute-done), channel_id=1, source_target_pairs={{1,2},{2,1},{5,6},{6,5},{9,10},{10,9},{13,14},{14,13},{17,18},{18,... | collective-permute-start | bytes 3538952 | tf_op jit(solution)/shard_map/ppermute | solution.py:261
  31.7 4.7 %copy-start.2 = (bf16[4608,256]{1,0:T(8,128)(2,1)S(1)}, bf16[4608,256]{1,0:T(8,128)(2,1)}, u32[]{:S(2)}) copy-start(bf16[4608,256]{1,0:T(8,128)(2,1)} %param.8) | copy-start | bytes 7077892
  33.1 20.0 %collective-permute-start.2 = (bf16[784,512]{1,0:T(8,128)(2,1)S(1)}, bf16[784,512]{1,0:T(8,128)(2,1)S(1)}, u32[]{:S(2)}, u32[]{:S(2)}) collective-permute-start(bf16[784,512]{1,0:T(8,128)(2,1)S(1)} %slice_select_fusion), channel_id=1, source_target_pairs={{0,1},{1,0},{2,3},{3,2},{4,5},{5,4},{6,7},{7,6},{8,9},{9,8},{10,11... | collective-permute-start | bytes 2408456 | tf_op jit(solution)/shard_map/ppermute | solution.py:261
  53.7 1.9 %copy-start = (f32[256,256]{1,0:T(8,128)S(1)}, f32[256,256]{1,0:T(8,128)}, u32[]{:S(2)}) copy-start(f32[256,256]{1,0:T(8,128)} %constant.32.clone.refs_1_.refs_5_.refs_6_) | copy-start | bytes 786436
  53.7 1.9 %copy-start.1 = (bf16[512,128]{1,0:T(8,128)(2,1)S(1)}, bf16[512,128]{1,0:T(8,128)(2,1)}, u32[]{:S(2)}) copy-start(bf16[512,128]{1,0:T(8,128)(2,1)} %constant.31.clone.refs_0_.refs_5_) | copy-start | bytes 393220
  54.3 13.1 %collective-permute-start.7 = (s16[272,512]{1,0:T(8,128)(2,1)S(1)}, s16[272,512]{1,0:T(8,128)(2,1)S(1)}, u32[]{:S(2)}, u32[]{:S(2)}) collective-permute-start(s16[272,512]{1,0:T(8,128)(2,1)S(1)} %get-tuple-element.47), channel_id=1, source_target_pairs={{1,0},{2,3},{5,4},{6,7},{9,8},{10,11},{13,12},{14,15},{17,16},{18,... | collective-permute-start | bytes 835592 | tf_op jit(solution)/shard_map/ppermute | solution.py:261
  57.2 10.3 %collective-permute-start.4 = (f32[128,128]{1,0:T(8,128)S(1)}, f32[128,128]{1,0:T(8,128)S(1)}, u32[]{:S(2)}, u32[]{:S(2)}) collective-permute-start(f32[128,128]{1,0:T(8,128)S(1)} %get-tuple-element.46), channel_id=1, source_target_pairs={{0,8},{4,12},{8,0},{12,4},{16,24},{20,28},{24,16},{28,20},{1,9},{5... | collective-permute-start | bytes 196616 | tf_op jit(solution)/shard_map/ppermute | solution.py:218
  58.7 8.7 %collective-permute-start.5 = (f32[128,128]{1,0:T(8,128)S(1)}, f32[128,128]{1,0:T(8,128)S(1)}, u32[]{:S(2)}, u32[]{:S(2)}) collective-permute-start(f32[128,128]{1,0:T(8,128)S(1)} %get-tuple-element.46), channel_id=1, source_target_pairs={{0,16},{4,20},{8,24},{12,28},{16,0},{20,4},{24,8},{28,12},{1,17},{... | collective-permute-start | bytes 196616 | tf_op jit(solution)/shard_map/ppermute | solution.py:218
  60.3 7.2 %collective-permute-start.6 = (f32[128,128]{1,0:T(8,128)S(1)}, f32[128,128]{1,0:T(8,128)S(1)}, u32[]{:S(2)}, u32[]{:S(2)}) collective-permute-start(f32[128,128]{1,0:T(8,128)S(1)} %get-tuple-element.46), channel_id=1, source_target_pairs={{0,24},{4,28},{8,16},{12,20},{16,8},{20,12},{24,0},{28,4},{1,25},{... | collective-permute-start | bytes 196616 | tf_op jit(solution)/shard_map/ppermute | solution.py:218
  67.5 5.2 %collective-permute-start.8 = (f32[64,128]{1,0:T(8,128)S(1)}, f32[64,128]{1,0:T(8,128)S(1)}, u32[]{:S(2)}, u32[]{:S(2)}) collective-permute-start(f32[64,128]{1,0:T(8,128)S(1)} %get-tuple-element.51), channel_id=1, source_target_pairs={{0,4},{4,0},{8,12},{12,8},{16,20},{20,16},{24,28},{28,24},{1,5},{5... | collective-permute-start | bytes 98312 | tf_op jit(solution)/shard_map/ppermute | solution.py:218
  67.6 7.2 %collective-permute-start.10 = (f32[64,128]{1,0:T(8,128)S(1)}, f32[64,128]{1,0:T(8,128)S(1)}, u32[]{:S(2)}, u32[]{:S(2)}) collective-permute-start(f32[64,128]{1,0:T(8,128)S(1)} %get-tuple-element.53), channel_id=1, source_target_pairs={{0,5},{1,4},{2,7},{3,6},{4,1},{5,0},{6,3},{7,2},{8,13},{9,12},{10,... | collective-permute-start | bytes 98312 | tf_op jit(solution)/shard_map/ppermute | solution.py:319
  72.7 3.9 %collective-permute-start.9 = (f32[64,128]{1,0:T(8,128)S(1)}, f32[64,128]{1,0:T(8,128)S(1)}, u32[]{:S(2)}, u32[]{:S(2)}) collective-permute-start(f32[64,128]{1,0:T(8,128)S(1)} %get-tuple-element.53), channel_id=1, source_target_pairs={{0,1},{1,0},{2,3},{3,2},{4,5},{5,4},{6,7},{7,6},{8,9},{9,8},{10,11... | collective-permute-start | bytes 98312 | tf_op jit(solution)/shard_map/ppermute | solution.py:319

commit v10 on v8

--- a/solution.py
+++ b/solution.py
@@ -1,5 +1,3 @@
-import functools
-
 import jax
 import jax.numpy as jnp
 import numpy as np
@@ -23,8 +21,8 @@
     return norm_scale * np.cos(np.pi * (sample_pos + 0.5) * frequency / order)
 
 
-def diagonal_blocks(width):
-    count = next(c for c in (4, 2, 1) if width % (c * order) == 0)
+def diagonal_blocks(*widths):
+    count = next(c for c in (4, 2, 1) if all(width % (c * order) == 0 for width in widths))
     return np.kron(np.eye(count), basis_matrix()).astype(np.float32)
 
 
@@ -89,9 +87,9 @@
     return jnp.concatenate(pieces, axis=0)
 
 
-def selected(x, masks, *basis_refs):
-    taken = rows_taken(on_rows(basis_refs[0], x, False), masks)
-    return within(on_columns(basis_refs[-1], taken, False), masks)
+def selected(x, masks, basis_ref):
+    taken = rows_taken(on_rows(basis_ref, x, False), masks)
+    return within(on_columns(basis_ref, taken, False), masks)
 
 
 def within(x, masks):
@@ -100,17 +98,17 @@
     )
 
 
-def restored(x, masks, *basis_refs):
-    by_columns = on_columns(basis_refs[-1], x, True)
+def restored(x, masks, basis_ref):
+    by_columns = on_columns(basis_ref, x, True)
     pieces = []
     for row, (at, _) in enumerate(masks):
         part = by_columns[row * band : (row + 1) * band]
         pieces += [jnp.where(at == step * band, part, 0.0) for step in range(steps)]
-    return on_rows(basis_refs[0], jnp.concatenate(pieces, axis=0), True)
-
-
-def bands_of(x, places, fold_ref, *basis_refs):
-    return folded(selected(x, masks_of(places, x.shape[0] // order), *basis_refs), fold_ref[...])
+    return on_rows(basis_ref, jnp.concatenate(pieces, axis=0), True)
+
+
+def bands_of(x, places, fold_ref, basis_ref):
+    return folded(selected(x, masks_of(places, x.shape[0] // order), basis_ref), fold_ref[...])
 
 
 def folded(x, fold):
@@ -154,52 +152,43 @@
     bands_ref[...] = bands_of(out_ref[...], places_ref[...], *matrix_refs)
 
 
-def helped_kernel(helped_ref, end_turned_ref, far_ref, out_ref, code_ref):
-    out_ref[...] = helped_ref[...] + dot(end_turned_ref[...], far_ref[...])
-    side = out_ref.shape[0]
-    code_ref[:side], code_ref[side:] = coded(out_ref[...])
-
-
-def last_rows_kernel(end_ref, m_ref, own_bands_ref, own_turned_ref, far_ref, helped_ref, *refs):
-    places_ref, end_places_ref, fold_ref, *basis_refs, out_ref, bands_ref = refs
-    rows, width = out_ref.shape
-    count = own_bands_ref.shape[0]
+def helped_kernel(helped_ref, turned_ref, far_ref, places_ref, *refs):
+    *matrix_refs, code_ref, bands_ref = refs
+    product = helped_ref[...] + dot(turned_ref[...], far_ref[...])
+    bands_ref[...] = bands_of(product, places_ref[...], *matrix_refs)
+    side = product.shape[0]
+    code_ref[:side], code_ref[side:] = coded(product)
+
+
+def last_rows_kernel(end_ref, m_ref, own_bands_ref, turned_ref, far_ref, places_ref, *refs):
+    *matrix_refs, out_ref, bands_ref = refs
 
     @pl.when(end_ref[0] == 1)
     def _():
         out_ref[...] = m_ref[...]
-        bands_ref[:count] = own_bands_ref[...]
-        bands_ref[count:] = jnp.zeros_like(own_bands_ref)
+        bands_ref[...] = own_bands_ref[...]
 
     @pl.when(end_ref[0] == 0)
     def _():
-        out_ref[...] = m_ref[...] + dot(own_turned_ref[...], far_ref[...])
-        both = jnp.concatenate([out_ref[...], helped_ref[...]], axis=1)
-        by_rows = on_rows(basis_refs[0], both, False)
-        masks = [masks_of(places[...], rows // order) for places in (places_ref, end_places_ref)]
-        taken = [rows_taken(by_rows[:, i * width :][:, :width], masks[i]) for i in range(2)]
-        coefficients = on_columns(basis_refs[-1], jnp.concatenate(taken, axis=0), False)
-        bands_ref[...] = folded(within(coefficients, masks[0] + masks[1]), fold_ref[...])
-
-
-def remove_kernel(count, *refs):
-    (m_ref, *code_refs), (end_ref, places_ref, *basis_refs, out_ref) = refs[:count], refs[count:]
+        out_ref[...] = m_ref[...] + dot(turned_ref[...], far_ref[...])
+        bands_ref[...] = bands_of(out_ref[...], places_ref[...], *matrix_refs)
+
+
+def remove_kernel(m_ref, *refs):
+    *code_refs, places_ref, basis_ref, out_ref = refs
     m = m_ref[...]
     if code_refs:
-        m = m + jnp.where(end_ref[:1, :] > 0, decoded(*code_refs), 0.0)
+        m = m + decoded(*code_refs)
     masks = masks_of(places_ref[...], m.shape[0] // order)
-    out_ref[...] = m - restored(selected(m, masks, *basis_refs), masks, *basis_refs)
-
-
-def update_kernel(own_count, count, *refs):
-    part_refs, (end_ref, places_ref, fold_ref, *basis_refs, out_ref) = refs[:count], refs[count:]
-    parts = [ref[...] for ref in part_refs]
-    bands = pair_sum(parts[:own_count])
-    if own_count < count:
-        bands = bands + jnp.where(end_ref[:1, : bands.shape[1]] > 0, pair_sum(parts[own_count:]), 0.0)
+    out_ref[...] = m - restored(selected(m, masks, basis_ref), masks, basis_ref)
+
+
+def update_kernel(*refs):
+    *part_refs, places_ref, fold_ref, basis_ref, out_ref = refs
+    bands = pair_sum([ref[...] for ref in part_refs])
     masks = masks_of(places_ref[...], out_ref.shape[0] // order)
     coefficients = within(spread(bands, fold_ref[...]), masks)
-    out_ref[...] = restored(coefficients, masks, *basis_refs).astype(out_ref.dtype)
+    out_ref[...] = restored(coefficients, masks, basis_ref).astype(out_ref.dtype)
 
 
 def pair_sum(parts):
@@ -214,32 +203,25 @@
         kernel,
         out_shape=out_shapes,
         in_specs=[pl.BlockSpec(memory_space=space) for space in spaces],
-        compiler_params=pltpu.CompilerParams(vmem_limit_bytes=32 * 2**20),
+        compiler_params=pltpu.CompilerParams(vmem_limit_bytes=16 * 2**20),
         cost_estimate=pl.CostEstimate(flops=4 * 10**8, bytes_accessed=4 * 10**6, transcendentals=0),
     )(*operands)
 
 
-def stages_of(axis):
-    size, stride, stages = lax.axis_size(axis), 1, []
-    while stride < size:
-        stages.append((stride, min(4, size // stride)))
-        stride *= stages[-1][1]
-    return stages
-
-
-def exchanged(x, axis, stride, count):
-    size = lax.axis_size(axis)
-    return [lax.ppermute(x, axis, [(i, i ^ (stride * k)) for i in range(size)]) for k in range(1, count)]
-
-
-def summed_but_last(x, axis, form, then=lambda x: x):
+def spread_sum(x, axis, behind=lambda x: x):
     size = lax.axis_size(axis)
     if size & (size - 1):
-        return form(lax.psum(x, axis)), (1, 1)
-    *stages, last = stages_of(axis) or [(1, 1)]
-    for stride, count in stages:
-        x = pair_sum([x] + then(exchanged(x, axis, stride, count)))
-    return form(x), last
+        return [lax.psum(x, axis)]
+    stride, parts = 1, [x]
+    while stride < size:
+        count = min(4, size // stride)
+        x = pair_sum(parts)
+        received = [
+            lax.ppermute(x, axis, [(i, i ^ (stride * k)) for i in range(size)]) for k in range(1, count)
+        ]
+        parts = [x] + (behind(received) if stride == 1 else received)
+        stride *= count
+    return parts
 
 
 def product(hidden_rows, grad_rows):
@@ -253,9 +235,8 @@
 def gathered(hidden, out_grad, carried, places, matrices):
     m = carried + product(hidden, lax.all_gather(out_grad, "tp", axis=0, tiled=True))
     folded = jax.ShapeDtypeStruct((m.shape[0] // steps, m.shape[1] // steps), jnp.float32)
-    bands, last = summed_but_last(call(bands_kernel, folded, m, places, *matrices), "rep", lambda x: x)
-    parts = [bands] + exchanged(bands, "rep", *last)
-    return [m], parts, len(parts), jnp.zeros((8, m.shape[1]), jnp.float32), places, matrices
+    bands = call(bands_kernel, folded, m, places, *matrices)
+    return [m], spread_sum(bands, "rep"), places, matrices
 
 
 def lined(hidden, out_grad, carried, places, matrices):
@@ -276,6 +257,7 @@
 
     both_ways = [(0, 1), (1, 0), (2, 3), (3, 2)]
     across = [(1, 2), (2, 1)]
+    outward = [(1, 0), (2, 3)]
 
     pair_grad = send(out_grad, both_ways)
     cross_grad = send(out_grad, across)
@@ -302,10 +284,10 @@
     full = jax.ShapeDtypeStruct(m.shape, jnp.float32)
     turned = jax.ShapeDtypeStruct((m.shape[0], tok), hidden.dtype)
     table = jax.ShapeDtypeStruct((place_rows, m.shape[1]), jnp.float32)
-    own_bands = jax.ShapeDtypeStruct((height, width), jnp.float32)
+    folded = jax.ShapeDtypeStruct((height, width), jnp.float32)
     m, helped, own_turned, end_turned, end_places, own_bands = call(
         swapped_kernel,
-        (full, full, turned, turned, table, own_bands),
+        (full, full, turned, turned, table, folded),
         m,
         far_hidden,
         cross_hidden,
@@ -316,21 +298,18 @@
     )
     far_grad = after(far_grad, m)
     code_shape = jax.ShapeDtypeStruct((m.shape[0] + code_rows, m.shape[1]), jnp.int16)
-    helped, code = call(helped_kernel, (full, code_shape), helped, end_turned, far_grad)
-    code = send(code, both_ways)
+    code, end_bands = call(
+        helped_kernel, (code_shape, folded), helped, end_turned, far_grad, end_places, *matrices
+    )
+    m, end_bands, code = lax.optimization_barrier((m, end_bands, code))
+    end_bands = send(end_bands, both_ways)
+    code = send(code, outward)
+    flag = end.astype(jnp.int32).reshape(1)
     m, bands = call(
-        last_rows_kernel,
-        (full, jax.ShapeDtypeStruct((2 * height, width), jnp.float32)),
-        end.astype(jnp.int32).reshape(1),
-        m,
-        own_bands,
-        own_turned,
-        far_grad,
-        helped,
-        places,
-        end_places,
-        *matrices,
-    )
+        last_rows_kernel, (full, folded), flag, m, own_bands, own_turned, far_grad, places, *matrices
+    )
+    end_bands, bands = lax.optimization_barrier((end_bands, bands))
+    bands = bands + jnp.where(end, end_bands, 0.0)
     exponents = code[m.shape[0] :]
 
     def behind_code(x):
@@ -338,54 +317,28 @@
         x, exponents = lax.optimization_barrier((x, exponents))
         return x
 
-    (bands, end_bands), (stride, count) = summed_but_last(
-        bands, "rep", lambda x: lax.optimization_barrier((x[:height], x[height:])), behind_code
-    )
-    own_sum = pair_sum([bands] + exchanged(bands, "rep", stride, count))
-    to_ends = []
-    for k in range(count):
-        perm = [
-            (i * 4 + a, (i ^ (stride * k)) * 4 + b) for i in range(lax.axis_size("rep")) for a, b in both_ways
-        ]
-        to_ends.append(lax.ppermute(end_bands, ("rep", "tp"), perm))
-    m, own_sum = lax.optimization_barrier((m, own_sum))
-    end_flag = jnp.full((8, m.shape[1]), end, jnp.float32)
-    return [m, code, exponents], [own_sum] + to_ends, 1, end_flag, places, matrices
+    parts = spread_sum(bands, "rep", behind_code)
+    return [m, code, exponents], parts, places, matrices
 
 
 def local(hidden, out_grad, momentum, band_rows, band_start_columns):
     row_count = hidden.shape[1]
     col_count = out_grad.shape[1]
     one_hot = jnp.asarray(np.kron(np.eye(col_count // order), np.ones((1, order))), jnp.float32)
-    bases = [diagonal_blocks(row_count), diagonal_blocks(col_count)]
-    if bases[0].shape == bases[1].shape:
-        bases = bases[:1]
-    matrices = tuple(jnp.asarray(x) for x in (fold_matrix(col_count), *bases))
+    matrices = (jnp.asarray(fold_matrix(col_count)), jnp.asarray(diagonal_blocks(row_count, col_count)))
     places = jnp.concatenate([band_rows, band_start_columns], axis=0).astype(jnp.float32)
     places = dot(places, one_hot)
     fits = out_grad.shape[0] % 384 == 0 and 2 * row_count == col_count and places.shape[0] <= place_rows
     form = lined if fits and lax.axis_size("tp") == 4 else gathered
-    m_parts, band_parts, own_count, end_flag, places, matrices = form(
+    m_parts, band_parts, places, matrices = form(
         hidden, out_grad, decay_rate * momentum[0], places, matrices
     )
     shape = (row_count, col_count)
     momentum_out = call(
-        functools.partial(remove_kernel, len(m_parts)),
-        jax.ShapeDtypeStruct(shape, jnp.float32),
-        *m_parts,
-        end_flag,
-        places,
-        *matrices[1:],
+        remove_kernel, jax.ShapeDtypeStruct(shape, jnp.float32), *m_parts, places, matrices[1]
     )
     *band_parts, momentum_out = lax.optimization_barrier((*band_parts, momentum_out))
-    update = call(
-        functools.partial(update_kernel, own_count, len(band_parts)),
-        jax.ShapeDtypeStruct(shape, jnp.bfloat16),
-        *band_parts,
-        end_flag,
-        places,
-        *matrices,
-    )
+    update = call(update_kernel, jax.ShapeDtypeStruct(shape, jnp.bfloat16), *band_parts, places, *matrices)
     return (momentum_out[None], update)
 
 

time: 79.4 us -> 76.4 us (0.962)
  local copies, waits for them, and re-layouts: 3.81 us -> 1.19 us
  waiting for transfers between devices: 40 us -> 41.3 us
    ppermute x5 -> x6, waiting for transfers between devices: 35.4 us -> 40.9 us  [send(): return lax.ppermute(x, 'tp', perm)]
    ppermute x6 -> x4, waiting for transfers between devices: 4.55 us -> 0.37 us  [spread_sum(): lax.ppermute(x, axis, [(i, i ^ stride * k) for i in range(size)])]
    unnamed x32 -> x16, local copies, waits for them, and re-layouts: 2.65 us -> 0.04 us
    ppermute x6 -> x4, starting transfers between devices: 5.49 us -> 3.44 us  [spread_sum(): lax.ppermute(x, axis, [(i, i ^ stride * k) for i in range(size)])]
    ppermute x5 -> x6, starting transfers between devices: 14.2 us -> 15.5 us  [send(): return lax.ppermute(x, 'tp', perm)]
    dot_general x4, matrix products: 4.89 us -> 4.1 us  [dot(): lax.dot_general(a, b, (dims, ((), ())), preferred_element_type=jnp.float32)]
  transfers between devices with their start and end apart: 11 -> 10, of which waited for: 8 -> 5; matrix products, arithmetic and copies ran while one was open for 12% -> 12% of each run, Pallas kernels for 4% -> 4%
where the time goes in v10:
time: 76.4 us; the launch traced here: 76.1 us
  waiting for transfers between devices  41.3 us (54%)
  starting transfers between devices  19 us (25%)
  Pallas kernels  6.11 us (8%)
  matrix products  4.1 us (5%)
  other arithmetic  3.56 us (5%)
  local copies, waits for them, and re-layouts  1.19 us (2%)
  between operations  0.86 us (1%)
    ppermute x6, waiting for transfers between devices, send(): return lax.ppermute(x, 'tp', perm)  40.9 us
    ppermute x6, starting transfers between devices, send(): return lax.ppermute(x, 'tp', perm)  15.5 us
    pallas_call x5, Pallas kernels, call(): pl.pallas_call(kernel, out_shape=out_shapes, in_specs=[pl.BlockSpec(memor...  6.11 us
    dot_general x4, matrix products, dot(): lax.dot_general(a, b, (dims, ((), ())), preferred_element_type=jnp.float32)  4.1 us
    ppermute x4, starting transfers between devices, spread_sum(): lax.ppermute(x, axis, [(i, i ^ stride * k) for i in range(size)])  3.44 us
  transfers between devices with their start and end apart: 10, of which 5 were waited for; matrix products, arithmetic and copies ran while one was open for 12% of the time, Pallas kernels for 4%

profile of v10, /device:TPU:0, one launch (start us, length us, event | category | flops | bytes accessed | tf_op | source)
XLA Modules:
  0.0 76.1 jit_solution(12194068376078959074)
XLA Ops:
  0.6 0.0 copy-start.5
  0.6 0.0 copy-start.3
  0.7 0.0 copy-start.7
  0.7 0.0 copy-start.6
  0.7 3.1 %collective-permute-start = (bf16[1152,512]{1,0:T(8,128)(2,1)}, bf16[1152,512]{1,0:T(8,128)(2,1)}, u32[]{:S(2)}, u32[]{:S(2)}) collective-permute-start(bf16[1152,512]{1,0:T(8,128)(2,1)} %param.9), channel_id=1, source_target_pairs={{0,1},{1,0},{2,3},{3,2},{4,5},{5,4},{6,7},{7,6},{8,9},{9,8},{10,11... | collective-permute-start | bytes 3538952 | tf_op jit(solution)/shard_map/ppermute | solution.py:256
  3.8 0.7 collective-permute-start.1
  4.5 0.0 copy-start.4
  4.5 1.1 %constant_dynamic-slice_fusion.3 = (bf16[384,256]{1,0:T(8,128)(2,1)S(1)}, bf16[384,256]{1,0:T(8,128)(2,1)S(1)}) fusion(bf16[4608,256]{1,0:T(8,128)(2,1)} %param.8, s32[]{:T(128)S(6)} %select_n.48, s32[]{:T(128)S(6)} %select_n.50), kind=kLoop, calls=%fused_computation.25 | loop fusion | bytes 786440 | tf_op jit(solution)/shard_map/dynamic_slice | solution.py:253
  5.6 1.2 %dynamic-slice_select_fusion = (bf16[768,256]{1,0:T(8,128)(2,1)S(1)}, bf16[768,256]{1,0:T(8,128)(2,1)S(1)}) fusion(bf16[4608,256]{1,0:T(8,128)(2,1)} %param.8, s32[]{:T(128)S(6)} %select_n.52, pred[]{:T(512)S(6)} %or.3, s32[]{:T(128)S(6)} %add.58), kind=kLoop, calls=%fused_computation.11 | loop fusion | flops 196608 | bytes 1572873 | tf_op jit(solution)/shard_map/jit(_where)/select_n | solution.py:275
  6.8 0.0 copy-done.5
  6.9 0.0 copy-done.7
  6.9 0.0 copy-done.6
  6.9 0.1 fusion.14
  7.0 0.0 copy-done.3
  7.0 0.0 copy-done.4
  7.0 1.6 %convolution_add_fusion.1 = f32[256,512]{1,0:T(8,128)S(1)} fusion(bf16[1152,512]{1,0:T(8,128)(2,1)S(1)} %copy-done.3, bf16[4608,256]{1,0:T(8,128)(2,1)} %param.8, s32[]{:T(128)S(6)} %select_n.54, f32[1,256,512]{2,1,0:T(8,128)S(1)} %copy-done.4), kind=kOutput, calls=%fused_computation.4 | convolution fusion | flops 302252032 | bytes 2818052 | tf_op jit(solution)/shard_map/dot_general | solution.py:45
  8.6 21.4 %collective-permute-done = bf16[1152,512]{1,0:T(8,128)(2,1)} collective-permute-done((bf16[1152,512]{1,0:T(8,128)(2,1)}, bf16[1152,512]{1,0:T(8,128)(2,1)}, u32[]{:S(2)}, u32[]{:S(2)}) %collective-permute-start) | collective-permute-done | bytes 1179680 | tf_op jit(solution)/shard_map/ppermute | solution.py:256
  30.0 0.7 collective-permute-start.3
  30.8 1.0 %fusion.2 = bf16[784,512]{1,0:T(8,128)(2,1)} fusion(bf16[8,512]{1,0:T(8,128)(2,1)S(1)} %get-tuple-element.66, bf16[768,256]{1,0:T(8,128)(2,1)S(1)} %get-tuple-element.63, bf16[384,256]{1,0:T(8,128)(2,1)S(1)} %get-tuple-element.65, bf16[384,256]{1,0:T(8,128)(2,1)S(1)} %get-tuple-element.64), kind=kLoop, calls=%fused_computation.5 | loop fusion | flops 4014080 | bytes 1597440 | tf_op jit(solution)/shard_map/concatenate | solution.py:274
  31.8 0.0 collective-permute-done.1.cross_ref
  31.8 1.4 %slice_select_fusion = bf16[784,512]{1,0:T(8,128)(2,1)S(1)} fusion(bf16[784,512]{1,0:T(8,128)(2,1)} %fusion.2, bf16[1152,512]{1,0:T(8,128)(2,1)S(1)} %collective-permute-done.1.cross_ref, pred[]{:T(512)S(6)} %or.3), kind=kLoop, calls=%fused_computation.6 | loop fusion | flops 401408 | bytes 2408449 | tf_op jit(solution)/shard_map/jit(_where)/select_n | solution.py:280
  33.1 3.3 %collective-permute-start.2 = (bf16[784,512]{1,0:T(8,128)(2,1)S(1)}, bf16[784,512]{1,0:T(8,128)(2,1)S(1)}, u32[]{:S(2)}, u32[]{:S(2)}) collective-permute-start(bf16[784,512]{1,0:T(8,128)(2,1)S(1)} %slice_select_fusion), channel_id=1, source_target_pairs={{0,1},{1,0},{2,3},{3,2},{4,5},{5,4},{6,7},{7,6},{8,9},{9,8},{10,11... | collective-permute-start | bytes 2408456 | tf_op jit(solution)/shard_map/ppermute | solution.py:256
  36.4 0.0 copy-done.2
  36.4 0.5 fusion.3
  37.0 0.0 copy-start
  37.0 0.0 copy-start.1
  37.0 1.8 %fusion.1.m_ref = f32[256,512]{1,0:T(8,128)S(1)} fusion(f32[256,512]{1,0:T(8,128)S(1)} %fusion.3, f32[256,512]{1,0:T(8,128)S(1)} %convolution_add_fusion.1, bf16[1152,512]{1,0:T(8,128)(2,1)} %collective-permute-done, bf16[4608,256]{1,0:T(8,128)(2,1)S(1)} %copy-done.2, s32[]{:T(128)S(6)} %select_n.55), kind=kOutput, calls=%fused_computation.3 | convolution fusion | flops 302252032 | bytes 3342340 | tf_op jit(solution)/shard_map/dot_general | solution.py:45
  38.9 14.3 %collective-permute-done.2.swapped_ref = bf16[784,512]{1,0:T(8,128)(2,1)S(1)} collective-permute-done((bf16[784,512]{1,0:T(8,128)(2,1)S(1)}, bf16[784,512]{1,0:T(8,128)(2,1)S(1)}, u32[]{:S(2)}, u32[]{:S(2)}) %collective-permute-start.2) | collective-permute-done | bytes 802848 | tf_op jit(solution)/shard_map/ppermute | solution.py:256
  53.1 0.0 copy-done
  53.1 0.0 copy-done.1
  53.1 1.2 %shard_map.95 = (f32[256,512]{1,0:T(8,128)S(1)}, f32[256,512]{1,0:T(8,128)S(1)}, bf16[256,1152]{1,0:T(8,128)(2,1)S(1)}, bf16[256,1152]{1,0:T(8,128)(2,1)S(1)}, f...) custom-call(f32[256,512]{1,0:T(8,128)S(1)} %fusion.1.m_ref, ...), custom_call_target="tpu_custom_call" | custom-call | flops 400000000 | bytes 4000000 | tf_op jit(solution)/shard_map/pallas_call | solution.py:202
  54.3 0.0 collective-permute-done.3.far_ref
  54.3 1.3 %shard_map.96 = (s16[272,512]{1,0:T(8,128)(2,1)S(1)}, f32[64,128]{1,0:T(8,128)S(1)}) custom-call(f32[256,512]{1,0:T(8,128)S(1)} %get-tuple-element.40.helped_ref, bf16[256,1152]{1,0:T(8,128)(2,1)S(1)} %get-tuple-element.41.turned_ref, bf16[1152,512]{1,0:T(8,128)(2,1)S(1)} %collective-permute-done.3.far_ref, f32[16,512]{1,0:T(8,128)S(1)} %get-tuple-element.43.places_ref, ...), custom_call_target="tpu_custom_call" | custom-call | flops 400000000 | bytes 4000000 | tf_op jit(solution)/shard_map/pallas_call | solution.py:202
  55.6 6.5 %collective-permute-start.4 = (f32[64,128]{1,0:T(8,128)S(1)}, f32[64,128]{1,0:T(8,128)S(1)}, u32[]{:S(2)}, u32[]{:S(2)}) collective-permute-start(f32[64,128]{1,0:T(8,128)S(1)} %get-tuple-element.46), channel_id=1, source_target_pairs={{0,1},{1,0},{2,3},{3,2},{4,5},{5,4},{6,7},{7,6},{8,9},{9,8},{10,11... | collective-permute-start | bytes 98312 | tf_op jit(solution)/shard_map/ppermute | solution.py:256
  62.1 1.3 %collective-permute-start.8 = (s16[272,512]{1,0:T(8,128)(2,1)S(1)}, s16[272,512]{1,0:T(8,128)(2,1)S(1)}, u32[]{:S(2)}, u32[]{:S(2)}) collective-permute-start(s16[272,512]{1,0:T(8,128)(2,1)S(1)} %get-tuple-element.53), channel_id=1, source_target_pairs={{1,0},{2,3},{5,4},{6,7},{9,8},{10,11},{13,12},{14,15},{17,16},{18,... | collective-permute-start | bytes 835592 | tf_op jit(solution)/shard_map/ppermute | solution.py:256
  63.4 0.1 shard_map.97
  63.4 0.5 collective-permute-done.4
  64.0 0.0 collective-permute-start.5
  64.0 1.6 %collective-permute-start.6 = (f32[64,128]{1,0:T(8,128)S(1)}, f32[64,128]{1,0:T(8,128)S(1)}, u32[]{:S(2)}, u32[]{:S(2)}) collective-permute-start(f32[64,128]{1,0:T(8,128)S(1)} %select_add_fusion), channel_id=1, source_target_pairs={{0,8},{4,12},{8,0},{12,4},{16,24},{20,28},{24,16},{28,20},{1,9},{5... | collective-permute-start | bytes 98312 | tf_op jit(solution)/shard_map/ppermute | solution.py:220
  65.6 0.3 collective-permute-start.7
  65.9 4.7 %collective-permute-done.8.refs_0_ = s16[272,512]{1,0:T(8,128)(2,1)S(1)} collective-permute-done((s16[272,512]{1,0:T(8,128)(2,1)S(1)}, s16[272,512]{1,0:T(8,128)(2,1)S(1)}, u32[]{:S(2)}, u32[]{:S(2)}) %collective-permute-start.8) | collective-permute-done | bytes 278560 | tf_op jit(solution)/shard_map/ppermute | solution.py:256
  70.5 0.0 collective-permute-done.5
  70.5 0.0 collective-permute-done.6
  70.5 0.0 collective-permute-done.7
  70.6 1.6 %collective-permute-start.9 = (f32[64,128]{1,0:T(8,128)S(1)}, f32[64,128]{1,0:T(8,128)S(1)}, u32[]{:S(2)}, u32[]{:S(2)}) collective-permute-start(f32[64,128]{1,0:T(8,128)S(1)} %add_add_fusion.refs_0_), channel_id=1, source_target_pairs={{0,16},{4,20},{8,24},{12,28},{16,0},{20,4},{24,8},{28,12},{1,17},{... | collective-permute-start | bytes 98312 | tf_op jit(solution)/shard_map/ppermute | solution.py:220
  72.1 2.0 %shard_map.98 = f32[256,512]{1,0:T(8,128)} custom-call(f32[256,512]{1,0:T(8,128)S(1)} %get-tuple-element.57.m_ref, s16[272,512]{1,0:T(8,128)(2,1)S(1)} %collective-permute-done.8.refs_0_, s16[16,512]{1,0:T(8,128)(2,1)S(1)} %slice.16.refs_1_, f32[8,512]{1,0:T(8,128)S(1)} %get-tuple-element.36.places_ref.refs_2_, f32[256,256]{1,0:T(8,128)S(1)} %copy-done), custom_call_target="tpu_custom_call" | custom-call | flops 400000000 | bytes 4000000 | tf_op jit(solution)/shard_map/pallas_call | solution.py:202
  74.2 0.4 collective-permute-done.9.refs_1_
  74.5 1.6 %shard_map.99 = bf16[256,512]{1,0:T(8,128)(2,1)} custom-call(f32[64,128]{1,0:T(8,128)S(1)} %add_add_fusion.refs_0_, f32[64,128]{1,0:T(8,128)S(1)} %collective-permute-done.9.refs_1_, f32[8,512]{1,0:T(8,128)S(1)} %get-tuple-element.36.places_ref.refs_2_, bf16[512,128]{1,0:T(8,128)(2,1)S(1)} %copy-done.1, f32[256,256]{1,0:T(8,128)S(1)} %copy-done), custom_call_target="tpu_custom_call" | custom-call | flops 400000000 | bytes 4000000 | tf_op jit(solution)/shard_map/pallas_call | solution.py:202
  (5 shorter events, 0.1 us)
Async XLA Ops:
  0.6 6.2 %copy-start.5 = (bf16[8,512]{1,0:T(8,128)(2,1)S(1)}, bf16[8,512]{1,0:T(8,128)(2,1)}, u32[]{:S(2)}) copy-start(bf16[8,512]{1,0:T(8,128)(2,1)} %constant.53) | copy-start | bytes 24580
  0.6 6.4 %copy-start.3 = (bf16[1152,512]{1,0:T(8,128)(2,1)S(1)}, bf16[1152,512]{1,0:T(8,128)(2,1)}, u32[]{:S(2)}) copy-start(bf16[1152,512]{1,0:T(8,128)(2,1)} %param.9) | copy-start | bytes 3538948
  0.7 6.2 %copy-start.7 = (s32[4,8]{1,0:T(4,128)S(1)}, s32[4,8]{1,0:T(4,128)}, u32[]{:S(2)}) copy-start(s32[4,8]{1,0:T(4,128)} %param.11) | copy-start | bytes 388
  0.7 6.2 %copy-start.6 = (s32[4,8]{1,0:T(4,128)S(1)}, s32[4,8]{1,0:T(4,128)}, u32[]{:S(2)}) copy-start(s32[4,8]{1,0:T(4,128)} %param.12) | copy-start | bytes 388
  0.7 29.4 %collective-permute-start = (bf16[1152,512]{1,0:T(8,128)(2,1)}, bf16[1152,512]{1,0:T(8,128)(2,1)}, u32[]{:S(2)}, u32[]{:S(2)}) collective-permute-start(bf16[1152,512]{1,0:T(8,128)(2,1)} %param.9), channel_id=1, source_target_pairs={{0,1},{1,0},{2,3},{3,2},{4,5},{5,4},{6,7},{7,6},{8,9},{9,8},{10,11... | collective-permute-start | bytes 3538952 | tf_op jit(solution)/shard_map/ppermute | solution.py:256
  3.8 28.0 %collective-permute-start.1 = (bf16[1152,512]{1,0:T(8,128)(2,1)}, bf16[1152,512]{1,0:T(8,128)(2,1)S(1)}, u32[]{:S(2)}, u32[]{:S(2)}) collective-permute-start(bf16[1152,512]{1,0:T(8,128)(2,1)} %param.9), channel_id=1, source_target_pairs={{1,2},{2,1},{5,6},{6,5},{9,10},{10,9},{13,14},{14,13},{17,18},{18,... | collective-permute-start | bytes 3538952 | tf_op jit(solution)/shard_map/ppermute | solution.py:256
  4.5 2.5 %copy-start.4 = (f32[1,256,512]{2,1,0:T(8,128)S(1)}, f32[1,256,512]{2,1,0:T(8,128)}, u32[]{:S(2)}) copy-start(f32[1,256,512]{2,1,0:T(8,128)} %param.10) | copy-start | bytes 1572868
  30.0 24.3 %collective-permute-start.3 = (bf16[1152,512]{1,0:T(8,128)(2,1)}, bf16[1152,512]{1,0:T(8,128)(2,1)S(1)}, u32[]{:S(2)}, u32[]{:S(2)}) collective-permute-start(bf16[1152,512]{1,0:T(8,128)(2,1)} %collective-permute-done), channel_id=1, source_target_pairs={{1,2},{2,1},{5,6},{6,5},{9,10},{10,9},{13,14},{14,13},{17,18},{18,... | collective-permute-start | bytes 3538952 | tf_op jit(solution)/shard_map/ppermute | solution.py:256
  31.8 4.7 %copy-start.2 = (bf16[4608,256]{1,0:T(8,128)(2,1)S(1)}, bf16[4608,256]{1,0:T(8,128)(2,1)}, u32[]{:S(2)}) copy-start(bf16[4608,256]{1,0:T(8,128)(2,1)} %param.8) | copy-start | bytes 7077892
  33.1 20.0 %collective-permute-start.2 = (bf16[784,512]{1,0:T(8,128)(2,1)S(1)}, bf16[784,512]{1,0:T(8,128)(2,1)S(1)}, u32[]{:S(2)}, u32[]{:S(2)}) collective-permute-start(bf16[784,512]{1,0:T(8,128)(2,1)S(1)} %slice_select_fusion), channel_id=1, source_target_pairs={{0,1},{1,0},{2,3},{3,2},{4,5},{5,4},{6,7},{7,6},{8,9},{9,8},{10,11... | collective-permute-start | bytes 2408456 | tf_op jit(solution)/shard_map/ppermute | solution.py:256
  37.0 16.2 %copy-start = (f32[256,256]{1,0:T(8,128)S(1)}, f32[256,256]{1,0:T(8,128)}, u32[]{:S(2)}) copy-start(f32[256,256]{1,0:T(8,128)} %constant.34.clone.refs_1_.refs_3_.refs_4_) | copy-start | bytes 786436
  37.0 16.1 %copy-start.1 = (bf16[512,128]{1,0:T(8,128)(2,1)S(1)}, bf16[512,128]{1,0:T(8,128)(2,1)}, u32[]{:S(2)}) copy-start(bf16[512,128]{1,0:T(8,128)(2,1)} %constant.33.clone.refs_0_.refs_3_) | copy-start | bytes 393220
  55.6 8.4 %collective-permute-start.4 = (f32[64,128]{1,0:T(8,128)S(1)}, f32[64,128]{1,0:T(8,128)S(1)}, u32[]{:S(2)}, u32[]{:S(2)}) collective-permute-start(f32[64,128]{1,0:T(8,128)S(1)} %get-tuple-element.46), channel_id=1, source_target_pairs={{0,1},{1,0},{2,3},{3,2},{4,5},{5,4},{6,7},{7,6},{8,9},{9,8},{10,11... | collective-permute-start | bytes 98312 | tf_op jit(solution)/shard_map/ppermute | solution.py:256
  62.1 8.4 %collective-permute-start.8 = (s16[272,512]{1,0:T(8,128)(2,1)S(1)}, s16[272,512]{1,0:T(8,128)(2,1)S(1)}, u32[]{:S(2)}, u32[]{:S(2)}) collective-permute-start(s16[272,512]{1,0:T(8,128)(2,1)S(1)} %get-tuple-element.53), channel_id=1, source_target_pairs={{1,0},{2,3},{5,4},{6,7},{9,8},{10,11},{13,12},{14,15},{17,16},{18,... | collective-permute-start | bytes 835592 | tf_op jit(solution)/shard_map/ppermute | solution.py:256
  64.0 6.5 %collective-permute-start.5 = (f32[64,128]{1,0:T(8,128)S(1)}, f32[64,128]{1,0:T(8,128)S(1)}, u32[]{:S(2)}, u32[]{:S(2)}) collective-permute-start(f32[64,128]{1,0:T(8,128)S(1)} %select_add_fusion), channel_id=1, source_target_pairs={{0,4},{4,0},{8,12},{12,8},{16,20},{20,16},{24,28},{28,24},{1,5},{5... | collective-permute-start | bytes 98312 | tf_op jit(solution)/shard_map/ppermute | solution.py:220
  64.0 6.5 %collective-permute-start.6 = (f32[64,128]{1,0:T(8,128)S(1)}, f32[64,128]{1,0:T(8,128)S(1)}, u32[]{:S(2)}, u32[]{:S(2)}) collective-permute-start(f32[64,128]{1,0:T(8,128)S(1)} %select_add_fusion), channel_id=1, source_target_pairs={{0,8},{4,12},{8,0},{12,4},{16,24},{20,28},{24,16},{28,20},{1,9},{5... | collective-permute-start | bytes 98312 | tf_op jit(solution)/shard_map/ppermute | solution.py:220
  65.6 5.0 %collective-permute-start.7 = (f32[64,128]{1,0:T(8,128)S(1)}, f32[64,128]{1,0:T(8,128)S(1)}, u32[]{:S(2)}, u32[]{:S(2)}) collective-permute-start(f32[64,128]{1,0:T(8,128)S(1)} %select_add_fusion), channel_id=1, source_target_pairs={{0,12},{4,8},{8,4},{12,0},{16,28},{20,24},{24,20},{28,16},{1,13},{... | collective-permute-start | bytes 98312 | tf_op jit(solution)/shard_map/ppermute | solution.py:220
  70.6 4.0 %collective-permute-start.9 = (f32[64,128]{1,0:T(8,128)S(1)}, f32[64,128]{1,0:T(8,128)S(1)}, u32[]{:S(2)}, u32[]{:S(2)}) collective-permute-start(f32[64,128]{1,0:T(8,128)S(1)} %add_add_fusion.refs_0_), channel_id=1, source_target_pairs={{0,16},{4,20},{8,24},{12,28},{16,0},{20,4},{24,8},{28,12},{1,17},{... | collective-permute-start | bytes 98312 | tf_op jit(solution)/shard_map/ppermute | solution.py:220

commit v11 on v10

--- a/solution.py
+++ b/solution.py
@@ -133,9 +133,9 @@
     return values, row
 
 
-def decoded(code_ref, exponents_ref):
-    values = code_ref[: code_ref.shape[0] - code_rows].astype(jnp.int32).astype(jnp.float32)
-    exponents = exponents_ref[...].astype(jnp.int32).astype(jnp.float32)
+def decoded(ref):
+    values = ref[: ref.shape[0] - code_rows].astype(jnp.int32).astype(jnp.float32)
+    exponents = ref[ref.shape[0] - code_rows :].astype(jnp.int32).astype(jnp.float32)
     return values * jnp.exp2(exponents[:1] - 15.0)
 
 
@@ -153,23 +153,24 @@
 
 
 def helped_kernel(helped_ref, turned_ref, far_ref, places_ref, *refs):
-    *matrix_refs, code_ref, bands_ref = refs
-    product = helped_ref[...] + dot(turned_ref[...], far_ref[...])
-    bands_ref[...] = bands_of(product, places_ref[...], *matrix_refs)
-    side = product.shape[0]
-    code_ref[:side], code_ref[side:] = coded(product)
-
-
-def last_rows_kernel(end_ref, m_ref, own_bands_ref, turned_ref, far_ref, places_ref, *refs):
     *matrix_refs, out_ref, bands_ref = refs
+    out_ref[...] = helped_ref[...] + dot(turned_ref[...], far_ref[...])
+    bands_ref[...] = bands_of(out_ref[...], places_ref[...], *matrix_refs)
+
+
+def last_rows_kernel(end_ref, helped_ref, m_ref, own_bands_ref, turned_ref, far_ref, places_ref, *refs):
+    *matrix_refs, out_ref, bands_ref, code_ref = refs
 
     @pl.when(end_ref[0] == 1)
     def _():
         out_ref[...] = m_ref[...]
         bands_ref[...] = own_bands_ref[...]
+        code_ref[...] = jnp.zeros_like(code_ref)
 
     @pl.when(end_ref[0] == 0)
     def _():
+        side = m_ref.shape[0]
+        code_ref[:side], code_ref[side:] = coded(helped_ref[...])
         out_ref[...] = m_ref[...] + dot(turned_ref[...], far_ref[...])
         bands_ref[...] = bands_of(out_ref[...], places_ref[...], *matrix_refs)
 
@@ -177,8 +178,8 @@
 def remove_kernel(m_ref, *refs):
     *code_refs, places_ref, basis_ref, out_ref = refs
     m = m_ref[...]
-    if code_refs:
-        m = m + decoded(*code_refs)
+    for ref in code_refs:
+        m = m + decoded(ref)
     masks = masks_of(places_ref[...], m.shape[0] // order)
     out_ref[...] = m - restored(selected(m, masks, basis_ref), masks, basis_ref)
 
@@ -204,11 +205,11 @@
         out_shape=out_shapes,
         in_specs=[pl.BlockSpec(memory_space=space) for space in spaces],
         compiler_params=pltpu.CompilerParams(vmem_limit_bytes=16 * 2**20),
-        cost_estimate=pl.CostEstimate(flops=4 * 10**8, bytes_accessed=4 * 10**6, transcendentals=0),
+        cost_estimate=pl.CostEstimate(flops=300000000, bytes_accessed=4000000, transcendentals=0),
     )(*operands)
 
 
-def spread_sum(x, axis, behind=lambda x: x):
+def spread_sum(x, axis):
     size = lax.axis_size(axis)
     if size & (size - 1):
         return [lax.psum(x, axis)]
@@ -216,10 +217,9 @@
     while stride < size:
         count = min(4, size // stride)
         x = pair_sum(parts)
-        received = [
+        parts = [x] + [
             lax.ppermute(x, axis, [(i, i ^ (stride * k)) for i in range(size)]) for k in range(1, count)
         ]
-        parts = [x] + (behind(received) if stride == 1 else received)
         stride *= count
     return parts
 
@@ -297,28 +297,30 @@
         *matrices,
     )
     far_grad = after(far_grad, m)
+    helped, end_bands = call(
+        helped_kernel, (full, folded), helped, end_turned, far_grad, end_places, *matrices
+    )
+    m, end_bands = lax.optimization_barrier((m, end_bands))
+    end_bands = send(end_bands, both_ways)
     code_shape = jax.ShapeDtypeStruct((m.shape[0] + code_rows, m.shape[1]), jnp.int16)
-    code, end_bands = call(
-        helped_kernel, (code_shape, folded), helped, end_turned, far_grad, end_places, *matrices
-    )
-    m, end_bands, code = lax.optimization_barrier((m, end_bands, code))
-    end_bands = send(end_bands, both_ways)
+    flag = end.astype(jnp.int32).reshape(1)
+    m, bands, code = call(
+        last_rows_kernel,
+        (full, folded, code_shape),
+        flag,
+        helped,
+        m,
+        own_bands,
+        own_turned,
+        far_grad,
+        places,
+        *matrices,
+    )
     code = send(code, outward)
-    flag = end.astype(jnp.int32).reshape(1)
-    m, bands = call(
-        last_rows_kernel, (full, folded), flag, m, own_bands, own_turned, far_grad, places, *matrices
-    )
     end_bands, bands = lax.optimization_barrier((end_bands, bands))
     bands = bands + jnp.where(end, end_bands, 0.0)
-    exponents = code[m.shape[0] :]
-
-    def behind_code(x):
-        nonlocal exponents
-        x, exponents = lax.optimization_barrier((x, exponents))
-        return x
-
-    parts = spread_sum(bands, "rep", behind_code)
-    return [m, code, exponents], parts, places, matrices
+    parts = spread_sum(bands, "rep")
+    return [m, code], parts, places, matrices
 
 
 def local(hidden, out_grad, momentum, band_rows, band_start_columns):

time: 76.4 us -> 77.4 us (1.013)
  local copies, waits for them, and re-layouts: 1.19 us -> 4.89 us
  waiting for transfers between devices: 41.3 us -> 38.5 us
  starting transfers between devices: 19 us -> 18.2 us
  matrix products: 4.1 us -> 4.89 us
    ppermute x6, waiting for transfers between devices: 40.9 us -> 35.5 us  [send(): return lax.ppermute(x, 'tp', perm)]
    unnamed x16 -> x30, local copies, waits for them, and re-layouts: 0.04 us -> 3.74 us
    ppermute x4, waiting for transfers between devices: 0.37 us -> 3.04 us  [spread_sum(): lax.ppermute(x, axis, [(i, i ^ stride * k) for i in range(size)])]
    ppermute x6, starting transfers between devices: 15.5 us -> 14.7 us  [send(): return lax.ppermute(x, 'tp', perm)]
    dot_general x4, matrix products: 4.1 us -> 4.89 us  [dot(): lax.dot_general(a, b, (dims, ((), ())), preferred_element_type=jnp.float32)]
where the time goes in v11:
time: 77.4 us; the launch traced here: 77 us
  waiting for transfers between devices  38.5 us (50%)
  starting transfers between devices  18.2 us (24%)
  Pallas kernels  6.07 us (8%)
  local copies, waits for them, and re-layouts  4.89 us (6%)
  matrix products  4.89 us (6%)
  other arithmetic  3.55 us (5%)
  between operations  0.88 us (1%)
    ppermute x6, waiting for transfers between devices, send(): return lax.ppermute(x, 'tp', perm)  35.5 us
    ppermute x6, starting transfers between devices, send(): return lax.ppermute(x, 'tp', perm)  14.7 us
    pallas_call x5, Pallas kernels, call(): pl.pallas_call(kernel, out_shape=out_shapes, in_specs=[pl.BlockSpec(memor...  6.07 us
    dot_general x4, matrix products, dot(): lax.dot_general(a, b, (dims, ((), ())), preferred_element_type=jnp.float32)  4.89 us
    unnamed x30, local copies, waits for them, and re-layouts  3.74 us
    ppermute x4, starting transfers between devices, spread_sum(): lax.ppermute(x, axis, [(i, i ^ stride * k) for i in range(size)])  3.52 us
    ppermute x4, waiting for transfers between devices, spread_sum(): lax.ppermute(x, axis, [(i, i ^ stride * k) for i in range(size)])  3.04 us
  transfers between devices with their start and end apart: 10, of which 5 were waited for; matrix products, arithmetic and copies ran while one was open for 12% of the time, Pallas kernels for 4%

profile of v11, /device:TPU:0, one launch (start us, length us, event | category | flops | bytes accessed | tf_op | source)
XLA Modules:
  0.0 77.0 jit_solution(5427466382824932337)
XLA Ops:
  0.6 0.0 copy-start.12
  0.6 0.0 copy-start.10
  0.7 0.0 copy-start.14
  0.7 0.0 copy-start.13
  0.7 3.1 %collective-permute-start = (bf16[1152,512]{1,0:T(8,128)(2,1)}, bf16[1152,512]{1,0:T(8,128)(2,1)}, u32[]{:S(2)}, u32[]{:S(2)}) collective-permute-start(bf16[1152,512]{1,0:T(8,128)(2,1)} %param.9), channel_id=1, source_target_pairs={{0,1},{1,0},{2,3},{3,2},{4,5},{5,4},{6,7},{7,6},{8,9},{9,8},{10,11... | collective-permute-start | bytes 3538952 | tf_op jit(solution)/shard_map/ppermute | solution.py:256
  3.8 0.7 collective-permute-start.1
  4.5 0.0 copy-start.11
  4.5 1.1 %constant_dynamic-slice_fusion.3 = (bf16[384,256]{1,0:T(8,128)(2,1)S(1)}, bf16[384,256]{1,0:T(8,128)(2,1)S(1)}) fusion(bf16[4608,256]{1,0:T(8,128)(2,1)} %param.8, s32[]{:T(128)S(6)} %select_n.48, s32[]{:T(128)S(6)} %select_n.50), kind=kLoop, calls=%fused_computation.25 | loop fusion | bytes 786440 | tf_op jit(solution)/shard_map/dynamic_slice | solution.py:253
  5.6 1.2 %dynamic-slice_select_fusion = (bf16[768,256]{1,0:T(8,128)(2,1)S(1)}, bf16[768,256]{1,0:T(8,128)(2,1)S(1)}) fusion(bf16[4608,256]{1,0:T(8,128)(2,1)} %param.8, s32[]{:T(128)S(6)} %select_n.52, pred[]{:T(512)S(6)} %or.3, s32[]{:T(128)S(6)} %add.58), kind=kLoop, calls=%fused_computation.11 | loop fusion | flops 196608 | bytes 1572873 | tf_op jit(solution)/shard_map/jit(_where)/select_n | solution.py:275
  6.9 0.1 fusion.14
  7.0 2.4 %convolution_add_fusion.1 = f32[256,512]{1,0:T(8,128)} fusion(bf16[1152,512]{1,0:T(8,128)(2,1)S(1)} %copy-done.10, bf16[4608,256]{1,0:T(8,128)(2,1)} %param.8, s32[]{:T(128)S(6)} %select_n.54, f32[1,256,512]{2,1,0:T(8,128)S(1)} %copy-done.11), kind=kOutput, calls=%fused_computation.4 | convolution fusion | flops 302252032 | bytes 2818052 | tf_op jit(solution)/shard_map/dot_general | solution.py:45
  9.4 20.7 %collective-permute-done = bf16[1152,512]{1,0:T(8,128)(2,1)} collective-permute-done((bf16[1152,512]{1,0:T(8,128)(2,1)}, bf16[1152,512]{1,0:T(8,128)(2,1)}, u32[]{:S(2)}, u32[]{:S(2)}) %collective-permute-start) | collective-permute-done | bytes 1179680 | tf_op jit(solution)/shard_map/ppermute | solution.py:256
  30.0 0.7 collective-permute-start.3
  30.8 1.0 %fusion.2 = bf16[784,512]{1,0:T(8,128)(2,1)} fusion(bf16[8,512]{1,0:T(8,128)(2,1)S(1)} %get-tuple-element.58, bf16[768,256]{1,0:T(8,128)(2,1)S(1)} %get-tuple-element.55, bf16[384,256]{1,0:T(8,128)(2,1)S(1)} %get-tuple-element.57, bf16[384,256]{1,0:T(8,128)(2,1)S(1)} %get-tuple-element.56), kind=kLoop, calls=%fused_computation.5 | loop fusion | flops 4014080 | bytes 1597440 | tf_op jit(solution)/shard_map/concatenate | solution.py:274
  31.7 0.0 collective-permute-done.1.cross_ref
  31.7 1.4 %slice_select_fusion = bf16[784,512]{1,0:T(8,128)(2,1)S(1)} fusion(bf16[784,512]{1,0:T(8,128)(2,1)} %fusion.2, bf16[1152,512]{1,0:T(8,128)(2,1)S(1)} %collective-permute-done.1.cross_ref, pred[]{:T(512)S(6)} %or.3), kind=kLoop, calls=%fused_computation.6 | loop fusion | flops 401408 | bytes 2408449 | tf_op jit(solution)/shard_map/jit(_where)/select_n | solution.py:280
  33.1 0.0 copy-start.9
  33.1 3.3 %collective-permute-start.2 = (bf16[784,512]{1,0:T(8,128)(2,1)S(1)}, bf16[784,512]{1,0:T(8,128)(2,1)S(1)}, u32[]{:S(2)}, u32[]{:S(2)}) collective-permute-start(bf16[784,512]{1,0:T(8,128)(2,1)S(1)} %slice_select_fusion), channel_id=1, source_target_pairs={{0,1},{1,0},{2,3},{3,2},{4,5},{5,4},{6,7},{7,6},{8,9},{9,8},{10,11... | collective-permute-start | bytes 2408456 | tf_op jit(solution)/shard_map/ppermute | solution.py:256
  36.4 0.0 copy-done.8
  36.4 0.5 fusion.3
  37.0 0.0 copy-start
  37.0 0.0 copy-start.1
  37.0 1.8 %fusion.1.m_ref = f32[256,512]{1,0:T(8,128)S(1)} fusion(f32[256,512]{1,0:T(8,128)S(1)} %fusion.3, f32[256,512]{1,0:T(8,128)S(1)} %copy-done.9, bf16[1152,512]{1,0:T(8,128)(2,1)} %collective-permute-done, bf16[4608,256]{1,0:T(8,128)(2,1)S(1)} %copy-done.8, s32[]{:T(128)S(6)} %select_n.55), kind=kOutput, calls=%fused_computation.3 | convolution fusion | flops 302252032 | bytes 3342340 | tf_op jit(solution)/shard_map/dot_general | solution.py:45
  38.9 14.3 %collective-permute-done.2.swapped_ref = bf16[784,512]{1,0:T(8,128)(2,1)S(1)} collective-permute-done((bf16[784,512]{1,0:T(8,128)(2,1)S(1)}, bf16[784,512]{1,0:T(8,128)(2,1)S(1)}, u32[]{:S(2)}, u32[]{:S(2)}) %collective-permute-start.2) | collective-permute-done | bytes 802848 | tf_op jit(solution)/shard_map/ppermute | solution.py:256
  53.1 0.0 copy-done.1
  53.1 1.1 %shard_map.95 = (f32[256,512]{1,0:T(8,128)S(1)}, f32[256,512]{1,0:T(8,128)S(1)}, bf16[256,1152]{1,0:T(8,128)(2,1)S(1)}, bf16[256,1152]{1,0:T(8,128)(2,1)S(1)}, f...) custom-call(f32[256,512]{1,0:T(8,128)S(1)} %fusion.1.m_ref, ...), custom_call_target="tpu_custom_call" | custom-call | flops 300000000 | bytes 4000000 | tf_op jit(solution)/shard_map/pallas_call | solution.py:203
  54.3 0.8 %copy-done.2 = bf16[256,1152]{1,0:T(8,128)(2,1)} copy-done((bf16[256,1152]{1,0:T(8,128)(2,1)}, bf16[256,1152]{1,0:T(8,128)(2,1)S(1)}, u32[]{:S(2)}) %copy-start.2) | copy-done | bytes 589848
  55.1 0.0 collective-permute-done.3.far_ref
  55.1 1.3 %shard_map.96 = (f32[256,512]{1,0:T(8,128)S(1)}, f32[64,128]{1,0:T(8,128)S(1)}) custom-call(f32[256,512]{1,0:T(8,128)S(1)} %get-tuple-element.36.helped_ref, bf16[256,1152]{1,0:T(8,128)(2,1)S(1)} %get-tuple-element.37.turned_ref, bf16[1152,512]{1,0:T(8,128)(2,1)S(1)} %collective-permute-done.3.far_ref, f32[16,512]{1,0:T(8,128)S(1)} %get-tuple-element.39.places_ref, ...), custom_call_target="tpu_custom_call" | custom-call | flops 300000000 | bytes 4000000 | tf_op jit(solution)/shard_map/pallas_call | solution.py:203
  56.4 0.0 copy-start.6
  56.4 0.8 %copy-done.6 = f32[256,512]{1,0:T(8,128)} copy-done((f32[256,512]{1,0:T(8,128)}, f32[256,512]{1,0:T(8,128)S(1)}, u32[]{:S(2)}) %copy-start.6) | copy-done | bytes 524312
  57.2 5.6 %collective-permute-start.4 = (f32[64,128]{1,0:T(8,128)S(1)}, f32[64,128]{1,0:T(8,128)S(1)}, u32[]{:S(2)}, u32[]{:S(2)}) collective-permute-start(f32[64,128]{1,0:T(8,128)S(1)} %get-tuple-element.41), channel_id=1, source_target_pairs={{0,1},{1,0},{2,3},{3,2},{4,5},{5,4},{6,7},{7,6},{8,9},{9,8},{10,11... | collective-permute-start | bytes 98312 | tf_op jit(solution)/shard_map/ppermute | solution.py:256
  62.8 1.0 %copy-done.5 = f32[256,512]{1,0:T(8,128)S(1)} copy-done((f32[256,512]{1,0:T(8,128)S(1)}, f32[256,512]{1,0:T(8,128)}, u32[]{:S(2)}) %copy-start.5) | copy-done | bytes 524312
  63.8 1.0 %copy-done.7 = f32[256,512]{1,0:T(8,128)S(1)} copy-done((f32[256,512]{1,0:T(8,128)S(1)}, f32[256,512]{1,0:T(8,128)}, u32[]{:S(2)}) %copy-start.7) | copy-done | bytes 524312
  64.9 0.1 shard_map.97
  64.9 1.3 %collective-permute-start.9 = (s16[272,512]{1,0:T(8,128)(2,1)S(1)}, s16[272,512]{1,0:T(8,128)(2,1)S(1)}, u32[]{:S(2)}, u32[]{:S(2)}) collective-permute-start(s16[272,512]{1,0:T(8,128)(2,1)S(1)} %get-tuple-element.50), channel_id=1, source_target_pairs={{1,0},{2,3},{5,4},{6,7},{9,8},{10,11},{13,12},{14,15},{17,16},{18,... | collective-permute-start | bytes 835592 | tf_op jit(solution)/shard_map/ppermute | solution.py:256
  66.2 0.0 collective-permute-done.4
  66.3 0.1 collective-permute-start.5
  66.3 1.6 %collective-permute-start.6 = (f32[64,128]{1,0:T(8,128)S(1)}, f32[64,128]{1,0:T(8,128)S(1)}, u32[]{:S(2)}, u32[]{:S(2)}) collective-permute-start(f32[64,128]{1,0:T(8,128)S(1)} %select_add_fusion), channel_id=1, source_target_pairs={{0,8},{4,12},{8,0},{12,4},{16,24},{20,28},{24,16},{28,20},{1,9},{5... | collective-permute-start | bytes 98312 | tf_op jit(solution)/shard_map/ppermute | solution.py:221
  67.9 0.3 collective-permute-start.7
  68.2 0.0 collective-permute-done.5
  68.2 2.1 %collective-permute-done.6 = f32[64,128]{1,0:T(8,128)S(1)} collective-permute-done((f32[64,128]{1,0:T(8,128)S(1)}, f32[64,128]{1,0:T(8,128)S(1)}, u32[]{:S(2)}, u32[]{:S(2)}) %collective-permute-start.6) | collective-permute-done | bytes 32800 | tf_op jit(solution)/shard_map/ppermute | solution.py:221
  70.3 0.9 %collective-permute-done.7 = f32[64,128]{1,0:T(8,128)S(1)} collective-permute-done((f32[64,128]{1,0:T(8,128)S(1)}, f32[64,128]{1,0:T(8,128)S(1)}, u32[]{:S(2)}, u32[]{:S(2)}) %collective-permute-start.7) | collective-permute-done | bytes 32800 | tf_op jit(solution)/shard_map/ppermute | solution.py:221
  71.3 1.6 %collective-permute-start.8 = (f32[64,128]{1,0:T(8,128)S(1)}, f32[64,128]{1,0:T(8,128)S(1)}, u32[]{:S(2)}, u32[]{:S(2)}) collective-permute-start(f32[64,128]{1,0:T(8,128)S(1)} %add_add_fusion.refs_0_), channel_id=1, source_target_pairs={{0,16},{4,20},{8,24},{12,28},{16,0},{20,4},{24,8},{28,12},{1,17},{... | collective-permute-start | bytes 98312 | tf_op jit(solution)/shard_map/ppermute | solution.py:221
  72.8 0.5 collective-permute-done.9.refs_0_
  73.4 2.0 %shard_map.98 = f32[256,512]{1,0:T(8,128)} custom-call(f32[256,512]{1,0:T(8,128)S(1)} %get-tuple-element.49.m_ref, s16[272,512]{1,0:T(8,128)(2,1)S(1)} %collective-permute-done.9.refs_0_, f32[8,512]{1,0:T(8,128)S(1)} %get-tuple-element.32.places_ref.refs_1_.refs_2_, f32[256,256]{1,0:T(8,128)S(1)} %copy-done), custom_call_target="tpu_custom_call" | custom-call | flops 300000000 | bytes 4000000 | tf_op jit(solution)/shard_map/pallas_call | solution.py:203
  75.4 0.0 collective-permute-done.8.refs_1_
  75.4 1.6 %shard_map.99 = bf16[256,512]{1,0:T(8,128)(2,1)} custom-call(f32[64,128]{1,0:T(8,128)S(1)} %add_add_fusion.refs_0_, f32[64,128]{1,0:T(8,128)S(1)} %collective-permute-done.8.refs_1_, f32[8,512]{1,0:T(8,128)S(1)} %get-tuple-element.32.places_ref.refs_1_.refs_2_, bf16[512,128]{1,0:T(8,128)(2,1)S(1)} %copy-done.1, f32[256,256]{1,0:T(8,128)S(1)} %copy-done), custom_call_target="tpu_custom_call" | custom-call | flops 300000000 | bytes 4000000 | tf_op jit(solution)/shard_map/pallas_call | solution.py:203
  (18 shorter events, 0.1 us)
Async XLA Ops:
  0.6 6.2 %copy-start.12 = (bf16[8,512]{1,0:T(8,128)(2,1)S(1)}, bf16[8,512]{1,0:T(8,128)(2,1)}, u32[]{:S(2)}) copy-start(bf16[8,512]{1,0:T(8,128)(2,1)} %constant.53) | copy-start | bytes 24580
  0.6 6.4 %copy-start.10 = (bf16[1152,512]{1,0:T(8,128)(2,1)S(1)}, bf16[1152,512]{1,0:T(8,128)(2,1)}, u32[]{:S(2)}) copy-start(bf16[1152,512]{1,0:T(8,128)(2,1)} %param.9) | copy-start | bytes 3538948
  0.7 6.2 %copy-start.14 = (s32[4,8]{1,0:T(4,128)S(1)}, s32[4,8]{1,0:T(4,128)}, u32[]{:S(2)}) copy-start(s32[4,8]{1,0:T(4,128)} %param.11) | copy-start | bytes 388
  0.7 6.2 %copy-start.13 = (s32[4,8]{1,0:T(4,128)S(1)}, s32[4,8]{1,0:T(4,128)}, u32[]{:S(2)}) copy-start(s32[4,8]{1,0:T(4,128)} %param.12) | copy-start | bytes 388
  0.7 29.4 %collective-permute-start = (bf16[1152,512]{1,0:T(8,128)(2,1)}, bf16[1152,512]{1,0:T(8,128)(2,1)}, u32[]{:S(2)}, u32[]{:S(2)}) collective-permute-start(bf16[1152,512]{1,0:T(8,128)(2,1)} %param.9), channel_id=1, source_target_pairs={{0,1},{1,0},{2,3},{3,2},{4,5},{5,4},{6,7},{7,6},{8,9},{9,8},{10,11... | collective-permute-start | bytes 3538952 | tf_op jit(solution)/shard_map/ppermute | solution.py:256
  3.8 28.0 %collective-permute-start.1 = (bf16[1152,512]{1,0:T(8,128)(2,1)}, bf16[1152,512]{1,0:T(8,128)(2,1)S(1)}, u32[]{:S(2)}, u32[]{:S(2)}) collective-permute-start(bf16[1152,512]{1,0:T(8,128)(2,1)} %param.9), channel_id=1, source_target_pairs={{1,2},{2,1},{5,6},{6,5},{9,10},{10,9},{13,14},{14,13},{17,18},{18,... | collective-permute-start | bytes 3538952 | tf_op jit(solution)/shard_map/ppermute | solution.py:256
  4.5 2.5 %copy-start.11 = (f32[1,256,512]{2,1,0:T(8,128)S(1)}, f32[1,256,512]{2,1,0:T(8,128)}, u32[]{:S(2)}) copy-start(f32[1,256,512]{2,1,0:T(8,128)} %param.10) | copy-start | bytes 1572868
  30.0 25.1 %collective-permute-start.3 = (bf16[1152,512]{1,0:T(8,128)(2,1)}, bf16[1152,512]{1,0:T(8,128)(2,1)S(1)}, u32[]{:S(2)}, u32[]{:S(2)}) collective-permute-start(bf16[1152,512]{1,0:T(8,128)(2,1)} %collective-permute-done), channel_id=1, source_target_pairs={{1,2},{2,1},{5,6},{6,5},{9,10},{10,9},{13,14},{14,13},{17,18},{18,... | collective-permute-start | bytes 3538952 | tf_op jit(solution)/shard_map/ppermute | solution.py:256
  31.7 4.7 %copy-start.8 = (bf16[4608,256]{1,0:T(8,128)(2,1)S(1)}, bf16[4608,256]{1,0:T(8,128)(2,1)}, u32[]{:S(2)}) copy-start(bf16[4608,256]{1,0:T(8,128)(2,1)} %param.8) | copy-start | bytes 7077892
  33.1 3.9 %copy-start.9 = (f32[256,512]{1,0:T(8,128)S(1)}, f32[256,512]{1,0:T(8,128)}, u32[]{:S(2)}) copy-start(f32[256,512]{1,0:T(8,128)} %convolution_add_fusion.1) | copy-start | bytes 1572868
  33.1 20.0 %collective-permute-start.2 = (bf16[784,512]{1,0:T(8,128)(2,1)S(1)}, bf16[784,512]{1,0:T(8,128)(2,1)S(1)}, u32[]{:S(2)}, u32[]{:S(2)}) collective-permute-start(bf16[784,512]{1,0:T(8,128)(2,1)S(1)} %slice_select_fusion), channel_id=1, source_target_pairs={{0,1},{1,0},{2,3},{3,2},{4,5},{5,4},{6,7},{7,6},{8,9},{9,8},{10,11... | collective-permute-start | bytes 2408456 | tf_op jit(solution)/shard_map/ppermute | solution.py:256
  37.0 16.1 %copy-start = (f32[256,256]{1,0:T(8,128)S(1)}, f32[256,256]{1,0:T(8,128)}, u32[]{:S(2)}) copy-start(f32[256,256]{1,0:T(8,128)} %constant.34.clone.refs_1_.refs_2_.refs_4_) | copy-start | bytes 786436
  37.0 16.1 %copy-start.1 = (bf16[512,128]{1,0:T(8,128)(2,1)S(1)}, bf16[512,128]{1,0:T(8,128)(2,1)}, u32[]{:S(2)}) copy-start(bf16[512,128]{1,0:T(8,128)(2,1)} %constant.33.clone.refs_0_.refs_3_) | copy-start | bytes 393220
  54.3 0.8 %copy-start.2 = (bf16[256,1152]{1,0:T(8,128)(2,1)}, bf16[256,1152]{1,0:T(8,128)(2,1)S(1)}, u32[]{:S(2)}) copy-start(bf16[256,1152]{1,0:T(8,128)(2,1)S(1)} %get-tuple-element.45.turned_ref) | copy-start | bytes 1769476
  55.1 1.3 %copy-start.4 = (f32[256,512]{1,0:T(8,128)}, f32[256,512]{1,0:T(8,128)S(1)}, u32[]{:S(2)}) copy-start(f32[256,512]{1,0:T(8,128)S(1)} %get-tuple-element.43.m_ref) | copy-start | bytes 1572868
  55.1 7.7 %copy-start.3 = (bf16[256,1152]{1,0:T(8,128)(2,1)S(1)}, bf16[256,1152]{1,0:T(8,128)(2,1)}, u32[]{:S(2)}) copy-start(bf16[256,1152]{1,0:T(8,128)(2,1)} %copy-done.2) | copy-start | bytes 1769476
  56.4 0.8 %copy-start.6 = (f32[256,512]{1,0:T(8,128)}, f32[256,512]{1,0:T(8,128)S(1)}, u32[]{:S(2)}) copy-start(f32[256,512]{1,0:T(8,128)S(1)} %get-tuple-element.42.helped_ref) | copy-start | bytes 1572868
  57.2 9.1 %collective-permute-start.4 = (f32[64,128]{1,0:T(8,128)S(1)}, f32[64,128]{1,0:T(8,128)S(1)}, u32[]{:S(2)}, u32[]{:S(2)}) collective-permute-start(f32[64,128]{1,0:T(8,128)S(1)} %get-tuple-element.41), channel_id=1, source_target_pairs={{0,1},{1,0},{2,3},{3,2},{4,5},{5,4},{6,7},{7,6},{8,9},{9,8},{10,11... | collective-permute-start | bytes 98312 | tf_op jit(solution)/shard_map/ppermute | solution.py:256
  62.8 1.0 %copy-start.5 = (f32[256,512]{1,0:T(8,128)S(1)}, f32[256,512]{1,0:T(8,128)}, u32[]{:S(2)}) copy-start(f32[256,512]{1,0:T(8,128)} %copy-done.4) | copy-start | bytes 1572868
  63.8 1.0 %copy-start.7 = (f32[256,512]{1,0:T(8,128)S(1)}, f32[256,512]{1,0:T(8,128)}, u32[]{:S(2)}) copy-start(f32[256,512]{1,0:T(8,128)} %copy-done.6) | copy-start | bytes 1572868
  64.9 8.4 %collective-permute-start.9 = (s16[272,512]{1,0:T(8,128)(2,1)S(1)}, s16[272,512]{1,0:T(8,128)(2,1)S(1)}, u32[]{:S(2)}, u32[]{:S(2)}) collective-permute-start(s16[272,512]{1,0:T(8,128)(2,1)S(1)} %get-tuple-element.50), channel_id=1, source_target_pairs={{1,0},{2,3},{5,4},{6,7},{9,8},{10,11},{13,12},{14,15},{17,16},{18,... | collective-permute-start | bytes 835592 | tf_op jit(solution)/shard_map/ppermute | solution.py:256
  66.3 1.9 %collective-permute-start.5 = (f32[64,128]{1,0:T(8,128)S(1)}, f32[64,128]{1,0:T(8,128)S(1)}, u32[]{:S(2)}, u32[]{:S(2)}) collective-permute-start(f32[64,128]{1,0:T(8,128)S(1)} %select_add_fusion), channel_id=1, source_target_pairs={{0,4},{4,0},{8,12},{12,8},{16,20},{20,16},{24,28},{28,24},{1,5},{5... | collective-permute-start | bytes 98312 | tf_op jit(solution)/shard_map/ppermute | solution.py:221
  66.3 4.0 %collective-permute-start.6 = (f32[64,128]{1,0:T(8,128)S(1)}, f32[64,128]{1,0:T(8,128)S(1)}, u32[]{:S(2)}, u32[]{:S(2)}) collective-permute-start(f32[64,128]{1,0:T(8,128)S(1)} %select_add_fusion), channel_id=1, source_target_pairs={{0,8},{4,12},{8,0},{12,4},{16,24},{20,28},{24,16},{28,20},{1,9},{5... | collective-permute-start | bytes 98312 | tf_op jit(solution)/shard_map/ppermute | solution.py:221
  67.9 3.3 %collective-permute-start.7 = (f32[64,128]{1,0:T(8,128)S(1)}, f32[64,128]{1,0:T(8,128)S(1)}, u32[]{:S(2)}, u32[]{:S(2)}) collective-permute-start(f32[64,128]{1,0:T(8,128)S(1)} %select_add_fusion), channel_id=1, source_target_pairs={{0,12},{4,8},{8,4},{12,0},{16,28},{20,24},{24,20},{28,16},{1,13},{... | collective-permute-start | bytes 98312 | tf_op jit(solution)/shard_map/ppermute | solution.py:221
  71.3 4.2 %collective-permute-start.8 = (f32[64,128]{1,0:T(8,128)S(1)}, f32[64,128]{1,0:T(8,128)S(1)}, u32[]{:S(2)}, u32[]{:S(2)}) collective-permute-start(f32[64,128]{1,0:T(8,128)S(1)} %add_add_fusion.refs_0_), channel_id=1, source_target_pairs={{0,16},{4,20},{8,24},{12,28},{16,0},{20,4},{24,8},{28,12},{1,17},{... | collective-permute-start | bytes 98312 | tf_op jit(solution)/shard_map/ppermute | solution.py:221

commit v12 on v10

--- a/solution.py
+++ b/solution.py
@@ -133,9 +133,9 @@
     return values, row
 
 
-def decoded(code_ref, exponents_ref):
-    values = code_ref[: code_ref.shape[0] - code_rows].astype(jnp.int32).astype(jnp.float32)
-    exponents = exponents_ref[...].astype(jnp.int32).astype(jnp.float32)
+def decoded(ref):
+    values = ref[: ref.shape[0] - code_rows].astype(jnp.int32).astype(jnp.float32)
+    exponents = ref[ref.shape[0] - code_rows :].astype(jnp.int32).astype(jnp.float32)
     return values * jnp.exp2(exponents[:1] - 15.0)
 
 
@@ -177,8 +177,8 @@
 def remove_kernel(m_ref, *refs):
     *code_refs, places_ref, basis_ref, out_ref = refs
     m = m_ref[...]
-    if code_refs:
-        m = m + decoded(*code_refs)
+    for ref in code_refs:
+        m = m + decoded(ref)
     masks = masks_of(places_ref[...], m.shape[0] // order)
     out_ref[...] = m - restored(selected(m, masks, basis_ref), masks, basis_ref)
 
@@ -204,11 +204,11 @@
         out_shape=out_shapes,
         in_specs=[pl.BlockSpec(memory_space=space) for space in spaces],
         compiler_params=pltpu.CompilerParams(vmem_limit_bytes=16 * 2**20),
-        cost_estimate=pl.CostEstimate(flops=4 * 10**8, bytes_accessed=4 * 10**6, transcendentals=0),
+        cost_estimate=pl.CostEstimate(flops=22 * 10**7, bytes_accessed=3 * 10**6, transcendentals=0),
     )(*operands)
 
 
-def spread_sum(x, axis, behind=lambda x: x):
+def spread_sum(x, axis):
     size = lax.axis_size(axis)
     if size & (size - 1):
         return [lax.psum(x, axis)]
@@ -216,10 +216,9 @@
     while stride < size:
         count = min(4, size // stride)
         x = pair_sum(parts)
-        received = [
+        parts = [x] + [
             lax.ppermute(x, axis, [(i, i ^ (stride * k)) for i in range(size)]) for k in range(1, count)
         ]
-        parts = [x] + (behind(received) if stride == 1 else received)
         stride *= count
     return parts
 
@@ -310,15 +309,8 @@
     )
     end_bands, bands = lax.optimization_barrier((end_bands, bands))
     bands = bands + jnp.where(end, end_bands, 0.0)
-    exponents = code[m.shape[0] :]
-
-    def behind_code(x):
-        nonlocal exponents
-        x, exponents = lax.optimization_barrier((x, exponents))
-        return x
-
-    parts = spread_sum(bands, "rep", behind_code)
-    return [m, code, exponents], parts, places, matrices
+    parts = spread_sum(bands, "rep")
+    return [m, code], parts, places, matrices
 
 
 def local(hidden, out_grad, momentum, band_rows, band_start_columns):

time: 76.4 us -> 76.2 us (level); the launches traced: 76.1 us -> 75 us
  waiting for transfers between devices: 41.3 us -> 38.3 us
  local copies, waits for them, and re-layouts: 1.19 us -> 3.04 us
  matrix products: 4.1 us -> 4.89 us
    ppermute x6, waiting for transfers between devices: 40.9 us -> 34.9 us  [send(): return lax.ppermute(x, 'tp', perm)]
    ppermute x4, waiting for transfers between devices: 0.37 us -> 3.39 us  [spread_sum(): lax.ppermute(x, axis, [(i, i ^ stride * k) for i in range(size)])]
    unnamed x16 -> x26, local copies, waits for them, and re-layouts: 0.04 us -> 1.89 us
    ppermute x6, starting transfers between devices: 15.5 us -> 14.7 us  [send(): return lax.ppermute(x, 'tp', perm)]
    dot_general x4, matrix products: 4.1 us -> 4.89 us  [dot(): lax.dot_general(a, b, (dims, ((), ())), preferred_element_type=jnp.float32)]
  transfers between devices with their start and end apart: 10 -> 10, of which waited for: 5 -> 5; matrix products, arithmetic and copies ran while one was open for 12% -> 13% of each run, Pallas kernels for 4% -> 4%
where the time goes in v12:
time: 76.2 us; the launch traced here: 75 us
  waiting for transfers between devices  38.3 us (50%)
  starting transfers between devices  18.3 us (24%)
  Pallas kernels  6.09 us (8%)
  matrix products  4.89 us (6%)
  other arithmetic  3.55 us (5%)
  local copies, waits for them, and re-layouts  3.04 us (4%)
  between operations  0.89 us (1%)
    ppermute x6, waiting for transfers between devices, send(): return lax.ppermute(x, 'tp', perm)  34.9 us
    ppermute x6, starting transfers between devices, send(): return lax.ppermute(x, 'tp', perm)  14.7 us
    pallas_call x5, Pallas kernels, call(): pl.pallas_call(kernel, out_shape=out_shapes, in_specs=[pl.BlockSpec(memor...  6.09 us
    dot_general x4, matrix products, dot(): lax.dot_general(a, b, (dims, ((), ())), preferred_element_type=jnp.float32)  4.89 us
    ppermute x4, starting transfers between devices, spread_sum(): lax.ppermute(x, axis, [(i, i ^ stride * k) for i in range(size)])  3.52 us
    ppermute x4, waiting for transfers between devices, spread_sum(): lax.ppermute(x, axis, [(i, i ^ stride * k) for i in range(size)])  3.39 us
    unnamed x26, local copies, waits for them, and re-layouts  1.89 us
  transfers between devices with their start and end apart: 10, of which 5 were waited for; matrix products, arithmetic and copies ran while one was open for 13% of the time, Pallas kernels for 4%

profile of v12, /device:TPU:0, one launch (start us, length us, event | category | flops | bytes accessed | tf_op | source)
XLA Modules:
  0.0 75.0 jit_solution(4440559361725462216)
XLA Ops:
  0.6 0.0 copy-start.10
  0.6 0.0 copy-start.8
  0.7 0.0 copy-start.12
  0.7 0.0 copy-start.11
  0.7 3.1 %collective-permute-start = (bf16[1152,512]{1,0:T(8,128)(2,1)}, bf16[1152,512]{1,0:T(8,128)(2,1)}, u32[]{:S(2)}, u32[]{:S(2)}) collective-permute-start(bf16[1152,512]{1,0:T(8,128)(2,1)} %param.9), channel_id=1, source_target_pairs={{0,1},{1,0},{2,3},{3,2},{4,5},{5,4},{6,7},{7,6},{8,9},{9,8},{10,11... | collective-permute-start | bytes 3538952 | tf_op jit(solution)/shard_map/ppermute | solution.py:255
  3.8 0.7 collective-permute-start.1
  4.5 0.0 copy-start.9
  4.5 1.1 %constant_dynamic-slice_fusion.3 = (bf16[384,256]{1,0:T(8,128)(2,1)S(1)}, bf16[384,256]{1,0:T(8,128)(2,1)S(1)}) fusion(bf16[4608,256]{1,0:T(8,128)(2,1)} %param.8, s32[]{:T(128)S(6)} %select_n.48, s32[]{:T(128)S(6)} %select_n.50), kind=kLoop, calls=%fused_computation.25 | loop fusion | bytes 786440 | tf_op jit(solution)/shard_map/dynamic_slice | solution.py:252
  5.6 1.2 %dynamic-slice_select_fusion = (bf16[768,256]{1,0:T(8,128)(2,1)S(1)}, bf16[768,256]{1,0:T(8,128)(2,1)S(1)}) fusion(bf16[4608,256]{1,0:T(8,128)(2,1)} %param.8, s32[]{:T(128)S(6)} %select_n.52, pred[]{:T(512)S(6)} %or.3, s32[]{:T(128)S(6)} %add.58), kind=kLoop, calls=%fused_computation.11 | loop fusion | flops 196608 | bytes 1572873 | tf_op jit(solution)/shard_map/jit(_where)/select_n | solution.py:274
  6.8 0.0 copy-done.10
  6.9 0.0 copy-done.12
  6.9 0.0 copy-done.11
  6.9 0.1 fusion.14
  7.0 2.4 %convolution_add_fusion.1 = f32[256,512]{1,0:T(8,128)} fusion(bf16[1152,512]{1,0:T(8,128)(2,1)S(1)} %copy-done.8, bf16[4608,256]{1,0:T(8,128)(2,1)} %param.8, s32[]{:T(128)S(6)} %select_n.54, f32[1,256,512]{2,1,0:T(8,128)S(1)} %copy-done.9), kind=kOutput, calls=%fused_computation.4 | convolution fusion | flops 302252032 | bytes 2818052 | tf_op jit(solution)/shard_map/dot_general | solution.py:45
  9.4 20.7 %collective-permute-done = bf16[1152,512]{1,0:T(8,128)(2,1)} collective-permute-done((bf16[1152,512]{1,0:T(8,128)(2,1)}, bf16[1152,512]{1,0:T(8,128)(2,1)}, u32[]{:S(2)}, u32[]{:S(2)}) %collective-permute-start) | collective-permute-done | bytes 1179680 | tf_op jit(solution)/shard_map/ppermute | solution.py:255
  30.0 0.7 collective-permute-start.3
  30.8 1.0 %fusion.2 = bf16[784,512]{1,0:T(8,128)(2,1)} fusion(bf16[8,512]{1,0:T(8,128)(2,1)S(1)} %get-tuple-element.58, bf16[768,256]{1,0:T(8,128)(2,1)S(1)} %get-tuple-element.55, bf16[384,256]{1,0:T(8,128)(2,1)S(1)} %get-tuple-element.57, bf16[384,256]{1,0:T(8,128)(2,1)S(1)} %get-tuple-element.56), kind=kLoop, calls=%fused_computation.5 | loop fusion | flops 4014080 | bytes 1597440 | tf_op jit(solution)/shard_map/concatenate | solution.py:273
  31.7 0.0 collective-permute-done.1.cross_ref
  31.8 1.4 %slice_select_fusion = bf16[784,512]{1,0:T(8,128)(2,1)S(1)} fusion(bf16[784,512]{1,0:T(8,128)(2,1)} %fusion.2, bf16[1152,512]{1,0:T(8,128)(2,1)S(1)} %collective-permute-done.1.cross_ref, pred[]{:T(512)S(6)} %or.3), kind=kLoop, calls=%fused_computation.6 | loop fusion | flops 401408 | bytes 2408449 | tf_op jit(solution)/shard_map/jit(_where)/select_n | solution.py:279
  33.1 0.0 copy-start.7
  33.1 3.3 %collective-permute-start.2 = (bf16[784,512]{1,0:T(8,128)(2,1)S(1)}, bf16[784,512]{1,0:T(8,128)(2,1)S(1)}, u32[]{:S(2)}, u32[]{:S(2)}) collective-permute-start(bf16[784,512]{1,0:T(8,128)(2,1)S(1)} %slice_select_fusion), channel_id=1, source_target_pairs={{0,1},{1,0},{2,3},{3,2},{4,5},{5,4},{6,7},{7,6},{8,9},{9,8},{10,11... | collective-permute-start | bytes 2408456 | tf_op jit(solution)/shard_map/ppermute | solution.py:255
  36.5 0.5 fusion.3
  37.0 0.0 copy-start
  37.0 0.0 copy-start.1
  37.0 1.8 %fusion.1.m_ref = f32[256,512]{1,0:T(8,128)S(1)} fusion(f32[256,512]{1,0:T(8,128)S(1)} %fusion.3, f32[256,512]{1,0:T(8,128)S(1)} %copy-done.7, bf16[1152,512]{1,0:T(8,128)(2,1)} %collective-permute-done, bf16[4608,256]{1,0:T(8,128)(2,1)S(1)} %copy-done.6, s32[]{:T(128)S(6)} %select_n.55), kind=kOutput, calls=%fused_computation.3 | convolution fusion | flops 302252032 | bytes 3342340 | tf_op jit(solution)/shard_map/dot_general | solution.py:45
  38.9 14.3 %collective-permute-done.2.swapped_ref = bf16[784,512]{1,0:T(8,128)(2,1)S(1)} collective-permute-done((bf16[784,512]{1,0:T(8,128)(2,1)S(1)}, bf16[784,512]{1,0:T(8,128)(2,1)S(1)}, u32[]{:S(2)}, u32[]{:S(2)}) %collective-permute-start.2) | collective-permute-done | bytes 802848 | tf_op jit(solution)/shard_map/ppermute | solution.py:255
  53.1 0.0 copy-done
  53.2 1.2 %shard_map.95 = (f32[256,512]{1,0:T(8,128)S(1)}, f32[256,512]{1,0:T(8,128)S(1)}, bf16[256,1152]{1,0:T(8,128)(2,1)S(1)}, bf16[256,1152]{1,0:T(8,128)(2,1)S(1)}, f...) custom-call(f32[256,512]{1,0:T(8,128)S(1)} %fusion.1.m_ref, ...), custom_call_target="tpu_custom_call" | custom-call | flops 220000000 | bytes 3000000 | tf_op jit(solution)/shard_map/pallas_call | solution.py:202
  54.3 0.0 copy-start.2
  54.3 0.8 %copy-done.2 = bf16[256,1152]{1,0:T(8,128)(2,1)} copy-done((bf16[256,1152]{1,0:T(8,128)(2,1)}, bf16[256,1152]{1,0:T(8,128)(2,1)S(1)}, u32[]{:S(2)}) %copy-start.2) | copy-done | bytes 589848
  55.1 0.0 collective-permute-done.3.far_ref
  55.1 1.3 %shard_map.96 = (s16[272,512]{1,0:T(8,128)(2,1)S(1)}, f32[64,128]{1,0:T(8,128)S(1)}) custom-call(f32[256,512]{1,0:T(8,128)S(1)} %get-tuple-element.36.helped_ref, bf16[256,1152]{1,0:T(8,128)(2,1)S(1)} %get-tuple-element.37.turned_ref, bf16[1152,512]{1,0:T(8,128)(2,1)S(1)} %collective-permute-done.3.far_ref, f32[16,512]{1,0:T(8,128)S(1)} %get-tuple-element.39.places_ref, ...), custom_call_target="tpu_custom_call" | custom-call | flops 220000000 | bytes 3000000 | tf_op jit(solution)/shard_map/pallas_call | solution.py:202
  56.4 5.7 %collective-permute-start.4 = (f32[64,128]{1,0:T(8,128)S(1)}, f32[64,128]{1,0:T(8,128)S(1)}, u32[]{:S(2)}, u32[]{:S(2)}) collective-permute-start(f32[64,128]{1,0:T(8,128)S(1)} %get-tuple-element.42), channel_id=1, source_target_pairs={{0,1},{1,0},{2,3},{3,2},{4,5},{5,4},{6,7},{7,6},{8,9},{9,8},{10,11... | collective-permute-start | bytes 98312 | tf_op jit(solution)/shard_map/ppermute | solution.py:255
  62.1 1.3 %collective-permute-start.9 = (s16[272,512]{1,0:T(8,128)(2,1)S(1)}, s16[272,512]{1,0:T(8,128)(2,1)S(1)}, u32[]{:S(2)}, u32[]{:S(2)}) collective-permute-start(s16[272,512]{1,0:T(8,128)(2,1)S(1)} %get-tuple-element.50), channel_id=1, source_target_pairs={{1,0},{2,3},{5,4},{6,7},{9,8},{10,11},{13,12},{14,15},{17,16},{18,... | collective-permute-start | bytes 835592 | tf_op jit(solution)/shard_map/ppermute | solution.py:255
  63.4 0.0 copy-start.5
  63.4 1.0 %copy-done.5 = f32[256,512]{1,0:T(8,128)S(1)} copy-done((f32[256,512]{1,0:T(8,128)S(1)}, f32[256,512]{1,0:T(8,128)}, u32[]{:S(2)}) %copy-start.5) | copy-done | bytes 524312
  64.5 0.0 collective-permute-done.4
  64.5 0.1 collective-permute-start.5
  64.6 1.6 %collective-permute-start.6 = (f32[64,128]{1,0:T(8,128)S(1)}, f32[64,128]{1,0:T(8,128)S(1)}, u32[]{:S(2)}, u32[]{:S(2)}) collective-permute-start(f32[64,128]{1,0:T(8,128)S(1)} %select_add_fusion), channel_id=1, source_target_pairs={{0,8},{4,12},{8,0},{12,4},{16,24},{20,28},{24,16},{28,20},{1,9},{5... | collective-permute-start | bytes 98312 | tf_op jit(solution)/shard_map/ppermute | solution.py:220
  66.2 0.3 collective-permute-start.7
  66.5 0.0 collective-permute-done.5
  66.5 2.1 %collective-permute-done.6 = f32[64,128]{1,0:T(8,128)S(1)} collective-permute-done((f32[64,128]{1,0:T(8,128)S(1)}, f32[64,128]{1,0:T(8,128)S(1)}, u32[]{:S(2)}, u32[]{:S(2)}) %collective-permute-start.6) | collective-permute-done | bytes 32800 | tf_op jit(solution)/shard_map/ppermute | solution.py:220
  68.6 0.9 %collective-permute-done.7 = f32[64,128]{1,0:T(8,128)S(1)} collective-permute-done((f32[64,128]{1,0:T(8,128)S(1)}, f32[64,128]{1,0:T(8,128)S(1)}, u32[]{:S(2)}, u32[]{:S(2)}) %collective-permute-start.7) | collective-permute-done | bytes 32800 | tf_op jit(solution)/shard_map/ppermute | solution.py:220
  69.5 1.6 %collective-permute-start.8 = (f32[64,128]{1,0:T(8,128)S(1)}, f32[64,128]{1,0:T(8,128)S(1)}, u32[]{:S(2)}, u32[]{:S(2)}) collective-permute-start(f32[64,128]{1,0:T(8,128)S(1)} %add_add_fusion.refs_0_), channel_id=1, source_target_pairs={{0,16},{4,20},{8,24},{12,28},{16,0},{20,4},{24,8},{28,12},{1,17},{... | collective-permute-start | bytes 98312 | tf_op jit(solution)/shard_map/ppermute | solution.py:220
  71.1 0.0 collective-permute-done.9.refs_0_
  71.1 2.0 %shard_map.98 = f32[256,512]{1,0:T(8,128)} custom-call(f32[256,512]{1,0:T(8,128)S(1)} %get-tuple-element.49.m_ref, s16[272,512]{1,0:T(8,128)(2,1)S(1)} %collective-permute-done.9.refs_0_, f32[8,512]{1,0:T(8,128)S(1)} %get-tuple-element.32.places_ref.refs_1_.refs_2_, f32[256,256]{1,0:T(8,128)S(1)} %copy-done), custom_call_target="tpu_custom_call" | custom-call | flops 220000000 | bytes 3000000 | tf_op jit(solution)/shard_map/pallas_call | solution.py:202
  73.1 0.4 collective-permute-done.8.refs_1_
  73.5 1.6 %shard_map.99 = bf16[256,512]{1,0:T(8,128)(2,1)} custom-call(f32[64,128]{1,0:T(8,128)S(1)} %add_add_fusion.refs_0_, f32[64,128]{1,0:T(8,128)S(1)} %collective-permute-done.8.refs_1_, f32[8,512]{1,0:T(8,128)S(1)} %get-tuple-element.32.places_ref.refs_1_.refs_2_, bf16[512,128]{1,0:T(8,128)(2,1)S(1)} %copy-done.1, f32[256,256]{1,0:T(8,128)S(1)} %copy-done), custom_call_target="tpu_custom_call" | custom-call | flops 220000000 | bytes 3000000 | tf_op jit(solution)/shard_map/pallas_call | solution.py:202
  (14 shorter events, 0.1 us)
Async XLA Ops:
  0.6 6.2 %copy-start.10 = (bf16[8,512]{1,0:T(8,128)(2,1)S(1)}, bf16[8,512]{1,0:T(8,128)(2,1)}, u32[]{:S(2)}) copy-start(bf16[8,512]{1,0:T(8,128)(2,1)} %constant.53) | copy-start | bytes 24580
  0.6 6.4 %copy-start.8 = (bf16[1152,512]{1,0:T(8,128)(2,1)S(1)}, bf16[1152,512]{1,0:T(8,128)(2,1)}, u32[]{:S(2)}) copy-start(bf16[1152,512]{1,0:T(8,128)(2,1)} %param.9) | copy-start | bytes 3538948
  0.7 6.2 %copy-start.12 = (s32[4,8]{1,0:T(4,128)S(1)}, s32[4,8]{1,0:T(4,128)}, u32[]{:S(2)}) copy-start(s32[4,8]{1,0:T(4,128)} %param.11) | copy-start | bytes 388
  0.7 6.2 %copy-start.11 = (s32[4,8]{1,0:T(4,128)S(1)}, s32[4,8]{1,0:T(4,128)}, u32[]{:S(2)}) copy-start(s32[4,8]{1,0:T(4,128)} %param.12) | copy-start | bytes 388
  0.7 29.4 %collective-permute-start = (bf16[1152,512]{1,0:T(8,128)(2,1)}, bf16[1152,512]{1,0:T(8,128)(2,1)}, u32[]{:S(2)}, u32[]{:S(2)}) collective-permute-start(bf16[1152,512]{1,0:T(8,128)(2,1)} %param.9), channel_id=1, source_target_pairs={{0,1},{1,0},{2,3},{3,2},{4,5},{5,4},{6,7},{7,6},{8,9},{9,8},{10,11... | collective-permute-start | bytes 3538952 | tf_op jit(solution)/shard_map/ppermute | solution.py:255
  3.8 28.0 %collective-permute-start.1 = (bf16[1152,512]{1,0:T(8,128)(2,1)}, bf16[1152,512]{1,0:T(8,128)(2,1)S(1)}, u32[]{:S(2)}, u32[]{:S(2)}) collective-permute-start(bf16[1152,512]{1,0:T(8,128)(2,1)} %param.9), channel_id=1, source_target_pairs={{1,2},{2,1},{5,6},{6,5},{9,10},{10,9},{13,14},{14,13},{17,18},{18,... | collective-permute-start | bytes 3538952 | tf_op jit(solution)/shard_map/ppermute | solution.py:255
  4.5 2.5 %copy-start.9 = (f32[1,256,512]{2,1,0:T(8,128)S(1)}, f32[1,256,512]{2,1,0:T(8,128)}, u32[]{:S(2)}) copy-start(f32[1,256,512]{2,1,0:T(8,128)} %param.10) | copy-start | bytes 1572868
  30.0 25.1 %collective-permute-start.3 = (bf16[1152,512]{1,0:T(8,128)(2,1)}, bf16[1152,512]{1,0:T(8,128)(2,1)S(1)}, u32[]{:S(2)}, u32[]{:S(2)}) collective-permute-start(bf16[1152,512]{1,0:T(8,128)(2,1)} %collective-permute-done), channel_id=1, source_target_pairs={{1,2},{2,1},{5,6},{6,5},{9,10},{10,9},{13,14},{14,13},{17,18},{18,... | collective-permute-start | bytes 3538952 | tf_op jit(solution)/shard_map/ppermute | solution.py:255
  31.7 4.7 %copy-start.6 = (bf16[4608,256]{1,0:T(8,128)(2,1)S(1)}, bf16[4608,256]{1,0:T(8,128)(2,1)}, u32[]{:S(2)}) copy-start(bf16[4608,256]{1,0:T(8,128)(2,1)} %param.8) | copy-start | bytes 7077892
  33.1 3.9 %copy-start.7 = (f32[256,512]{1,0:T(8,128)S(1)}, f32[256,512]{1,0:T(8,128)}, u32[]{:S(2)}) copy-start(f32[256,512]{1,0:T(8,128)} %convolution_add_fusion.1) | copy-start | bytes 1572868
  33.1 20.0 %collective-permute-start.2 = (bf16[784,512]{1,0:T(8,128)(2,1)S(1)}, bf16[784,512]{1,0:T(8,128)(2,1)S(1)}, u32[]{:S(2)}, u32[]{:S(2)}) collective-permute-start(bf16[784,512]{1,0:T(8,128)(2,1)S(1)} %slice_select_fusion), channel_id=1, source_target_pairs={{0,1},{1,0},{2,3},{3,2},{4,5},{5,4},{6,7},{7,6},{8,9},{9,8},{10,11... | collective-permute-start | bytes 2408456 | tf_op jit(solution)/shard_map/ppermute | solution.py:255
  37.0 16.1 %copy-start = (f32[256,256]{1,0:T(8,128)S(1)}, f32[256,256]{1,0:T(8,128)}, u32[]{:S(2)}) copy-start(f32[256,256]{1,0:T(8,128)} %constant.34.clone.refs_1_.refs_2_.refs_4_) | copy-start | bytes 786436
  37.0 16.1 %copy-start.1 = (bf16[512,128]{1,0:T(8,128)(2,1)S(1)}, bf16[512,128]{1,0:T(8,128)(2,1)}, u32[]{:S(2)}) copy-start(bf16[512,128]{1,0:T(8,128)(2,1)} %constant.33.clone.refs_0_.refs_3_) | copy-start | bytes 393220
  54.3 0.8 %copy-start.2 = (bf16[256,1152]{1,0:T(8,128)(2,1)}, bf16[256,1152]{1,0:T(8,128)(2,1)S(1)}, u32[]{:S(2)}) copy-start(bf16[256,1152]{1,0:T(8,128)(2,1)S(1)} %get-tuple-element.45.turned_ref) | copy-start | bytes 1769476
  55.1 1.3 %copy-start.4 = (f32[256,512]{1,0:T(8,128)}, f32[256,512]{1,0:T(8,128)S(1)}, u32[]{:S(2)}) copy-start(f32[256,512]{1,0:T(8,128)S(1)} %get-tuple-element.43.m_ref) | copy-start | bytes 1572868
  55.1 8.3 %copy-start.3 = (bf16[256,1152]{1,0:T(8,128)(2,1)S(1)}, bf16[256,1152]{1,0:T(8,128)(2,1)}, u32[]{:S(2)}) copy-start(bf16[256,1152]{1,0:T(8,128)(2,1)} %copy-done.2) | copy-start | bytes 1769476
  56.4 8.0 %collective-permute-start.4 = (f32[64,128]{1,0:T(8,128)S(1)}, f32[64,128]{1,0:T(8,128)S(1)}, u32[]{:S(2)}, u32[]{:S(2)}) collective-permute-start(f32[64,128]{1,0:T(8,128)S(1)} %get-tuple-element.42), channel_id=1, source_target_pairs={{0,1},{1,0},{2,3},{3,2},{4,5},{5,4},{6,7},{7,6},{8,9},{9,8},{10,11... | collective-permute-start | bytes 98312 | tf_op jit(solution)/shard_map/ppermute | solution.py:255
  62.1 9.0 %collective-permute-start.9 = (s16[272,512]{1,0:T(8,128)(2,1)S(1)}, s16[272,512]{1,0:T(8,128)(2,1)S(1)}, u32[]{:S(2)}, u32[]{:S(2)}) collective-permute-start(s16[272,512]{1,0:T(8,128)(2,1)S(1)} %get-tuple-element.50), channel_id=1, source_target_pairs={{1,0},{2,3},{5,4},{6,7},{9,8},{10,11},{13,12},{14,15},{17,16},{18,... | collective-permute-start | bytes 835592 | tf_op jit(solution)/shard_map/ppermute | solution.py:255
  63.4 1.0 %copy-start.5 = (f32[256,512]{1,0:T(8,128)S(1)}, f32[256,512]{1,0:T(8,128)}, u32[]{:S(2)}) copy-start(f32[256,512]{1,0:T(8,128)} %copy-done.4) | copy-start | bytes 1572868
  64.5 1.9 %collective-permute-start.5 = (f32[64,128]{1,0:T(8,128)S(1)}, f32[64,128]{1,0:T(8,128)S(1)}, u32[]{:S(2)}, u32[]{:S(2)}) collective-permute-start(f32[64,128]{1,0:T(8,128)S(1)} %select_add_fusion), channel_id=1, source_target_pairs={{0,4},{4,0},{8,12},{12,8},{16,20},{20,16},{24,28},{28,24},{1,5},{5... | collective-permute-start | bytes 98312 | tf_op jit(solution)/shard_map/ppermute | solution.py:220
  64.6 4.0 %collective-permute-start.6 = (f32[64,128]{1,0:T(8,128)S(1)}, f32[64,128]{1,0:T(8,128)S(1)}, u32[]{:S(2)}, u32[]{:S(2)}) collective-permute-start(f32[64,128]{1,0:T(8,128)S(1)} %select_add_fusion), channel_id=1, source_target_pairs={{0,8},{4,12},{8,0},{12,4},{16,24},{20,28},{24,16},{28,20},{1,9},{5... | collective-permute-start | bytes 98312 | tf_op jit(solution)/shard_map/ppermute | solution.py:220
  66.2 3.3 %collective-permute-start.7 = (f32[64,128]{1,0:T(8,128)S(1)}, f32[64,128]{1,0:T(8,128)S(1)}, u32[]{:S(2)}, u32[]{:S(2)}) collective-permute-start(f32[64,128]{1,0:T(8,128)S(1)} %select_add_fusion), channel_id=1, source_target_pairs={{0,12},{4,8},{8,4},{12,0},{16,28},{20,24},{24,20},{28,16},{1,13},{... | collective-permute-start | bytes 98312 | tf_op jit(solution)/shard_map/ppermute | solution.py:220
  69.5 4.0 %collective-permute-start.8 = (f32[64,128]{1,0:T(8,128)S(1)}, f32[64,128]{1,0:T(8,128)S(1)}, u32[]{:S(2)}, u32[]{:S(2)}) collective-permute-start(f32[64,128]{1,0:T(8,128)S(1)} %add_add_fusion.refs_0_), channel_id=1, source_target_pairs={{0,16},{4,20},{8,24},{12,28},{16,0},{20,4},{24,8},{28,12},{1,17},{... | collective-permute-start | bytes 98312 | tf_op jit(solution)/shard_map/ppermute | solution.py:220

commit v13 on v12

--- a/solution.py
+++ b/solution.py
@@ -203,8 +203,8 @@
         kernel,
         out_shape=out_shapes,
         in_specs=[pl.BlockSpec(memory_space=space) for space in spaces],
-        compiler_params=pltpu.CompilerParams(vmem_limit_bytes=16 * 2**20),
-        cost_estimate=pl.CostEstimate(flops=22 * 10**7, bytes_accessed=3 * 10**6, transcendentals=0),
+        compiler_params=pltpu.CompilerParams(vmem_limit_bytes=8 * 2**20),
+        cost_estimate=pl.CostEstimate(flops=3 * 10**8, bytes_accessed=4 * 10**6, transcendentals=0),
     )(*operands)
 
 
@@ -302,11 +302,12 @@
     )
     m, end_bands, code = lax.optimization_barrier((m, end_bands, code))
     end_bands = send(end_bands, both_ways)
-    code = send(code, outward)
     flag = end.astype(jnp.int32).reshape(1)
     m, bands = call(
         last_rows_kernel, (full, folded), flag, m, own_bands, own_turned, far_grad, places, *matrices
     )
+    bands, code = lax.optimization_barrier((bands, code))
+    code = send(code, outward)
     end_bands, bands = lax.optimization_barrier((end_bands, bands))
     bands = bands + jnp.where(end, end_bands, 0.0)
     parts = spread_sum(bands, "rep")

time: 76.2 us -> 75.6 us (level); the launches traced: 75 us -> 75.2 us
  no operation moved by 1% of the time
where the time goes in v13:
time: 75.6 us; the launch traced here: 75.2 us
  waiting for transfers between devices  38.5 us (51%)
  starting transfers between devices  18.3 us (24%)
  Pallas kernels  6.1 us (8%)
  matrix products  4.9 us (6%)
  other arithmetic  3.55 us (5%)
  local copies, waits for them, and re-layouts  3.05 us (4%)
  between operations  0.88 us (1%)
    ppermute x6, waiting for transfers between devices, send(): return lax.ppermute(x, 'tp', perm)  35.5 us
    ppermute x6, starting transfers between devices, send(): return lax.ppermute(x, 'tp', perm)  14.7 us
    pallas_call x5, Pallas kernels, call(): pl.pallas_call(kernel, out_shape=out_shapes, in_specs=[pl.BlockSpec(memor...  6.1 us
    dot_general x4, matrix products, dot(): lax.dot_general(a, b, (dims, ((), ())), preferred_element_type=jnp.float32)  4.9 us
    ppermute x4, starting transfers between devices, spread_sum(): lax.ppermute(x, axis, [(i, i ^ stride * k) for i in range(size)])  3.52 us
    ppermute x4, waiting for transfers between devices, spread_sum(): lax.ppermute(x, axis, [(i, i ^ stride * k) for i in range(size)])  3.04 us
    unnamed x26, local copies, waits for them, and re-layouts  1.9 us
  transfers between devices with their start and end apart: 10, of which 5 were waited for; matrix products, arithmetic and copies ran while one was open for 13% of the time, Pallas kernels for 4%

profile of v13, /device:TPU:0, one launch (start us, length us, event | category | flops | bytes accessed | tf_op | source)
XLA Modules:
  0.0 75.2 jit_solution(2446484542624786682)
XLA Ops:
  0.6 0.0 copy-start.10
  0.6 0.0 copy-start.8
  0.7 0.0 copy-start.12
  0.7 0.0 copy-start.11
  0.7 3.1 %collective-permute-start = (bf16[1152,512]{1,0:T(8,128)(2,1)}, bf16[1152,512]{1,0:T(8,128)(2,1)}, u32[]{:S(2)}, u32[]{:S(2)}) collective-permute-start(bf16[1152,512]{1,0:T(8,128)(2,1)} %param.9), channel_id=1, source_target_pairs={{0,1},{1,0},{2,3},{3,2},{4,5},{5,4},{6,7},{7,6},{8,9},{9,8},{10,11... | collective-permute-start | bytes 3538952 | tf_op jit(solution)/shard_map/ppermute | solution.py:255
  3.8 0.7 collective-permute-start.1
  4.5 0.0 copy-start.9
  4.5 1.1 %constant_dynamic-slice_fusion.3 = (bf16[384,256]{1,0:T(8,128)(2,1)S(1)}, bf16[384,256]{1,0:T(8,128)(2,1)S(1)}) fusion(bf16[4608,256]{1,0:T(8,128)(2,1)} %param.8, s32[]{:T(128)S(6)} %select_n.48, s32[]{:T(128)S(6)} %select_n.50), kind=kLoop, calls=%fused_computation.25 | loop fusion | bytes 786440 | tf_op jit(solution)/shard_map/dynamic_slice | solution.py:252
  5.6 1.2 %dynamic-slice_select_fusion = (bf16[768,256]{1,0:T(8,128)(2,1)S(1)}, bf16[768,256]{1,0:T(8,128)(2,1)S(1)}) fusion(bf16[4608,256]{1,0:T(8,128)(2,1)} %param.8, s32[]{:T(128)S(6)} %select_n.52, pred[]{:T(512)S(6)} %or.3, s32[]{:T(128)S(6)} %add.58), kind=kLoop, calls=%fused_computation.11 | loop fusion | flops 196608 | bytes 1572873 | tf_op jit(solution)/shard_map/jit(_where)/select_n | solution.py:274
  6.8 0.0 copy-done.10
  6.9 0.0 copy-done.12
  6.9 0.1 fusion.14
  7.0 0.0 copy-done.8
  7.0 2.4 %convolution_add_fusion.1 = f32[256,512]{1,0:T(8,128)} fusion(bf16[1152,512]{1,0:T(8,128)(2,1)S(1)} %copy-done.8, bf16[4608,256]{1,0:T(8,128)(2,1)} %param.8, s32[]{:T(128)S(6)} %select_n.54, f32[1,256,512]{2,1,0:T(8,128)S(1)} %copy-done.9), kind=kOutput, calls=%fused_computation.4 | convolution fusion | flops 302252032 | bytes 2818052 | tf_op jit(solution)/shard_map/dot_general | solution.py:45
  9.4 20.7 %collective-permute-done = bf16[1152,512]{1,0:T(8,128)(2,1)} collective-permute-done((bf16[1152,512]{1,0:T(8,128)(2,1)}, bf16[1152,512]{1,0:T(8,128)(2,1)}, u32[]{:S(2)}, u32[]{:S(2)}) %collective-permute-start) | collective-permute-done | bytes 1179680 | tf_op jit(solution)/shard_map/ppermute | solution.py:255
  30.0 0.7 collective-permute-start.3
  30.8 1.0 %fusion.2 = bf16[784,512]{1,0:T(8,128)(2,1)} fusion(bf16[8,512]{1,0:T(8,128)(2,1)S(1)} %get-tuple-element.62, bf16[768,256]{1,0:T(8,128)(2,1)S(1)} %get-tuple-element.59, bf16[384,256]{1,0:T(8,128)(2,1)S(1)} %get-tuple-element.61, bf16[384,256]{1,0:T(8,128)(2,1)S(1)} %get-tuple-element.60), kind=kLoop, calls=%fused_computation.5 | loop fusion | flops 4014080 | bytes 1597440 | tf_op jit(solution)/shard_map/concatenate | solution.py:273
  31.7 0.0 collective-permute-done.1.cross_ref
  31.8 1.4 %slice_select_fusion = bf16[784,512]{1,0:T(8,128)(2,1)S(1)} fusion(bf16[784,512]{1,0:T(8,128)(2,1)} %fusion.2, bf16[1152,512]{1,0:T(8,128)(2,1)S(1)} %collective-permute-done.1.cross_ref, pred[]{:T(512)S(6)} %or.3), kind=kLoop, calls=%fused_computation.6 | loop fusion | flops 401408 | bytes 2408449 | tf_op jit(solution)/shard_map/jit(_where)/select_n | solution.py:279
  33.1 0.0 copy-start.7
  33.1 3.3 %collective-permute-start.2 = (bf16[784,512]{1,0:T(8,128)(2,1)S(1)}, bf16[784,512]{1,0:T(8,128)(2,1)S(1)}, u32[]{:S(2)}, u32[]{:S(2)}) collective-permute-start(bf16[784,512]{1,0:T(8,128)(2,1)S(1)} %slice_select_fusion), channel_id=1, source_target_pairs={{0,1},{1,0},{2,3},{3,2},{4,5},{5,4},{6,7},{7,6},{8,9},{9,8},{10,11... | collective-permute-start | bytes 2408456 | tf_op jit(solution)/shard_map/ppermute | solution.py:255
  36.4 0.0 copy-done.6
  36.5 0.5 fusion.3
  37.0 0.0 copy-start
  37.0 0.0 copy-start.1
  37.0 1.9 %fusion.1.m_ref = f32[256,512]{1,0:T(8,128)S(1)} fusion(f32[256,512]{1,0:T(8,128)S(1)} %fusion.3, f32[256,512]{1,0:T(8,128)S(1)} %copy-done.7, bf16[1152,512]{1,0:T(8,128)(2,1)} %collective-permute-done, bf16[4608,256]{1,0:T(8,128)(2,1)S(1)} %copy-done.6, s32[]{:T(128)S(6)} %select_n.55), kind=kOutput, calls=%fused_computation.3 | convolution fusion | flops 302252032 | bytes 3342340 | tf_op jit(solution)/shard_map/dot_general | solution.py:45
  38.9 14.3 %collective-permute-done.2.swapped_ref = bf16[784,512]{1,0:T(8,128)(2,1)S(1)} collective-permute-done((bf16[784,512]{1,0:T(8,128)(2,1)S(1)}, bf16[784,512]{1,0:T(8,128)(2,1)S(1)}, u32[]{:S(2)}, u32[]{:S(2)}) %collective-permute-start.2) | collective-permute-done | bytes 802848 | tf_op jit(solution)/shard_map/ppermute | solution.py:255
  53.2 0.0 copy-done.1
  53.2 1.2 %shard_map.95 = (f32[256,512]{1,0:T(8,128)S(1)}, f32[256,512]{1,0:T(8,128)S(1)}, bf16[256,1152]{1,0:T(8,128)(2,1)S(1)}, bf16[256,1152]{1,0:T(8,128)(2,1)S(1)}, f...) custom-call(f32[256,512]{1,0:T(8,128)S(1)} %fusion.1.m_ref, ...), custom_call_target="tpu_custom_call" | custom-call | flops 300000000 | bytes 4000000 | tf_op jit(solution)/shard_map/pallas_call | solution.py:202
  54.3 0.8 %copy-done.2 = bf16[256,1152]{1,0:T(8,128)(2,1)} copy-done((bf16[256,1152]{1,0:T(8,128)(2,1)}, bf16[256,1152]{1,0:T(8,128)(2,1)S(1)}, u32[]{:S(2)}) %copy-start.2) | copy-done | bytes 589848
  55.1 0.0 collective-permute-done.3.far_ref
  55.1 1.3 %shard_map.96 = (s16[272,512]{1,0:T(8,128)(2,1)S(1)}, f32[64,128]{1,0:T(8,128)S(1)}) custom-call(f32[256,512]{1,0:T(8,128)S(1)} %get-tuple-element.38.helped_ref, bf16[256,1152]{1,0:T(8,128)(2,1)S(1)} %get-tuple-element.39.turned_ref, bf16[1152,512]{1,0:T(8,128)(2,1)S(1)} %collective-permute-done.3.far_ref, f32[16,512]{1,0:T(8,128)S(1)} %get-tuple-element.41.places_ref, ...), custom_call_target="tpu_custom_call" | custom-call | flops 300000000 | bytes 4000000 | tf_op jit(solution)/shard_map/pallas_call | solution.py:202
  56.4 5.7 %collective-permute-start.4 = (f32[64,128]{1,0:T(8,128)S(1)}, f32[64,128]{1,0:T(8,128)S(1)}, u32[]{:S(2)}, u32[]{:S(2)}) collective-permute-start(f32[64,128]{1,0:T(8,128)S(1)} %get-tuple-element.44), channel_id=1, source_target_pairs={{0,1},{1,0},{2,3},{3,2},{4,5},{5,4},{6,7},{7,6},{8,9},{9,8},{10,11... | collective-permute-start | bytes 98312 | tf_op jit(solution)/shard_map/ppermute | solution.py:255
  62.1 0.0 copy-done.3
  62.1 1.0 %copy-done.5 = f32[256,512]{1,0:T(8,128)S(1)} copy-done((f32[256,512]{1,0:T(8,128)S(1)}, f32[256,512]{1,0:T(8,128)}, u32[]{:S(2)}) %copy-start.5) | copy-done | bytes 524312
  63.2 1.3 %collective-permute-start.9 = (s16[272,512]{1,0:T(8,128)(2,1)S(1)}, s16[272,512]{1,0:T(8,128)(2,1)S(1)}, u32[]{:S(2)}, u32[]{:S(2)}) collective-permute-start(s16[272,512]{1,0:T(8,128)(2,1)S(1)} %get-tuple-element.54), channel_id=1, source_target_pairs={{1,0},{2,3},{5,4},{6,7},{9,8},{10,11},{13,12},{14,15},{17,16},{18,... | collective-permute-start | bytes 835592 | tf_op jit(solution)/shard_map/ppermute | solution.py:255
  64.5 0.0 collective-permute-done.4
  64.5 0.1 collective-permute-start.5
  64.6 1.6 %collective-permute-start.6 = (f32[64,128]{1,0:T(8,128)S(1)}, f32[64,128]{1,0:T(8,128)S(1)}, u32[]{:S(2)}, u32[]{:S(2)}) collective-permute-start(f32[64,128]{1,0:T(8,128)S(1)} %select_add_fusion), channel_id=1, source_target_pairs={{0,8},{4,12},{8,0},{12,4},{16,24},{20,28},{24,16},{28,20},{1,9},{5... | collective-permute-start | bytes 98312 | tf_op jit(solution)/shard_map/ppermute | solution.py:220
  66.2 0.3 collective-permute-start.7
  66.5 0.0 collective-permute-done.5
  66.5 2.1 %collective-permute-done.6 = f32[64,128]{1,0:T(8,128)S(1)} collective-permute-done((f32[64,128]{1,0:T(8,128)S(1)}, f32[64,128]{1,0:T(8,128)S(1)}, u32[]{:S(2)}, u32[]{:S(2)}) %collective-permute-start.6) | collective-permute-done | bytes 32800 | tf_op jit(solution)/shard_map/ppermute | solution.py:220
  68.6 0.9 %collective-permute-done.7 = f32[64,128]{1,0:T(8,128)S(1)} collective-permute-done((f32[64,128]{1,0:T(8,128)S(1)}, f32[64,128]{1,0:T(8,128)S(1)}, u32[]{:S(2)}, u32[]{:S(2)}) %collective-permute-start.7) | collective-permute-done | bytes 32800 | tf_op jit(solution)/shard_map/ppermute | solution.py:220
  69.5 1.6 %collective-permute-start.8 = (f32[64,128]{1,0:T(8,128)S(1)}, f32[64,128]{1,0:T(8,128)S(1)}, u32[]{:S(2)}, u32[]{:S(2)}) collective-permute-start(f32[64,128]{1,0:T(8,128)S(1)} %add_add_fusion.refs_0_), channel_id=1, source_target_pairs={{0,16},{4,20},{8,24},{12,28},{16,0},{20,4},{24,8},{28,12},{1,17},{... | collective-permute-start | bytes 98312 | tf_op jit(solution)/shard_map/ppermute | solution.py:220
  71.1 0.5 collective-permute-done.9.refs_0_
  71.6 2.0 %shard_map.98 = f32[256,512]{1,0:T(8,128)} custom-call(f32[256,512]{1,0:T(8,128)S(1)} %get-tuple-element.53.m_ref, s16[272,512]{1,0:T(8,128)(2,1)S(1)} %collective-permute-done.9.refs_0_, f32[8,512]{1,0:T(8,128)S(1)} %get-tuple-element.34.places_ref.refs_1_.refs_2_, f32[256,256]{1,0:T(8,128)S(1)} %copy-done), custom_call_target="tpu_custom_call" | custom-call | flops 300000000 | bytes 4000000 | tf_op jit(solution)/shard_map/pallas_call | solution.py:202
  73.7 0.0 collective-permute-done.8.refs_1_
  73.7 1.6 %shard_map.99 = bf16[256,512]{1,0:T(8,128)(2,1)} custom-call(f32[64,128]{1,0:T(8,128)S(1)} %add_add_fusion.refs_0_, f32[64,128]{1,0:T(8,128)S(1)} %collective-permute-done.8.refs_1_, f32[8,512]{1,0:T(8,128)S(1)} %get-tuple-element.34.places_ref.refs_1_.refs_2_, bf16[512,128]{1,0:T(8,128)(2,1)S(1)} %copy-done.1, f32[256,256]{1,0:T(8,128)S(1)} %copy-done), custom_call_target="tpu_custom_call" | custom-call | flops 300000000 | bytes 4000000 | tf_op jit(solution)/shard_map/pallas_call | solution.py:202
  (14 shorter events, 0.1 us)
Async XLA Ops:
  0.6 6.2 %copy-start.10 = (bf16[8,512]{1,0:T(8,128)(2,1)S(1)}, bf16[8,512]{1,0:T(8,128)(2,1)}, u32[]{:S(2)}) copy-start(bf16[8,512]{1,0:T(8,128)(2,1)} %constant.53) | copy-start | bytes 24580
  0.6 6.4 %copy-start.8 = (bf16[1152,512]{1,0:T(8,128)(2,1)S(1)}, bf16[1152,512]{1,0:T(8,128)(2,1)}, u32[]{:S(2)}) copy-start(bf16[1152,512]{1,0:T(8,128)(2,1)} %param.9) | copy-start | bytes 3538948
  0.7 6.2 %copy-start.12 = (s32[4,8]{1,0:T(4,128)S(1)}, s32[4,8]{1,0:T(4,128)}, u32[]{:S(2)}) copy-start(s32[4,8]{1,0:T(4,128)} %param.11) | copy-start | bytes 388
  0.7 6.2 %copy-start.11 = (s32[4,8]{1,0:T(4,128)S(1)}, s32[4,8]{1,0:T(4,128)}, u32[]{:S(2)}) copy-start(s32[4,8]{1,0:T(4,128)} %param.12) | copy-start | bytes 388
  0.7 29.4 %collective-permute-start = (bf16[1152,512]{1,0:T(8,128)(2,1)}, bf16[1152,512]{1,0:T(8,128)(2,1)}, u32[]{:S(2)}, u32[]{:S(2)}) collective-permute-start(bf16[1152,512]{1,0:T(8,128)(2,1)} %param.9), channel_id=1, source_target_pairs={{0,1},{1,0},{2,3},{3,2},{4,5},{5,4},{6,7},{7,6},{8,9},{9,8},{10,11... | collective-permute-start | bytes 3538952 | tf_op jit(solution)/shard_map/ppermute | solution.py:255
  3.8 28.0 %collective-permute-start.1 = (bf16[1152,512]{1,0:T(8,128)(2,1)}, bf16[1152,512]{1,0:T(8,128)(2,1)S(1)}, u32[]{:S(2)}, u32[]{:S(2)}) collective-permute-start(bf16[1152,512]{1,0:T(8,128)(2,1)} %param.9), channel_id=1, source_target_pairs={{1,2},{2,1},{5,6},{6,5},{9,10},{10,9},{13,14},{14,13},{17,18},{18,... | collective-permute-start | bytes 3538952 | tf_op jit(solution)/shard_map/ppermute | solution.py:255
  4.5 2.5 %copy-start.9 = (f32[1,256,512]{2,1,0:T(8,128)S(1)}, f32[1,256,512]{2,1,0:T(8,128)}, u32[]{:S(2)}) copy-start(f32[1,256,512]{2,1,0:T(8,128)} %param.10) | copy-start | bytes 1572868
  30.0 25.1 %collective-permute-start.3 = (bf16[1152,512]{1,0:T(8,128)(2,1)}, bf16[1152,512]{1,0:T(8,128)(2,1)S(1)}, u32[]{:S(2)}, u32[]{:S(2)}) collective-permute-start(bf16[1152,512]{1,0:T(8,128)(2,1)} %collective-permute-done), channel_id=1, source_target_pairs={{1,2},{2,1},{5,6},{6,5},{9,10},{10,9},{13,14},{14,13},{17,18},{18,... | collective-permute-start | bytes 3538952 | tf_op jit(solution)/shard_map/ppermute | solution.py:255
  31.7 4.7 %copy-start.6 = (bf16[4608,256]{1,0:T(8,128)(2,1)S(1)}, bf16[4608,256]{1,0:T(8,128)(2,1)}, u32[]{:S(2)}) copy-start(bf16[4608,256]{1,0:T(8,128)(2,1)} %param.8) | copy-start | bytes 7077892
  33.1 3.9 %copy-start.7 = (f32[256,512]{1,0:T(8,128)S(1)}, f32[256,512]{1,0:T(8,128)}, u32[]{:S(2)}) copy-start(f32[256,512]{1,0:T(8,128)} %convolution_add_fusion.1) | copy-start | bytes 1572868
  33.1 20.0 %collective-permute-start.2 = (bf16[784,512]{1,0:T(8,128)(2,1)S(1)}, bf16[784,512]{1,0:T(8,128)(2,1)S(1)}, u32[]{:S(2)}, u32[]{:S(2)}) collective-permute-start(bf16[784,512]{1,0:T(8,128)(2,1)S(1)} %slice_select_fusion), channel_id=1, source_target_pairs={{0,1},{1,0},{2,3},{3,2},{4,5},{5,4},{6,7},{7,6},{8,9},{9,8},{10,11... | collective-permute-start | bytes 2408456 | tf_op jit(solution)/shard_map/ppermute | solution.py:255
  37.0 16.1 %copy-start = (f32[256,256]{1,0:T(8,128)S(1)}, f32[256,256]{1,0:T(8,128)}, u32[]{:S(2)}) copy-start(f32[256,256]{1,0:T(8,128)} %constant.34.clone.refs_1_.refs_2_.refs_4_) | copy-start | bytes 786436
  37.0 16.1 %copy-start.1 = (bf16[512,128]{1,0:T(8,128)(2,1)S(1)}, bf16[512,128]{1,0:T(8,128)(2,1)}, u32[]{:S(2)}) copy-start(bf16[512,128]{1,0:T(8,128)(2,1)} %constant.33.clone.refs_0_.refs_3_) | copy-start | bytes 393220
  54.3 0.8 %copy-start.2 = (bf16[256,1152]{1,0:T(8,128)(2,1)}, bf16[256,1152]{1,0:T(8,128)(2,1)S(1)}, u32[]{:S(2)}) copy-start(bf16[256,1152]{1,0:T(8,128)(2,1)S(1)} %get-tuple-element.47.turned_ref) | copy-start | bytes 1769476
  55.1 1.3 %copy-start.4 = (f32[256,512]{1,0:T(8,128)}, f32[256,512]{1,0:T(8,128)S(1)}, u32[]{:S(2)}) copy-start(f32[256,512]{1,0:T(8,128)S(1)} %get-tuple-element.45.m_ref) | copy-start | bytes 1572868
  55.1 7.0 %copy-start.3 = (bf16[256,1152]{1,0:T(8,128)(2,1)S(1)}, bf16[256,1152]{1,0:T(8,128)(2,1)}, u32[]{:S(2)}) copy-start(bf16[256,1152]{1,0:T(8,128)(2,1)} %copy-done.2) | copy-start | bytes 1769476
  56.4 8.0 %collective-permute-start.4 = (f32[64,128]{1,0:T(8,128)S(1)}, f32[64,128]{1,0:T(8,128)S(1)}, u32[]{:S(2)}, u32[]{:S(2)}) collective-permute-start(f32[64,128]{1,0:T(8,128)S(1)} %get-tuple-element.44), channel_id=1, source_target_pairs={{0,1},{1,0},{2,3},{3,2},{4,5},{5,4},{6,7},{7,6},{8,9},{9,8},{10,11... | collective-permute-start | bytes 98312 | tf_op jit(solution)/shard_map/ppermute | solution.py:255
  62.1 1.0 %copy-start.5 = (f32[256,512]{1,0:T(8,128)S(1)}, f32[256,512]{1,0:T(8,128)}, u32[]{:S(2)}) copy-start(f32[256,512]{1,0:T(8,128)} %copy-done.4) | copy-start | bytes 1572868
  63.2 8.4 %collective-permute-start.9 = (s16[272,512]{1,0:T(8,128)(2,1)S(1)}, s16[272,512]{1,0:T(8,128)(2,1)S(1)}, u32[]{:S(2)}, u32[]{:S(2)}) collective-permute-start(s16[272,512]{1,0:T(8,128)(2,1)S(1)} %get-tuple-element.54), channel_id=1, source_target_pairs={{1,0},{2,3},{5,4},{6,7},{9,8},{10,11},{13,12},{14,15},{17,16},{18,... | collective-permute-start | bytes 835592 | tf_op jit(solution)/shard_map/ppermute | solution.py:255
  64.5 1.9 %collective-permute-start.5 = (f32[64,128]{1,0:T(8,128)S(1)}, f32[64,128]{1,0:T(8,128)S(1)}, u32[]{:S(2)}, u32[]{:S(2)}) collective-permute-start(f32[64,128]{1,0:T(8,128)S(1)} %select_add_fusion), channel_id=1, source_target_pairs={{0,4},{4,0},{8,12},{12,8},{16,20},{20,16},{24,28},{28,24},{1,5},{5... | collective-permute-start | bytes 98312 | tf_op jit(solution)/shard_map/ppermute | solution.py:220
  64.6 4.0 %collective-permute-start.6 = (f32[64,128]{1,0:T(8,128)S(1)}, f32[64,128]{1,0:T(8,128)S(1)}, u32[]{:S(2)}, u32[]{:S(2)}) collective-permute-start(f32[64,128]{1,0:T(8,128)S(1)} %select_add_fusion), channel_id=1, source_target_pairs={{0,8},{4,12},{8,0},{12,4},{16,24},{20,28},{24,16},{28,20},{1,9},{5... | collective-permute-start | bytes 98312 | tf_op jit(solution)/shard_map/ppermute | solution.py:220
  66.2 3.3 %collective-permute-start.7 = (f32[64,128]{1,0:T(8,128)S(1)}, f32[64,128]{1,0:T(8,128)S(1)}, u32[]{:S(2)}, u32[]{:S(2)}) collective-permute-start(f32[64,128]{1,0:T(8,128)S(1)} %select_add_fusion), channel_id=1, source_target_pairs={{0,12},{4,8},{8,4},{12,0},{16,28},{20,24},{24,20},{28,16},{1,13},{... | collective-permute-start | bytes 98312 | tf_op jit(solution)/shard_map/ppermute | solution.py:220
  69.5 4.2 %collective-permute-start.8 = (f32[64,128]{1,0:T(8,128)S(1)}, f32[64,128]{1,0:T(8,128)S(1)}, u32[]{:S(2)}, u32[]{:S(2)}) collective-permute-start(f32[64,128]{1,0:T(8,128)S(1)} %add_add_fusion.refs_0_), channel_id=1, source_target_pairs={{0,16},{4,20},{8,24},{12,28},{16,0},{20,4},{24,8},{28,12},{1,17},{... | collective-permute-start | bytes 98312 | tf_op jit(solution)/shard_map/ppermute | solution.py:220

commit v14 on v13

--- a/solution.py
+++ b/solution.py
@@ -174,13 +174,14 @@
         bands_ref[...] = bands_of(out_ref[...], places_ref[...], *matrix_refs)
 
 
-def remove_kernel(m_ref, *refs):
-    *code_refs, places_ref, basis_ref, out_ref = refs
-    m = m_ref[...]
-    for ref in code_refs:
-        m = m + decoded(ref)
-    masks = masks_of(places_ref[...], m.shape[0] // order)
-    out_ref[...] = m - restored(selected(m, masks, basis_ref), masks, basis_ref)
+def remove_kernel(m_ref, bands_ref, places_ref, fold_ref, basis_ref, out_ref):
+    masks = masks_of(places_ref[...], out_ref.shape[0] // order)
+    coefficients = within(spread(bands_ref[...], fold_ref[...]), masks)
+    out_ref[...] = m_ref[...] - restored(coefficients, masks, basis_ref)
+
+
+def add_kernel(x_ref, code_ref, out_ref):
+    out_ref[...] = x_ref[...] + decoded(code_ref)
 
 
 def update_kernel(*refs):
@@ -203,8 +204,8 @@
         kernel,
         out_shape=out_shapes,
         in_specs=[pl.BlockSpec(memory_space=space) for space in spaces],
-        compiler_params=pltpu.CompilerParams(vmem_limit_bytes=8 * 2**20),
-        cost_estimate=pl.CostEstimate(flops=3 * 10**8, bytes_accessed=4 * 10**6, transcendentals=0),
+        compiler_params=pltpu.CompilerParams(vmem_limit_bytes=16 * 2**20),
+        cost_estimate=pl.CostEstimate(flops=4 * 10**8, bytes_accessed=4 * 10**6, transcendentals=0),
     )(*operands)
 
 
@@ -235,7 +236,7 @@
     m = carried + product(hidden, lax.all_gather(out_grad, "tp", axis=0, tiled=True))
     folded = jax.ShapeDtypeStruct((m.shape[0] // steps, m.shape[1] // steps), jnp.float32)
     bands = call(bands_kernel, folded, m, places, *matrices)
-    return [m], spread_sum(bands, "rep"), places, matrices
+    return m, bands, None, spread_sum(bands, "rep"), places, matrices
 
 
 def lined(hidden, out_grad, carried, places, matrices):
@@ -311,7 +312,7 @@
     end_bands, bands = lax.optimization_barrier((end_bands, bands))
     bands = bands + jnp.where(end, end_bands, 0.0)
     parts = spread_sum(bands, "rep")
-    return [m, code], parts, places, matrices
+    return m, bands, code, parts, places, matrices
 
 
 def local(hidden, out_grad, momentum, band_rows, band_start_columns):
@@ -323,15 +324,15 @@
     places = dot(places, one_hot)
     fits = out_grad.shape[0] % 384 == 0 and 2 * row_count == col_count and places.shape[0] <= place_rows
     form = lined if fits and lax.axis_size("tp") == 4 else gathered
-    m_parts, band_parts, places, matrices = form(
+    m, bands, code, band_parts, places, matrices = form(
         hidden, out_grad, decay_rate * momentum[0], places, matrices
     )
-    shape = (row_count, col_count)
-    momentum_out = call(
-        remove_kernel, jax.ShapeDtypeStruct(shape, jnp.float32), *m_parts, places, matrices[1]
-    )
+    full = jax.ShapeDtypeStruct(m.shape, jnp.float32)
+    momentum_out = call(remove_kernel, full, m, bands, places, *matrices)
+    if code is not None:
+        momentum_out = call(add_kernel, full, momentum_out, code)
     *band_parts, momentum_out = lax.optimization_barrier((*band_parts, momentum_out))
-    update = call(update_kernel, jax.ShapeDtypeStruct(shape, jnp.bfloat16), *band_parts, places, *matrices)
+    update = call(update_kernel, jax.ShapeDtypeStruct(m.shape, jnp.bfloat16), *band_parts, places, *matrices)
     return (momentum_out[None], update)
 
 

time: 75.6 us -> 74.8 us (0.989)
  local copies, waits for them, and re-layouts: 3.05 us -> 1.19 us
  waiting for transfers between devices: 38.5 us -> 40 us
  matrix products: 4.9 us -> 4.1 us
    unnamed x26 -> x16, local copies, waits for them, and re-layouts: 1.9 us -> 0.04 us
    ppermute x6, waiting for transfers between devices: 35.5 us -> 36.3 us  [send(): return lax.ppermute(x, 'tp', perm)]
    ppermute x6, starting transfers between devices: 14.7 us -> 15.6 us  [send(): return lax.ppermute(x, 'tp', perm)]
    dot_general x4, matrix products: 4.9 us -> 4.1 us  [dot(): lax.dot_general(a, b, (dims, ((), ())), preferred_element_type=jnp.float32)]
    pallas_call x5 -> x6, Pallas kernels: 6.1 us -> 5.78 us  [call(): pl.pallas_call(kernel, out_shape=out_shapes, in_specs=[pl.BlockSpec(memor...]
  transfers between devices with their start and end apart: 10 -> 10, of which waited for: 5 -> 7; matrix products, arithmetic and copies ran while one was open for 13% -> 12% of each run, Pallas kernels for 4% -> 4%
where the time goes in v14:
time: 74.8 us; the launch traced here: 74.5 us
  waiting for transfers between devices  40 us (53%)
  starting transfers between devices  19 us (25%)
  Pallas kernels  5.78 us (8%)
  matrix products  4.1 us (5%)
  other arithmetic  3.56 us (5%)
  local copies, waits for them, and re-layouts  1.19 us (2%)
  between operations  0.85 us (1%)
    ppermute x6, waiting for transfers between devices, send(): return lax.ppermute(x, 'tp', perm)  36.3 us
    ppermute x6, starting transfers between devices, send(): return lax.ppermute(x, 'tp', perm)  15.6 us
    pallas_call x6, Pallas kernels, call(): pl.pallas_call(kernel, out_shape=out_shapes, in_specs=[pl.BlockSpec(memor...  5.78 us
    dot_general x4, matrix products, dot(): lax.dot_general(a, b, (dims, ((), ())), preferred_element_type=jnp.float32)  4.1 us
    ppermute x4, waiting for transfers between devices, spread_sum(): lax.ppermute(x, axis, [(i, i ^ stride * k) for i in range(size)])  3.64 us
    ppermute x4, starting transfers between devices, spread_sum(): lax.ppermute(x, axis, [(i, i ^ stride * k) for i in range(size)])  3.44 us
  transfers between devices with their start and end apart: 10, of which 7 were waited for; matrix products, arithmetic and copies ran while one was open for 12% of the time, Pallas kernels for 4%

profile of v14, /device:TPU:0, one launch (start us, length us, event | category | flops | bytes accessed | tf_op | source)
XLA Modules:
  0.0 74.5 jit_solution(6067308647671685152)
XLA Ops:
  0.6 0.0 copy-start.5
  0.6 0.0 copy-start.3
  0.7 0.0 copy-start.7
  0.7 0.0 copy-start.6
  0.7 3.1 %collective-permute-start = (bf16[1152,512]{1,0:T(8,128)(2,1)}, bf16[1152,512]{1,0:T(8,128)(2,1)}, u32[]{:S(2)}, u32[]{:S(2)}) collective-permute-start(bf16[1152,512]{1,0:T(8,128)(2,1)} %param.9), channel_id=1, source_target_pairs={{0,1},{1,0},{2,3},{3,2},{4,5},{5,4},{6,7},{7,6},{8,9},{9,8},{10,11... | collective-permute-start | bytes 3538952 | tf_op jit(solution)/shard_map/ppermute | solution.py:256
  3.8 0.7 collective-permute-start.1
  4.5 0.0 copy-start.4
  4.5 1.1 %constant_dynamic-slice_fusion.3 = (bf16[384,256]{1,0:T(8,128)(2,1)S(1)}, bf16[384,256]{1,0:T(8,128)(2,1)S(1)}) fusion(bf16[4608,256]{1,0:T(8,128)(2,1)} %param.8, s32[]{:T(128)S(6)} %select_n.48, s32[]{:T(128)S(6)} %select_n.50), kind=kLoop, calls=%fused_computation.25 | loop fusion | bytes 786440 | tf_op jit(solution)/shard_map/dynamic_slice | solution.py:253
  5.6 1.2 %dynamic-slice_select_fusion = (bf16[768,256]{1,0:T(8,128)(2,1)S(1)}, bf16[768,256]{1,0:T(8,128)(2,1)S(1)}) fusion(bf16[4608,256]{1,0:T(8,128)(2,1)} %param.8, s32[]{:T(128)S(6)} %select_n.52, pred[]{:T(512)S(6)} %or.3, s32[]{:T(128)S(6)} %add.58), kind=kLoop, calls=%fused_computation.11 | loop fusion | flops 196608 | bytes 1572873 | tf_op jit(solution)/shard_map/jit(_where)/select_n | solution.py:275
  6.8 0.0 copy-done.5
  6.9 0.0 copy-done.7
  6.9 0.0 copy-done.6
  6.9 0.1 fusion.14
  7.0 0.0 copy-done.3
  7.0 0.0 copy-done.4
  7.0 1.6 %convolution_add_fusion.1 = f32[256,512]{1,0:T(8,128)S(1)} fusion(bf16[1152,512]{1,0:T(8,128)(2,1)S(1)} %copy-done.3, bf16[4608,256]{1,0:T(8,128)(2,1)} %param.8, s32[]{:T(128)S(6)} %select_n.54, f32[1,256,512]{2,1,0:T(8,128)S(1)} %copy-done.4), kind=kOutput, calls=%fused_computation.4 | convolution fusion | flops 302252032 | bytes 2818052 | tf_op jit(solution)/shard_map/dot_general | solution.py:45
  8.6 21.5 %collective-permute-done = bf16[1152,512]{1,0:T(8,128)(2,1)} collective-permute-done((bf16[1152,512]{1,0:T(8,128)(2,1)}, bf16[1152,512]{1,0:T(8,128)(2,1)}, u32[]{:S(2)}, u32[]{:S(2)}) %collective-permute-start) | collective-permute-done | bytes 1179680 | tf_op jit(solution)/shard_map/ppermute | solution.py:256
  30.0 0.7 collective-permute-start.3
  30.8 1.0 %fusion.2 = bf16[784,512]{1,0:T(8,128)(2,1)} fusion(bf16[8,512]{1,0:T(8,128)(2,1)S(1)} %get-tuple-element.62, bf16[768,256]{1,0:T(8,128)(2,1)S(1)} %get-tuple-element.59, bf16[384,256]{1,0:T(8,128)(2,1)S(1)} %get-tuple-element.61, bf16[384,256]{1,0:T(8,128)(2,1)S(1)} %get-tuple-element.60), kind=kLoop, calls=%fused_computation.5 | loop fusion | flops 4014080 | bytes 1597440 | tf_op jit(solution)/shard_map/concatenate | solution.py:274
  31.8 0.0 collective-permute-done.1.cross_ref
  31.8 1.4 %slice_select_fusion = bf16[784,512]{1,0:T(8,128)(2,1)S(1)} fusion(bf16[784,512]{1,0:T(8,128)(2,1)} %fusion.2, bf16[1152,512]{1,0:T(8,128)(2,1)S(1)} %collective-permute-done.1.cross_ref, pred[]{:T(512)S(6)} %or.3), kind=kLoop, calls=%fused_computation.6 | loop fusion | flops 401408 | bytes 2408449 | tf_op jit(solution)/shard_map/jit(_where)/select_n | solution.py:280
  33.1 3.3 %collective-permute-start.2 = (bf16[784,512]{1,0:T(8,128)(2,1)S(1)}, bf16[784,512]{1,0:T(8,128)(2,1)S(1)}, u32[]{:S(2)}, u32[]{:S(2)}) collective-permute-start(bf16[784,512]{1,0:T(8,128)(2,1)S(1)} %slice_select_fusion), channel_id=1, source_target_pairs={{0,1},{1,0},{2,3},{3,2},{4,5},{5,4},{6,7},{7,6},{8,9},{9,8},{10,11... | collective-permute-start | bytes 2408456 | tf_op jit(solution)/shard_map/ppermute | solution.py:256
  36.4 0.0 copy-done.2
  36.4 0.5 fusion.3
  37.0 0.0 copy-start
  37.0 0.0 copy-start.1
  37.0 1.8 %fusion.1.m_ref = f32[256,512]{1,0:T(8,128)S(1)} fusion(f32[256,512]{1,0:T(8,128)S(1)} %fusion.3, f32[256,512]{1,0:T(8,128)S(1)} %convolution_add_fusion.1, bf16[1152,512]{1,0:T(8,128)(2,1)} %collective-permute-done, bf16[4608,256]{1,0:T(8,128)(2,1)S(1)} %copy-done.2, s32[]{:T(128)S(6)} %select_n.55), kind=kOutput, calls=%fused_computation.3 | convolution fusion | flops 302252032 | bytes 3342340 | tf_op jit(solution)/shard_map/dot_general | solution.py:45
  38.9 14.3 %collective-permute-done.2.swapped_ref = bf16[784,512]{1,0:T(8,128)(2,1)S(1)} collective-permute-done((bf16[784,512]{1,0:T(8,128)(2,1)S(1)}, bf16[784,512]{1,0:T(8,128)(2,1)S(1)}, u32[]{:S(2)}, u32[]{:S(2)}) %collective-permute-start.2) | collective-permute-done | bytes 802848 | tf_op jit(solution)/shard_map/ppermute | solution.py:256
  53.1 0.0 copy-done
  53.1 0.0 copy-done.1
  53.1 1.2 %shard_map.95 = (f32[256,512]{1,0:T(8,128)S(1)}, f32[256,512]{1,0:T(8,128)S(1)}, bf16[256,1152]{1,0:T(8,128)(2,1)S(1)}, bf16[256,1152]{1,0:T(8,128)(2,1)S(1)}, f...) custom-call(f32[256,512]{1,0:T(8,128)S(1)} %fusion.1.m_ref, ...), custom_call_target="tpu_custom_call" | custom-call | flops 400000000 | bytes 4000000 | tf_op jit(solution)/shard_map/pallas_call | solution.py:203
  54.3 0.0 collective-permute-done.3.far_ref
  54.3 1.3 %shard_map.96 = (s16[272,512]{1,0:T(8,128)(2,1)S(1)}, f32[64,128]{1,0:T(8,128)S(1)}) custom-call(f32[256,512]{1,0:T(8,128)S(1)} %get-tuple-element.38.helped_ref, bf16[256,1152]{1,0:T(8,128)(2,1)S(1)} %get-tuple-element.39.turned_ref, bf16[1152,512]{1,0:T(8,128)(2,1)S(1)} %collective-permute-done.3.far_ref, f32[16,512]{1,0:T(8,128)S(1)} %get-tuple-element.41.places_ref, ...), custom_call_target="tpu_custom_call" | custom-call | flops 400000000 | bytes 4000000 | tf_op jit(solution)/shard_map/pallas_call | solution.py:203
  55.6 6.5 %collective-permute-start.4 = (f32[64,128]{1,0:T(8,128)S(1)}, f32[64,128]{1,0:T(8,128)S(1)}, u32[]{:S(2)}, u32[]{:S(2)}) collective-permute-start(f32[64,128]{1,0:T(8,128)S(1)} %get-tuple-element.44), channel_id=1, source_target_pairs={{0,1},{1,0},{2,3},{3,2},{4,5},{5,4},{6,7},{7,6},{8,9},{9,8},{10,11... | collective-permute-start | bytes 98312 | tf_op jit(solution)/shard_map/ppermute | solution.py:256
  62.1 1.3 %collective-permute-start.9 = (s16[272,512]{1,0:T(8,128)(2,1)S(1)}, s16[272,512]{1,0:T(8,128)(2,1)S(1)}, u32[]{:S(2)}, u32[]{:S(2)}) collective-permute-start(s16[272,512]{1,0:T(8,128)(2,1)S(1)} %get-tuple-element.54), channel_id=1, source_target_pairs={{1,0},{2,3},{5,4},{6,7},{9,8},{10,11},{13,12},{14,15},{17,16},{18,... | collective-permute-start | bytes 835592 | tf_op jit(solution)/shard_map/ppermute | solution.py:256
  63.4 0.5 collective-permute-done.4
  64.0 0.0 collective-permute-start.5
  64.0 1.6 %collective-permute-start.6 = (f32[64,128]{1,0:T(8,128)S(1)}, f32[64,128]{1,0:T(8,128)S(1)}, u32[]{:S(2)}, u32[]{:S(2)}) collective-permute-start(f32[64,128]{1,0:T(8,128)S(1)} %select_add_fusion.bands_ref), channel_id=1, source_target_pairs={{0,8},{4,12},{8,0},{12,4},{16,24},{20,28},{24,16},{28,20},{1,9},{5... | collective-permute-start | bytes 98312 | tf_op jit(solution)/shard_map/ppermute | solution.py:221
  65.6 0.3 collective-permute-start.7
  65.9 0.8 %shard_map.98.x_ref = f32[256,512]{1,0:T(8,128)S(1)} custom-call(f32[256,512]{1,0:T(8,128)S(1)} %get-tuple-element.53.m_ref, f32[64,128]{1,0:T(8,128)S(1)} %select_add_fusion.bands_ref, f32[8,512]{1,0:T(8,128)S(1)} %get-tuple-element.34.places_ref.refs_2_, bf16[512,128]{1,0:T(8,128)(2,1)S(1)} %copy-done.1, f32[256,256]{1,0:T(8,128)S(1)} %copy-done), custom_call_target="tpu_custom_call" | custom-call | flops 400000000 | bytes 4000000 | tf_op jit(solution)/shard_map/pallas_call | solution.py:203
  66.7 0.0 collective-permute-done.5
  66.7 1.3 %collective-permute-done.6 = f32[64,128]{1,0:T(8,128)S(1)} collective-permute-done((f32[64,128]{1,0:T(8,128)S(1)}, f32[64,128]{1,0:T(8,128)S(1)}, u32[]{:S(2)}, u32[]{:S(2)}) %collective-permute-start.6) | collective-permute-done | bytes 32800 | tf_op jit(solution)/shard_map/ppermute | solution.py:221
  68.0 0.9 %collective-permute-done.7 = f32[64,128]{1,0:T(8,128)S(1)} collective-permute-done((f32[64,128]{1,0:T(8,128)S(1)}, f32[64,128]{1,0:T(8,128)S(1)}, u32[]{:S(2)}, u32[]{:S(2)}) %collective-permute-start.7) | collective-permute-done | bytes 32800 | tf_op jit(solution)/shard_map/ppermute | solution.py:221
  68.9 1.6 %collective-permute-start.8 = (f32[64,128]{1,0:T(8,128)S(1)}, f32[64,128]{1,0:T(8,128)S(1)}, u32[]{:S(2)}, u32[]{:S(2)}) collective-permute-start(f32[64,128]{1,0:T(8,128)S(1)} %add_add_fusion.refs_0_), channel_id=1, source_target_pairs={{0,16},{4,20},{8,24},{12,28},{16,0},{20,4},{24,8},{28,12},{1,17},{... | collective-permute-start | bytes 98312 | tf_op jit(solution)/shard_map/ppermute | solution.py:221
  70.5 0.1 collective-permute-done.9.code_ref
  70.6 0.9 %shard_map.99 = f32[256,512]{1,0:T(8,128)} custom-call(f32[256,512]{1,0:T(8,128)S(1)} %shard_map.98.x_ref, s16[272,512]{1,0:T(8,128)(2,1)S(1)} %collective-permute-done.9.code_ref), custom_call_target="tpu_custom_call" | custom-call | flops 400000000 | bytes 4000000 | tf_op jit(solution)/shard_map/pallas_call | solution.py:203
  71.4 1.5 %collective-permute-done.8.refs_1_ = f32[64,128]{1,0:T(8,128)S(1)} collective-permute-done((f32[64,128]{1,0:T(8,128)S(1)}, f32[64,128]{1,0:T(8,128)S(1)}, u32[]{:S(2)}, u32[]{:S(2)}) %collective-permute-start.8) | collective-permute-done | bytes 32800 | tf_op jit(solution)/shard_map/ppermute | solution.py:221
  72.9 1.6 %shard_map.100 = bf16[256,512]{1,0:T(8,128)(2,1)} custom-call(f32[64,128]{1,0:T(8,128)S(1)} %add_add_fusion.refs_0_, f32[64,128]{1,0:T(8,128)S(1)} %collective-permute-done.8.refs_1_, f32[8,512]{1,0:T(8,128)S(1)} %get-tuple-element.34.places_ref.refs_2_, bf16[512,128]{1,0:T(8,128)(2,1)S(1)} %copy-done.1, f32[256,256]{1,0:T(8,128)S(1)} %copy-done), custom_call_target="tpu_custom_call" | custom-call | flops 400000000 | bytes 4000000 | tf_op jit(solution)/shard_map/pallas_call | solution.py:203
  (5 shorter events, 0.1 us)
Async XLA Ops:
  0.6 6.2 %copy-start.5 = (bf16[8,512]{1,0:T(8,128)(2,1)S(1)}, bf16[8,512]{1,0:T(8,128)(2,1)}, u32[]{:S(2)}) copy-start(bf16[8,512]{1,0:T(8,128)(2,1)} %constant.53) | copy-start | bytes 24580
  0.6 6.4 %copy-start.3 = (bf16[1152,512]{1,0:T(8,128)(2,1)S(1)}, bf16[1152,512]{1,0:T(8,128)(2,1)}, u32[]{:S(2)}) copy-start(bf16[1152,512]{1,0:T(8,128)(2,1)} %param.9) | copy-start | bytes 3538948
  0.7 6.2 %copy-start.7 = (s32[4,8]{1,0:T(4,128)S(1)}, s32[4,8]{1,0:T(4,128)}, u32[]{:S(2)}) copy-start(s32[4,8]{1,0:T(4,128)} %param.11) | copy-start | bytes 388
  0.7 6.2 %copy-start.6 = (s32[4,8]{1,0:T(4,128)S(1)}, s32[4,8]{1,0:T(4,128)}, u32[]{:S(2)}) copy-start(s32[4,8]{1,0:T(4,128)} %param.12) | copy-start | bytes 388
  0.7 29.4 %collective-permute-start = (bf16[1152,512]{1,0:T(8,128)(2,1)}, bf16[1152,512]{1,0:T(8,128)(2,1)}, u32[]{:S(2)}, u32[]{:S(2)}) collective-permute-start(bf16[1152,512]{1,0:T(8,128)(2,1)} %param.9), channel_id=1, source_target_pairs={{0,1},{1,0},{2,3},{3,2},{4,5},{5,4},{6,7},{7,6},{8,9},{9,8},{10,11... | collective-permute-start | bytes 3538952 | tf_op jit(solution)/shard_map/ppermute | solution.py:256
  3.8 28.0 %collective-permute-start.1 = (bf16[1152,512]{1,0:T(8,128)(2,1)}, bf16[1152,512]{1,0:T(8,128)(2,1)S(1)}, u32[]{:S(2)}, u32[]{:S(2)}) collective-permute-start(bf16[1152,512]{1,0:T(8,128)(2,1)} %param.9), channel_id=1, source_target_pairs={{1,2},{2,1},{5,6},{6,5},{9,10},{10,9},{13,14},{14,13},{17,18},{18,... | collective-permute-start | bytes 3538952 | tf_op jit(solution)/shard_map/ppermute | solution.py:256
  4.5 2.5 %copy-start.4 = (f32[1,256,512]{2,1,0:T(8,128)S(1)}, f32[1,256,512]{2,1,0:T(8,128)}, u32[]{:S(2)}) copy-start(f32[1,256,512]{2,1,0:T(8,128)} %param.10) | copy-start | bytes 1572868
  30.0 24.3 %collective-permute-start.3 = (bf16[1152,512]{1,0:T(8,128)(2,1)}, bf16[1152,512]{1,0:T(8,128)(2,1)S(1)}, u32[]{:S(2)}, u32[]{:S(2)}) collective-permute-start(bf16[1152,512]{1,0:T(8,128)(2,1)} %collective-permute-done), channel_id=1, source_target_pairs={{1,2},{2,1},{5,6},{6,5},{9,10},{10,9},{13,14},{14,13},{17,18},{18,... | collective-permute-start | bytes 3538952 | tf_op jit(solution)/shard_map/ppermute | solution.py:256
  31.8 4.7 %copy-start.2 = (bf16[4608,256]{1,0:T(8,128)(2,1)S(1)}, bf16[4608,256]{1,0:T(8,128)(2,1)}, u32[]{:S(2)}) copy-start(bf16[4608,256]{1,0:T(8,128)(2,1)} %param.8) | copy-start | bytes 7077892
  33.1 20.0 %collective-permute-start.2 = (bf16[784,512]{1,0:T(8,128)(2,1)S(1)}, bf16[784,512]{1,0:T(8,128)(2,1)S(1)}, u32[]{:S(2)}, u32[]{:S(2)}) collective-permute-start(bf16[784,512]{1,0:T(8,128)(2,1)S(1)} %slice_select_fusion), channel_id=1, source_target_pairs={{0,1},{1,0},{2,3},{3,2},{4,5},{5,4},{6,7},{7,6},{8,9},{9,8},{10,11... | collective-permute-start | bytes 2408456 | tf_op jit(solution)/shard_map/ppermute | solution.py:256
  37.0 16.2 %copy-start = (f32[256,256]{1,0:T(8,128)S(1)}, f32[256,256]{1,0:T(8,128)}, u32[]{:S(2)}) copy-start(f32[256,256]{1,0:T(8,128)} %constant.34.clone.refs_1_.basis_ref.refs_4_) | copy-start | bytes 786436
  37.0 16.1 %copy-start.1 = (bf16[512,128]{1,0:T(8,128)(2,1)S(1)}, bf16[512,128]{1,0:T(8,128)(2,1)}, u32[]{:S(2)}) copy-start(bf16[512,128]{1,0:T(8,128)(2,1)} %constant.33.clone.refs_0_.fold_ref.refs_3_) | copy-start | bytes 393220
  55.6 8.4 %collective-permute-start.4 = (f32[64,128]{1,0:T(8,128)S(1)}, f32[64,128]{1,0:T(8,128)S(1)}, u32[]{:S(2)}, u32[]{:S(2)}) collective-permute-start(f32[64,128]{1,0:T(8,128)S(1)} %get-tuple-element.44), channel_id=1, source_target_pairs={{0,1},{1,0},{2,3},{3,2},{4,5},{5,4},{6,7},{7,6},{8,9},{9,8},{10,11... | collective-permute-start | bytes 98312 | tf_op jit(solution)/shard_map/ppermute | solution.py:256
  62.1 8.4 %collective-permute-start.9 = (s16[272,512]{1,0:T(8,128)(2,1)S(1)}, s16[272,512]{1,0:T(8,128)(2,1)S(1)}, u32[]{:S(2)}, u32[]{:S(2)}) collective-permute-start(s16[272,512]{1,0:T(8,128)(2,1)S(1)} %get-tuple-element.54), channel_id=1, source_target_pairs={{1,0},{2,3},{5,4},{6,7},{9,8},{10,11},{13,12},{14,15},{17,16},{18,... | collective-permute-start | bytes 835592 | tf_op jit(solution)/shard_map/ppermute | solution.py:256
  64.0 2.7 %collective-permute-start.5 = (f32[64,128]{1,0:T(8,128)S(1)}, f32[64,128]{1,0:T(8,128)S(1)}, u32[]{:S(2)}, u32[]{:S(2)}) collective-permute-start(f32[64,128]{1,0:T(8,128)S(1)} %select_add_fusion.bands_ref), channel_id=1, source_target_pairs={{0,4},{4,0},{8,12},{12,8},{16,20},{20,16},{24,28},{28,24},{1,5},{5... | collective-permute-start | bytes 98312 | tf_op jit(solution)/shard_map/ppermute | solution.py:221
  64.0 4.0 %collective-permute-start.6 = (f32[64,128]{1,0:T(8,128)S(1)}, f32[64,128]{1,0:T(8,128)S(1)}, u32[]{:S(2)}, u32[]{:S(2)}) collective-permute-start(f32[64,128]{1,0:T(8,128)S(1)} %select_add_fusion.bands_ref), channel_id=1, source_target_pairs={{0,8},{4,12},{8,0},{12,4},{16,24},{20,28},{24,16},{28,20},{1,9},{5... | collective-permute-start | bytes 98312 | tf_op jit(solution)/shard_map/ppermute | solution.py:221
  65.6 3.4 %collective-permute-start.7 = (f32[64,128]{1,0:T(8,128)S(1)}, f32[64,128]{1,0:T(8,128)S(1)}, u32[]{:S(2)}, u32[]{:S(2)}) collective-permute-start(f32[64,128]{1,0:T(8,128)S(1)} %select_add_fusion.bands_ref), channel_id=1, source_target_pairs={{0,12},{4,8},{8,4},{12,0},{16,28},{20,24},{24,20},{28,16},{1,13},{... | collective-permute-start | bytes 98312 | tf_op jit(solution)/shard_map/ppermute | solution.py:221
  68.9 4.0 %collective-permute-start.8 = (f32[64,128]{1,0:T(8,128)S(1)}, f32[64,128]{1,0:T(8,128)S(1)}, u32[]{:S(2)}, u32[]{:S(2)}) collective-permute-start(f32[64,128]{1,0:T(8,128)S(1)} %add_add_fusion.refs_0_), channel_id=1, source_target_pairs={{0,16},{4,20},{8,24},{12,28},{16,0},{20,4},{24,8},{28,12},{1,17},{... | collective-permute-start | bytes 98312 | tf_op jit(solution)/shard_map/ppermute | solution.py:221

commit v15 on v14

--- a/solution.py
+++ b/solution.py
@@ -215,7 +215,7 @@
         return [lax.psum(x, axis)]
     stride, parts = 1, [x]
     while stride < size:
-        count = min(4, size // stride)
+        count = min(4 if stride > 1 else 2, size // stride)
         x = pair_sum(parts)
         parts = [x] + [
             lax.ppermute(x, axis, [(i, i ^ (stride * k)) for i in range(size)]) for k in range(1, count)

time: 74.8 us -> 74.9 us (level)
    ppermute x6, waiting for transfers between devices: 36.3 us -> 38.2 us  [send(): return lax.ppermute(x, 'tp', perm)]
    ppermute x4, waiting for transfers between devices: 3.64 us -> 1.92 us  [spread_sum(): lax.ppermute(x, axis, [(i, i ^ stride * k) for i in range(size)])]
  transfers between devices with their start and end apart: 10 -> 10, of which waited for: 7 -> 6; matrix products, arithmetic and copies ran while one was open for 12% -> 12% of each run, Pallas kernels for 4% -> 4%
where the time goes in v15:
time: 74.9 us; the launch traced here: 74.6 us
  waiting for transfers between devices  40.1 us (54%)
  starting transfers between devices  19 us (25%)
  Pallas kernels  5.77 us (8%)
  matrix products  4.1 us (5%)
  other arithmetic  3.56 us (5%)
  local copies, waits for them, and re-layouts  1.19 us (2%)
  between operations  0.84 us (1%)
    ppermute x6, waiting for transfers between devices, send(): return lax.ppermute(x, 'tp', perm)  38.2 us
    ppermute x6, starting transfers between devices, send(): return lax.ppermute(x, 'tp', perm)  15.6 us
    pallas_call x6, Pallas kernels, call(): pl.pallas_call(kernel, out_shape=out_shapes, in_specs=[pl.BlockSpec(memor...  5.77 us
    dot_general x4, matrix products, dot(): lax.dot_general(a, b, (dims, ((), ())), preferred_element_type=jnp.float32)  4.1 us
    ppermute x4, starting transfers between devices, spread_sum(): lax.ppermute(x, axis, [(i, i ^ stride * k) for i in range(size)])  3.49 us
    ppermute x4, waiting for transfers between devices, spread_sum(): lax.ppermute(x, axis, [(i, i ^ stride * k) for i in range(size)])  1.92 us
  transfers between devices with their start and end apart: 10, of which 6 were waited for; matrix products, arithmetic and copies ran while one was open for 12% of the time, Pallas kernels for 4%

profile of v15, /device:TPU:0, one launch (start us, length us, event | category | flops | bytes accessed | tf_op | source)
XLA Modules:
  0.0 74.6 jit_solution(1135286970446793636)
XLA Ops:
  0.6 0.0 copy-start.5
  0.6 0.0 copy-start.3
  0.7 0.0 copy-start.7
  0.7 0.0 copy-start.6
  0.7 3.1 %collective-permute-start = (bf16[1152,512]{1,0:T(8,128)(2,1)}, bf16[1152,512]{1,0:T(8,128)(2,1)}, u32[]{:S(2)}, u32[]{:S(2)}) collective-permute-start(bf16[1152,512]{1,0:T(8,128)(2,1)} %param.9), channel_id=1, source_target_pairs={{0,1},{1,0},{2,3},{3,2},{4,5},{5,4},{6,7},{7,6},{8,9},{9,8},{10,11... | collective-permute-start | bytes 3538952 | tf_op jit(solution)/shard_map/ppermute | solution.py:256
  3.8 0.7 collective-permute-start.1
  4.5 0.0 copy-start.4
  4.5 1.1 %constant_dynamic-slice_fusion.3 = (bf16[384,256]{1,0:T(8,128)(2,1)S(1)}, bf16[384,256]{1,0:T(8,128)(2,1)S(1)}) fusion(bf16[4608,256]{1,0:T(8,128)(2,1)} %param.8, s32[]{:T(128)S(6)} %select_n.48, s32[]{:T(128)S(6)} %select_n.50), kind=kLoop, calls=%fused_computation.24 | loop fusion | bytes 786440 | tf_op jit(solution)/shard_map/dynamic_slice | solution.py:253
  5.6 1.2 %dynamic-slice_select_fusion = (bf16[768,256]{1,0:T(8,128)(2,1)S(1)}, bf16[768,256]{1,0:T(8,128)(2,1)S(1)}) fusion(bf16[4608,256]{1,0:T(8,128)(2,1)} %param.8, s32[]{:T(128)S(6)} %select_n.52, pred[]{:T(512)S(6)} %or.3, s32[]{:T(128)S(6)} %add.50), kind=kLoop, calls=%fused_computation.11 | loop fusion | flops 196608 | bytes 1572873 | tf_op jit(solution)/shard_map/jit(_where)/select_n | solution.py:275
  6.8 0.0 copy-done.5
  6.9 0.0 copy-done.7
  6.9 0.0 copy-done.6
  6.9 0.1 fusion.14
  7.0 0.0 copy-done.3
  7.0 0.0 copy-done.4
  7.0 1.6 %convolution_add_fusion.1 = f32[256,512]{1,0:T(8,128)S(1)} fusion(bf16[1152,512]{1,0:T(8,128)(2,1)S(1)} %copy-done.3, bf16[4608,256]{1,0:T(8,128)(2,1)} %param.8, s32[]{:T(128)S(6)} %select_n.54, f32[1,256,512]{2,1,0:T(8,128)S(1)} %copy-done.4), kind=kOutput, calls=%fused_computation.4 | convolution fusion | flops 302252032 | bytes 2818052 | tf_op jit(solution)/shard_map/dot_general | solution.py:45
  8.6 21.5 %collective-permute-done = bf16[1152,512]{1,0:T(8,128)(2,1)} collective-permute-done((bf16[1152,512]{1,0:T(8,128)(2,1)}, bf16[1152,512]{1,0:T(8,128)(2,1)}, u32[]{:S(2)}, u32[]{:S(2)}) %collective-permute-start) | collective-permute-done | bytes 1179680 | tf_op jit(solution)/shard_map/ppermute | solution.py:256
  30.0 0.7 collective-permute-start.3
  30.8 1.0 %fusion.2 = bf16[784,512]{1,0:T(8,128)(2,1)} fusion(bf16[8,512]{1,0:T(8,128)(2,1)S(1)} %get-tuple-element.66, bf16[768,256]{1,0:T(8,128)(2,1)S(1)} %get-tuple-element.63, bf16[384,256]{1,0:T(8,128)(2,1)S(1)} %get-tuple-element.65, bf16[384,256]{1,0:T(8,128)(2,1)S(1)} %get-tuple-element.64), kind=kLoop, calls=%fused_computation.5 | loop fusion | flops 4014080 | bytes 1597440 | tf_op jit(solution)/shard_map/concatenate | solution.py:274
  31.8 0.0 collective-permute-done.1.cross_ref
  31.8 1.4 %slice_select_fusion = bf16[784,512]{1,0:T(8,128)(2,1)S(1)} fusion(bf16[784,512]{1,0:T(8,128)(2,1)} %fusion.2, bf16[1152,512]{1,0:T(8,128)(2,1)S(1)} %collective-permute-done.1.cross_ref, pred[]{:T(512)S(6)} %or.3), kind=kLoop, calls=%fused_computation.6 | loop fusion | flops 401408 | bytes 2408449 | tf_op jit(solution)/shard_map/jit(_where)/select_n | solution.py:280
  33.1 3.3 %collective-permute-start.2 = (bf16[784,512]{1,0:T(8,128)(2,1)S(1)}, bf16[784,512]{1,0:T(8,128)(2,1)S(1)}, u32[]{:S(2)}, u32[]{:S(2)}) collective-permute-start(bf16[784,512]{1,0:T(8,128)(2,1)S(1)} %slice_select_fusion), channel_id=1, source_target_pairs={{0,1},{1,0},{2,3},{3,2},{4,5},{5,4},{6,7},{7,6},{8,9},{9,8},{10,11... | collective-permute-start | bytes 2408456 | tf_op jit(solution)/shard_map/ppermute | solution.py:256
  36.4 0.0 copy-done.2
  36.4 0.5 fusion.3
  37.0 0.0 copy-start
  37.0 0.0 copy-start.1
  37.0 1.8 %fusion.1.m_ref = f32[256,512]{1,0:T(8,128)S(1)} fusion(f32[256,512]{1,0:T(8,128)S(1)} %fusion.3, f32[256,512]{1,0:T(8,128)S(1)} %convolution_add_fusion.1, bf16[1152,512]{1,0:T(8,128)(2,1)} %collective-permute-done, bf16[4608,256]{1,0:T(8,128)(2,1)S(1)} %copy-done.2, s32[]{:T(128)S(6)} %select_n.55), kind=kOutput, calls=%fused_computation.3 | convolution fusion | flops 302252032 | bytes 3342340 | tf_op jit(solution)/shard_map/dot_general | solution.py:45
  38.9 14.3 %collective-permute-done.2.swapped_ref = bf16[784,512]{1,0:T(8,128)(2,1)S(1)} collective-permute-done((bf16[784,512]{1,0:T(8,128)(2,1)S(1)}, bf16[784,512]{1,0:T(8,128)(2,1)S(1)}, u32[]{:S(2)}, u32[]{:S(2)}) %collective-permute-start.2) | collective-permute-done | bytes 802848 | tf_op jit(solution)/shard_map/ppermute | solution.py:256
  53.1 0.0 copy-done
  53.1 0.0 copy-done.1
  53.1 1.2 %shard_map.95 = (f32[256,512]{1,0:T(8,128)S(1)}, f32[256,512]{1,0:T(8,128)S(1)}, bf16[256,1152]{1,0:T(8,128)(2,1)S(1)}, bf16[256,1152]{1,0:T(8,128)(2,1)S(1)}, f...) custom-call(f32[256,512]{1,0:T(8,128)S(1)} %fusion.1.m_ref, ...), custom_call_target="tpu_custom_call" | custom-call | flops 400000000 | bytes 4000000 | tf_op jit(solution)/shard_map/pallas_call | solution.py:203
  54.3 0.0 collective-permute-done.3.far_ref
  54.3 1.3 %shard_map.96 = (s16[272,512]{1,0:T(8,128)(2,1)S(1)}, f32[64,128]{1,0:T(8,128)S(1)}) custom-call(f32[256,512]{1,0:T(8,128)S(1)} %get-tuple-element.40.helped_ref, bf16[256,1152]{1,0:T(8,128)(2,1)S(1)} %get-tuple-element.41.turned_ref, bf16[1152,512]{1,0:T(8,128)(2,1)S(1)} %collective-permute-done.3.far_ref, f32[16,512]{1,0:T(8,128)S(1)} %get-tuple-element.43.places_ref, ...), custom_call_target="tpu_custom_call" | custom-call | flops 400000000 | bytes 4000000 | tf_op jit(solution)/shard_map/pallas_call | solution.py:203
  55.6 6.5 %collective-permute-start.4 = (f32[64,128]{1,0:T(8,128)S(1)}, f32[64,128]{1,0:T(8,128)S(1)}, u32[]{:S(2)}, u32[]{:S(2)}) collective-permute-start(f32[64,128]{1,0:T(8,128)S(1)} %get-tuple-element.46), channel_id=1, source_target_pairs={{0,1},{1,0},{2,3},{3,2},{4,5},{5,4},{6,7},{7,6},{8,9},{9,8},{10,11... | collective-permute-start | bytes 98312 | tf_op jit(solution)/shard_map/ppermute | solution.py:256
  62.1 1.3 %collective-permute-start.9 = (s16[272,512]{1,0:T(8,128)(2,1)S(1)}, s16[272,512]{1,0:T(8,128)(2,1)S(1)}, u32[]{:S(2)}, u32[]{:S(2)}) collective-permute-start(s16[272,512]{1,0:T(8,128)(2,1)S(1)} %get-tuple-element.56), channel_id=1, source_target_pairs={{1,0},{2,3},{5,4},{6,7},{9,8},{10,11},{13,12},{14,15},{17,16},{18,... | collective-permute-start | bytes 835592 | tf_op jit(solution)/shard_map/ppermute | solution.py:256
  63.4 0.5 collective-permute-done.4
  64.0 0.0 collective-permute-start.5
  64.0 0.8 %shard_map.98.x_ref = f32[256,512]{1,0:T(8,128)S(1)} custom-call(f32[256,512]{1,0:T(8,128)S(1)} %get-tuple-element.55.m_ref, f32[64,128]{1,0:T(8,128)S(1)} %select_add_fusion.bands_ref, f32[8,512]{1,0:T(8,128)S(1)} %get-tuple-element.36.places_ref.refs_4_, bf16[512,128]{1,0:T(8,128)(2,1)S(1)} %copy-done.1, f32[256,256]{1,0:T(8,128)S(1)} %copy-done), custom_call_target="tpu_custom_call" | custom-call | flops 400000000 | bytes 4000000 | tf_op jit(solution)/shard_map/pallas_call | solution.py:203
  64.9 0.3 collective-permute-done.5
  65.2 1.5 %collective-permute-start.6 = (f32[64,128]{1,0:T(8,128)S(1)}, f32[64,128]{1,0:T(8,128)S(1)}, u32[]{:S(2)}, u32[]{:S(2)}) collective-permute-start(f32[64,128]{1,0:T(8,128)S(1)} %add.48.refs_0_), channel_id=1, source_target_pairs={{0,8},{4,12},{8,0},{12,4},{16,24},{20,28},{24,16},{28,20},{1,9},{5... | collective-permute-start | bytes 98312 | tf_op jit(solution)/shard_map/ppermute | solution.py:221
  66.7 1.5 %collective-permute-start.7 = (f32[64,128]{1,0:T(8,128)S(1)}, f32[64,128]{1,0:T(8,128)S(1)}, u32[]{:S(2)}, u32[]{:S(2)}) collective-permute-start(f32[64,128]{1,0:T(8,128)S(1)} %add.48.refs_0_), channel_id=1, source_target_pairs={{0,16},{4,20},{8,24},{12,28},{16,0},{20,4},{24,8},{28,12},{1,17},{... | collective-permute-start | bytes 98312 | tf_op jit(solution)/shard_map/ppermute | solution.py:221
  68.2 0.5 collective-permute-start.8
  68.7 1.9 %collective-permute-done.9.code_ref = s16[272,512]{1,0:T(8,128)(2,1)S(1)} collective-permute-done((s16[272,512]{1,0:T(8,128)(2,1)S(1)}, s16[272,512]{1,0:T(8,128)(2,1)S(1)}, u32[]{:S(2)}, u32[]{:S(2)}) %collective-permute-start.9) | collective-permute-done | bytes 278560 | tf_op jit(solution)/shard_map/ppermute | solution.py:256
  70.6 0.9 %shard_map.99 = f32[256,512]{1,0:T(8,128)} custom-call(f32[256,512]{1,0:T(8,128)S(1)} %shard_map.98.x_ref, s16[272,512]{1,0:T(8,128)(2,1)S(1)} %collective-permute-done.9.code_ref), custom_call_target="tpu_custom_call" | custom-call | flops 400000000 | bytes 4000000 | tf_op jit(solution)/shard_map/pallas_call | solution.py:203
  71.4 0.0 collective-permute-done.6.refs_1_
  71.5 0.0 collective-permute-done.7.refs_2_
  71.5 1.6 %collective-permute-done.8.refs_3_ = f32[64,128]{1,0:T(8,128)S(1)} collective-permute-done((f32[64,128]{1,0:T(8,128)S(1)}, f32[64,128]{1,0:T(8,128)S(1)}, u32[]{:S(2)}, u32[]{:S(2)}) %collective-permute-start.8) | collective-permute-done | bytes 32800 | tf_op jit(solution)/shard_map/ppermute | solution.py:221
  73.0 1.6 %shard_map.100 = bf16[256,512]{1,0:T(8,128)(2,1)} custom-call(f32[64,128]{1,0:T(8,128)S(1)} %add.48.refs_0_, f32[64,128]{1,0:T(8,128)S(1)} %collective-permute-done.6.refs_1_, f32[64,128]{1,0:T(8,128)S(1)} %collective-permute-done.7.refs_2_, f32[64,128]{1,0:T(8,128)S(1)} %collective-permute-done.8.refs_3_, ...), custom_call_target="tpu_custom_call" | custom-call | flops 400000000 | bytes 4000000 | tf_op jit(solution)/shard_map/pallas_call | solution.py:203
  (5 shorter events, 0.1 us)
Async XLA Ops:
  0.6 6.2 %copy-start.5 = (bf16[8,512]{1,0:T(8,128)(2,1)S(1)}, bf16[8,512]{1,0:T(8,128)(2,1)}, u32[]{:S(2)}) copy-start(bf16[8,512]{1,0:T(8,128)(2,1)} %constant.53) | copy-start | bytes 24580
  0.6 6.4 %copy-start.3 = (bf16[1152,512]{1,0:T(8,128)(2,1)S(1)}, bf16[1152,512]{1,0:T(8,128)(2,1)}, u32[]{:S(2)}) copy-start(bf16[1152,512]{1,0:T(8,128)(2,1)} %param.9) | copy-start | bytes 3538948
  0.7 6.2 %copy-start.7 = (s32[4,8]{1,0:T(4,128)S(1)}, s32[4,8]{1,0:T(4,128)}, u32[]{:S(2)}) copy-start(s32[4,8]{1,0:T(4,128)} %param.11) | copy-start | bytes 388
  0.7 6.2 %copy-start.6 = (s32[4,8]{1,0:T(4,128)S(1)}, s32[4,8]{1,0:T(4,128)}, u32[]{:S(2)}) copy-start(s32[4,8]{1,0:T(4,128)} %param.12) | copy-start | bytes 388
  0.7 29.4 %collective-permute-start = (bf16[1152,512]{1,0:T(8,128)(2,1)}, bf16[1152,512]{1,0:T(8,128)(2,1)}, u32[]{:S(2)}, u32[]{:S(2)}) collective-permute-start(bf16[1152,512]{1,0:T(8,128)(2,1)} %param.9), channel_id=1, source_target_pairs={{0,1},{1,0},{2,3},{3,2},{4,5},{5,4},{6,7},{7,6},{8,9},{9,8},{10,11... | collective-permute-start | bytes 3538952 | tf_op jit(solution)/shard_map/ppermute | solution.py:256
  3.8 28.0 %collective-permute-start.1 = (bf16[1152,512]{1,0:T(8,128)(2,1)}, bf16[1152,512]{1,0:T(8,128)(2,1)S(1)}, u32[]{:S(2)}, u32[]{:S(2)}) collective-permute-start(bf16[1152,512]{1,0:T(8,128)(2,1)} %param.9), channel_id=1, source_target_pairs={{1,2},{2,1},{5,6},{6,5},{9,10},{10,9},{13,14},{14,13},{17,18},{18,... | collective-permute-start | bytes 3538952 | tf_op jit(solution)/shard_map/ppermute | solution.py:256
  4.5 2.5 %copy-start.4 = (f32[1,256,512]{2,1,0:T(8,128)S(1)}, f32[1,256,512]{2,1,0:T(8,128)}, u32[]{:S(2)}) copy-start(f32[1,256,512]{2,1,0:T(8,128)} %param.10) | copy-start | bytes 1572868
  30.0 24.3 %collective-permute-start.3 = (bf16[1152,512]{1,0:T(8,128)(2,1)}, bf16[1152,512]{1,0:T(8,128)(2,1)S(1)}, u32[]{:S(2)}, u32[]{:S(2)}) collective-permute-start(bf16[1152,512]{1,0:T(8,128)(2,1)} %collective-permute-done), channel_id=1, source_target_pairs={{1,2},{2,1},{5,6},{6,5},{9,10},{10,9},{13,14},{14,13},{17,18},{18,... | collective-permute-start | bytes 3538952 | tf_op jit(solution)/shard_map/ppermute | solution.py:256
  31.8 4.7 %copy-start.2 = (bf16[4608,256]{1,0:T(8,128)(2,1)S(1)}, bf16[4608,256]{1,0:T(8,128)(2,1)}, u32[]{:S(2)}) copy-start(bf16[4608,256]{1,0:T(8,128)(2,1)} %param.8) | copy-start | bytes 7077892
  33.1 20.0 %collective-permute-start.2 = (bf16[784,512]{1,0:T(8,128)(2,1)S(1)}, bf16[784,512]{1,0:T(8,128)(2,1)S(1)}, u32[]{:S(2)}, u32[]{:S(2)}) collective-permute-start(bf16[784,512]{1,0:T(8,128)(2,1)S(1)} %slice_select_fusion), channel_id=1, source_target_pairs={{0,1},{1,0},{2,3},{3,2},{4,5},{5,4},{6,7},{7,6},{8,9},{9,8},{10,11... | collective-permute-start | bytes 2408456 | tf_op jit(solution)/shard_map/ppermute | solution.py:256
  37.0 16.2 %copy-start = (f32[256,256]{1,0:T(8,128)S(1)}, f32[256,256]{1,0:T(8,128)}, u32[]{:S(2)}) copy-start(f32[256,256]{1,0:T(8,128)} %constant.34.clone.refs_1_.basis_ref.refs_6_) | copy-start | bytes 786436
  37.0 16.1 %copy-start.1 = (bf16[512,128]{1,0:T(8,128)(2,1)S(1)}, bf16[512,128]{1,0:T(8,128)(2,1)}, u32[]{:S(2)}) copy-start(bf16[512,128]{1,0:T(8,128)(2,1)} %constant.33.clone.refs_0_.fold_ref.refs_5_) | copy-start | bytes 393220
  55.6 8.4 %collective-permute-start.4 = (f32[64,128]{1,0:T(8,128)S(1)}, f32[64,128]{1,0:T(8,128)S(1)}, u32[]{:S(2)}, u32[]{:S(2)}) collective-permute-start(f32[64,128]{1,0:T(8,128)S(1)} %get-tuple-element.46), channel_id=1, source_target_pairs={{0,1},{1,0},{2,3},{3,2},{4,5},{5,4},{6,7},{7,6},{8,9},{9,8},{10,11... | collective-permute-start | bytes 98312 | tf_op jit(solution)/shard_map/ppermute | solution.py:256
  62.1 8.4 %collective-permute-start.9 = (s16[272,512]{1,0:T(8,128)(2,1)S(1)}, s16[272,512]{1,0:T(8,128)(2,1)S(1)}, u32[]{:S(2)}, u32[]{:S(2)}) collective-permute-start(s16[272,512]{1,0:T(8,128)(2,1)S(1)} %get-tuple-element.56), channel_id=1, source_target_pairs={{1,0},{2,3},{5,4},{6,7},{9,8},{10,11},{13,12},{14,15},{17,16},{18,... | collective-permute-start | bytes 835592 | tf_op jit(solution)/shard_map/ppermute | solution.py:256
  64.0 1.2 %collective-permute-start.5 = (f32[64,128]{1,0:T(8,128)S(1)}, f32[64,128]{1,0:T(8,128)S(1)}, u32[]{:S(2)}, u32[]{:S(2)}) collective-permute-start(f32[64,128]{1,0:T(8,128)S(1)} %select_add_fusion.bands_ref), channel_id=1, source_target_pairs={{0,4},{4,0},{8,12},{12,8},{16,20},{20,16},{24,28},{28,24},{1,5},{5... | collective-permute-start | bytes 98312 | tf_op jit(solution)/shard_map/ppermute | solution.py:221
  65.2 6.2 %collective-permute-start.6 = (f32[64,128]{1,0:T(8,128)S(1)}, f32[64,128]{1,0:T(8,128)S(1)}, u32[]{:S(2)}, u32[]{:S(2)}) collective-permute-start(f32[64,128]{1,0:T(8,128)S(1)} %add.48.refs_0_), channel_id=1, source_target_pairs={{0,8},{4,12},{8,0},{12,4},{16,24},{20,28},{24,16},{28,20},{1,9},{5... | collective-permute-start | bytes 98312 | tf_op jit(solution)/shard_map/ppermute | solution.py:221
  66.7 4.8 %collective-permute-start.7 = (f32[64,128]{1,0:T(8,128)S(1)}, f32[64,128]{1,0:T(8,128)S(1)}, u32[]{:S(2)}, u32[]{:S(2)}) collective-permute-start(f32[64,128]{1,0:T(8,128)S(1)} %add.48.refs_0_), channel_id=1, source_target_pairs={{0,16},{4,20},{8,24},{12,28},{16,0},{20,4},{24,8},{28,12},{1,17},{... | collective-permute-start | bytes 98312 | tf_op jit(solution)/shard_map/ppermute | solution.py:221
  68.2 4.8 %collective-permute-start.8 = (f32[64,128]{1,0:T(8,128)S(1)}, f32[64,128]{1,0:T(8,128)S(1)}, u32[]{:S(2)}, u32[]{:S(2)}) collective-permute-start(f32[64,128]{1,0:T(8,128)S(1)} %add.48.refs_0_), channel_id=1, source_target_pairs={{0,24},{4,28},{8,16},{12,20},{16,8},{20,12},{24,0},{28,4},{1,25},{... | collective-permute-start | bytes 98312 | tf_op jit(solution)/shard_map/ppermute | solution.py:221

commit v16 on v14

--- a/solution.py
+++ b/solution.py
@@ -256,7 +256,7 @@
         return lax.ppermute(x, "tp", perm)
 
     both_ways = [(0, 1), (1, 0), (2, 3), (3, 2)]
-    across = [(1, 2), (2, 1)]
+    across = [(1, 2), (2, 1), (0, 0), (3, 3)]
     outward = [(1, 0), (2, 3)]
 
     pair_grad = send(out_grad, both_ways)
@@ -273,12 +273,15 @@
     place_part = jnp.pad(places.astype(hidden.dtype), ((0, place_rows - places.shape[0]), (0, 0)))
     helped_hidden = jnp.concatenate([helped_hidden, place_part], axis=0)
     cross_hidden = jnp.where(end, rows_of(cross, 0, handed), 0)
-    helped_hidden, cross_hidden, m = lax.optimization_barrier((helped_hidden, cross_hidden, m))
+    middle_hidden = jnp.where(end, 0, rows_of(cross))
+    helped_hidden, cross_hidden, middle_hidden, m = lax.optimization_barrier(
+        (helped_hidden, cross_hidden, middle_hidden, m)
+    )
 
     far_grad = send(pair_grad, across)
     cross_grad, matrices, places = after((cross_grad, matrices, places), pair_grad, m)
     swapped = send(jnp.where(end, helped_hidden, cross_grad[: handed + place_rows]), both_ways)
-    m = m + product(rows_of(me ^ 1), pair_grad) + product(rows_of(cross), cross_grad)
+    m = m + product(rows_of(me ^ 1), pair_grad) + product(middle_hidden, cross_grad)
 
     height, width = m.shape[0] // steps, m.shape[1] // steps
     full = jax.ShapeDtypeStruct(m.shape, jnp.float32)

time: 74.8 us -> 74.8 us (level)
  waiting for transfers between devices: 40 us -> 37 us
  Pallas kernels: 5.78 us -> 6.9 us
  starting transfers between devices: 19 us -> 20.1 us
  matrix products: 4.1 us -> 5.12 us
    ppermute x6, waiting for transfers between devices: 36.3 us -> 33.4 us  [send(): return lax.ppermute(x, 'tp', perm)]
    pallas_call x6, Pallas kernels: 5.78 us -> 6.9 us  [call(): pl.pallas_call(kernel, out_shape=out_shapes, in_specs=[pl.BlockSpec(memor...]
    ppermute x6, starting transfers between devices: 15.6 us -> 16.6 us  [send(): return lax.ppermute(x, 'tp', perm)]
    dot_general x4, matrix products: 4.1 us -> 5.12 us  [dot(): lax.dot_general(a, b, (dims, ((), ())), preferred_element_type=jnp.float32)]
    dynamic_slice x0 -> x1, other arithmetic: none -> 0.92 us  [rows_of(): return lax.dynamic_slice_in_dim(hidden, part * tok + start, stop - start, 0)]
    concatenate x1, other arithmetic: 0.97 us -> 0.05 us  [lined(): helped_hidden = jnp.concatenate([helped_hidden, place_part], axis=0)]
  transfers between devices with their start and end apart: 10 -> 10, of which waited for: 7 -> 7; matrix products, arithmetic and copies ran while one was open for 12% -> 13% of each run, Pallas kernels for 4% -> 5%
where the time goes in v16:
time: 74.8 us; the launch traced here: 74.5 us
  waiting for transfers between devices  37 us (49%)
  starting transfers between devices  20.1 us (27%)
  Pallas kernels  6.9 us (9%)
  matrix products  5.12 us (7%)
  other arithmetic  3.3 us (4%)
  local copies, waits for them, and re-layouts  1.25 us (2%)
  between operations  0.83 us (1%)
    ppermute x6, waiting for transfers between devices, send(): return lax.ppermute(x, 'tp', perm)  33.4 us
    ppermute x6, starting transfers between devices, send(): return lax.ppermute(x, 'tp', perm)  16.6 us
    pallas_call x6, Pallas kernels, call(): pl.pallas_call(kernel, out_shape=out_shapes, in_specs=[pl.BlockSpec(memor...  6.9 us
    dot_general x4, matrix products, dot(): lax.dot_general(a, b, (dims, ((), ())), preferred_element_type=jnp.float32)  5.12 us
    ppermute x4, waiting for transfers between devices, spread_sum(): lax.ppermute(x, axis, [(i, i ^ stride * k) for i in range(size)])  3.64 us
    ppermute x4, starting transfers between devices, spread_sum(): lax.ppermute(x, axis, [(i, i ^ stride * k) for i in range(size)])  3.44 us
  transfers between devices with their start and end apart: 10, of which 7 were waited for; matrix products, arithmetic and copies ran while one was open for 13% of the time, Pallas kernels for 5%

profile of v16, /device:TPU:0, one launch (start us, length us, event | category | flops | bytes accessed | tf_op | source)
XLA Modules:
  0.0 74.5 jit_solution(2681356910878537097)
XLA Ops:
  0.6 0.0 copy-start.6
  0.6 0.0 copy-start.8
  0.7 0.0 copy-start.7
  0.7 3.1 %collective-permute-start = (bf16[1152,512]{1,0:T(8,128)(2,1)}, bf16[1152,512]{1,0:T(8,128)(2,1)}, u32[]{:S(2)}, u32[]{:S(2)}) collective-permute-start(bf16[1152,512]{1,0:T(8,128)(2,1)} %param.9), channel_id=1, source_target_pairs={{0,1},{1,0},{2,3},{3,2},{4,5},{5,4},{6,7},{7,6},{8,9},{9,8},{10,11... | collective-permute-start | bytes 3538952 | tf_op jit(solution)/shard_map/ppermute | solution.py:256
  3.8 1.9 %collective-permute-start.1 = (bf16[1152,512]{1,0:T(8,128)(2,1)}, bf16[1152,512]{1,0:T(8,128)(2,1)S(1)}, u32[]{:S(2)}, u32[]{:S(2)}) collective-permute-start(bf16[1152,512]{1,0:T(8,128)(2,1)} %param.9), channel_id=1, source_target_pairs={{1,2},{2,1},{0,0},{3,3},{5,6},{6,5},{4,4},{7,7},{9,10},{10,9},{8,8... | collective-permute-start | bytes 3538952 | tf_op jit(solution)/shard_map/ppermute | solution.py:256
  5.7 1.2 %constant_dynamic-slice_fusion.3 = (bf16[384,256]{1,0:T(8,128)(2,1)S(1)}, bf16[384,256]{1,0:T(8,128)(2,1)S(1)}) fusion(bf16[4608,256]{1,0:T(8,128)(2,1)} %param.8, s32[]{:T(128)S(6)} %select_n.56, s32[]{:T(128)S(6)} %select_n.58), kind=kLoop, calls=%fused_computation.23 | loop fusion | bytes 786440 | tf_op jit(solution)/shard_map/dynamic_slice | solution.py:253
  6.9 0.0 copy-start.4
  6.9 0.0 copy-start.5
  6.9 1.3 %dynamic-slice_select_fusion.1 = (bf16[768,256]{1,0:T(8,128)(2,1)S(1)}, bf16[768,256]{1,0:T(8,128)(2,1)S(1)}) fusion(bf16[4608,256]{1,0:T(8,128)(2,1)} %param.8, s32[]{:T(128)S(6)} %select_n.60, pred[]{:T(512)S(6)} %or.3, s32[]{:T(128)S(6)} %add.58), kind=kLoop, calls=%fused_computation.10 | loop fusion | flops 196608 | bytes 1572873 | tf_op jit(solution)/shard_map/jit(_where)/select_n | solution.py:275
  8.2 0.0 copy-done.6
  8.2 0.0 copy-done.8
  8.2 0.0 copy-done.7
  8.2 0.1 fusion.11
  8.4 0.0 copy-done.2
  8.4 0.9 %constant_dynamic-slice_fusion.2 = (bf16[1152,256]{1,0:T(8,128)(2,1)S(1)}, bf16[1152,256]{1,0:T(8,128)(2,1)}) fusion(bf16[4608,256]{1,0:T(8,128)(2,1)S(1)} %copy-done.2, s32[]{:T(128)S(6)} %select_n.58, s32[]{:T(128)S(6)} %select_n.60, pred[]{:T(512)S(6)} %or.3), kind=kLoop, calls=%fused_computation.22 | loop fusion | flops 294912 | bytes 2359305 | tf_op jit(solution)/shard_map/dynamic_slice | solution.py:253
  9.3 0.0 copy-done.4
  9.3 0.0 copy-done.5
  9.3 1.3 %convolution_add_fusion.1 = f32[256,512]{1,0:T(8,128)} fusion(bf16[1152,512]{1,0:T(8,128)(2,1)S(1)} %copy-done.4, bf16[4608,256]{1,0:T(8,128)(2,1)S(1)} %copy-done.2, s32[]{:T(128)S(6)} %select_n.64, f32[1,256,512]{2,1,0:T(8,128)S(1)} %copy-done.5), kind=kOutput, calls=%fused_computation.4 | convolution fusion | flops 302252032 | bytes 2818052 | tf_op jit(solution)/shard_map/dot_general | solution.py:45
  10.6 19.4 %collective-permute-done = bf16[1152,512]{1,0:T(8,128)(2,1)} collective-permute-done((bf16[1152,512]{1,0:T(8,128)(2,1)}, bf16[1152,512]{1,0:T(8,128)(2,1)}, u32[]{:S(2)}, u32[]{:S(2)}) %collective-permute-start) | collective-permute-done | bytes 1179680 | tf_op jit(solution)/shard_map/ppermute | solution.py:256
  30.0 1.9 %collective-permute-start.3 = (bf16[1152,512]{1,0:T(8,128)(2,1)}, bf16[1152,512]{1,0:T(8,128)(2,1)S(1)}, u32[]{:S(2)}, u32[]{:S(2)}) collective-permute-start(bf16[1152,512]{1,0:T(8,128)(2,1)} %collective-permute-done), channel_id=1, source_target_pairs={{1,2},{2,1},{0,0},{3,3},{5,6},{6,5},{4,4},{7,7},{9,10},{10,9},{8,8... | collective-permute-start | bytes 3538952 | tf_op jit(solution)/shard_map/ppermute | solution.py:256
  32.0 0.1 fusion.2
  32.0 0.0 collective-permute-done.1.cross_ref
  32.0 1.0 %slice_select_fusion = bf16[784,512]{1,0:T(8,128)(2,1)} fusion(bf16[784,512]{1,0:T(8,128)(2,1)S(1)} %fusion.2, bf16[1152,512]{1,0:T(8,128)(2,1)S(1)} %collective-permute-done.1.cross_ref, pred[]{:T(512)S(6)} %or.3), kind=kLoop, calls=%fused_computation.6 | loop fusion | flops 401408 | bytes 2408449 | tf_op jit(solution)/shard_map/jit(_where)/select_n | solution.py:283
  33.0 3.3 %collective-permute-start.2 = (bf16[784,512]{1,0:T(8,128)(2,1)}, bf16[784,512]{1,0:T(8,128)(2,1)}, u32[]{:S(2)}, u32[]{:S(2)}) collective-permute-start(bf16[784,512]{1,0:T(8,128)(2,1)} %slice_select_fusion), channel_id=1, source_target_pairs={{0,1},{1,0},{2,3},{3,2},{4,5},{5,4},{6,7},{7,6},{8,9},{9,8},{10,11... | collective-permute-start | bytes 2408456 | tf_op jit(solution)/shard_map/ppermute | solution.py:256
  36.3 1.6 %fusion.12 = f32[256,512]{1,0:T(8,128)S(1)} fusion(bf16[1152,256]{1,0:T(8,128)(2,1)} %get-tuple-element.32, bf16[1152,512]{1,0:T(8,128)(2,1)S(1)} %collective-permute-done.1.cross_ref), kind=kOutput, calls=%fused_computation.25 | convolution fusion | flops 301989888 | bytes 2293760 | tf_op jit(solution)/shard_map/dot_general | solution.py:45
  38.0 0.0 copy-start
  38.0 0.0 copy-start.1
  38.0 2.0 %fusion.1.m_ref = f32[256,512]{1,0:T(8,128)S(1)} fusion(f32[256,512]{1,0:T(8,128)S(1)} %fusion.12, f32[256,512]{1,0:T(8,128)S(1)} %copy-done.3, bf16[1152,512]{1,0:T(8,128)(2,1)} %collective-permute-done, bf16[4608,256]{1,0:T(8,128)(2,1)} %param.8, s32[]{:T(128)S(6)} %select_n.65), kind=kOutput, calls=%fused_computation.3 | convolution fusion | flops 302252032 | bytes 3342340 | tf_op jit(solution)/shard_map/dot_general | solution.py:45
  40.0 13.3 %collective-permute-done.2.swapped_ref = bf16[784,512]{1,0:T(8,128)(2,1)} collective-permute-done((bf16[784,512]{1,0:T(8,128)(2,1)}, bf16[784,512]{1,0:T(8,128)(2,1)}, u32[]{:S(2)}, u32[]{:S(2)}) %collective-permute-start.2) | collective-permute-done | bytes 802848 | tf_op jit(solution)/shard_map/ppermute | solution.py:256
  53.4 0.0 copy-done
  53.4 2.3 %shard_map.95 = (f32[256,512]{1,0:T(8,128)S(1)}, f32[256,512]{1,0:T(8,128)S(1)}, bf16[256,1152]{1,0:T(8,128)(2,1)S(1)}, bf16[256,1152]{1,0:T(8,128)(2,1)S(1)}, f...) custom-call(f32[256,512]{1,0:T(8,128)S(1)} %fusion.1.m_ref, bf16[1152,256]{1,0:T(8,128)(2,1)S(1)} %get-tuple-element.60.far_hidden_ref, ...), custom_call_target="tpu_custom_call" | custom-call | flops 400000000 | bytes 4000000 | tf_op jit(solution)/shard_map/pallas_call | solution.py:203
  55.7 0.0 collective-permute-done.3.far_ref
  55.7 1.3 %shard_map.96 = (s16[272,512]{1,0:T(8,128)(2,1)S(1)}, f32[64,128]{1,0:T(8,128)S(1)}) custom-call(f32[256,512]{1,0:T(8,128)S(1)} %get-tuple-element.40.helped_ref, bf16[256,1152]{1,0:T(8,128)(2,1)S(1)} %get-tuple-element.41.turned_ref, bf16[1152,512]{1,0:T(8,128)(2,1)S(1)} %collective-permute-done.3.far_ref, f32[16,512]{1,0:T(8,128)S(1)} %get-tuple-element.43.places_ref, ...), custom_call_target="tpu_custom_call" | custom-call | flops 400000000 | bytes 4000000 | tf_op jit(solution)/shard_map/pallas_call | solution.py:203
  57.0 5.1 %collective-permute-start.4 = (f32[64,128]{1,0:T(8,128)S(1)}, f32[64,128]{1,0:T(8,128)S(1)}, u32[]{:S(2)}, u32[]{:S(2)}) collective-permute-start(f32[64,128]{1,0:T(8,128)S(1)} %get-tuple-element.46), channel_id=1, source_target_pairs={{0,1},{1,0},{2,3},{3,2},{4,5},{5,4},{6,7},{7,6},{8,9},{9,8},{10,11... | collective-permute-start | bytes 98312 | tf_op jit(solution)/shard_map/ppermute | solution.py:256
  62.1 1.3 %collective-permute-start.9 = (s16[272,512]{1,0:T(8,128)(2,1)S(1)}, s16[272,512]{1,0:T(8,128)(2,1)S(1)}, u32[]{:S(2)}, u32[]{:S(2)}) collective-permute-start(s16[272,512]{1,0:T(8,128)(2,1)S(1)} %get-tuple-element.56), channel_id=1, source_target_pairs={{1,0},{2,3},{5,4},{6,7},{9,8},{10,11},{13,12},{14,15},{17,16},{18,... | collective-permute-start | bytes 835592 | tf_op jit(solution)/shard_map/ppermute | solution.py:256
  63.4 0.5 collective-permute-done.4
  64.0 0.0 collective-permute-start.5
  64.0 1.6 %collective-permute-start.6 = (f32[64,128]{1,0:T(8,128)S(1)}, f32[64,128]{1,0:T(8,128)S(1)}, u32[]{:S(2)}, u32[]{:S(2)}) collective-permute-start(f32[64,128]{1,0:T(8,128)S(1)} %select_add_fusion.bands_ref), channel_id=1, source_target_pairs={{0,8},{4,12},{8,0},{12,4},{16,24},{20,28},{24,16},{28,20},{1,9},{5... | collective-permute-start | bytes 98312 | tf_op jit(solution)/shard_map/ppermute | solution.py:221
  65.5 0.3 collective-permute-start.7
  65.8 0.8 %shard_map.98.x_ref = f32[256,512]{1,0:T(8,128)S(1)} custom-call(f32[256,512]{1,0:T(8,128)S(1)} %get-tuple-element.55.m_ref, f32[64,128]{1,0:T(8,128)S(1)} %select_add_fusion.bands_ref, f32[8,512]{1,0:T(8,128)S(1)} %get-tuple-element.36.places_ref.refs_2_, bf16[512,128]{1,0:T(8,128)(2,1)S(1)} %copy-done.1, f32[256,256]{1,0:T(8,128)S(1)} %copy-done), custom_call_target="tpu_custom_call" | custom-call | flops 400000000 | bytes 4000000 | tf_op jit(solution)/shard_map/pallas_call | solution.py:203
  66.7 0.0 collective-permute-done.5
  66.7 1.3 %collective-permute-done.6 = f32[64,128]{1,0:T(8,128)S(1)} collective-permute-done((f32[64,128]{1,0:T(8,128)S(1)}, f32[64,128]{1,0:T(8,128)S(1)}, u32[]{:S(2)}, u32[]{:S(2)}) %collective-permute-start.6) | collective-permute-done | bytes 32800 | tf_op jit(solution)/shard_map/ppermute | solution.py:221
  68.0 0.9 %collective-permute-done.7 = f32[64,128]{1,0:T(8,128)S(1)} collective-permute-done((f32[64,128]{1,0:T(8,128)S(1)}, f32[64,128]{1,0:T(8,128)S(1)}, u32[]{:S(2)}, u32[]{:S(2)}) %collective-permute-start.7) | collective-permute-done | bytes 32800 | tf_op jit(solution)/shard_map/ppermute | solution.py:221
  68.9 1.6 %collective-permute-start.8 = (f32[64,128]{1,0:T(8,128)S(1)}, f32[64,128]{1,0:T(8,128)S(1)}, u32[]{:S(2)}, u32[]{:S(2)}) collective-permute-start(f32[64,128]{1,0:T(8,128)S(1)} %add_add_fusion.refs_0_), channel_id=1, source_target_pairs={{0,16},{4,20},{8,24},{12,28},{16,0},{20,4},{24,8},{28,12},{1,17},{... | collective-permute-start | bytes 98312 | tf_op jit(solution)/shard_map/ppermute | solution.py:221
  70.5 0.1 collective-permute-done.9.code_ref
  70.6 0.9 %shard_map.99 = f32[256,512]{1,0:T(8,128)} custom-call(f32[256,512]{1,0:T(8,128)S(1)} %shard_map.98.x_ref, s16[272,512]{1,0:T(8,128)(2,1)S(1)} %collective-permute-done.9.code_ref), custom_call_target="tpu_custom_call" | custom-call | flops 400000000 | bytes 4000000 | tf_op jit(solution)/shard_map/pallas_call | solution.py:203
  71.4 1.4 %collective-permute-done.8.refs_1_ = f32[64,128]{1,0:T(8,128)S(1)} collective-permute-done((f32[64,128]{1,0:T(8,128)S(1)}, f32[64,128]{1,0:T(8,128)S(1)}, u32[]{:S(2)}, u32[]{:S(2)}) %collective-permute-start.8) | collective-permute-done | bytes 32800 | tf_op jit(solution)/shard_map/ppermute | solution.py:221
  72.9 1.6 %shard_map.100 = bf16[256,512]{1,0:T(8,128)(2,1)} custom-call(f32[64,128]{1,0:T(8,128)S(1)} %add_add_fusion.refs_0_, f32[64,128]{1,0:T(8,128)S(1)} %collective-permute-done.8.refs_1_, f32[8,512]{1,0:T(8,128)S(1)} %get-tuple-element.36.places_ref.refs_2_, bf16[512,128]{1,0:T(8,128)(2,1)S(1)} %copy-done.1, f32[256,256]{1,0:T(8,128)S(1)} %copy-done), custom_call_target="tpu_custom_call" | custom-call | flops 400000000 | bytes 4000000 | tf_op jit(solution)/shard_map/pallas_call | solution.py:203
  (7 shorter events, 0.1 us)
Async XLA Ops:
  0.6 7.6 %copy-start.6 = (bf16[8,512]{1,0:T(8,128)(2,1)S(1)}, bf16[8,512]{1,0:T(8,128)(2,1)}, u32[]{:S(2)}) copy-start(bf16[8,512]{1,0:T(8,128)(2,1)} %constant.52) | copy-start | bytes 24580
  0.6 7.6 %copy-start.8 = (s32[4,8]{1,0:T(4,128)S(1)}, s32[4,8]{1,0:T(4,128)}, u32[]{:S(2)}) copy-start(s32[4,8]{1,0:T(4,128)} %param.11) | copy-start | bytes 388
  0.7 7.6 %copy-start.7 = (s32[4,8]{1,0:T(4,128)S(1)}, s32[4,8]{1,0:T(4,128)}, u32[]{:S(2)}) copy-start(s32[4,8]{1,0:T(4,128)} %param.12) | copy-start | bytes 388
  0.7 29.4 %collective-permute-start = (bf16[1152,512]{1,0:T(8,128)(2,1)}, bf16[1152,512]{1,0:T(8,128)(2,1)}, u32[]{:S(2)}, u32[]{:S(2)}) collective-permute-start(bf16[1152,512]{1,0:T(8,128)(2,1)} %param.9), channel_id=1, source_target_pairs={{0,1},{1,0},{2,3},{3,2},{4,5},{5,4},{6,7},{7,6},{8,9},{9,8},{10,11... | collective-permute-start | bytes 3538952 | tf_op jit(solution)/shard_map/ppermute | solution.py:256
  3.8 28.3 %collective-permute-start.1 = (bf16[1152,512]{1,0:T(8,128)(2,1)}, bf16[1152,512]{1,0:T(8,128)(2,1)S(1)}, u32[]{:S(2)}, u32[]{:S(2)}) collective-permute-start(bf16[1152,512]{1,0:T(8,128)(2,1)} %param.9), channel_id=1, source_target_pairs={{1,2},{2,1},{0,0},{3,3},{5,6},{6,5},{4,4},{7,7},{9,10},{10,9},{8,8... | collective-permute-start | bytes 3538952 | tf_op jit(solution)/shard_map/ppermute | solution.py:256
  5.7 2.7 %copy-start.2 = (bf16[4608,256]{1,0:T(8,128)(2,1)S(1)}, bf16[4608,256]{1,0:T(8,128)(2,1)}, u32[]{:S(2)}) copy-start(bf16[4608,256]{1,0:T(8,128)(2,1)} %param.8) | copy-start | bytes 7077892
  6.9 2.4 %copy-start.4 = (bf16[1152,512]{1,0:T(8,128)(2,1)S(1)}, bf16[1152,512]{1,0:T(8,128)(2,1)}, u32[]{:S(2)}) copy-start(bf16[1152,512]{1,0:T(8,128)(2,1)} %param.9) | copy-start | bytes 3538948
  6.9 2.4 %copy-start.5 = (f32[1,256,512]{2,1,0:T(8,128)S(1)}, f32[1,256,512]{2,1,0:T(8,128)}, u32[]{:S(2)}) copy-start(f32[1,256,512]{2,1,0:T(8,128)} %param.10) | copy-start | bytes 1572868
  30.0 25.6 %collective-permute-start.3 = (bf16[1152,512]{1,0:T(8,128)(2,1)}, bf16[1152,512]{1,0:T(8,128)(2,1)S(1)}, u32[]{:S(2)}, u32[]{:S(2)}) collective-permute-start(bf16[1152,512]{1,0:T(8,128)(2,1)} %collective-permute-done), channel_id=1, source_target_pairs={{1,2},{2,1},{0,0},{3,3},{5,6},{6,5},{4,4},{7,7},{9,10},{10,9},{8,8... | collective-permute-start | bytes 3538952 | tf_op jit(solution)/shard_map/ppermute | solution.py:256
  33.0 20.4 %collective-permute-start.2 = (bf16[784,512]{1,0:T(8,128)(2,1)}, bf16[784,512]{1,0:T(8,128)(2,1)}, u32[]{:S(2)}, u32[]{:S(2)}) collective-permute-start(bf16[784,512]{1,0:T(8,128)(2,1)} %slice_select_fusion), channel_id=1, source_target_pairs={{0,1},{1,0},{2,3},{3,2},{4,5},{5,4},{6,7},{7,6},{8,9},{9,8},{10,11... | collective-permute-start | bytes 2408456 | tf_op jit(solution)/shard_map/ppermute | solution.py:256
  36.3 1.6 %copy-start.3 = (f32[256,512]{1,0:T(8,128)S(1)}, f32[256,512]{1,0:T(8,128)}, u32[]{:S(2)}) copy-start(f32[256,512]{1,0:T(8,128)} %convolution_add_fusion.1) | copy-start | bytes 1572868
  38.0 15.4 %copy-start = (f32[256,256]{1,0:T(8,128)S(1)}, f32[256,256]{1,0:T(8,128)}, u32[]{:S(2)}) copy-start(f32[256,256]{1,0:T(8,128)} %constant.34.clone.refs_1_.basis_ref.refs_4_) | copy-start | bytes 786436
  38.0 15.4 %copy-start.1 = (bf16[512,128]{1,0:T(8,128)(2,1)S(1)}, bf16[512,128]{1,0:T(8,128)(2,1)}, u32[]{:S(2)}) copy-start(bf16[512,128]{1,0:T(8,128)(2,1)} %constant.33.clone.refs_0_.fold_ref.refs_3_) | copy-start | bytes 393220
  57.0 7.0 %collective-permute-start.4 = (f32[64,128]{1,0:T(8,128)S(1)}, f32[64,128]{1,0:T(8,128)S(1)}, u32[]{:S(2)}, u32[]{:S(2)}) collective-permute-start(f32[64,128]{1,0:T(8,128)S(1)} %get-tuple-element.46), channel_id=1, source_target_pairs={{0,1},{1,0},{2,3},{3,2},{4,5},{5,4},{6,7},{7,6},{8,9},{9,8},{10,11... | collective-permute-start | bytes 98312 | tf_op jit(solution)/shard_map/ppermute | solution.py:256
  62.1 8.4 %collective-permute-start.9 = (s16[272,512]{1,0:T(8,128)(2,1)S(1)}, s16[272,512]{1,0:T(8,128)(2,1)S(1)}, u32[]{:S(2)}, u32[]{:S(2)}) collective-permute-start(s16[272,512]{1,0:T(8,128)(2,1)S(1)} %get-tuple-element.56), channel_id=1, source_target_pairs={{1,0},{2,3},{5,4},{6,7},{9,8},{10,11},{13,12},{14,15},{17,16},{18,... | collective-permute-start | bytes 835592 | tf_op jit(solution)/shard_map/ppermute | solution.py:256
  64.0 2.7 %collective-permute-start.5 = (f32[64,128]{1,0:T(8,128)S(1)}, f32[64,128]{1,0:T(8,128)S(1)}, u32[]{:S(2)}, u32[]{:S(2)}) collective-permute-start(f32[64,128]{1,0:T(8,128)S(1)} %select_add_fusion.bands_ref), channel_id=1, source_target_pairs={{0,4},{4,0},{8,12},{12,8},{16,20},{20,16},{24,28},{28,24},{1,5},{5... | collective-permute-start | bytes 98312 | tf_op jit(solution)/shard_map/ppermute | solution.py:221
  64.0 4.0 %collective-permute-start.6 = (f32[64,128]{1,0:T(8,128)S(1)}, f32[64,128]{1,0:T(8,128)S(1)}, u32[]{:S(2)}, u32[]{:S(2)}) collective-permute-start(f32[64,128]{1,0:T(8,128)S(1)} %select_add_fusion.bands_ref), channel_id=1, source_target_pairs={{0,8},{4,12},{8,0},{12,4},{16,24},{20,28},{24,16},{28,20},{1,9},{5... | collective-permute-start | bytes 98312 | tf_op jit(solution)/shard_map/ppermute | solution.py:221
  65.5 3.4 %collective-permute-start.7 = (f32[64,128]{1,0:T(8,128)S(1)}, f32[64,128]{1,0:T(8,128)S(1)}, u32[]{:S(2)}, u32[]{:S(2)}) collective-permute-start(f32[64,128]{1,0:T(8,128)S(1)} %select_add_fusion.bands_ref), channel_id=1, source_target_pairs={{0,12},{4,8},{8,4},{12,0},{16,28},{20,24},{24,20},{28,16},{1,13},{... | collective-permute-start | bytes 98312 | tf_op jit(solution)/shard_map/ppermute | solution.py:221
  68.9 4.0 %collective-permute-start.8 = (f32[64,128]{1,0:T(8,128)S(1)}, f32[64,128]{1,0:T(8,128)S(1)}, u32[]{:S(2)}, u32[]{:S(2)}) collective-permute-start(f32[64,128]{1,0:T(8,128)S(1)} %add_add_fusion.refs_0_), channel_id=1, source_target_pairs={{0,16},{4,20},{8,24},{12,28},{16,0},{20,4},{24,8},{28,12},{1,17},{... | collective-permute-start | bytes 98312 | tf_op jit(solution)/shard_map/ppermute | solution.py:221

commit v17 on v14

--- a/solution.py
+++ b/solution.py
@@ -139,15 +139,18 @@
     return values * jnp.exp2(exponents[:1] - 15.0)
 
 
-def swapped_kernel(m_ref, far_hidden_ref, cross_hidden_ref, cross_ref, swapped_ref, places_ref, *refs):
+def swapped_kernel(m_ref, hidden_ref, cross_hidden_ref, cross_ref, far_ref, swapped_ref, places_ref, *refs):
     *matrix_refs, out_ref, helped_ref, own_turned_ref, end_turned_ref, end_places_ref, bands_ref = refs
-    handed, side = swapped_ref.shape[0] - place_rows, out_ref.shape[0]
+    handed, side = far_ref.shape[0], out_ref.shape[0]
     alone = cross_ref.shape[0] - handed
     out_ref[...] = m_ref[...] + dot(cross_hidden_ref[...], swapped_ref[:handed], ((0,), (0,)))
-    helped_ref[...] = dot(swapped_ref[:alone, :side], cross_ref[handed:], ((0,), (0,)))
-    own_turned_ref[...] = far_hidden_ref[...].T
-    end_turned_ref[:, : handed - alone] = swapped_ref[alone:handed, :side].T
-    end_turned_ref[:, handed - alone :] = swapped_ref[:handed, side:].T
+    helped_ref[...] = (
+        dot(swapped_ref[:alone, :side], cross_ref[handed:], ((0,), (0,)))
+        + dot(swapped_ref[alone:handed, :side], far_ref[: handed - alone], ((0,), (0,)))
+        + dot(swapped_ref[:alone, side:], far_ref[handed - alone :], ((0,), (0,)))
+    )
+    own_turned_ref[...] = hidden_ref[...].T
+    end_turned_ref[...] = swapped_ref[alone:handed, side:].T
     end_places_ref[...] = swapped_ref[handed:].astype(jnp.float32)
     bands_ref[...] = bands_of(out_ref[...], places_ref[...], *matrix_refs)
 
@@ -259,9 +262,10 @@
     across = [(1, 2), (2, 1)]
     outward = [(1, 0), (2, 3)]
 
-    pair_grad = send(out_grad, both_ways)
     cross_grad = send(out_grad, across)
     m = carried + product(rows_of(me), out_grad)
+    own, m = lax.optimization_barrier((out_grad, m))
+    pair_parts = [send(own[:handed], both_ways), send(own[handed:], both_ways)]
     far_hidden = rows_of(far)
     helped_hidden = jnp.concatenate(
         [
@@ -275,28 +279,35 @@
     cross_hidden = jnp.where(end, rows_of(cross, 0, handed), 0)
     helped_hidden, cross_hidden, m = lax.optimization_barrier((helped_hidden, cross_hidden, m))
 
-    far_grad = send(pair_grad, across)
-    cross_grad, matrices, places = after((cross_grad, matrices, places), pair_grad, m)
+    far_head = send(pair_parts[0], across)
+    m = m + product(rows_of(me ^ 1, 0, handed), pair_parts[0])
+    pair_rest, m = lax.optimization_barrier((pair_parts[1], m))
+    far_parts = [far_head, send(pair_rest, across)]
+    cross_grad, matrices, places = after((cross_grad, matrices, places), pair_parts[0], m)
     swapped = send(jnp.where(end, helped_hidden, cross_grad[: handed + place_rows]), both_ways)
-    m = m + product(rows_of(me ^ 1), pair_grad) + product(rows_of(cross), cross_grad)
+    far_parts[0], pair_rest, cross_grad = lax.optimization_barrier((far_parts[0], pair_rest, cross_grad))
+    m = m + product(rows_of(me ^ 1, handed), pair_rest)
+    m = m + product(rows_of(cross), cross_grad) + product(far_hidden[:handed], far_parts[0])
+    m, swapped = lax.optimization_barrier((m, swapped))
 
     height, width = m.shape[0] // steps, m.shape[1] // steps
     full = jax.ShapeDtypeStruct(m.shape, jnp.float32)
-    turned = jax.ShapeDtypeStruct((m.shape[0], tok), hidden.dtype)
+    turned = jax.ShapeDtypeStruct((m.shape[0], alone), hidden.dtype)
     table = jax.ShapeDtypeStruct((place_rows, m.shape[1]), jnp.float32)
     folded = jax.ShapeDtypeStruct((height, width), jnp.float32)
     m, helped, own_turned, end_turned, end_places, own_bands = call(
         swapped_kernel,
         (full, full, turned, turned, table, folded),
         m,
-        far_hidden,
+        far_hidden[handed:],
         cross_hidden,
         cross_grad,
+        far_parts[0],
         swapped,
         places,
         *matrices,
     )
-    far_grad = after(far_grad, m)
+    far_grad = after(far_parts[1], m)
     code_shape = jax.ShapeDtypeStruct((m.shape[0] + code_rows, m.shape[1]), jnp.int16)
     code, end_bands = call(
         helped_kernel, (code_shape, folded), helped, end_turned, far_grad, end_places, *matrices

time: 74.8 us -> 78 us (1.043)
  waiting for transfers between devices: 40 us -> 32.1 us
  starting transfers between devices: 19 us -> 26.2 us
  local copies, waits for them, and re-layouts: 1.19 us -> 4.18 us
  matrix products: 4.1 us -> 7.07 us
  other arithmetic: 3.56 us -> 1.35 us
    ppermute x6 -> x8, waiting for transfers between devices: 36.3 us -> 29.1 us  [send(): return lax.ppermute(x, 'tp', perm)]
    ppermute x6 -> x8, starting transfers between devices: 15.6 us -> 22.8 us  [send(): return lax.ppermute(x, 'tp', perm)]
    slice x0 -> x3, local copies, waits for them, and re-layouts: none -> 4.15 us  [the longest x2 2.99 us: lined(): pair_parts = [send(own[:handed], both_ways), send(own[handed:], both_ways)]]
    dot_general x4 -> x6, matrix products: 4.1 us -> 7.07 us  [dot(): lax.dot_general(a, b, (dims, ((), ())), preferred_element_type=jnp.float32)]
    select_n x1, other arithmetic: 1.38 us -> 0.09 us  [lined(): jnp.where(end, helped_hidden, cross_grad[:handed + place_rows])]
    dynamic_slice x2 -> x0, local copies, waits for them, and re-layouts: 1.15 us -> none  [rows_of(): return lax.dynamic_slice_in_dim(hidden, part * tok + start, stop - start, 0)]
    concatenate x1, other arithmetic: 0.97 us -> 0.06 us  [lined(): helped_hidden = jnp.concatenate([helped_hidden, place_part], axis=0)]
  transfers between devices with their start and end apart: 10 -> 12, of which waited for: 7 -> 8; matrix products, arithmetic and copies ran while one was open for 12% -> 11% of each run, Pallas kernels for 4% -> 4%
where the time goes in v17:
time: 78 us; the launch traced here: 77.6 us
  waiting for transfers between devices  32.1 us (41%)
  starting transfers between devices  26.2 us (34%)
  matrix products  7.07 us (9%)
  Pallas kernels  5.87 us (8%)
  local copies, waits for them, and re-layouts  4.18 us (5%)
  other arithmetic  1.35 us (2%)
  between operations  0.85 us (1%)
    ppermute x8, waiting for transfers between devices, send(): return lax.ppermute(x, 'tp', perm)  29.1 us
    ppermute x8, starting transfers between devices, send(): return lax.ppermute(x, 'tp', perm)  22.8 us
    dot_general x6, matrix products, dot(): lax.dot_general(a, b, (dims, ((), ())), preferred_element_type=jnp.float32)  7.07 us
    pallas_call x6, Pallas kernels, call(): pl.pallas_call(kernel, out_shape=out_shapes, in_specs=[pl.BlockSpec(memor...  5.87 us
    ppermute x4, starting transfers between devices, spread_sum(): lax.ppermute(x, axis, [(i, i ^ stride * k) for i in range(size)])  3.44 us
    slice x2, local copies, waits for them, and re-layouts, lined(): pair_parts = [send(own[:handed], both_ways), send(own[handed:], both_ways)]  2.99 us
    ppermute x4, waiting for transfers between devices, spread_sum(): lax.ppermute(x, axis, [(i, i ^ stride * k) for i in range(size)])  2.95 us
  transfers between devices with their start and end apart: 12, of which 8 were waited for; matrix products, arithmetic and copies ran while one was open for 11% of the time, Pallas kernels for 4%

profile of v17, /device:TPU:0, one launch (start us, length us, event | category | flops | bytes accessed | tf_op | source)
XLA Modules:
  0.0 77.6 jit_solution(12119720262532465113)
XLA Ops:
  0.6 2.9 %convolution_add_fusion.2 = f32[256,512]{1,0:T(8,128)} fusion(bf16[1152,512]{1,0:T(8,128)(2,1)} %param.9, bf16[4608,256]{1,0:T(8,128)(2,1)} %param.8, s32[]{:T(128)S(6)} %select_n.50, f32[1,256,512]{2,1,0:T(8,128)} %param.10), kind=kOutput, calls=%fused_computation.5 | convolution fusion | flops 302252032 | bytes 2818052 | tf_op jit(solution)/shard_map/dot_general | solution.py:45
  3.5 1.2 %slice.24 = bf16[768,512]{1,0:T(8,128)(2,1)S(1)} slice(bf16[1152,512]{1,0:T(8,128)(2,1)} %param.9), slice={[0:768], [0:512]} | slice | bytes 1572864 | tf_op jit(solution)/shard_map/slice | solution.py:268
  4.8 3.1 %collective-permute-start.1 = (bf16[768,512]{1,0:T(8,128)(2,1)S(1)}, bf16[768,512]{1,0:T(8,128)(2,1)}, u32[]{:S(2)}, u32[]{:S(2)}) collective-permute-start(bf16[768,512]{1,0:T(8,128)(2,1)S(1)} %slice.24), channel_id=1, source_target_pairs={{0,1},{1,0},{2,3},{3,2},{4,5},{5,4},{6,7},{7,6},{8,9},{9,8},{10,11... | collective-permute-start | bytes 2359304 | tf_op jit(solution)/shard_map/ppermute | solution.py:259
  7.9 0.7 collective-permute-start.3
  8.6 1.8 %slice.21 = bf16[384,512]{1,0:T(8,128)(2,1)} slice(bf16[1152,512]{1,0:T(8,128)(2,1)} %param.9), slice={[768:1152], [0:512]} | slice | bytes 786432 | tf_op jit(solution)/shard_map/slice | solution.py:268
  10.4 4.3 %collective-permute-start = (bf16[384,512]{1,0:T(8,128)(2,1)}, bf16[384,512]{1,0:T(8,128)(2,1)}, u32[]{:S(2)}, u32[]{:S(2)}) collective-permute-start(bf16[384,512]{1,0:T(8,128)(2,1)} %slice.21), channel_id=1, source_target_pairs={{0,1},{1,0},{2,3},{3,2},{4,5},{5,4},{6,7},{7,6},{8,9},{9,8},{10,11... | collective-permute-start | bytes 1179656 | tf_op jit(solution)/shard_map/ppermute | solution.py:259
  14.7 1.2 %dynamic-slice_select_fusion = (bf16[768,256]{1,0:T(8,128)(2,1)S(1)}, bf16[768,256]{1,0:T(8,128)(2,1)S(1)}) fusion(bf16[4608,256]{1,0:T(8,128)(2,1)} %param.8, s32[]{:T(128)S(6)} %select_n.56, pred[]{:T(512)S(6)} %or.3, s32[]{:T(128)S(6)} %add.76), kind=kLoop, calls=%fused_computation.14 | loop fusion | flops 196608 | bytes 1572873 | tf_op jit(solution)/shard_map/jit(_where)/select_n | solution.py:279
  15.9 0.0 copy-done.3
  15.9 0.0 copy-done.4
  15.9 0.0 copy-done.5
  15.9 0.1 fusion.18
  16.0 10.3 %collective-permute-done.1 = bf16[768,512]{1,0:T(8,128)(2,1)} collective-permute-done((bf16[768,512]{1,0:T(8,128)(2,1)S(1)}, bf16[768,512]{1,0:T(8,128)(2,1)}, u32[]{:S(2)}, u32[]{:S(2)}) %collective-permute-start.1) | collective-permute-done | bytes 786464 | tf_op jit(solution)/shard_map/ppermute | solution.py:259
  26.3 0.7 collective-permute-start.2
  27.0 1.2 %constant_dynamic-slice_fusion.2 = (bf16[384,256]{1,0:T(8,128)(2,1)S(1)}, bf16[384,256]{1,0:T(8,128)(2,1)S(1)}, bf16[384,256]{1,0:T(8,128)(2,1)S(1)}) fusion(bf16[4608,256]{1,0:T(8,128)(2,1)} %param.8, s32[]{:T(128)S(6)} %add.77, s32[]{:T(128)S(6)} %select_n.54, s32[]{:T(128)S(6)} %select_n.52), kind=kLoop, calls=%fused_computation.29 | loop fusion | bytes 1179660 | tf_op jit(solution)/shard_map/slice | solution.py:302
  28.2 0.1 fusion.2
  28.3 1.8 %convolution_add_fusion = f32[256,512]{1,0:T(8,128)S(1)} fusion(f32[256,512]{1,0:T(8,128)} %convolution_add_fusion.2, bf16[768,512]{1,0:T(8,128)(2,1)} %collective-permute-done.1, bf16[4608,256]{1,0:T(8,128)(2,1)} %param.8, s32[]{:T(128)S(6)} %select_n.58), kind=kOutput, calls=%fused_computation.2 | convolution fusion | flops 201457664 | bytes 2228228 | tf_op jit(solution)/shard_map/dot_general | solution.py:45
  30.1 0.0 copy-start.2
  30.1 3.8 %collective-permute-done = bf16[384,512]{1,0:T(8,128)(2,1)} collective-permute-done((bf16[384,512]{1,0:T(8,128)(2,1)}, bf16[384,512]{1,0:T(8,128)(2,1)}, u32[]{:S(2)}, u32[]{:S(2)}) %collective-permute-start) | collective-permute-done | bytes 393248 | tf_op jit(solution)/shard_map/ppermute | solution.py:259
  33.9 0.7 collective-permute-start.5
  34.6 0.0 collective-permute-done.3.cross_ref
  34.6 0.1 slice_select_fusion
  34.7 5.4 %collective-permute-start.4 = (bf16[784,512]{1,0:T(8,128)(2,1)S(1)}, bf16[784,512]{1,0:T(8,128)(2,1)S(1)}, u32[]{:S(2)}, u32[]{:S(2)}) collective-permute-start(bf16[784,512]{1,0:T(8,128)(2,1)S(1)} %slice_select_fusion), channel_id=1, source_target_pairs={{0,1},{1,0},{2,3},{3,2},{4,5},{5,4},{6,7},{7,6},{8,9},{9,8},{10,11... | collective-permute-start | bytes 2408456 | tf_op jit(solution)/shard_map/ppermute | solution.py:259
  40.1 0.0 collective-permute-done.2.far_ref
  40.1 1.3 %convolution_add_fusion.3 = f32[256,512]{1,0:T(8,128)S(1)} fusion(f32[256,512]{1,0:T(8,128)S(1)} %convolution_add_fusion, bf16[384,512]{1,0:T(8,128)(2,1)} %collective-permute-done, bf16[4608,256]{1,0:T(8,128)(2,1)S(1)} %copy-done.2, s32[]{:T(128)S(6)} %select_n.59), kind=kOutput, calls=%fused_computation.6 | convolution fusion | flops 100794368 | bytes 1638404 | tf_op jit(solution)/shard_map/dot_general | solution.py:45
  41.4 0.4 fusion.5
  41.8 0.0 copy-start
  41.9 0.0 copy-start.1
  41.9 0.5 fusion.1.m_ref
  42.4 13.6 %collective-permute-done.4.swapped_ref = bf16[784,512]{1,0:T(8,128)(2,1)S(1)} collective-permute-done((bf16[784,512]{1,0:T(8,128)(2,1)S(1)}, bf16[784,512]{1,0:T(8,128)(2,1)S(1)}, u32[]{:S(2)}, u32[]{:S(2)}) %collective-permute-start.4) | collective-permute-done | bytes 802848 | tf_op jit(solution)/shard_map/ppermute | solution.py:259
  56.1 0.0 copy-done
  56.1 1.5 %shard_map.95 = (f32[256,512]{1,0:T(8,128)S(1)}, f32[256,512]{1,0:T(8,128)S(1)}, bf16[256,384]{1,0:T(8,128)(2,1)S(1)}, bf16[256,384]{1,0:T(8,128)(2,1)S(1)}, f32...) custom-call(f32[256,512]{1,0:T(8,128)S(1)} %fusion.1.m_ref, bf16[384,256]{1,0:T(8,128)(2,1)S(1)} %get-tuple-element.76.hidden_ref, ...), custom_call_target="tpu_custom_call" | custom-call | flops 400000000 | bytes 4000000 | tf_op jit(solution)/shard_map/pallas_call | solution.py:206
  57.5 0.0 collective-permute-done.5.far_ref
  57.5 1.1 %shard_map.96 = (s16[272,512]{1,0:T(8,128)(2,1)S(1)}, f32[64,128]{1,0:T(8,128)S(1)}) custom-call(f32[256,512]{1,0:T(8,128)S(1)} %get-tuple-element.56.helped_ref, bf16[256,384]{1,0:T(8,128)(2,1)S(1)} %get-tuple-element.57.turned_ref, bf16[384,512]{1,0:T(8,128)(2,1)S(1)} %collective-permute-done.5.far_ref, f32[16,512]{1,0:T(8,128)S(1)} %get-tuple-element.59.places_ref, ...), custom_call_target="tpu_custom_call" | custom-call | flops 400000000 | bytes 4000000 | tf_op jit(solution)/shard_map/pallas_call | solution.py:206
  58.6 6.6 %collective-permute-start.6 = (f32[64,128]{1,0:T(8,128)S(1)}, f32[64,128]{1,0:T(8,128)S(1)}, u32[]{:S(2)}, u32[]{:S(2)}) collective-permute-start(f32[64,128]{1,0:T(8,128)S(1)} %get-tuple-element.62), channel_id=1, source_target_pairs={{0,1},{1,0},{2,3},{3,2},{4,5},{5,4},{6,7},{7,6},{8,9},{9,8},{10,11... | collective-permute-start | bytes 98312 | tf_op jit(solution)/shard_map/ppermute | solution.py:259
  65.3 1.3 %collective-permute-start.11 = (s16[272,512]{1,0:T(8,128)(2,1)S(1)}, s16[272,512]{1,0:T(8,128)(2,1)S(1)}, u32[]{:S(2)}, u32[]{:S(2)}) collective-permute-start(s16[272,512]{1,0:T(8,128)(2,1)S(1)} %get-tuple-element.72), channel_id=1, source_target_pairs={{1,0},{2,3},{5,4},{6,7},{9,8},{10,11},{13,12},{14,15},{17,16},{18,... | collective-permute-start | bytes 835592 | tf_op jit(solution)/shard_map/ppermute | solution.py:259
  66.6 0.5 collective-permute-done.6
  67.1 0.0 collective-permute-start.7
  67.2 1.6 %collective-permute-start.8 = (f32[64,128]{1,0:T(8,128)S(1)}, f32[64,128]{1,0:T(8,128)S(1)}, u32[]{:S(2)}, u32[]{:S(2)}) collective-permute-start(f32[64,128]{1,0:T(8,128)S(1)} %select_add_fusion.bands_ref), channel_id=1, source_target_pairs={{0,8},{4,12},{8,0},{12,4},{16,24},{20,28},{24,16},{28,20},{1,9},{5... | collective-permute-start | bytes 98312 | tf_op jit(solution)/shard_map/ppermute | solution.py:224
  68.7 0.3 collective-permute-start.9
  69.0 0.8 %shard_map.98.x_ref = f32[256,512]{1,0:T(8,128)S(1)} custom-call(f32[256,512]{1,0:T(8,128)S(1)} %get-tuple-element.71.m_ref, f32[64,128]{1,0:T(8,128)S(1)} %select_add_fusion.bands_ref, f32[8,512]{1,0:T(8,128)S(1)} %get-tuple-element.52.places_ref.refs_2_, bf16[512,128]{1,0:T(8,128)(2,1)S(1)} %copy-done.1, f32[256,256]{1,0:T(8,128)S(1)} %copy-done), custom_call_target="tpu_custom_call" | custom-call | flops 400000000 | bytes 4000000 | tf_op jit(solution)/shard_map/pallas_call | solution.py:206
  69.9 0.0 collective-permute-done.7
  69.9 1.3 %collective-permute-done.8 = f32[64,128]{1,0:T(8,128)S(1)} collective-permute-done((f32[64,128]{1,0:T(8,128)S(1)}, f32[64,128]{1,0:T(8,128)S(1)}, u32[]{:S(2)}, u32[]{:S(2)}) %collective-permute-start.8) | collective-permute-done | bytes 32800 | tf_op jit(solution)/shard_map/ppermute | solution.py:224
  71.1 0.9 %collective-permute-done.9 = f32[64,128]{1,0:T(8,128)S(1)} collective-permute-done((f32[64,128]{1,0:T(8,128)S(1)}, f32[64,128]{1,0:T(8,128)S(1)}, u32[]{:S(2)}, u32[]{:S(2)}) %collective-permute-start.9) | collective-permute-done | bytes 32800 | tf_op jit(solution)/shard_map/ppermute | solution.py:224
  72.1 1.6 %collective-permute-start.10 = (f32[64,128]{1,0:T(8,128)S(1)}, f32[64,128]{1,0:T(8,128)S(1)}, u32[]{:S(2)}, u32[]{:S(2)}) collective-permute-start(f32[64,128]{1,0:T(8,128)S(1)} %add_add_fusion.refs_0_), channel_id=1, source_target_pairs={{0,16},{4,20},{8,24},{12,28},{16,0},{20,4},{24,8},{28,12},{1,17},{... | collective-permute-start | bytes 98312 | tf_op jit(solution)/shard_map/ppermute | solution.py:224
  73.7 0.8 collective-permute-done.11.code_ref
  74.4 0.9 %shard_map.99 = f32[256,512]{1,0:T(8,128)} custom-call(f32[256,512]{1,0:T(8,128)S(1)} %shard_map.98.x_ref, s16[272,512]{1,0:T(8,128)(2,1)S(1)} %collective-permute-done.11.code_ref), custom_call_target="tpu_custom_call" | custom-call | flops 400000000 | bytes 4000000 | tf_op jit(solution)/shard_map/pallas_call | solution.py:206
  75.3 0.8 collective-permute-done.10.refs_1_
  76.1 1.6 %shard_map.100 = bf16[256,512]{1,0:T(8,128)(2,1)} custom-call(f32[64,128]{1,0:T(8,128)S(1)} %add_add_fusion.refs_0_, f32[64,128]{1,0:T(8,128)S(1)} %collective-permute-done.10.refs_1_, f32[8,512]{1,0:T(8,128)S(1)} %get-tuple-element.52.places_ref.refs_2_, bf16[512,128]{1,0:T(8,128)(2,1)S(1)} %copy-done.1, f32[256,256]{1,0:T(8,128)S(1)} %copy-done), custom_call_target="tpu_custom_call" | custom-call | flops 400000000 | bytes 4000000 | tf_op jit(solution)/shard_map/pallas_call | solution.py:206
  (8 shorter events, 0.1 us)
Async XLA Ops:
  3.5 12.3 %copy-start.3 = (bf16[8,512]{1,0:T(8,128)(2,1)S(1)}, bf16[8,512]{1,0:T(8,128)(2,1)}, u32[]{:S(2)}) copy-start(bf16[8,512]{1,0:T(8,128)(2,1)} %constant.57) | copy-start | bytes 24580
  3.5 12.4 %copy-start.4 = (s32[4,8]{1,0:T(4,128)S(1)}, s32[4,8]{1,0:T(4,128)}, u32[]{:S(2)}) copy-start(s32[4,8]{1,0:T(4,128)} %param.12) | copy-start | bytes 388
  3.5 12.4 %copy-start.5 = (s32[4,8]{1,0:T(4,128)S(1)}, s32[4,8]{1,0:T(4,128)}, u32[]{:S(2)}) copy-start(s32[4,8]{1,0:T(4,128)} %param.11) | copy-start | bytes 388
  4.8 21.6 %collective-permute-start.1 = (bf16[768,512]{1,0:T(8,128)(2,1)S(1)}, bf16[768,512]{1,0:T(8,128)(2,1)}, u32[]{:S(2)}, u32[]{:S(2)}) collective-permute-start(bf16[768,512]{1,0:T(8,128)(2,1)S(1)} %slice.24), channel_id=1, source_target_pairs={{0,1},{1,0},{2,3},{3,2},{4,5},{5,4},{6,7},{7,6},{8,9},{9,8},{10,11... | collective-permute-start | bytes 2359304 | tf_op jit(solution)/shard_map/ppermute | solution.py:259
  7.9 26.8 %collective-permute-start.3 = (bf16[1152,512]{1,0:T(8,128)(2,1)}, bf16[1152,512]{1,0:T(8,128)(2,1)S(1)}, u32[]{:S(2)}, u32[]{:S(2)}) collective-permute-start(bf16[1152,512]{1,0:T(8,128)(2,1)} %param.9), channel_id=1, source_target_pairs={{1,2},{2,1},{5,6},{6,5},{9,10},{10,9},{13,14},{14,13},{17,18},{18,... | collective-permute-start | bytes 3538952 | tf_op jit(solution)/shard_map/ppermute | solution.py:259
  10.4 23.6 %collective-permute-start = (bf16[384,512]{1,0:T(8,128)(2,1)}, bf16[384,512]{1,0:T(8,128)(2,1)}, u32[]{:S(2)}, u32[]{:S(2)}) collective-permute-start(bf16[384,512]{1,0:T(8,128)(2,1)} %slice.21), channel_id=1, source_target_pairs={{0,1},{1,0},{2,3},{3,2},{4,5},{5,4},{6,7},{7,6},{8,9},{9,8},{10,11... | collective-permute-start | bytes 1179656 | tf_op jit(solution)/shard_map/ppermute | solution.py:259
  26.3 13.8 %collective-permute-start.2 = (bf16[768,512]{1,0:T(8,128)(2,1)}, bf16[768,512]{1,0:T(8,128)(2,1)S(1)}, u32[]{:S(2)}, u32[]{:S(2)}) collective-permute-start(bf16[768,512]{1,0:T(8,128)(2,1)} %collective-permute-done.1), channel_id=1, source_target_pairs={{1,2},{2,1},{5,6},{6,5},{9,10},{10,9},{13,14},{14,13},{17,18},{18,... | collective-permute-start | bytes 2359304 | tf_op jit(solution)/shard_map/ppermute | solution.py:259
  30.1 10.0 %copy-start.2 = (bf16[4608,256]{1,0:T(8,128)(2,1)S(1)}, bf16[4608,256]{1,0:T(8,128)(2,1)}, u32[]{:S(2)}) copy-start(bf16[4608,256]{1,0:T(8,128)(2,1)} %param.8) | copy-start | bytes 7077892
  33.9 23.6 %collective-permute-start.5 = (bf16[384,512]{1,0:T(8,128)(2,1)}, bf16[384,512]{1,0:T(8,128)(2,1)S(1)}, u32[]{:S(2)}, u32[]{:S(2)}) collective-permute-start(bf16[384,512]{1,0:T(8,128)(2,1)} %collective-permute-done), channel_id=1, source_target_pairs={{1,2},{2,1},{5,6},{6,5},{9,10},{10,9},{13,14},{14,13},{17,18},{18,... | collective-permute-start | bytes 1179656 | tf_op jit(solution)/shard_map/ppermute | solution.py:259
  34.7 21.3 %collective-permute-start.4 = (bf16[784,512]{1,0:T(8,128)(2,1)S(1)}, bf16[784,512]{1,0:T(8,128)(2,1)S(1)}, u32[]{:S(2)}, u32[]{:S(2)}) collective-permute-start(bf16[784,512]{1,0:T(8,128)(2,1)S(1)} %slice_select_fusion), channel_id=1, source_target_pairs={{0,1},{1,0},{2,3},{3,2},{4,5},{5,4},{6,7},{7,6},{8,9},{9,8},{10,11... | collective-permute-start | bytes 2408456 | tf_op jit(solution)/shard_map/ppermute | solution.py:259
  41.8 14.2 %copy-start = (f32[256,256]{1,0:T(8,128)S(1)}, f32[256,256]{1,0:T(8,128)}, u32[]{:S(2)}) copy-start(f32[256,256]{1,0:T(8,128)} %constant.35.clone.refs_1_.basis_ref.refs_4_) | copy-start | bytes 786436
  41.9 14.2 %copy-start.1 = (bf16[512,128]{1,0:T(8,128)(2,1)S(1)}, bf16[512,128]{1,0:T(8,128)(2,1)}, u32[]{:S(2)}) copy-start(bf16[512,128]{1,0:T(8,128)(2,1)} %constant.34.clone.refs_0_.fold_ref.refs_3_) | copy-start | bytes 393220
  58.6 8.5 %collective-permute-start.6 = (f32[64,128]{1,0:T(8,128)S(1)}, f32[64,128]{1,0:T(8,128)S(1)}, u32[]{:S(2)}, u32[]{:S(2)}) collective-permute-start(f32[64,128]{1,0:T(8,128)S(1)} %get-tuple-element.62), channel_id=1, source_target_pairs={{0,1},{1,0},{2,3},{3,2},{4,5},{5,4},{6,7},{7,6},{8,9},{9,8},{10,11... | collective-permute-start | bytes 98312 | tf_op jit(solution)/shard_map/ppermute | solution.py:259
  65.3 9.1 %collective-permute-start.11 = (s16[272,512]{1,0:T(8,128)(2,1)S(1)}, s16[272,512]{1,0:T(8,128)(2,1)S(1)}, u32[]{:S(2)}, u32[]{:S(2)}) collective-permute-start(s16[272,512]{1,0:T(8,128)(2,1)S(1)} %get-tuple-element.72), channel_id=1, source_target_pairs={{1,0},{2,3},{5,4},{6,7},{9,8},{10,11},{13,12},{14,15},{17,16},{18,... | collective-permute-start | bytes 835592 | tf_op jit(solution)/shard_map/ppermute | solution.py:259
  67.1 2.7 %collective-permute-start.7 = (f32[64,128]{1,0:T(8,128)S(1)}, f32[64,128]{1,0:T(8,128)S(1)}, u32[]{:S(2)}, u32[]{:S(2)}) collective-permute-start(f32[64,128]{1,0:T(8,128)S(1)} %select_add_fusion.bands_ref), channel_id=1, source_target_pairs={{0,4},{4,0},{8,12},{12,8},{16,20},{20,16},{24,28},{28,24},{1,5},{5... | collective-permute-start | bytes 98312 | tf_op jit(solution)/shard_map/ppermute | solution.py:224
  67.2 4.0 %collective-permute-start.8 = (f32[64,128]{1,0:T(8,128)S(1)}, f32[64,128]{1,0:T(8,128)S(1)}, u32[]{:S(2)}, u32[]{:S(2)}) collective-permute-start(f32[64,128]{1,0:T(8,128)S(1)} %select_add_fusion.bands_ref), channel_id=1, source_target_pairs={{0,8},{4,12},{8,0},{12,4},{16,24},{20,28},{24,16},{28,20},{1,9},{5... | collective-permute-start | bytes 98312 | tf_op jit(solution)/shard_map/ppermute | solution.py:224
  68.7 3.4 %collective-permute-start.9 = (f32[64,128]{1,0:T(8,128)S(1)}, f32[64,128]{1,0:T(8,128)S(1)}, u32[]{:S(2)}, u32[]{:S(2)}) collective-permute-start(f32[64,128]{1,0:T(8,128)S(1)} %select_add_fusion.bands_ref), channel_id=1, source_target_pairs={{0,12},{4,8},{8,4},{12,0},{16,28},{20,24},{24,20},{28,16},{1,13},{... | collective-permute-start | bytes 98312 | tf_op jit(solution)/shard_map/ppermute | solution.py:224
  72.1 4.0 %collective-permute-start.10 = (f32[64,128]{1,0:T(8,128)S(1)}, f32[64,128]{1,0:T(8,128)S(1)}, u32[]{:S(2)}, u32[]{:S(2)}) collective-permute-start(f32[64,128]{1,0:T(8,128)S(1)} %add_add_fusion.refs_0_), channel_id=1, source_target_pairs={{0,16},{4,20},{8,24},{12,28},{16,0},{20,4},{24,8},{28,12},{1,17},{... | collective-permute-start | bytes 98312 | tf_op jit(solution)/shard_map/ppermute | solution.py:224

commit v18 on v17

--- a/solution.py
+++ b/solution.py
@@ -264,8 +264,7 @@
 
     cross_grad = send(out_grad, across)
     m = carried + product(rows_of(me), out_grad)
-    own, m = lax.optimization_barrier((out_grad, m))
-    pair_parts = [send(own[:handed], both_ways), send(own[handed:], both_ways)]
+    pair_parts = [send(out_grad[:handed], both_ways), send(out_grad[handed:], both_ways)]
     far_hidden = rows_of(far)
     helped_hidden = jnp.concatenate(
         [

time: 78 us -> 75.2 us (0.964)
  waiting for transfers between devices: 32.1 us -> 29.9 us
  local copies, waits for them, and re-layouts: 4.18 us -> 3.24 us
    ppermute x8, waiting for transfers between devices: 29.1 us -> 26.9 us  [send(): return lax.ppermute(x, 'tp', perm)]
    slice x2, local copies, waits for them, and re-layouts: 2.99 us -> 2.05 us  [the longest x1 1.28 us: lined(): out_grad[:handed]]
  transfers between devices with their start and end apart: 12 -> 12, of which waited for: 8 -> 8; matrix products, arithmetic and copies ran while one was open for 11% -> 14% of each run, Pallas kernels for 4% -> 4%
where the time goes in v18:
time: 75.2 us; the launch traced here: 74.8 us
  waiting for transfers between devices  29.9 us (40%)
  starting transfers between devices  26.2 us (35%)
  matrix products  7.29 us (10%)
  Pallas kernels  5.87 us (8%)
  local copies, waits for them, and re-layouts  3.24 us (4%)
  other arithmetic  1.41 us (2%)
  between operations  0.84 us (1%)
    ppermute x8, waiting for transfers between devices, send(): return lax.ppermute(x, 'tp', perm)  26.9 us
    ppermute x8, starting transfers between devices, send(): return lax.ppermute(x, 'tp', perm)  22.8 us
    dot_general x6, matrix products, dot(): lax.dot_general(a, b, (dims, ((), ())), preferred_element_type=jnp.float32)  7.29 us
    pallas_call x6, Pallas kernels, call(): pl.pallas_call(kernel, out_shape=out_shapes, in_specs=[pl.BlockSpec(memor...  5.87 us
    ppermute x4, starting transfers between devices, spread_sum(): lax.ppermute(x, axis, [(i, i ^ stride * k) for i in range(size)])  3.44 us
    ppermute x4, waiting for transfers between devices, spread_sum(): lax.ppermute(x, axis, [(i, i ^ stride * k) for i in range(size)])  2.95 us
  transfers between devices with their start and end apart: 12, of which 8 were waited for; matrix products, arithmetic and copies ran while one was open for 14% of the time, Pallas kernels for 4%

profile of v18, /device:TPU:0, one launch (start us, length us, event | category | flops | bytes accessed | tf_op | source)
XLA Modules:
  0.0 74.8 jit_solution(8278169061808070480)
XLA Ops:
  0.6 0.0 copy-start.3
  0.6 1.3 %slice.24 = bf16[768,512]{1,0:T(8,128)(2,1)S(1)} slice(bf16[1152,512]{1,0:T(8,128)(2,1)} %param.9), slice={[0:768], [0:512]} | slice | bytes 1572864 | tf_op jit(solution)/shard_map/slice | solution.py:267
  1.9 3.1 %collective-permute-start.1 = (bf16[768,512]{1,0:T(8,128)(2,1)S(1)}, bf16[768,512]{1,0:T(8,128)(2,1)}, u32[]{:S(2)}, u32[]{:S(2)}) collective-permute-start(bf16[768,512]{1,0:T(8,128)(2,1)S(1)} %slice.24), channel_id=1, source_target_pairs={{0,1},{1,0},{2,3},{3,2},{4,5},{5,4},{6,7},{7,6},{8,9},{9,8},{10,11... | collective-permute-start | bytes 2359304 | tf_op jit(solution)/shard_map/ppermute | solution.py:259
  5.0 0.7 collective-permute-start.3
  5.7 0.0 copy-done.3
  5.8 0.8 %slice.21 = bf16[384,512]{1,0:T(8,128)(2,1)} slice(bf16[1152,512]{1,0:T(8,128)(2,1)S(1)} %copy-done.3), slice={[768:1152], [0:512]} | slice | bytes 786432 | tf_op jit(solution)/shard_map/slice | solution.py:267
  6.5 4.3 %collective-permute-start = (bf16[384,512]{1,0:T(8,128)(2,1)}, bf16[384,512]{1,0:T(8,128)(2,1)}, u32[]{:S(2)}, u32[]{:S(2)}) collective-permute-start(bf16[384,512]{1,0:T(8,128)(2,1)} %slice.21), channel_id=1, source_target_pairs={{0,1},{1,0},{2,3},{3,2},{4,5},{5,4},{6,7},{7,6},{8,9},{9,8},{10,11... | collective-permute-start | bytes 1179656 | tf_op jit(solution)/shard_map/ppermute | solution.py:259
  10.9 1.2 %dynamic-slice_select_fusion = (bf16[768,256]{1,0:T(8,128)(2,1)S(1)}, bf16[768,256]{1,0:T(8,128)(2,1)S(1)}) fusion(bf16[4608,256]{1,0:T(8,128)(2,1)} %param.8, s32[]{:T(128)S(6)} %select_n.55, pred[]{:T(512)S(6)} %or.3, s32[]{:T(128)S(6)} %add.76), kind=kLoop, calls=%fused_computation.14 | loop fusion | flops 196608 | bytes 1572873 | tf_op jit(solution)/shard_map/jit(_where)/select_n | solution.py:278
  12.1 0.9 %fusion.18 = (bf16[8,512]{1,0:T(8,128)(2,1)S(1)}, f32[8,512]{1,0:T(8,128)S(1)}) fusion(bf16[8,512]{1,0:T(8,128)(2,1)} %constant.57, s32[4,8]{1,0:T(4,128)} %param.12, s32[4,8]{1,0:T(4,128)} %param.11), kind=kOutput, calls=%fused_computation.32 | convolution fusion | flops 69760 | bytes 33024 | tf_op jit(solution)/shard_map/dot_general | solution.py:45
  13.0 0.0 copy-done.4
  13.0 2.4 %convolution_add_fusion.2 = f32[256,512]{1,0:T(8,128)} fusion(bf16[1152,512]{1,0:T(8,128)(2,1)S(1)} %copy-done.3, bf16[4608,256]{1,0:T(8,128)(2,1)} %param.8, s32[]{:T(128)S(6)} %select_n.57, f32[1,256,512]{2,1,0:T(8,128)S(1)} %copy-done.4), kind=kOutput, calls=%fused_computation.5 | convolution fusion | flops 302252032 | bytes 2818052 | tf_op jit(solution)/shard_map/dot_general | solution.py:45
  15.3 8.1 %collective-permute-done.1 = bf16[768,512]{1,0:T(8,128)(2,1)} collective-permute-done((bf16[768,512]{1,0:T(8,128)(2,1)S(1)}, bf16[768,512]{1,0:T(8,128)(2,1)}, u32[]{:S(2)}, u32[]{:S(2)}) %collective-permute-start.1) | collective-permute-done | bytes 786464 | tf_op jit(solution)/shard_map/ppermute | solution.py:259
  23.5 0.7 collective-permute-start.2
  24.2 1.2 %constant_dynamic-slice_fusion.2 = (bf16[384,256]{1,0:T(8,128)(2,1)S(1)}, bf16[384,256]{1,0:T(8,128)(2,1)S(1)}, bf16[384,256]{1,0:T(8,128)(2,1)S(1)}) fusion(bf16[4608,256]{1,0:T(8,128)(2,1)} %param.8, s32[]{:T(128)S(6)} %add.77, s32[]{:T(128)S(6)} %select_n.53, s32[]{:T(128)S(6)} %select_n.51), kind=kLoop, calls=%fused_computation.30 | loop fusion | bytes 1179660 | tf_op jit(solution)/shard_map/slice | solution.py:301
  25.4 0.1 fusion.2
  25.4 1.8 %convolution_add_fusion = f32[256,512]{1,0:T(8,128)S(1)} fusion(f32[256,512]{1,0:T(8,128)} %convolution_add_fusion.2, bf16[768,512]{1,0:T(8,128)(2,1)} %collective-permute-done.1, bf16[4608,256]{1,0:T(8,128)(2,1)} %param.8, s32[]{:T(128)S(6)} %select_n.58), kind=kOutput, calls=%fused_computation.2 | convolution fusion | flops 201457664 | bytes 2228228 | tf_op jit(solution)/shard_map/dot_general | solution.py:45
  27.2 0.0 copy-start.2
  27.3 3.8 %collective-permute-done = bf16[384,512]{1,0:T(8,128)(2,1)} collective-permute-done((bf16[384,512]{1,0:T(8,128)(2,1)}, bf16[384,512]{1,0:T(8,128)(2,1)}, u32[]{:S(2)}, u32[]{:S(2)}) %collective-permute-start) | collective-permute-done | bytes 393248 | tf_op jit(solution)/shard_map/ppermute | solution.py:259
  31.1 0.7 collective-permute-start.5
  31.8 0.0 collective-permute-done.3.cross_ref
  31.8 0.1 slice_select_fusion
  31.9 5.4 %collective-permute-start.4 = (bf16[784,512]{1,0:T(8,128)(2,1)S(1)}, bf16[784,512]{1,0:T(8,128)(2,1)S(1)}, u32[]{:S(2)}, u32[]{:S(2)}) collective-permute-start(bf16[784,512]{1,0:T(8,128)(2,1)S(1)} %slice_select_fusion), channel_id=1, source_target_pairs={{0,1},{1,0},{2,3},{3,2},{4,5},{5,4},{6,7},{7,6},{8,9},{9,8},{10,11... | collective-permute-start | bytes 2408456 | tf_op jit(solution)/shard_map/ppermute | solution.py:259
  37.3 0.0 collective-permute-done.2.far_ref
  37.3 0.0 copy-done.2
  37.3 1.3 %convolution_add_fusion.3 = f32[256,512]{1,0:T(8,128)S(1)} fusion(f32[256,512]{1,0:T(8,128)S(1)} %convolution_add_fusion, bf16[384,512]{1,0:T(8,128)(2,1)} %collective-permute-done, bf16[4608,256]{1,0:T(8,128)(2,1)S(1)} %copy-done.2, s32[]{:T(128)S(6)} %select_n.59), kind=kOutput, calls=%fused_computation.6 | convolution fusion | flops 100794368 | bytes 1638404 | tf_op jit(solution)/shard_map/dot_general | solution.py:45
  38.6 0.4 fusion.5
  39.0 0.0 copy-start
  39.0 0.0 copy-start.1
  39.0 0.5 fusion.1.m_ref
  39.6 13.6 %collective-permute-done.4.swapped_ref = bf16[784,512]{1,0:T(8,128)(2,1)S(1)} collective-permute-done((bf16[784,512]{1,0:T(8,128)(2,1)S(1)}, bf16[784,512]{1,0:T(8,128)(2,1)S(1)}, u32[]{:S(2)}, u32[]{:S(2)}) %collective-permute-start.4) | collective-permute-done | bytes 802848 | tf_op jit(solution)/shard_map/ppermute | solution.py:259
  53.2 1.5 %shard_map.95 = (f32[256,512]{1,0:T(8,128)S(1)}, f32[256,512]{1,0:T(8,128)S(1)}, bf16[256,384]{1,0:T(8,128)(2,1)S(1)}, bf16[256,384]{1,0:T(8,128)(2,1)S(1)}, f32...) custom-call(f32[256,512]{1,0:T(8,128)S(1)} %fusion.1.m_ref, bf16[384,256]{1,0:T(8,128)(2,1)S(1)} %get-tuple-element.72.hidden_ref, ...), custom_call_target="tpu_custom_call" | custom-call | flops 400000000 | bytes 4000000 | tf_op jit(solution)/shard_map/pallas_call | solution.py:206
  54.7 0.0 collective-permute-done.5.far_ref
  54.7 1.1 %shard_map.96 = (s16[272,512]{1,0:T(8,128)(2,1)S(1)}, f32[64,128]{1,0:T(8,128)S(1)}) custom-call(f32[256,512]{1,0:T(8,128)S(1)} %get-tuple-element.52.helped_ref, bf16[256,384]{1,0:T(8,128)(2,1)S(1)} %get-tuple-element.53.turned_ref, bf16[384,512]{1,0:T(8,128)(2,1)S(1)} %collective-permute-done.5.far_ref, f32[16,512]{1,0:T(8,128)S(1)} %get-tuple-element.55.places_ref, ...), custom_call_target="tpu_custom_call" | custom-call | flops 400000000 | bytes 4000000 | tf_op jit(solution)/shard_map/pallas_call | solution.py:206
  55.8 6.6 %collective-permute-start.6 = (f32[64,128]{1,0:T(8,128)S(1)}, f32[64,128]{1,0:T(8,128)S(1)}, u32[]{:S(2)}, u32[]{:S(2)}) collective-permute-start(f32[64,128]{1,0:T(8,128)S(1)} %get-tuple-element.58), channel_id=1, source_target_pairs={{0,1},{1,0},{2,3},{3,2},{4,5},{5,4},{6,7},{7,6},{8,9},{9,8},{10,11... | collective-permute-start | bytes 98312 | tf_op jit(solution)/shard_map/ppermute | solution.py:259
  62.4 1.3 %collective-permute-start.11 = (s16[272,512]{1,0:T(8,128)(2,1)S(1)}, s16[272,512]{1,0:T(8,128)(2,1)S(1)}, u32[]{:S(2)}, u32[]{:S(2)}) collective-permute-start(s16[272,512]{1,0:T(8,128)(2,1)S(1)} %get-tuple-element.68), channel_id=1, source_target_pairs={{1,0},{2,3},{5,4},{6,7},{9,8},{10,11},{13,12},{14,15},{17,16},{18,... | collective-permute-start | bytes 835592 | tf_op jit(solution)/shard_map/ppermute | solution.py:259
  63.7 0.5 collective-permute-done.6
  64.3 0.0 collective-permute-start.7
  64.3 1.6 %collective-permute-start.8 = (f32[64,128]{1,0:T(8,128)S(1)}, f32[64,128]{1,0:T(8,128)S(1)}, u32[]{:S(2)}, u32[]{:S(2)}) collective-permute-start(f32[64,128]{1,0:T(8,128)S(1)} %select_add_fusion.bands_ref), channel_id=1, source_target_pairs={{0,8},{4,12},{8,0},{12,4},{16,24},{20,28},{24,16},{28,20},{1,9},{5... | collective-permute-start | bytes 98312 | tf_op jit(solution)/shard_map/ppermute | solution.py:224
  65.9 0.3 collective-permute-start.9
  66.2 0.8 %shard_map.98.x_ref = f32[256,512]{1,0:T(8,128)S(1)} custom-call(f32[256,512]{1,0:T(8,128)S(1)} %get-tuple-element.67.m_ref, f32[64,128]{1,0:T(8,128)S(1)} %select_add_fusion.bands_ref, f32[8,512]{1,0:T(8,128)S(1)} %get-tuple-element.48.places_ref.refs_2_, bf16[512,128]{1,0:T(8,128)(2,1)S(1)} %copy-done.1, f32[256,256]{1,0:T(8,128)S(1)} %copy-done), custom_call_target="tpu_custom_call" | custom-call | flops 400000000 | bytes 4000000 | tf_op jit(solution)/shard_map/pallas_call | solution.py:206
  67.0 0.0 collective-permute-done.7
  67.0 1.3 %collective-permute-done.8 = f32[64,128]{1,0:T(8,128)S(1)} collective-permute-done((f32[64,128]{1,0:T(8,128)S(1)}, f32[64,128]{1,0:T(8,128)S(1)}, u32[]{:S(2)}, u32[]{:S(2)}) %collective-permute-start.8) | collective-permute-done | bytes 32800 | tf_op jit(solution)/shard_map/ppermute | solution.py:224
  68.3 0.9 %collective-permute-done.9 = f32[64,128]{1,0:T(8,128)S(1)} collective-permute-done((f32[64,128]{1,0:T(8,128)S(1)}, f32[64,128]{1,0:T(8,128)S(1)}, u32[]{:S(2)}, u32[]{:S(2)}) %collective-permute-start.9) | collective-permute-done | bytes 32800 | tf_op jit(solution)/shard_map/ppermute | solution.py:224
  69.2 1.6 %collective-permute-start.10 = (f32[64,128]{1,0:T(8,128)S(1)}, f32[64,128]{1,0:T(8,128)S(1)}, u32[]{:S(2)}, u32[]{:S(2)}) collective-permute-start(f32[64,128]{1,0:T(8,128)S(1)} %add_add_fusion.refs_0_), channel_id=1, source_target_pairs={{0,16},{4,20},{8,24},{12,28},{16,0},{20,4},{24,8},{28,12},{1,17},{... | collective-permute-start | bytes 98312 | tf_op jit(solution)/shard_map/ppermute | solution.py:224
  70.8 0.8 %collective-permute-done.11.code_ref = s16[272,512]{1,0:T(8,128)(2,1)S(1)} collective-permute-done((s16[272,512]{1,0:T(8,128)(2,1)S(1)}, s16[272,512]{1,0:T(8,128)(2,1)S(1)}, u32[]{:S(2)}, u32[]{:S(2)}) %collective-permute-start.11) | collective-permute-done | bytes 278560 | tf_op jit(solution)/shard_map/ppermute | solution.py:259
  71.6 0.9 %shard_map.99 = f32[256,512]{1,0:T(8,128)} custom-call(f32[256,512]{1,0:T(8,128)S(1)} %shard_map.98.x_ref, s16[272,512]{1,0:T(8,128)(2,1)S(1)} %collective-permute-done.11.code_ref), custom_call_target="tpu_custom_call" | custom-call | flops 400000000 | bytes 4000000 | tf_op jit(solution)/shard_map/pallas_call | solution.py:206
  72.5 0.8 %collective-permute-done.10.refs_1_ = f32[64,128]{1,0:T(8,128)S(1)} collective-permute-done((f32[64,128]{1,0:T(8,128)S(1)}, f32[64,128]{1,0:T(8,128)S(1)}, u32[]{:S(2)}, u32[]{:S(2)}) %collective-permute-start.10) | collective-permute-done | bytes 32800 | tf_op jit(solution)/shard_map/ppermute | solution.py:224
  73.2 1.6 %shard_map.100 = bf16[256,512]{1,0:T(8,128)(2,1)} custom-call(f32[64,128]{1,0:T(8,128)S(1)} %add_add_fusion.refs_0_, f32[64,128]{1,0:T(8,128)S(1)} %collective-permute-done.10.refs_1_, f32[8,512]{1,0:T(8,128)S(1)} %get-tuple-element.48.places_ref.refs_2_, bf16[512,128]{1,0:T(8,128)(2,1)S(1)} %copy-done.1, f32[256,256]{1,0:T(8,128)S(1)} %copy-done), custom_call_target="tpu_custom_call" | custom-call | flops 400000000 | bytes 4000000 | tf_op jit(solution)/shard_map/pallas_call | solution.py:206
  (6 shorter events, 0.1 us)
Async XLA Ops:
  0.6 5.1 %copy-start.3 = (bf16[1152,512]{1,0:T(8,128)(2,1)S(1)}, bf16[1152,512]{1,0:T(8,128)(2,1)}, u32[]{:S(2)}) copy-start(bf16[1152,512]{1,0:T(8,128)(2,1)} %param.9) | copy-start | bytes 3538948
  1.9 21.6 %collective-permute-start.1 = (bf16[768,512]{1,0:T(8,128)(2,1)S(1)}, bf16[768,512]{1,0:T(8,128)(2,1)}, u32[]{:S(2)}, u32[]{:S(2)}) collective-permute-start(bf16[768,512]{1,0:T(8,128)(2,1)S(1)} %slice.24), channel_id=1, source_target_pairs={{0,1},{1,0},{2,3},{3,2},{4,5},{5,4},{6,7},{7,6},{8,9},{9,8},{10,11... | collective-permute-start | bytes 2359304 | tf_op jit(solution)/shard_map/ppermute | solution.py:259
  5.0 26.8 %collective-permute-start.3 = (bf16[1152,512]{1,0:T(8,128)(2,1)}, bf16[1152,512]{1,0:T(8,128)(2,1)S(1)}, u32[]{:S(2)}, u32[]{:S(2)}) collective-permute-start(bf16[1152,512]{1,0:T(8,128)(2,1)} %param.9), channel_id=1, source_target_pairs={{1,2},{2,1},{5,6},{6,5},{9,10},{10,9},{13,14},{14,13},{17,18},{18,... | collective-permute-start | bytes 3538952 | tf_op jit(solution)/shard_map/ppermute | solution.py:259
  6.5 24.6 %collective-permute-start = (bf16[384,512]{1,0:T(8,128)(2,1)}, bf16[384,512]{1,0:T(8,128)(2,1)}, u32[]{:S(2)}, u32[]{:S(2)}) collective-permute-start(bf16[384,512]{1,0:T(8,128)(2,1)} %slice.21), channel_id=1, source_target_pairs={{0,1},{1,0},{2,3},{3,2},{4,5},{5,4},{6,7},{7,6},{8,9},{9,8},{10,11... | collective-permute-start | bytes 1179656 | tf_op jit(solution)/shard_map/ppermute | solution.py:259
  10.8 2.1 %copy-start.4 = (f32[1,256,512]{2,1,0:T(8,128)S(1)}, f32[1,256,512]{2,1,0:T(8,128)}, u32[]{:S(2)}) copy-start(f32[1,256,512]{2,1,0:T(8,128)} %param.10) | copy-start | bytes 1572868
  23.5 13.8 %collective-permute-start.2 = (bf16[768,512]{1,0:T(8,128)(2,1)}, bf16[768,512]{1,0:T(8,128)(2,1)S(1)}, u32[]{:S(2)}, u32[]{:S(2)}) collective-permute-start(bf16[768,512]{1,0:T(8,128)(2,1)} %collective-permute-done.1), channel_id=1, source_target_pairs={{1,2},{2,1},{5,6},{6,5},{9,10},{10,9},{13,14},{14,13},{17,18},{18,... | collective-permute-start | bytes 2359304 | tf_op jit(solution)/shard_map/ppermute | solution.py:259
  27.2 10.0 %copy-start.2 = (bf16[4608,256]{1,0:T(8,128)(2,1)S(1)}, bf16[4608,256]{1,0:T(8,128)(2,1)}, u32[]{:S(2)}) copy-start(bf16[4608,256]{1,0:T(8,128)(2,1)} %param.8) | copy-start | bytes 7077892
  31.1 23.6 %collective-permute-start.5 = (bf16[384,512]{1,0:T(8,128)(2,1)}, bf16[384,512]{1,0:T(8,128)(2,1)S(1)}, u32[]{:S(2)}, u32[]{:S(2)}) collective-permute-start(bf16[384,512]{1,0:T(8,128)(2,1)} %collective-permute-done), channel_id=1, source_target_pairs={{1,2},{2,1},{5,6},{6,5},{9,10},{10,9},{13,14},{14,13},{17,18},{18,... | collective-permute-start | bytes 1179656 | tf_op jit(solution)/shard_map/ppermute | solution.py:259
  31.9 21.3 %collective-permute-start.4 = (bf16[784,512]{1,0:T(8,128)(2,1)S(1)}, bf16[784,512]{1,0:T(8,128)(2,1)S(1)}, u32[]{:S(2)}, u32[]{:S(2)}) collective-permute-start(bf16[784,512]{1,0:T(8,128)(2,1)S(1)} %slice_select_fusion), channel_id=1, source_target_pairs={{0,1},{1,0},{2,3},{3,2},{4,5},{5,4},{6,7},{7,6},{8,9},{9,8},{10,11... | collective-permute-start | bytes 2408456 | tf_op jit(solution)/shard_map/ppermute | solution.py:259
  39.0 14.2 %copy-start = (f32[256,256]{1,0:T(8,128)S(1)}, f32[256,256]{1,0:T(8,128)}, u32[]{:S(2)}) copy-start(f32[256,256]{1,0:T(8,128)} %constant.35.clone.refs_1_.basis_ref.refs_4_) | copy-start | bytes 786436
  39.0 14.2 %copy-start.1 = (bf16[512,128]{1,0:T(8,128)(2,1)S(1)}, bf16[512,128]{1,0:T(8,128)(2,1)}, u32[]{:S(2)}) copy-start(bf16[512,128]{1,0:T(8,128)(2,1)} %constant.34.clone.refs_0_.fold_ref.refs_3_) | copy-start | bytes 393220
  55.8 8.5 %collective-permute-start.6 = (f32[64,128]{1,0:T(8,128)S(1)}, f32[64,128]{1,0:T(8,128)S(1)}, u32[]{:S(2)}, u32[]{:S(2)}) collective-permute-start(f32[64,128]{1,0:T(8,128)S(1)} %get-tuple-element.58), channel_id=1, source_target_pairs={{0,1},{1,0},{2,3},{3,2},{4,5},{5,4},{6,7},{7,6},{8,9},{9,8},{10,11... | collective-permute-start | bytes 98312 | tf_op jit(solution)/shard_map/ppermute | solution.py:259
  62.4 9.1 %collective-permute-start.11 = (s16[272,512]{1,0:T(8,128)(2,1)S(1)}, s16[272,512]{1,0:T(8,128)(2,1)S(1)}, u32[]{:S(2)}, u32[]{:S(2)}) collective-permute-start(s16[272,512]{1,0:T(8,128)(2,1)S(1)} %get-tuple-element.68), channel_id=1, source_target_pairs={{1,0},{2,3},{5,4},{6,7},{9,8},{10,11},{13,12},{14,15},{17,16},{18,... | collective-permute-start | bytes 835592 | tf_op jit(solution)/shard_map/ppermute | solution.py:259
  64.3 2.7 %collective-permute-start.7 = (f32[64,128]{1,0:T(8,128)S(1)}, f32[64,128]{1,0:T(8,128)S(1)}, u32[]{:S(2)}, u32[]{:S(2)}) collective-permute-start(f32[64,128]{1,0:T(8,128)S(1)} %select_add_fusion.bands_ref), channel_id=1, source_target_pairs={{0,4},{4,0},{8,12},{12,8},{16,20},{20,16},{24,28},{28,24},{1,5},{5... | collective-permute-start | bytes 98312 | tf_op jit(solution)/shard_map/ppermute | solution.py:224
  64.3 4.0 %collective-permute-start.8 = (f32[64,128]{1,0:T(8,128)S(1)}, f32[64,128]{1,0:T(8,128)S(1)}, u32[]{:S(2)}, u32[]{:S(2)}) collective-permute-start(f32[64,128]{1,0:T(8,128)S(1)} %select_add_fusion.bands_ref), channel_id=1, source_target_pairs={{0,8},{4,12},{8,0},{12,4},{16,24},{20,28},{24,16},{28,20},{1,9},{5... | collective-permute-start | bytes 98312 | tf_op jit(solution)/shard_map/ppermute | solution.py:224
  65.9 3.4 %collective-permute-start.9 = (f32[64,128]{1,0:T(8,128)S(1)}, f32[64,128]{1,0:T(8,128)S(1)}, u32[]{:S(2)}, u32[]{:S(2)}) collective-permute-start(f32[64,128]{1,0:T(8,128)S(1)} %select_add_fusion.bands_ref), channel_id=1, source_target_pairs={{0,12},{4,8},{8,4},{12,0},{16,28},{20,24},{24,20},{28,16},{1,13},{... | collective-permute-start | bytes 98312 | tf_op jit(solution)/shard_map/ppermute | solution.py:224
  69.2 4.0 %collective-permute-start.10 = (f32[64,128]{1,0:T(8,128)S(1)}, f32[64,128]{1,0:T(8,128)S(1)}, u32[]{:S(2)}, u32[]{:S(2)}) collective-permute-start(f32[64,128]{1,0:T(8,128)S(1)} %add_add_fusion.refs_0_), channel_id=1, source_target_pairs={{0,16},{4,20},{8,24},{12,28},{16,0},{20,4},{24,8},{28,12},{1,17},{... | collective-permute-start | bytes 98312 | tf_op jit(solution)/shard_map/ppermute | solution.py:224

commit v19 on v18

--- a/solution.py
+++ b/solution.py
@@ -276,15 +276,19 @@
     place_part = jnp.pad(places.astype(hidden.dtype), ((0, place_rows - places.shape[0]), (0, 0)))
     helped_hidden = jnp.concatenate([helped_hidden, place_part], axis=0)
     cross_hidden = jnp.where(end, rows_of(cross, 0, handed), 0)
-    helped_hidden, cross_hidden, m = lax.optimization_barrier((helped_hidden, cross_hidden, m))
-
-    far_head = send(pair_parts[0], across)
-    m = m + product(rows_of(me ^ 1, 0, handed), pair_parts[0])
-    pair_rest, m = lax.optimization_barrier((pair_parts[1], m))
+    pair_head, helped_hidden, cross_hidden, m = lax.optimization_barrier(
+        (pair_parts[0], helped_hidden, cross_hidden, m)
+    )
+    far_head = send(pair_head, across)
+    first = pair_head[:16]
+    pair_rest, first = lax.optimization_barrier((pair_parts[1], first))
     far_parts = [far_head, send(pair_rest, across)]
-    cross_grad, matrices, places = after((cross_grad, matrices, places), pair_parts[0], m)
+    cross_grad, matrices, places = after((cross_grad, matrices, places), pair_head, m)
     swapped = send(jnp.where(end, helped_hidden, cross_grad[: handed + place_rows]), both_ways)
-    far_parts[0], pair_rest, cross_grad = lax.optimization_barrier((far_parts[0], pair_rest, cross_grad))
+    far_parts[0], pair_head, pair_rest, cross_grad = lax.optimization_barrier(
+        (far_parts[0], pair_head, pair_rest, cross_grad)
+    )
+    m = m + product(rows_of(me ^ 1, 0, 16), first) + product(rows_of(me ^ 1, 16, handed), pair_head[16:])
     m = m + product(rows_of(me ^ 1, handed), pair_rest)
     m = m + product(rows_of(cross), cross_grad) + product(far_hidden[:handed], far_parts[0])
     m, swapped = lax.optimization_barrier((m, swapped))

time: 75.2 us -> 77.4 us (1.029)
  starting transfers between devices: 26.2 us -> 21.4 us
  other arithmetic: 1.41 us -> 4.32 us
  local copies, waits for them, and re-layouts: 3.24 us -> 5.92 us
  waiting for transfers between devices: 29.9 us -> 32.1 us
    ppermute x8, starting transfers between devices: 22.8 us -> 17.9 us  [send(): return lax.ppermute(x, 'tp', perm)]
    ppermute x8, waiting for transfers between devices: 26.9 us -> 29.5 us  [send(): return lax.ppermute(x, 'tp', perm)]
    concatenate x1, other arithmetic: 0.06 us -> 1.88 us  [lined(): helped_hidden = jnp.concatenate([helped_hidden, place_part], axis=0)]
    select_n x1, other arithmetic: 0.09 us -> 1.23 us  [lined(): jnp.where(end, helped_hidden, cross_grad[:handed + place_rows])]
    slice x0 -> x1, local copies, waits for them, and re-layouts: none -> 0.87 us  [lined(): first = pair_head[:16]]
    slice x1, local copies, waits for them, and re-layouts: 1.28 us -> 2.07 us  [lined(): out_grad[:handed]]
    dot_general x6 -> x7, matrix products: 7.29 us -> 6.56 us  [dot(): lax.dot_general(a, b, (dims, ((), ())), preferred_element_type=jnp.float32)]
  transfers between devices with their start and end apart: 12 -> 12, of which waited for: 8 -> 8; matrix products, arithmetic and copies ran while one was open for 14% -> 22% of each run, Pallas kernels for 4% -> 4%
where the time goes in v19:
time: 77.4 us; the launch traced here: 76.9 us
  waiting for transfers between devices  32.1 us (41%)
  starting transfers between devices  21.4 us (28%)
  matrix products  6.56 us (8%)
  local copies, waits for them, and re-layouts  5.92 us (8%)
  Pallas kernels  5.86 us (8%)
  other arithmetic  4.32 us (6%)
  between operations  0.81 us (1%)
    ppermute x8, waiting for transfers between devices, send(): return lax.ppermute(x, 'tp', perm)  29.5 us
    ppermute x8, starting transfers between devices, send(): return lax.ppermute(x, 'tp', perm)  17.9 us
    dot_general x7, matrix products, dot(): lax.dot_general(a, b, (dims, ((), ())), preferred_element_type=jnp.float32)  6.56 us
    pallas_call x6, Pallas kernels, call(): pl.pallas_call(kernel, out_shape=out_shapes, in_specs=[pl.BlockSpec(memor...  5.86 us
    ppermute x4, starting transfers between devices, spread_sum(): lax.ppermute(x, axis, [(i, i ^ stride * k) for i in range(size)])  3.45 us
    ppermute x4, waiting for transfers between devices, spread_sum(): lax.ppermute(x, axis, [(i, i ^ stride * k) for i in range(size)])  2.59 us
    slice x1, local copies, waits for them, and re-layouts, lined(): out_grad[:handed]  2.07 us
    slice x1, local copies, waits for them, and re-layouts, lined(): far_hidden[handed:]  1.93 us
  transfers between devices with their start and end apart: 12, of which 8 were waited for; matrix products, arithmetic and copies ran while one was open for 22% of the time, Pallas kernels for 4%

profile of v19, /device:TPU:0, one launch (start us, length us, event | category | flops | bytes accessed | tf_op | source)
XLA Modules:
  0.0 76.9 jit_solution(2095382433985761689)
XLA Ops:
  0.6 0.7 collective-permute-start.3
  1.4 2.1 %slice.27 = bf16[768,512]{1,0:T(8,128)(2,1)} slice(bf16[1152,512]{1,0:T(8,128)(2,1)} %param.9), slice={[0:768], [0:512]} | slice | bytes 1572864 | tf_op jit(solution)/shard_map/slice | solution.py:267
  3.4 5.8 %collective-permute-start = (bf16[768,512]{1,0:T(8,128)(2,1)}, bf16[768,512]{1,0:T(8,128)(2,1)}, u32[]{:S(2)}, u32[]{:S(2)}) collective-permute-start(bf16[768,512]{1,0:T(8,128)(2,1)} %slice.27), channel_id=1, source_target_pairs={{0,1},{1,0},{2,3},{3,2},{4,5},{5,4},{6,7},{7,6},{8,9},{9,8},{10,11... | collective-permute-start | bytes 2359304 | tf_op jit(solution)/shard_map/ppermute | solution.py:259
  9.2 1.2 %dynamic-slice_select_fusion = (bf16[768,256]{1,0:T(8,128)(2,1)S(1)}, bf16[768,256]{1,0:T(8,128)(2,1)S(1)}) fusion(bf16[4608,256]{1,0:T(8,128)(2,1)} %param.8, s32[]{:T(128)S(6)} %select_n.58, pred[]{:T(512)S(6)} %or.3, s32[]{:T(128)S(6)} %add.90), kind=kLoop, calls=%fused_computation.17 | loop fusion | flops 196608 | bytes 1572873 | tf_op jit(solution)/shard_map/jit(_where)/select_n | solution.py:278
  10.4 0.0 copy-start.2
  10.4 1.9 %constant_dynamic-slice_fusion.2 = (bf16[384,256]{1,0:T(8,128)(2,1)S(1)}, bf16[384,256]{1,0:T(8,128)(2,1)S(1)}, bf16[384,256]{1,0:T(8,128)(2,1)}) fusion(bf16[4608,256]{1,0:T(8,128)(2,1)} %param.8, s32[]{:T(128)S(6)} %add.91, s32[]{:T(128)S(6)} %select_n.56, s32[]{:T(128)S(6)} %select_n.54), kind=kLoop, calls=%fused_computation.37 | loop fusion | bytes 1179660 | tf_op jit(solution)/shard_map/slice | solution.py:305
  12.4 0.9 %fusion.27 = (bf16[8,512]{1,0:T(8,128)(2,1)S(1)}, f32[8,512]{1,0:T(8,128)S(1)}) fusion(bf16[8,512]{1,0:T(8,128)(2,1)} %constant.65, s32[4,8]{1,0:T(4,128)} %param.12, s32[4,8]{1,0:T(4,128)} %param.11), kind=kOutput, calls=%fused_computation.39 | convolution fusion | flops 69760 | bytes 33024 | tf_op jit(solution)/shard_map/dot_general | solution.py:45
  13.3 1.9 %fusion.5 = bf16[784,512]{1,0:T(8,128)(2,1)} fusion(bf16[8,512]{1,0:T(8,128)(2,1)S(1)} %get-tuple-element.81, bf16[768,256]{1,0:T(8,128)(2,1)S(1)} %get-tuple-element.80, bf16[384,256]{1,0:T(8,128)(2,1)S(1)} %get-tuple-element.77, bf16[384,256]{1,0:T(8,128)(2,1)} %get-tuple-element.78), kind=kLoop, calls=%fused_computation.8 | loop fusion | flops 4014080 | bytes 1597440 | tf_op jit(solution)/shard_map/concatenate | solution.py:277
  15.2 0.0 copy-done.2
  15.2 1.6 %convolution_add_fusion.1 = f32[256,512]{1,0:T(8,128)S(1)} fusion(bf16[1152,512]{1,0:T(8,128)(2,1)S(1)} %copy-done.2, bf16[4608,256]{1,0:T(8,128)(2,1)} %param.8, s32[]{:T(128)S(6)} %select_n.60, f32[1,256,512]{2,1,0:T(8,128)S(1)} %copy-done.4), kind=kOutput, calls=%fused_computation.3 | convolution fusion | flops 302252032 | bytes 2818052 | tf_op jit(solution)/shard_map/dot_general | solution.py:45
  16.8 10.0 %collective-permute-done = bf16[768,512]{1,0:T(8,128)(2,1)} collective-permute-done((bf16[768,512]{1,0:T(8,128)(2,1)}, bf16[768,512]{1,0:T(8,128)(2,1)}, u32[]{:S(2)}, u32[]{:S(2)}) %collective-permute-start) | collective-permute-done | bytes 786464 | tf_op jit(solution)/shard_map/ppermute | solution.py:259
  26.8 0.7 collective-permute-start.2
  27.5 1.0 %slice.30 = bf16[384,512]{1,0:T(8,128)(2,1)S(1)} slice(bf16[1152,512]{1,0:T(8,128)(2,1)} %param.9), slice={[768:1152], [0:512]} | slice | bytes 786432 | tf_op jit(solution)/shard_map/slice | solution.py:267
  28.5 3.5 %collective-permute-start.1 = (bf16[384,512]{1,0:T(8,128)(2,1)S(1)}, bf16[384,512]{1,0:T(8,128)(2,1)}, u32[]{:S(2)}, u32[]{:S(2)}) collective-permute-start(bf16[384,512]{1,0:T(8,128)(2,1)S(1)} %slice.30), channel_id=1, source_target_pairs={{0,1},{1,0},{2,3},{3,2},{4,5},{5,4},{6,7},{7,6},{8,9},{9,8},{10,11... | collective-permute-start | bytes 1179656 | tf_op jit(solution)/shard_map/ppermute | solution.py:259
  32.0 0.9 %slice.31 = bf16[16,512]{1,0:T(8,128)(2,1)S(1)} slice(bf16[768,512]{1,0:T(8,128)(2,1)} %collective-permute-done), slice={[0:16], [0:512]} | slice | bytes 32768 | tf_op jit(solution)/shard_map/slice | solution.py:283
  32.9 6.9 %collective-permute-done.1 = bf16[384,512]{1,0:T(8,128)(2,1)} collective-permute-done((bf16[384,512]{1,0:T(8,128)(2,1)S(1)}, bf16[384,512]{1,0:T(8,128)(2,1)}, u32[]{:S(2)}, u32[]{:S(2)}) %collective-permute-start.1) | collective-permute-done | bytes 393248 | tf_op jit(solution)/shard_map/ppermute | solution.py:259
  39.7 0.7 collective-permute-start.5
  40.4 0.0 collective-permute-done.3.cross_ref
  40.4 1.2 %slice_select_fusion = bf16[784,512]{1,0:T(8,128)(2,1)S(1)} fusion(bf16[784,512]{1,0:T(8,128)(2,1)} %fusion.5, bf16[1152,512]{1,0:T(8,128)(2,1)S(1)} %collective-permute-done.3.cross_ref, pred[]{:T(512)S(6)} %or.3), kind=kLoop, calls=%fused_computation.9 | loop fusion | flops 401408 | bytes 2408449 | tf_op jit(solution)/shard_map/jit(_where)/select_n | solution.py:287
  41.7 3.5 %collective-permute-start.4 = (bf16[784,512]{1,0:T(8,128)(2,1)S(1)}, bf16[784,512]{1,0:T(8,128)(2,1)S(1)}, u32[]{:S(2)}, u32[]{:S(2)}) collective-permute-start(bf16[784,512]{1,0:T(8,128)(2,1)S(1)} %slice_select_fusion), channel_id=1, source_target_pairs={{0,1},{1,0},{2,3},{3,2},{4,5},{5,4},{6,7},{7,6},{8,9},{9,8},{10,11... | collective-permute-start | bytes 2408456 | tf_op jit(solution)/shard_map/ppermute | solution.py:259
  45.1 0.0 collective-permute-done.2.far_ref
  45.1 0.5 fusion.8
  45.7 0.4 fusion.11
  46.1 1.5 %fusion.6 = f32[256,512]{1,0:T(8,128)S(1)} fusion(bf16[768,512]{1,0:T(8,128)(2,1)} %collective-permute-done, bf16[4608,256]{1,0:T(8,128)(2,1)S(1)} %copy-done.3, s32[]{:T(128)S(6)} %select_n.62), kind=kOutput, calls=%fused_computation.10 | convolution fusion | flops 197132288 | bytes 1679364 | tf_op jit(solution)/shard_map/dot_general | solution.py:45
  47.6 1.3 %fusion.14 = f32[256,512]{1,0:T(8,128)S(1)} fusion(bf16[384,512]{1,0:T(8,128)(2,1)} %collective-permute-done.1, bf16[4608,256]{1,0:T(8,128)(2,1)S(1)} %copy-done.3, s32[]{:T(128)S(6)} %select_n.63), kind=kOutput, calls=%fused_computation.19 | convolution fusion | flops 100663296 | bytes 1114116 | tf_op jit(solution)/shard_map/dot_general | solution.py:45
  48.9 0.0 copy-start
  49.0 0.0 copy-start.1
  49.0 0.3 fusion.4.m_ref
  49.3 11.1 %collective-permute-done.4.swapped_ref = bf16[784,512]{1,0:T(8,128)(2,1)S(1)} collective-permute-done((bf16[784,512]{1,0:T(8,128)(2,1)S(1)}, bf16[784,512]{1,0:T(8,128)(2,1)S(1)}, u32[]{:S(2)}, u32[]{:S(2)}) %collective-permute-start.4) | collective-permute-done | bytes 802848 | tf_op jit(solution)/shard_map/ppermute | solution.py:259
  60.4 0.0 copy-done.1
  60.4 1.5 %shard_map.95 = (f32[256,512]{1,0:T(8,128)S(1)}, f32[256,512]{1,0:T(8,128)S(1)}, bf16[256,384]{1,0:T(8,128)(2,1)S(1)}, bf16[256,384]{1,0:T(8,128)(2,1)S(1)}, f32...) custom-call(f32[256,512]{1,0:T(8,128)S(1)} %fusion.4.m_ref, bf16[384,256]{1,0:T(8,128)(2,1)S(1)} %get-tuple-element.76.hidden_ref, ...), custom_call_target="tpu_custom_call" | custom-call | flops 400000000 | bytes 4000000 | tf_op jit(solution)/shard_map/pallas_call | solution.py:206
  61.8 0.0 collective-permute-done.5.far_ref
  61.8 1.1 %shard_map.96 = (s16[272,512]{1,0:T(8,128)(2,1)S(1)}, f32[64,128]{1,0:T(8,128)S(1)}) custom-call(f32[256,512]{1,0:T(8,128)S(1)} %get-tuple-element.56.helped_ref, bf16[256,384]{1,0:T(8,128)(2,1)S(1)} %get-tuple-element.57.turned_ref, bf16[384,512]{1,0:T(8,128)(2,1)S(1)} %collective-permute-done.5.far_ref, f32[16,512]{1,0:T(8,128)S(1)} %get-tuple-element.59.places_ref, ...), custom_call_target="tpu_custom_call" | custom-call | flops 400000000 | bytes 4000000 | tf_op jit(solution)/shard_map/pallas_call | solution.py:206
  62.9 1.8 %collective-permute-start.6 = (f32[64,128]{1,0:T(8,128)S(1)}, f32[64,128]{1,0:T(8,128)S(1)}, u32[]{:S(2)}, u32[]{:S(2)}) collective-permute-start(f32[64,128]{1,0:T(8,128)S(1)} %get-tuple-element.62), channel_id=1, source_target_pairs={{0,1},{1,0},{2,3},{3,2},{4,5},{5,4},{6,7},{7,6},{8,9},{9,8},{10,11... | collective-permute-start | bytes 98312 | tf_op jit(solution)/shard_map/ppermute | solution.py:259
  64.8 1.3 %collective-permute-start.11 = (s16[272,512]{1,0:T(8,128)(2,1)S(1)}, s16[272,512]{1,0:T(8,128)(2,1)S(1)}, u32[]{:S(2)}, u32[]{:S(2)}) collective-permute-start(s16[272,512]{1,0:T(8,128)(2,1)S(1)} %get-tuple-element.72), channel_id=1, source_target_pairs={{1,0},{2,3},{5,4},{6,7},{9,8},{10,11},{13,12},{14,15},{17,16},{18,... | collective-permute-start | bytes 835592 | tf_op jit(solution)/shard_map/ppermute | solution.py:259
  66.1 1.2 %collective-permute-done.6 = f32[64,128]{1,0:T(8,128)S(1)} collective-permute-done((f32[64,128]{1,0:T(8,128)S(1)}, f32[64,128]{1,0:T(8,128)S(1)}, u32[]{:S(2)}, u32[]{:S(2)}) %collective-permute-start.6) | collective-permute-done | bytes 32800 | tf_op jit(solution)/shard_map/ppermute | solution.py:259
  67.3 0.0 collective-permute-start.9
  67.3 1.6 %collective-permute-start.8 = (f32[64,128]{1,0:T(8,128)S(1)}, f32[64,128]{1,0:T(8,128)S(1)}, u32[]{:S(2)}, u32[]{:S(2)}) collective-permute-start(f32[64,128]{1,0:T(8,128)S(1)} %select_add_fusion.bands_ref), channel_id=1, source_target_pairs={{0,8},{4,12},{8,0},{12,4},{16,24},{20,28},{24,16},{28,20},{1,9},{5... | collective-permute-start | bytes 98312 | tf_op jit(solution)/shard_map/ppermute | solution.py:224
  68.9 0.3 collective-permute-start.7
  69.2 0.8 %shard_map.98.x_ref = f32[256,512]{1,0:T(8,128)S(1)} custom-call(f32[256,512]{1,0:T(8,128)S(1)} %get-tuple-element.71.m_ref, f32[64,128]{1,0:T(8,128)S(1)} %select_add_fusion.bands_ref, f32[8,512]{1,0:T(8,128)S(1)} %get-tuple-element.52.places_ref.refs_2_, bf16[512,128]{1,0:T(8,128)(2,1)S(1)} %copy-done.1, f32[256,256]{1,0:T(8,128)S(1)} %copy-done), custom_call_target="tpu_custom_call" | custom-call | flops 400000000 | bytes 4000000 | tf_op jit(solution)/shard_map/pallas_call | solution.py:206
  70.0 0.9 %collective-permute-done.9 = f32[64,128]{1,0:T(8,128)S(1)} collective-permute-done((f32[64,128]{1,0:T(8,128)S(1)}, f32[64,128]{1,0:T(8,128)S(1)}, u32[]{:S(2)}, u32[]{:S(2)}) %collective-permute-start.9) | collective-permute-done | bytes 32800 | tf_op jit(solution)/shard_map/ppermute | solution.py:224
  71.0 0.4 collective-permute-done.8
  71.4 0.0 collective-permute-done.7
  71.4 1.6 %collective-permute-start.10 = (f32[64,128]{1,0:T(8,128)S(1)}, f32[64,128]{1,0:T(8,128)S(1)}, u32[]{:S(2)}, u32[]{:S(2)}) collective-permute-start(f32[64,128]{1,0:T(8,128)S(1)} %add_add_fusion.refs_0_), channel_id=1, source_target_pairs={{0,16},{4,20},{8,24},{12,28},{16,0},{20,4},{24,8},{28,12},{1,17},{... | collective-permute-start | bytes 98312 | tf_op jit(solution)/shard_map/ppermute | solution.py:224
  73.0 0.3 collective-permute-done.11.code_ref
  73.2 0.9 %shard_map.99 = f32[256,512]{1,0:T(8,128)} custom-call(f32[256,512]{1,0:T(8,128)S(1)} %shard_map.98.x_ref, s16[272,512]{1,0:T(8,128)(2,1)S(1)} %collective-permute-done.11.code_ref), custom_call_target="tpu_custom_call" | custom-call | flops 400000000 | bytes 4000000 | tf_op jit(solution)/shard_map/pallas_call | solution.py:206
  74.1 1.3 %collective-permute-done.10.refs_1_ = f32[64,128]{1,0:T(8,128)S(1)} collective-permute-done((f32[64,128]{1,0:T(8,128)S(1)}, f32[64,128]{1,0:T(8,128)S(1)}, u32[]{:S(2)}, u32[]{:S(2)}) %collective-permute-start.10) | collective-permute-done | bytes 32800 | tf_op jit(solution)/shard_map/ppermute | solution.py:224
  75.4 1.6 %shard_map.100 = bf16[256,512]{1,0:T(8,128)(2,1)} custom-call(f32[64,128]{1,0:T(8,128)S(1)} %add_add_fusion.refs_0_, f32[64,128]{1,0:T(8,128)S(1)} %collective-permute-done.10.refs_1_, f32[8,512]{1,0:T(8,128)S(1)} %get-tuple-element.52.places_ref.refs_2_, bf16[512,128]{1,0:T(8,128)(2,1)S(1)} %copy-done.1, f32[256,256]{1,0:T(8,128)S(1)} %copy-done), custom_call_target="tpu_custom_call" | custom-call | flops 400000000 | bytes 4000000 | tf_op jit(solution)/shard_map/pallas_call | solution.py:206
  (8 shorter events, 0.1 us)
Async XLA Ops:
  0.6 39.8 %collective-permute-start.3 = (bf16[1152,512]{1,0:T(8,128)(2,1)}, bf16[1152,512]{1,0:T(8,128)(2,1)S(1)}, u32[]{:S(2)}, u32[]{:S(2)}) collective-permute-start(bf16[1152,512]{1,0:T(8,128)(2,1)} %param.9), channel_id=1, source_target_pairs={{1,2},{2,1},{5,6},{6,5},{9,10},{10,9},{13,14},{14,13},{17,18},{18,... | collective-permute-start | bytes 3538952 | tf_op jit(solution)/shard_map/ppermute | solution.py:259
  3.4 23.4 %collective-permute-start = (bf16[768,512]{1,0:T(8,128)(2,1)}, bf16[768,512]{1,0:T(8,128)(2,1)}, u32[]{:S(2)}, u32[]{:S(2)}) collective-permute-start(bf16[768,512]{1,0:T(8,128)(2,1)} %slice.27), channel_id=1, source_target_pairs={{0,1},{1,0},{2,3},{3,2},{4,5},{5,4},{6,7},{7,6},{8,9},{9,8},{10,11... | collective-permute-start | bytes 2359304 | tf_op jit(solution)/shard_map/ppermute | solution.py:259
  10.4 4.7 %copy-start.2 = (bf16[1152,512]{1,0:T(8,128)(2,1)S(1)}, bf16[1152,512]{1,0:T(8,128)(2,1)}, u32[]{:S(2)}) copy-start(bf16[1152,512]{1,0:T(8,128)(2,1)} %param.9) | copy-start | bytes 3538948
  12.4 2.8 %copy-start.4 = (f32[1,256,512]{2,1,0:T(8,128)S(1)}, f32[1,256,512]{2,1,0:T(8,128)}, u32[]{:S(2)}) copy-start(f32[1,256,512]{2,1,0:T(8,128)} %param.10) | copy-start | bytes 1572868
  26.8 18.3 %collective-permute-start.2 = (bf16[768,512]{1,0:T(8,128)(2,1)}, bf16[768,512]{1,0:T(8,128)(2,1)S(1)}, u32[]{:S(2)}, u32[]{:S(2)}) collective-permute-start(bf16[768,512]{1,0:T(8,128)(2,1)} %collective-permute-done), channel_id=1, source_target_pairs={{1,2},{2,1},{5,6},{6,5},{9,10},{10,9},{13,14},{14,13},{17,18},{18,... | collective-permute-start | bytes 2359304 | tf_op jit(solution)/shard_map/ppermute | solution.py:259
  28.5 11.2 %collective-permute-start.1 = (bf16[384,512]{1,0:T(8,128)(2,1)S(1)}, bf16[384,512]{1,0:T(8,128)(2,1)}, u32[]{:S(2)}, u32[]{:S(2)}) collective-permute-start(bf16[384,512]{1,0:T(8,128)(2,1)S(1)} %slice.30), channel_id=1, source_target_pairs={{0,1},{1,0},{2,3},{3,2},{4,5},{5,4},{6,7},{7,6},{8,9},{9,8},{10,11... | collective-permute-start | bytes 1179656 | tf_op jit(solution)/shard_map/ppermute | solution.py:259
  32.0 13.2 %copy-start.3 = (bf16[4608,256]{1,0:T(8,128)(2,1)S(1)}, bf16[4608,256]{1,0:T(8,128)(2,1)}, u32[]{:S(2)}) copy-start(bf16[4608,256]{1,0:T(8,128)(2,1)} %param.8) | copy-start | bytes 7077892
  39.7 22.1 %collective-permute-start.5 = (bf16[384,512]{1,0:T(8,128)(2,1)}, bf16[384,512]{1,0:T(8,128)(2,1)S(1)}, u32[]{:S(2)}, u32[]{:S(2)}) collective-permute-start(bf16[384,512]{1,0:T(8,128)(2,1)} %collective-permute-done.1), channel_id=1, source_target_pairs={{1,2},{2,1},{5,6},{6,5},{9,10},{10,9},{13,14},{14,13},{17,18},{18,... | collective-permute-start | bytes 1179656 | tf_op jit(solution)/shard_map/ppermute | solution.py:259
  41.7 18.7 %collective-permute-start.4 = (bf16[784,512]{1,0:T(8,128)(2,1)S(1)}, bf16[784,512]{1,0:T(8,128)(2,1)S(1)}, u32[]{:S(2)}, u32[]{:S(2)}) collective-permute-start(bf16[784,512]{1,0:T(8,128)(2,1)S(1)} %slice_select_fusion), channel_id=1, source_target_pairs={{0,1},{1,0},{2,3},{3,2},{4,5},{5,4},{6,7},{7,6},{8,9},{9,8},{10,11... | collective-permute-start | bytes 2408456 | tf_op jit(solution)/shard_map/ppermute | solution.py:259
  48.9 11.4 %copy-start = (f32[256,256]{1,0:T(8,128)S(1)}, f32[256,256]{1,0:T(8,128)}, u32[]{:S(2)}) copy-start(f32[256,256]{1,0:T(8,128)} %constant.39.clone.refs_1_.basis_ref.refs_4_) | copy-start | bytes 786436
  49.0 11.4 %copy-start.1 = (bf16[512,128]{1,0:T(8,128)(2,1)S(1)}, bf16[512,128]{1,0:T(8,128)(2,1)}, u32[]{:S(2)}) copy-start(bf16[512,128]{1,0:T(8,128)(2,1)} %constant.38.clone.refs_0_.fold_ref.refs_3_) | copy-start | bytes 393220
  62.9 4.4 %collective-permute-start.6 = (f32[64,128]{1,0:T(8,128)S(1)}, f32[64,128]{1,0:T(8,128)S(1)}, u32[]{:S(2)}, u32[]{:S(2)}) collective-permute-start(f32[64,128]{1,0:T(8,128)S(1)} %get-tuple-element.62), channel_id=1, source_target_pairs={{0,1},{1,0},{2,3},{3,2},{4,5},{5,4},{6,7},{7,6},{8,9},{9,8},{10,11... | collective-permute-start | bytes 98312 | tf_op jit(solution)/shard_map/ppermute | solution.py:259
  64.8 8.4 %collective-permute-start.11 = (s16[272,512]{1,0:T(8,128)(2,1)S(1)}, s16[272,512]{1,0:T(8,128)(2,1)S(1)}, u32[]{:S(2)}, u32[]{:S(2)}) collective-permute-start(s16[272,512]{1,0:T(8,128)(2,1)S(1)} %get-tuple-element.72), channel_id=1, source_target_pairs={{1,0},{2,3},{5,4},{6,7},{9,8},{10,11},{13,12},{14,15},{17,16},{18,... | collective-permute-start | bytes 835592 | tf_op jit(solution)/shard_map/ppermute | solution.py:259
  67.3 3.6 %collective-permute-start.9 = (f32[64,128]{1,0:T(8,128)S(1)}, f32[64,128]{1,0:T(8,128)S(1)}, u32[]{:S(2)}, u32[]{:S(2)}) collective-permute-start(f32[64,128]{1,0:T(8,128)S(1)} %select_add_fusion.bands_ref), channel_id=1, source_target_pairs={{0,12},{4,8},{8,4},{12,0},{16,28},{20,24},{24,20},{28,16},{1,13},{... | collective-permute-start | bytes 98312 | tf_op jit(solution)/shard_map/ppermute | solution.py:224
  67.3 4.0 %collective-permute-start.8 = (f32[64,128]{1,0:T(8,128)S(1)}, f32[64,128]{1,0:T(8,128)S(1)}, u32[]{:S(2)}, u32[]{:S(2)}) collective-permute-start(f32[64,128]{1,0:T(8,128)S(1)} %select_add_fusion.bands_ref), channel_id=1, source_target_pairs={{0,8},{4,12},{8,0},{12,4},{16,24},{20,28},{24,16},{28,20},{1,9},{5... | collective-permute-start | bytes 98312 | tf_op jit(solution)/shard_map/ppermute | solution.py:224
  68.9 2.5 %collective-permute-start.7 = (f32[64,128]{1,0:T(8,128)S(1)}, f32[64,128]{1,0:T(8,128)S(1)}, u32[]{:S(2)}, u32[]{:S(2)}) collective-permute-start(f32[64,128]{1,0:T(8,128)S(1)} %select_add_fusion.bands_ref), channel_id=1, source_target_pairs={{0,4},{4,0},{8,12},{12,8},{16,20},{20,16},{24,28},{28,24},{1,5},{5... | collective-permute-start | bytes 98312 | tf_op jit(solution)/shard_map/ppermute | solution.py:224
  71.4 4.0 %collective-permute-start.10 = (f32[64,128]{1,0:T(8,128)S(1)}, f32[64,128]{1,0:T(8,128)S(1)}, u32[]{:S(2)}, u32[]{:S(2)}) collective-permute-start(f32[64,128]{1,0:T(8,128)S(1)} %add_add_fusion.refs_0_), channel_id=1, source_target_pairs={{0,16},{4,20},{8,24},{12,28},{16,0},{20,4},{24,8},{28,12},{1,17},{... | collective-permute-start | bytes 98312 | tf_op jit(solution)/shard_map/ppermute | solution.py:224

commit v20 on v19

--- a/solution.py
+++ b/solution.py
@@ -280,15 +280,12 @@
         (pair_parts[0], helped_hidden, cross_hidden, m)
     )
     far_head = send(pair_head, across)
-    first = pair_head[:16]
-    pair_rest, first = lax.optimization_barrier((pair_parts[1], first))
+    m = m + product(rows_of(me ^ 1, 0, handed), pair_head)
+    pair_rest, m = lax.optimization_barrier((pair_parts[1], m))
     far_parts = [far_head, send(pair_rest, across)]
     cross_grad, matrices, places = after((cross_grad, matrices, places), pair_head, m)
     swapped = send(jnp.where(end, helped_hidden, cross_grad[: handed + place_rows]), both_ways)
-    far_parts[0], pair_head, pair_rest, cross_grad = lax.optimization_barrier(
-        (far_parts[0], pair_head, pair_rest, cross_grad)
-    )
-    m = m + product(rows_of(me ^ 1, 0, 16), first) + product(rows_of(me ^ 1, 16, handed), pair_head[16:])
+    far_parts[0], pair_rest, cross_grad = lax.optimization_barrier((far_parts[0], pair_rest, cross_grad))
     m = m + product(rows_of(me ^ 1, handed), pair_rest)
     m = m + product(rows_of(cross), cross_grad) + product(far_hidden[:handed], far_parts[0])
     m, swapped = lax.optimization_barrier((m, swapped))

time: 77.4 us -> 78.2 us (1.010)
  waiting for transfers between devices: 32.1 us -> 33.8 us
  starting transfers between devices: 21.4 us -> 22.5 us
  other arithmetic: 4.32 us -> 3.25 us
  local copies, waits for them, and re-layouts: 5.92 us -> 5.07 us
    select_n x1, other arithmetic: 1.23 us -> 0.09 us  [lined(): jnp.where(end, helped_hidden, cross_grad[:handed + place_rows])]
    ppermute x8, starting transfers between devices: 17.9 us -> 19.1 us  [send(): return lax.ppermute(x, 'tp', perm)]
    ppermute x4, waiting for transfers between devices: 2.59 us -> 3.71 us  [spread_sum(): lax.ppermute(x, axis, [(i, i ^ stride * k) for i in range(size)])]
    slice x1 -> x0, local copies, waits for them, and re-layouts: 0.87 us -> none  [lined(): first = pair_head[:16]]
    dot_general x7 -> x6, matrix products: 6.56 us -> 6.53 us  [dot(): lax.dot_general(a, b, (dims, ((), ())), preferred_element_type=jnp.float32)]
  transfers between devices with their start and end apart: 12 -> 12, of which waited for: 8 -> 7; matrix products, arithmetic and copies ran while one was open for 22% -> 19% of each run, Pallas kernels for 4% -> 4%
where the time goes in v20:
time: 78.2 us; the launch traced here: 77.8 us
  waiting for transfers between devices  33.8 us (43%)
  starting transfers between devices  22.5 us (29%)
  matrix products  6.53 us (8%)
  Pallas kernels  5.87 us (8%)
  local copies, waits for them, and re-layouts  5.07 us (6%)
  other arithmetic  3.25 us (4%)
  between operations  0.84 us (1%)
    ppermute x8, waiting for transfers between devices, send(): return lax.ppermute(x, 'tp', perm)  30 us
    ppermute x8, starting transfers between devices, send(): return lax.ppermute(x, 'tp', perm)  19.1 us
    dot_general x6, matrix products, dot(): lax.dot_general(a, b, (dims, ((), ())), preferred_element_type=jnp.float32)  6.53 us
    pallas_call x6, Pallas kernels, call(): pl.pallas_call(kernel, out_shape=out_shapes, in_specs=[pl.BlockSpec(memor...  5.87 us
    ppermute x4, waiting for transfers between devices, spread_sum(): lax.ppermute(x, axis, [(i, i ^ stride * k) for i in range(size)])  3.71 us
    ppermute x4, starting transfers between devices, spread_sum(): lax.ppermute(x, axis, [(i, i ^ stride * k) for i in range(size)])  3.45 us
    slice x1, local copies, waits for them, and re-layouts, lined(): out_grad[:handed]  2.08 us
    slice x1, local copies, waits for them, and re-layouts, lined(): far_hidden[handed:]  1.93 us
  transfers between devices with their start and end apart: 12, of which 7 were waited for; matrix products, arithmetic and copies ran while one was open for 19% of the time, Pallas kernels for 4%

profile of v20, /device:TPU:0, one launch (start us, length us, event | category | flops | bytes accessed | tf_op | source)
XLA Modules:
  0.0 77.8 jit_solution(4817069063257398107)
XLA Ops:
  0.6 0.7 collective-permute-start.3
  1.4 2.1 %slice.22 = bf16[768,512]{1,0:T(8,128)(2,1)} slice(bf16[1152,512]{1,0:T(8,128)(2,1)} %param.9), slice={[0:768], [0:512]} | slice | bytes 1572864 | tf_op jit(solution)/shard_map/slice | solution.py:267
  3.4 5.8 %collective-permute-start.1 = (bf16[768,512]{1,0:T(8,128)(2,1)}, bf16[768,512]{1,0:T(8,128)(2,1)}, u32[]{:S(2)}, u32[]{:S(2)}) collective-permute-start(bf16[768,512]{1,0:T(8,128)(2,1)} %slice.22), channel_id=1, source_target_pairs={{0,1},{1,0},{2,3},{3,2},{4,5},{5,4},{6,7},{7,6},{8,9},{9,8},{10,11... | collective-permute-start | bytes 2359304 | tf_op jit(solution)/shard_map/ppermute | solution.py:259
  9.2 1.2 %dynamic-slice_select_fusion = (bf16[768,256]{1,0:T(8,128)(2,1)S(1)}, bf16[768,256]{1,0:T(8,128)(2,1)S(1)}) fusion(bf16[4608,256]{1,0:T(8,128)(2,1)} %param.8, s32[]{:T(128)S(6)} %select_n.55, pred[]{:T(512)S(6)} %or.3, s32[]{:T(128)S(6)} %add.76), kind=kLoop, calls=%fused_computation.15 | loop fusion | flops 196608 | bytes 1572873 | tf_op jit(solution)/shard_map/jit(_where)/select_n | solution.py:278
  10.4 0.0 copy-start.3
  10.4 1.9 %constant_dynamic-slice_fusion.2 = (bf16[384,256]{1,0:T(8,128)(2,1)S(1)}, bf16[384,256]{1,0:T(8,128)(2,1)S(1)}, bf16[384,256]{1,0:T(8,128)(2,1)}) fusion(bf16[4608,256]{1,0:T(8,128)(2,1)} %param.8, s32[]{:T(128)S(6)} %add.77, s32[]{:T(128)S(6)} %select_n.53, s32[]{:T(128)S(6)} %select_n.51), kind=kLoop, calls=%fused_computation.31 | loop fusion | bytes 1179660 | tf_op jit(solution)/shard_map/slice | solution.py:302
  12.4 0.9 %fusion.21 = (bf16[8,512]{1,0:T(8,128)(2,1)S(1)}, f32[8,512]{1,0:T(8,128)S(1)}) fusion(bf16[8,512]{1,0:T(8,128)(2,1)} %constant.58, s32[4,8]{1,0:T(4,128)} %param.12, s32[4,8]{1,0:T(4,128)} %param.11), kind=kOutput, calls=%fused_computation.33 | convolution fusion | flops 69760 | bytes 33024 | tf_op jit(solution)/shard_map/dot_general | solution.py:45
  13.3 1.9 %fusion.3 = bf16[784,512]{1,0:T(8,128)(2,1)} fusion(bf16[8,512]{1,0:T(8,128)(2,1)S(1)} %get-tuple-element.79, bf16[768,256]{1,0:T(8,128)(2,1)S(1)} %get-tuple-element.78, bf16[384,256]{1,0:T(8,128)(2,1)S(1)} %get-tuple-element.75, bf16[384,256]{1,0:T(8,128)(2,1)} %get-tuple-element.76), kind=kLoop, calls=%fused_computation.6 | loop fusion | flops 4014080 | bytes 1597440 | tf_op jit(solution)/shard_map/concatenate | solution.py:277
  15.2 0.0 copy-done.3
  15.2 0.0 copy-done.5
  15.2 1.6 %convolution_add_fusion = f32[256,512]{1,0:T(8,128)S(1)} fusion(bf16[1152,512]{1,0:T(8,128)(2,1)S(1)} %copy-done.3, bf16[4608,256]{1,0:T(8,128)(2,1)} %param.8, s32[]{:T(128)S(6)} %select_n.57, f32[1,256,512]{2,1,0:T(8,128)S(1)} %copy-done.5), kind=kOutput, calls=%fused_computation.2 | convolution fusion | flops 302252032 | bytes 2818052 | tf_op jit(solution)/shard_map/dot_general | solution.py:45
  16.8 10.0 %collective-permute-done.1 = bf16[768,512]{1,0:T(8,128)(2,1)} collective-permute-done((bf16[768,512]{1,0:T(8,128)(2,1)}, bf16[768,512]{1,0:T(8,128)(2,1)}, u32[]{:S(2)}, u32[]{:S(2)}) %collective-permute-start.1) | collective-permute-done | bytes 786464 | tf_op jit(solution)/shard_map/ppermute | solution.py:259
  26.8 0.7 collective-permute-start.2
  27.5 1.0 %slice.21 = bf16[384,512]{1,0:T(8,128)(2,1)S(1)} slice(bf16[1152,512]{1,0:T(8,128)(2,1)} %param.9), slice={[768:1152], [0:512]} | slice | bytes 786432 | tf_op jit(solution)/shard_map/slice | solution.py:267
  28.5 3.5 %collective-permute-start = (bf16[384,512]{1,0:T(8,128)(2,1)S(1)}, bf16[384,512]{1,0:T(8,128)(2,1)}, u32[]{:S(2)}, u32[]{:S(2)}) collective-permute-start(bf16[384,512]{1,0:T(8,128)(2,1)S(1)} %slice.21), channel_id=1, source_target_pairs={{0,1},{1,0},{2,3},{3,2},{4,5},{5,4},{6,7},{7,6},{8,9},{9,8},{10,11... | collective-permute-start | bytes 1179656 | tf_op jit(solution)/shard_map/ppermute | solution.py:259
  32.0 1.7 %fusion.9 = f32[256,512]{1,0:T(8,128)S(1)} fusion(bf16[768,512]{1,0:T(8,128)(2,1)} %collective-permute-done.1, bf16[4608,256]{1,0:T(8,128)(2,1)} %param.8, s32[]{:T(128)S(6)} %select_n.58), kind=kOutput, calls=%fused_computation.13 | convolution fusion | flops 201326592 | bytes 1703940 | tf_op jit(solution)/shard_map/dot_general | solution.py:45
  33.7 0.0 copy-start.2
  33.7 0.1 add.65
  33.8 5.9 %collective-permute-done = bf16[384,512]{1,0:T(8,128)(2,1)} collective-permute-done((bf16[384,512]{1,0:T(8,128)(2,1)S(1)}, bf16[384,512]{1,0:T(8,128)(2,1)}, u32[]{:S(2)}, u32[]{:S(2)}) %collective-permute-start) | collective-permute-done | bytes 393248 | tf_op jit(solution)/shard_map/ppermute | solution.py:259
  39.7 0.7 collective-permute-start.5
  40.4 0.0 collective-permute-done.3.cross_ref
  40.5 0.1 slice_select_fusion
  40.5 4.6 %collective-permute-start.4 = (bf16[784,512]{1,0:T(8,128)(2,1)S(1)}, bf16[784,512]{1,0:T(8,128)(2,1)S(1)}, u32[]{:S(2)}, u32[]{:S(2)}) collective-permute-start(bf16[784,512]{1,0:T(8,128)(2,1)S(1)} %slice_select_fusion), channel_id=1, source_target_pairs={{0,1},{1,0},{2,3},{3,2},{4,5},{5,4},{6,7},{7,6},{8,9},{9,8},{10,11... | collective-permute-start | bytes 2408456 | tf_op jit(solution)/shard_map/ppermute | solution.py:259
  45.1 0.0 collective-permute-done.2.far_ref
  45.2 0.5 fusion.4
  45.7 0.4 fusion.7
  46.1 0.0 copy-start
  46.1 0.0 copy-start.1
  46.1 1.4 %fusion.2.m_ref = f32[256,512]{1,0:T(8,128)S(1)} fusion(f32[256,512]{1,0:T(8,128)S(1)} %fusion.7, f32[256,512]{1,0:T(8,128)S(1)} %fusion.4, f32[256,512]{1,0:T(8,128)S(1)} %add.65, bf16[384,512]{1,0:T(8,128)(2,1)} %collective-permute-done, bf16[4608,256]{1,0:T(8,128)(2,1)S(1)} %copy-done.2, s32[]{:T(128)S(6)} %select_n.59), kind=kOutput, calls=%fused_computation.5 | convolution fusion | flops 101056512 | bytes 2686980 | tf_op jit(solution)/shard_map/dot_general | solution.py:45
  47.5 12.8 %collective-permute-done.4.swapped_ref = bf16[784,512]{1,0:T(8,128)(2,1)S(1)} collective-permute-done((bf16[784,512]{1,0:T(8,128)(2,1)S(1)}, bf16[784,512]{1,0:T(8,128)(2,1)S(1)}, u32[]{:S(2)}, u32[]{:S(2)}) %collective-permute-start.4) | collective-permute-done | bytes 802848 | tf_op jit(solution)/shard_map/ppermute | solution.py:259
  60.4 1.5 %shard_map.95 = (f32[256,512]{1,0:T(8,128)S(1)}, f32[256,512]{1,0:T(8,128)S(1)}, bf16[256,384]{1,0:T(8,128)(2,1)S(1)}, bf16[256,384]{1,0:T(8,128)(2,1)S(1)}, f32...) custom-call(f32[256,512]{1,0:T(8,128)S(1)} %fusion.2.m_ref, bf16[384,256]{1,0:T(8,128)(2,1)S(1)} %get-tuple-element.74.hidden_ref, ...), custom_call_target="tpu_custom_call" | custom-call | flops 400000000 | bytes 4000000 | tf_op jit(solution)/shard_map/pallas_call | solution.py:206
  61.8 0.0 collective-permute-done.5.far_ref
  61.8 1.1 %shard_map.96 = (s16[272,512]{1,0:T(8,128)(2,1)S(1)}, f32[64,128]{1,0:T(8,128)S(1)}) custom-call(f32[256,512]{1,0:T(8,128)S(1)} %get-tuple-element.54.helped_ref, bf16[256,384]{1,0:T(8,128)(2,1)S(1)} %get-tuple-element.55.turned_ref, bf16[384,512]{1,0:T(8,128)(2,1)S(1)} %collective-permute-done.5.far_ref, f32[16,512]{1,0:T(8,128)S(1)} %get-tuple-element.57.places_ref, ...), custom_call_target="tpu_custom_call" | custom-call | flops 400000000 | bytes 4000000 | tf_op jit(solution)/shard_map/pallas_call | solution.py:206
  62.9 1.8 %collective-permute-start.6 = (f32[64,128]{1,0:T(8,128)S(1)}, f32[64,128]{1,0:T(8,128)S(1)}, u32[]{:S(2)}, u32[]{:S(2)}) collective-permute-start(f32[64,128]{1,0:T(8,128)S(1)} %get-tuple-element.60), channel_id=1, source_target_pairs={{0,1},{1,0},{2,3},{3,2},{4,5},{5,4},{6,7},{7,6},{8,9},{9,8},{10,11... | collective-permute-start | bytes 98312 | tf_op jit(solution)/shard_map/ppermute | solution.py:259
  64.8 1.3 %collective-permute-start.11 = (s16[272,512]{1,0:T(8,128)(2,1)S(1)}, s16[272,512]{1,0:T(8,128)(2,1)S(1)}, u32[]{:S(2)}, u32[]{:S(2)}) collective-permute-start(s16[272,512]{1,0:T(8,128)(2,1)S(1)} %get-tuple-element.70), channel_id=1, source_target_pairs={{1,0},{2,3},{5,4},{6,7},{9,8},{10,11},{13,12},{14,15},{17,16},{18,... | collective-permute-start | bytes 835592 | tf_op jit(solution)/shard_map/ppermute | solution.py:259
  66.1 1.2 %collective-permute-done.6 = f32[64,128]{1,0:T(8,128)S(1)} collective-permute-done((f32[64,128]{1,0:T(8,128)S(1)}, f32[64,128]{1,0:T(8,128)S(1)}, u32[]{:S(2)}, u32[]{:S(2)}) %collective-permute-start.6) | collective-permute-done | bytes 32800 | tf_op jit(solution)/shard_map/ppermute | solution.py:259
  67.3 0.0 collective-permute-start.7
  67.3 1.6 %collective-permute-start.8 = (f32[64,128]{1,0:T(8,128)S(1)}, f32[64,128]{1,0:T(8,128)S(1)}, u32[]{:S(2)}, u32[]{:S(2)}) collective-permute-start(f32[64,128]{1,0:T(8,128)S(1)} %select_add_fusion.bands_ref), channel_id=1, source_target_pairs={{0,8},{4,12},{8,0},{12,4},{16,24},{20,28},{24,16},{28,20},{1,9},{5... | collective-permute-start | bytes 98312 | tf_op jit(solution)/shard_map/ppermute | solution.py:224
  68.9 0.3 collective-permute-start.9
  69.2 0.8 %shard_map.98.x_ref = f32[256,512]{1,0:T(8,128)S(1)} custom-call(f32[256,512]{1,0:T(8,128)S(1)} %get-tuple-element.69.m_ref, f32[64,128]{1,0:T(8,128)S(1)} %select_add_fusion.bands_ref, f32[8,512]{1,0:T(8,128)S(1)} %get-tuple-element.50.places_ref.refs_2_, bf16[512,128]{1,0:T(8,128)(2,1)S(1)} %copy-done.1, f32[256,256]{1,0:T(8,128)S(1)} %copy-done), custom_call_target="tpu_custom_call" | custom-call | flops 400000000 | bytes 4000000 | tf_op jit(solution)/shard_map/pallas_call | solution.py:206
  70.0 0.0 collective-permute-done.7
  70.1 1.3 %collective-permute-done.8 = f32[64,128]{1,0:T(8,128)S(1)} collective-permute-done((f32[64,128]{1,0:T(8,128)S(1)}, f32[64,128]{1,0:T(8,128)S(1)}, u32[]{:S(2)}, u32[]{:S(2)}) %collective-permute-start.8) | collective-permute-done | bytes 32800 | tf_op jit(solution)/shard_map/ppermute | solution.py:224
  71.3 0.9 %collective-permute-done.9 = f32[64,128]{1,0:T(8,128)S(1)} collective-permute-done((f32[64,128]{1,0:T(8,128)S(1)}, f32[64,128]{1,0:T(8,128)S(1)}, u32[]{:S(2)}, u32[]{:S(2)}) %collective-permute-start.9) | collective-permute-done | bytes 32800 | tf_op jit(solution)/shard_map/ppermute | solution.py:224
  72.3 1.6 %collective-permute-start.10 = (f32[64,128]{1,0:T(8,128)S(1)}, f32[64,128]{1,0:T(8,128)S(1)}, u32[]{:S(2)}, u32[]{:S(2)}) collective-permute-start(f32[64,128]{1,0:T(8,128)S(1)} %add_add_fusion.refs_0_), channel_id=1, source_target_pairs={{0,16},{4,20},{8,24},{12,28},{16,0},{20,4},{24,8},{28,12},{1,17},{... | collective-permute-start | bytes 98312 | tf_op jit(solution)/shard_map/ppermute | solution.py:224
  73.9 0.0 collective-permute-done.11.code_ref
  73.9 0.9 %shard_map.99 = f32[256,512]{1,0:T(8,128)} custom-call(f32[256,512]{1,0:T(8,128)S(1)} %shard_map.98.x_ref, s16[272,512]{1,0:T(8,128)(2,1)S(1)} %collective-permute-done.11.code_ref), custom_call_target="tpu_custom_call" | custom-call | flops 400000000 | bytes 4000000 | tf_op jit(solution)/shard_map/pallas_call | solution.py:206
  74.7 1.5 %collective-permute-done.10.refs_1_ = f32[64,128]{1,0:T(8,128)S(1)} collective-permute-done((f32[64,128]{1,0:T(8,128)S(1)}, f32[64,128]{1,0:T(8,128)S(1)}, u32[]{:S(2)}, u32[]{:S(2)}) %collective-permute-start.10) | collective-permute-done | bytes 32800 | tf_op jit(solution)/shard_map/ppermute | solution.py:224
  76.2 1.6 %shard_map.100 = bf16[256,512]{1,0:T(8,128)(2,1)} custom-call(f32[64,128]{1,0:T(8,128)S(1)} %add_add_fusion.refs_0_, f32[64,128]{1,0:T(8,128)S(1)} %collective-permute-done.10.refs_1_, f32[8,512]{1,0:T(8,128)S(1)} %get-tuple-element.50.places_ref.refs_2_, bf16[512,128]{1,0:T(8,128)(2,1)S(1)} %copy-done.1, f32[256,256]{1,0:T(8,128)S(1)} %copy-done), custom_call_target="tpu_custom_call" | custom-call | flops 400000000 | bytes 4000000 | tf_op jit(solution)/shard_map/pallas_call | solution.py:206
  (9 shorter events, 0.1 us)
Async XLA Ops:
  0.6 39.8 %collective-permute-start.3 = (bf16[1152,512]{1,0:T(8,128)(2,1)}, bf16[1152,512]{1,0:T(8,128)(2,1)S(1)}, u32[]{:S(2)}, u32[]{:S(2)}) collective-permute-start(bf16[1152,512]{1,0:T(8,128)(2,1)} %param.9), channel_id=1, source_target_pairs={{1,2},{2,1},{5,6},{6,5},{9,10},{10,9},{13,14},{14,13},{17,18},{18,... | collective-permute-start | bytes 3538952 | tf_op jit(solution)/shard_map/ppermute | solution.py:259
  3.4 23.4 %collective-permute-start.1 = (bf16[768,512]{1,0:T(8,128)(2,1)}, bf16[768,512]{1,0:T(8,128)(2,1)}, u32[]{:S(2)}, u32[]{:S(2)}) collective-permute-start(bf16[768,512]{1,0:T(8,128)(2,1)} %slice.22), channel_id=1, source_target_pairs={{0,1},{1,0},{2,3},{3,2},{4,5},{5,4},{6,7},{7,6},{8,9},{9,8},{10,11... | collective-permute-start | bytes 2359304 | tf_op jit(solution)/shard_map/ppermute | solution.py:259
  10.4 4.7 %copy-start.3 = (bf16[1152,512]{1,0:T(8,128)(2,1)S(1)}, bf16[1152,512]{1,0:T(8,128)(2,1)}, u32[]{:S(2)}) copy-start(bf16[1152,512]{1,0:T(8,128)(2,1)} %param.9) | copy-start | bytes 3538948
  12.4 2.8 %copy-start.5 = (f32[1,256,512]{2,1,0:T(8,128)S(1)}, f32[1,256,512]{2,1,0:T(8,128)}, u32[]{:S(2)}) copy-start(f32[1,256,512]{2,1,0:T(8,128)} %param.10) | copy-start | bytes 1572868
  26.8 18.3 %collective-permute-start.2 = (bf16[768,512]{1,0:T(8,128)(2,1)}, bf16[768,512]{1,0:T(8,128)(2,1)S(1)}, u32[]{:S(2)}, u32[]{:S(2)}) collective-permute-start(bf16[768,512]{1,0:T(8,128)(2,1)} %collective-permute-done.1), channel_id=1, source_target_pairs={{1,2},{2,1},{5,6},{6,5},{9,10},{10,9},{13,14},{14,13},{17,18},{18,... | collective-permute-start | bytes 2359304 | tf_op jit(solution)/shard_map/ppermute | solution.py:259
  28.5 11.2 %collective-permute-start = (bf16[384,512]{1,0:T(8,128)(2,1)S(1)}, bf16[384,512]{1,0:T(8,128)(2,1)}, u32[]{:S(2)}, u32[]{:S(2)}) collective-permute-start(bf16[384,512]{1,0:T(8,128)(2,1)S(1)} %slice.21), channel_id=1, source_target_pairs={{0,1},{1,0},{2,3},{3,2},{4,5},{5,4},{6,7},{7,6},{8,9},{9,8},{10,11... | collective-permute-start | bytes 1179656 | tf_op jit(solution)/shard_map/ppermute | solution.py:259
  32.0 8.4 %copy-start.4 = (bf16[784,512]{1,0:T(8,128)(2,1)S(1)}, bf16[784,512]{1,0:T(8,128)(2,1)}, u32[]{:S(2)}) copy-start(bf16[784,512]{1,0:T(8,128)(2,1)} %fusion.3) | copy-start | bytes 2408452
  33.7 11.4 %copy-start.2 = (bf16[4608,256]{1,0:T(8,128)(2,1)S(1)}, bf16[4608,256]{1,0:T(8,128)(2,1)}, u32[]{:S(2)}) copy-start(bf16[4608,256]{1,0:T(8,128)(2,1)} %param.8) | copy-start | bytes 7077892
  39.7 22.1 %collective-permute-start.5 = (bf16[384,512]{1,0:T(8,128)(2,1)}, bf16[384,512]{1,0:T(8,128)(2,1)S(1)}, u32[]{:S(2)}, u32[]{:S(2)}) collective-permute-start(bf16[384,512]{1,0:T(8,128)(2,1)} %collective-permute-done), channel_id=1, source_target_pairs={{1,2},{2,1},{5,6},{6,5},{9,10},{10,9},{13,14},{14,13},{17,18},{18,... | collective-permute-start | bytes 1179656 | tf_op jit(solution)/shard_map/ppermute | solution.py:259
  40.5 19.8 %collective-permute-start.4 = (bf16[784,512]{1,0:T(8,128)(2,1)S(1)}, bf16[784,512]{1,0:T(8,128)(2,1)S(1)}, u32[]{:S(2)}, u32[]{:S(2)}) collective-permute-start(bf16[784,512]{1,0:T(8,128)(2,1)S(1)} %slice_select_fusion), channel_id=1, source_target_pairs={{0,1},{1,0},{2,3},{3,2},{4,5},{5,4},{6,7},{7,6},{8,9},{9,8},{10,11... | collective-permute-start | bytes 2408456 | tf_op jit(solution)/shard_map/ppermute | solution.py:259
  46.1 14.3 %copy-start = (f32[256,256]{1,0:T(8,128)S(1)}, f32[256,256]{1,0:T(8,128)}, u32[]{:S(2)}) copy-start(f32[256,256]{1,0:T(8,128)} %constant.35.clone.refs_1_.basis_ref.refs_4_) | copy-start | bytes 786436
  46.1 14.3 %copy-start.1 = (bf16[512,128]{1,0:T(8,128)(2,1)S(1)}, bf16[512,128]{1,0:T(8,128)(2,1)}, u32[]{:S(2)}) copy-start(bf16[512,128]{1,0:T(8,128)(2,1)} %constant.34.clone.refs_0_.fold_ref.refs_3_) | copy-start | bytes 393220
  62.9 4.4 %collective-permute-start.6 = (f32[64,128]{1,0:T(8,128)S(1)}, f32[64,128]{1,0:T(8,128)S(1)}, u32[]{:S(2)}, u32[]{:S(2)}) collective-permute-start(f32[64,128]{1,0:T(8,128)S(1)} %get-tuple-element.60), channel_id=1, source_target_pairs={{0,1},{1,0},{2,3},{3,2},{4,5},{5,4},{6,7},{7,6},{8,9},{9,8},{10,11... | collective-permute-start | bytes 98312 | tf_op jit(solution)/shard_map/ppermute | solution.py:259
  64.8 9.1 %collective-permute-start.11 = (s16[272,512]{1,0:T(8,128)(2,1)S(1)}, s16[272,512]{1,0:T(8,128)(2,1)S(1)}, u32[]{:S(2)}, u32[]{:S(2)}) collective-permute-start(s16[272,512]{1,0:T(8,128)(2,1)S(1)} %get-tuple-element.70), channel_id=1, source_target_pairs={{1,0},{2,3},{5,4},{6,7},{9,8},{10,11},{13,12},{14,15},{17,16},{18,... | collective-permute-start | bytes 835592 | tf_op jit(solution)/shard_map/ppermute | solution.py:259
  67.3 2.7 %collective-permute-start.7 = (f32[64,128]{1,0:T(8,128)S(1)}, f32[64,128]{1,0:T(8,128)S(1)}, u32[]{:S(2)}, u32[]{:S(2)}) collective-permute-start(f32[64,128]{1,0:T(8,128)S(1)} %select_add_fusion.bands_ref), channel_id=1, source_target_pairs={{0,4},{4,0},{8,12},{12,8},{16,20},{20,16},{24,28},{28,24},{1,5},{5... | collective-permute-start | bytes 98312 | tf_op jit(solution)/shard_map/ppermute | solution.py:224
  67.3 4.0 %collective-permute-start.8 = (f32[64,128]{1,0:T(8,128)S(1)}, f32[64,128]{1,0:T(8,128)S(1)}, u32[]{:S(2)}, u32[]{:S(2)}) collective-permute-start(f32[64,128]{1,0:T(8,128)S(1)} %select_add_fusion.bands_ref), channel_id=1, source_target_pairs={{0,8},{4,12},{8,0},{12,4},{16,24},{20,28},{24,16},{28,20},{1,9},{5... | collective-permute-start | bytes 98312 | tf_op jit(solution)/shard_map/ppermute | solution.py:224
  68.9 3.4 %collective-permute-start.9 = (f32[64,128]{1,0:T(8,128)S(1)}, f32[64,128]{1,0:T(8,128)S(1)}, u32[]{:S(2)}, u32[]{:S(2)}) collective-permute-start(f32[64,128]{1,0:T(8,128)S(1)} %select_add_fusion.bands_ref), channel_id=1, source_target_pairs={{0,12},{4,8},{8,4},{12,0},{16,28},{20,24},{24,20},{28,16},{1,13},{... | collective-permute-start | bytes 98312 | tf_op jit(solution)/shard_map/ppermute | solution.py:224
  72.3 4.0 %collective-permute-start.10 = (f32[64,128]{1,0:T(8,128)S(1)}, f32[64,128]{1,0:T(8,128)S(1)}, u32[]{:S(2)}, u32[]{:S(2)}) collective-permute-start(f32[64,128]{1,0:T(8,128)S(1)} %add_add_fusion.refs_0_), channel_id=1, source_target_pairs={{0,16},{4,20},{8,24},{12,28},{16,0},{20,4},{24,8},{28,12},{1,17},{... | collective-permute-start | bytes 98312 | tf_op jit(solution)/shard_map/ppermute | solution.py:224

commit v21 on v20

--- a/solution.py
+++ b/solution.py
@@ -281,10 +281,11 @@
     )
     far_head = send(pair_head, across)
     m = m + product(rows_of(me ^ 1, 0, handed), pair_head)
-    pair_rest, m = lax.optimization_barrier((pair_parts[1], m))
+    cross_grad, matrices, places = after((cross_grad, matrices, places), pair_head, m)
+    to_swap = jnp.where(end, helped_hidden, cross_grad[: handed + place_rows])
+    swapped = send(to_swap, both_ways)
+    pair_rest, m, to_swap = lax.optimization_barrier((pair_parts[1], m, to_swap))
     far_parts = [far_head, send(pair_rest, across)]
-    cross_grad, matrices, places = after((cross_grad, matrices, places), pair_head, m)
-    swapped = send(jnp.where(end, helped_hidden, cross_grad[: handed + place_rows]), both_ways)
     far_parts[0], pair_rest, cross_grad = lax.optimization_barrier((far_parts[0], pair_rest, cross_grad))
     m = m + product(rows_of(me ^ 1, handed), pair_rest)
     m = m + product(rows_of(cross), cross_grad) + product(far_hidden[:handed], far_parts[0])

time: 78.2 us -> 74.6 us (0.954)
  starting transfers between devices: 22.5 us -> 18.7 us
    ppermute x8, starting transfers between devices: 19.1 us -> 15.3 us  [send(): return lax.ppermute(x, 'tp', perm)]
  transfers between devices with their start and end apart: 12 -> 12, of which waited for: 7 -> 7; matrix products, arithmetic and copies ran while one was open for 19% -> 20% of each run, Pallas kernels for 4% -> 4%
where the time goes in v21:
time: 74.6 us; the launch traced here: 74.1 us
  waiting for transfers between devices  33.9 us (45%)
  starting transfers between devices  18.7 us (25%)
  matrix products  6.46 us (9%)
  Pallas kernels  5.86 us (8%)
  local copies, waits for them, and re-layouts  5.07 us (7%)
  other arithmetic  3.25 us (4%)
  between operations  0.85 us (1%)
    ppermute x8, waiting for transfers between devices, send(): return lax.ppermute(x, 'tp', perm)  30.2 us
    ppermute x8, starting transfers between devices, send(): return lax.ppermute(x, 'tp', perm)  15.3 us
    dot_general x6, matrix products, dot(): lax.dot_general(a, b, (dims, ((), ())), preferred_element_type=jnp.float32)  6.46 us
    pallas_call x6, Pallas kernels, call(): pl.pallas_call(kernel, out_shape=out_shapes, in_specs=[pl.BlockSpec(memor...  5.86 us
    ppermute x4, waiting for transfers between devices, spread_sum(): lax.ppermute(x, axis, [(i, i ^ stride * k) for i in range(size)])  3.72 us
    ppermute x4, starting transfers between devices, spread_sum(): lax.ppermute(x, axis, [(i, i ^ stride * k) for i in range(size)])  3.43 us
    slice x1, local copies, waits for them, and re-layouts, lined(): out_grad[:handed]  2.08 us
    slice x1, local copies, waits for them, and re-layouts, lined(): far_hidden[handed:]  1.93 us
  transfers between devices with their start and end apart: 12, of which 7 were waited for; matrix products, arithmetic and copies ran while one was open for 20% of the time, Pallas kernels for 4%

profile of v21, /device:TPU:0, one launch (start us, length us, event | category | flops | bytes accessed | tf_op | source)
XLA Modules:
  0.0 74.1 jit_solution(4343796000081743973)
XLA Ops:
  0.6 0.7 collective-permute-start.2
  1.4 2.1 %slice.22 = bf16[768,512]{1,0:T(8,128)(2,1)} slice(bf16[1152,512]{1,0:T(8,128)(2,1)} %param.9), slice={[0:768], [0:512]} | slice | bytes 1572864 | tf_op jit(solution)/shard_map/slice | solution.py:267
  3.4 5.8 %collective-permute-start.1 = (bf16[768,512]{1,0:T(8,128)(2,1)}, bf16[768,512]{1,0:T(8,128)(2,1)}, u32[]{:S(2)}, u32[]{:S(2)}) collective-permute-start(bf16[768,512]{1,0:T(8,128)(2,1)} %slice.22), channel_id=1, source_target_pairs={{0,1},{1,0},{2,3},{3,2},{4,5},{5,4},{6,7},{7,6},{8,9},{9,8},{10,11... | collective-permute-start | bytes 2359304 | tf_op jit(solution)/shard_map/ppermute | solution.py:259
  9.2 1.2 %dynamic-slice_select_fusion = (bf16[768,256]{1,0:T(8,128)(2,1)S(1)}, bf16[768,256]{1,0:T(8,128)(2,1)S(1)}) fusion(bf16[4608,256]{1,0:T(8,128)(2,1)} %param.8, s32[]{:T(128)S(6)} %select_n.55, pred[]{:T(512)S(6)} %or.3, s32[]{:T(128)S(6)} %add.76), kind=kLoop, calls=%fused_computation.13 | loop fusion | flops 196608 | bytes 1572873 | tf_op jit(solution)/shard_map/jit(_where)/select_n | solution.py:278
  10.4 0.0 copy-start.3
  10.4 1.9 %constant_dynamic-slice_fusion.2 = (bf16[384,256]{1,0:T(8,128)(2,1)S(1)}, bf16[384,256]{1,0:T(8,128)(2,1)S(1)}, bf16[384,256]{1,0:T(8,128)(2,1)}) fusion(bf16[4608,256]{1,0:T(8,128)(2,1)} %param.8, s32[]{:T(128)S(6)} %add.77, s32[]{:T(128)S(6)} %select_n.53, s32[]{:T(128)S(6)} %select_n.51), kind=kLoop, calls=%fused_computation.30 | loop fusion | bytes 1179660 | tf_op jit(solution)/shard_map/slice | solution.py:303
  12.4 0.9 %fusion.22 = (bf16[8,512]{1,0:T(8,128)(2,1)S(1)}, f32[8,512]{1,0:T(8,128)S(1)}) fusion(bf16[8,512]{1,0:T(8,128)(2,1)} %constant.57, s32[4,8]{1,0:T(4,128)} %param.12, s32[4,8]{1,0:T(4,128)} %param.11), kind=kOutput, calls=%fused_computation.32 | convolution fusion | flops 69760 | bytes 33024 | tf_op jit(solution)/shard_map/dot_general | solution.py:45
  13.3 1.9 %fusion.1 = bf16[784,512]{1,0:T(8,128)(2,1)} fusion(bf16[8,512]{1,0:T(8,128)(2,1)S(1)} %get-tuple-element.79, bf16[768,256]{1,0:T(8,128)(2,1)S(1)} %get-tuple-element.78, bf16[384,256]{1,0:T(8,128)(2,1)S(1)} %get-tuple-element.75, bf16[384,256]{1,0:T(8,128)(2,1)} %get-tuple-element.76), kind=kLoop, calls=%fused_computation.3 | loop fusion | flops 4014080 | bytes 1597440 | tf_op jit(solution)/shard_map/concatenate | solution.py:277
  15.2 0.0 copy-done.3
  15.2 0.0 copy-done.5
  15.2 1.6 %convolution_add_fusion = f32[256,512]{1,0:T(8,128)S(1)} fusion(bf16[1152,512]{1,0:T(8,128)(2,1)S(1)} %copy-done.3, bf16[4608,256]{1,0:T(8,128)(2,1)} %param.8, s32[]{:T(128)S(6)} %select_n.57, f32[1,256,512]{2,1,0:T(8,128)S(1)} %copy-done.5), kind=kOutput, calls=%fused_computation.2 | convolution fusion | flops 302252032 | bytes 2818052 | tf_op jit(solution)/shard_map/dot_general | solution.py:45
  16.8 10.0 %collective-permute-done.1 = bf16[768,512]{1,0:T(8,128)(2,1)} collective-permute-done((bf16[768,512]{1,0:T(8,128)(2,1)}, bf16[768,512]{1,0:T(8,128)(2,1)}, u32[]{:S(2)}, u32[]{:S(2)}) %collective-permute-start.1) | collective-permute-done | bytes 786464 | tf_op jit(solution)/shard_map/ppermute | solution.py:259
  26.8 0.7 collective-permute-start.3
  27.5 1.0 %slice.21 = bf16[384,512]{1,0:T(8,128)(2,1)S(1)} slice(bf16[1152,512]{1,0:T(8,128)(2,1)} %param.9), slice={[768:1152], [0:512]} | slice | bytes 786432 | tf_op jit(solution)/shard_map/slice | solution.py:267
  28.5 3.5 %collective-permute-start = (bf16[384,512]{1,0:T(8,128)(2,1)S(1)}, bf16[384,512]{1,0:T(8,128)(2,1)}, u32[]{:S(2)}, u32[]{:S(2)}) collective-permute-start(bf16[384,512]{1,0:T(8,128)(2,1)S(1)} %slice.21), channel_id=1, source_target_pairs={{0,1},{1,0},{2,3},{3,2},{4,5},{5,4},{6,7},{7,6},{8,9},{9,8},{10,11... | collective-permute-start | bytes 1179656 | tf_op jit(solution)/shard_map/ppermute | solution.py:259
  32.0 1.7 %fusion.9 = f32[256,512]{1,0:T(8,128)S(1)} fusion(bf16[768,512]{1,0:T(8,128)(2,1)} %collective-permute-done.1, bf16[4608,256]{1,0:T(8,128)(2,1)} %param.8, s32[]{:T(128)S(6)} %select_n.58), kind=kOutput, calls=%fused_computation.11 | convolution fusion | flops 201326592 | bytes 1703940 | tf_op jit(solution)/shard_map/dot_general | solution.py:45
  33.7 0.0 copy-start.2
  33.7 0.1 add.65
  33.8 0.0 collective-permute-done.2.cross_ref
  33.8 0.1 slice_select_fusion
  33.9 0.8 %collective-permute-start.4 = (bf16[784,512]{1,0:T(8,128)(2,1)S(1)}, bf16[784,512]{1,0:T(8,128)(2,1)S(1)}, u32[]{:S(2)}, u32[]{:S(2)}) collective-permute-start(bf16[784,512]{1,0:T(8,128)(2,1)S(1)} %slice_select_fusion), channel_id=1, source_target_pairs={{0,1},{1,0},{2,3},{3,2},{4,5},{5,4},{6,7},{7,6},{8,9},{9,8},{10,11... | collective-permute-start | bytes 2408456 | tf_op jit(solution)/shard_map/ppermute | solution.py:259
  34.8 7.4 %collective-permute-done = bf16[384,512]{1,0:T(8,128)(2,1)} collective-permute-done((bf16[384,512]{1,0:T(8,128)(2,1)S(1)}, bf16[384,512]{1,0:T(8,128)(2,1)}, u32[]{:S(2)}, u32[]{:S(2)}) %collective-permute-start) | collective-permute-done | bytes 393248 | tf_op jit(solution)/shard_map/ppermute | solution.py:259
  42.1 0.7 collective-permute-start.5
  42.8 0.0 collective-permute-done.3.far_ref
  42.8 0.5 fusion.2
  43.4 1.3 %fusion.11 = f32[256,512]{1,0:T(8,128)S(1)} fusion(bf16[384,512]{1,0:T(8,128)(2,1)} %collective-permute-done, bf16[4608,256]{1,0:T(8,128)(2,1)S(1)} %copy-done.2, s32[]{:T(128)S(6)} %select_n.61), kind=kOutput, calls=%fused_computation.14 | convolution fusion | flops 100663296 | bytes 1114116 | tf_op jit(solution)/shard_map/dot_general | solution.py:45
  44.7 0.0 copy-start
  44.7 0.0 copy-start.1
  44.7 0.4 add_add_fusion.m_ref
  45.1 11.7 %collective-permute-done.4.swapped_ref = bf16[784,512]{1,0:T(8,128)(2,1)S(1)} collective-permute-done((bf16[784,512]{1,0:T(8,128)(2,1)S(1)}, bf16[784,512]{1,0:T(8,128)(2,1)S(1)}, u32[]{:S(2)}, u32[]{:S(2)}) %collective-permute-start.4) | collective-permute-done | bytes 802848 | tf_op jit(solution)/shard_map/ppermute | solution.py:259
  56.9 1.4 %shard_map.95 = (f32[256,512]{1,0:T(8,128)S(1)}, f32[256,512]{1,0:T(8,128)S(1)}, bf16[256,384]{1,0:T(8,128)(2,1)S(1)}, bf16[256,384]{1,0:T(8,128)(2,1)S(1)}, f32...) custom-call(f32[256,512]{1,0:T(8,128)S(1)} %add_add_fusion.m_ref, bf16[384,256]{1,0:T(8,128)(2,1)S(1)} %get-tuple-element.74.hidden_ref, ...), custom_call_target="tpu_custom_call" | custom-call | flops 400000000 | bytes 4000000 | tf_op jit(solution)/shard_map/pallas_call | solution.py:206
  58.3 0.0 collective-permute-done.5.far_ref
  58.3 1.1 %shard_map.96 = (s16[272,512]{1,0:T(8,128)(2,1)S(1)}, f32[64,128]{1,0:T(8,128)S(1)}) custom-call(f32[256,512]{1,0:T(8,128)S(1)} %get-tuple-element.54.helped_ref, bf16[256,384]{1,0:T(8,128)(2,1)S(1)} %get-tuple-element.55.turned_ref, bf16[384,512]{1,0:T(8,128)(2,1)S(1)} %collective-permute-done.5.far_ref, f32[16,512]{1,0:T(8,128)S(1)} %get-tuple-element.57.places_ref, ...), custom_call_target="tpu_custom_call" | custom-call | flops 400000000 | bytes 4000000 | tf_op jit(solution)/shard_map/pallas_call | solution.py:206
  59.4 1.8 %collective-permute-start.6 = (f32[64,128]{1,0:T(8,128)S(1)}, f32[64,128]{1,0:T(8,128)S(1)}, u32[]{:S(2)}, u32[]{:S(2)}) collective-permute-start(f32[64,128]{1,0:T(8,128)S(1)} %get-tuple-element.60), channel_id=1, source_target_pairs={{0,1},{1,0},{2,3},{3,2},{4,5},{5,4},{6,7},{7,6},{8,9},{9,8},{10,11... | collective-permute-start | bytes 98312 | tf_op jit(solution)/shard_map/ppermute | solution.py:259
  61.3 1.3 %collective-permute-start.11 = (s16[272,512]{1,0:T(8,128)(2,1)S(1)}, s16[272,512]{1,0:T(8,128)(2,1)S(1)}, u32[]{:S(2)}, u32[]{:S(2)}) collective-permute-start(s16[272,512]{1,0:T(8,128)(2,1)S(1)} %get-tuple-element.70), channel_id=1, source_target_pairs={{1,0},{2,3},{5,4},{6,7},{9,8},{10,11},{13,12},{14,15},{17,16},{18,... | collective-permute-start | bytes 835592 | tf_op jit(solution)/shard_map/ppermute | solution.py:259
  62.6 1.1 %collective-permute-done.6 = f32[64,128]{1,0:T(8,128)S(1)} collective-permute-done((f32[64,128]{1,0:T(8,128)S(1)}, f32[64,128]{1,0:T(8,128)S(1)}, u32[]{:S(2)}, u32[]{:S(2)}) %collective-permute-start.6) | collective-permute-done | bytes 32800 | tf_op jit(solution)/shard_map/ppermute | solution.py:259
  63.7 0.0 collective-permute-start.7
  63.7 1.6 %collective-permute-start.8 = (f32[64,128]{1,0:T(8,128)S(1)}, f32[64,128]{1,0:T(8,128)S(1)}, u32[]{:S(2)}, u32[]{:S(2)}) collective-permute-start(f32[64,128]{1,0:T(8,128)S(1)} %select_add_fusion.bands_ref), channel_id=1, source_target_pairs={{0,8},{4,12},{8,0},{12,4},{16,24},{20,28},{24,16},{28,20},{1,9},{5... | collective-permute-start | bytes 98312 | tf_op jit(solution)/shard_map/ppermute | solution.py:224
  65.2 0.3 collective-permute-start.9
  65.5 0.9 %shard_map.98.x_ref = f32[256,512]{1,0:T(8,128)S(1)} custom-call(f32[256,512]{1,0:T(8,128)S(1)} %get-tuple-element.69.m_ref, f32[64,128]{1,0:T(8,128)S(1)} %select_add_fusion.bands_ref, f32[8,512]{1,0:T(8,128)S(1)} %get-tuple-element.50.places_ref.refs_2_, bf16[512,128]{1,0:T(8,128)(2,1)S(1)} %copy-done.1, f32[256,256]{1,0:T(8,128)S(1)} %copy-done), custom_call_target="tpu_custom_call" | custom-call | flops 400000000 | bytes 4000000 | tf_op jit(solution)/shard_map/pallas_call | solution.py:206
  66.4 0.0 collective-permute-done.7
  66.4 1.3 %collective-permute-done.8 = f32[64,128]{1,0:T(8,128)S(1)} collective-permute-done((f32[64,128]{1,0:T(8,128)S(1)}, f32[64,128]{1,0:T(8,128)S(1)}, u32[]{:S(2)}, u32[]{:S(2)}) %collective-permute-start.8) | collective-permute-done | bytes 32800 | tf_op jit(solution)/shard_map/ppermute | solution.py:224
  67.6 0.9 %collective-permute-done.9 = f32[64,128]{1,0:T(8,128)S(1)} collective-permute-done((f32[64,128]{1,0:T(8,128)S(1)}, f32[64,128]{1,0:T(8,128)S(1)}, u32[]{:S(2)}, u32[]{:S(2)}) %collective-permute-start.9) | collective-permute-done | bytes 32800 | tf_op jit(solution)/shard_map/ppermute | solution.py:224
  68.6 1.6 %collective-permute-start.10 = (f32[64,128]{1,0:T(8,128)S(1)}, f32[64,128]{1,0:T(8,128)S(1)}, u32[]{:S(2)}, u32[]{:S(2)}) collective-permute-start(f32[64,128]{1,0:T(8,128)S(1)} %add_add_fusion.1.refs_0_), channel_id=1, source_target_pairs={{0,16},{4,20},{8,24},{12,28},{16,0},{20,4},{24,8},{28,12},{1,17},{... | collective-permute-start | bytes 98312 | tf_op jit(solution)/shard_map/ppermute | solution.py:224
  70.2 0.0 collective-permute-done.11.code_ref
  70.2 0.9 %shard_map.99 = f32[256,512]{1,0:T(8,128)} custom-call(f32[256,512]{1,0:T(8,128)S(1)} %shard_map.98.x_ref, s16[272,512]{1,0:T(8,128)(2,1)S(1)} %collective-permute-done.11.code_ref), custom_call_target="tpu_custom_call" | custom-call | flops 400000000 | bytes 4000000 | tf_op jit(solution)/shard_map/pallas_call | solution.py:206
  71.0 1.5 %collective-permute-done.10.refs_1_ = f32[64,128]{1,0:T(8,128)S(1)} collective-permute-done((f32[64,128]{1,0:T(8,128)S(1)}, f32[64,128]{1,0:T(8,128)S(1)}, u32[]{:S(2)}, u32[]{:S(2)}) %collective-permute-start.10) | collective-permute-done | bytes 32800 | tf_op jit(solution)/shard_map/ppermute | solution.py:224
  72.6 1.6 %shard_map.100 = bf16[256,512]{1,0:T(8,128)(2,1)} custom-call(f32[64,128]{1,0:T(8,128)S(1)} %add_add_fusion.1.refs_0_, f32[64,128]{1,0:T(8,128)S(1)} %collective-permute-done.10.refs_1_, f32[8,512]{1,0:T(8,128)S(1)} %get-tuple-element.50.places_ref.refs_2_, bf16[512,128]{1,0:T(8,128)(2,1)S(1)} %copy-done.1, f32[256,256]{1,0:T(8,128)S(1)} %copy-done), custom_call_target="tpu_custom_call" | custom-call | flops 400000000 | bytes 4000000 | tf_op jit(solution)/shard_map/pallas_call | solution.py:206
  (9 shorter events, 0.1 us)
Async XLA Ops:
  0.6 33.2 %collective-permute-start.2 = (bf16[1152,512]{1,0:T(8,128)(2,1)}, bf16[1152,512]{1,0:T(8,128)(2,1)S(1)}, u32[]{:S(2)}, u32[]{:S(2)}) collective-permute-start(bf16[1152,512]{1,0:T(8,128)(2,1)} %param.9), channel_id=1, source_target_pairs={{1,2},{2,1},{5,6},{6,5},{9,10},{10,9},{13,14},{14,13},{17,18},{18,... | collective-permute-start | bytes 3538952 | tf_op jit(solution)/shard_map/ppermute | solution.py:259
  3.4 23.4 %collective-permute-start.1 = (bf16[768,512]{1,0:T(8,128)(2,1)}, bf16[768,512]{1,0:T(8,128)(2,1)}, u32[]{:S(2)}, u32[]{:S(2)}) collective-permute-start(bf16[768,512]{1,0:T(8,128)(2,1)} %slice.22), channel_id=1, source_target_pairs={{0,1},{1,0},{2,3},{3,2},{4,5},{5,4},{6,7},{7,6},{8,9},{9,8},{10,11... | collective-permute-start | bytes 2359304 | tf_op jit(solution)/shard_map/ppermute | solution.py:259
  10.4 4.7 %copy-start.3 = (bf16[1152,512]{1,0:T(8,128)(2,1)S(1)}, bf16[1152,512]{1,0:T(8,128)(2,1)}, u32[]{:S(2)}) copy-start(bf16[1152,512]{1,0:T(8,128)(2,1)} %param.9) | copy-start | bytes 3538948
  12.4 2.8 %copy-start.5 = (f32[1,256,512]{2,1,0:T(8,128)S(1)}, f32[1,256,512]{2,1,0:T(8,128)}, u32[]{:S(2)}) copy-start(f32[1,256,512]{2,1,0:T(8,128)} %param.10) | copy-start | bytes 1572868
  26.8 16.0 %collective-permute-start.3 = (bf16[768,512]{1,0:T(8,128)(2,1)}, bf16[768,512]{1,0:T(8,128)(2,1)S(1)}, u32[]{:S(2)}, u32[]{:S(2)}) collective-permute-start(bf16[768,512]{1,0:T(8,128)(2,1)} %collective-permute-done.1), channel_id=1, source_target_pairs={{1,2},{2,1},{5,6},{6,5},{9,10},{10,9},{13,14},{14,13},{17,18},{18,... | collective-permute-start | bytes 2359304 | tf_op jit(solution)/shard_map/ppermute | solution.py:259
  28.5 13.6 %collective-permute-start = (bf16[384,512]{1,0:T(8,128)(2,1)S(1)}, bf16[384,512]{1,0:T(8,128)(2,1)}, u32[]{:S(2)}, u32[]{:S(2)}) collective-permute-start(bf16[384,512]{1,0:T(8,128)(2,1)S(1)} %slice.21), channel_id=1, source_target_pairs={{0,1},{1,0},{2,3},{3,2},{4,5},{5,4},{6,7},{7,6},{8,9},{9,8},{10,11... | collective-permute-start | bytes 1179656 | tf_op jit(solution)/shard_map/ppermute | solution.py:259
  32.0 1.8 %copy-start.4 = (bf16[784,512]{1,0:T(8,128)(2,1)S(1)}, bf16[784,512]{1,0:T(8,128)(2,1)}, u32[]{:S(2)}) copy-start(bf16[784,512]{1,0:T(8,128)(2,1)} %fusion.1) | copy-start | bytes 2408452
  33.7 9.1 %copy-start.2 = (bf16[4608,256]{1,0:T(8,128)(2,1)S(1)}, bf16[4608,256]{1,0:T(8,128)(2,1)}, u32[]{:S(2)}) copy-start(bf16[4608,256]{1,0:T(8,128)(2,1)} %param.8) | copy-start | bytes 7077892
  33.9 22.9 %collective-permute-start.4 = (bf16[784,512]{1,0:T(8,128)(2,1)S(1)}, bf16[784,512]{1,0:T(8,128)(2,1)S(1)}, u32[]{:S(2)}, u32[]{:S(2)}) collective-permute-start(bf16[784,512]{1,0:T(8,128)(2,1)S(1)} %slice_select_fusion), channel_id=1, source_target_pairs={{0,1},{1,0},{2,3},{3,2},{4,5},{5,4},{6,7},{7,6},{8,9},{9,8},{10,11... | collective-permute-start | bytes 2408456 | tf_op jit(solution)/shard_map/ppermute | solution.py:259
  42.1 16.2 %collective-permute-start.5 = (bf16[384,512]{1,0:T(8,128)(2,1)}, bf16[384,512]{1,0:T(8,128)(2,1)S(1)}, u32[]{:S(2)}, u32[]{:S(2)}) collective-permute-start(bf16[384,512]{1,0:T(8,128)(2,1)} %collective-permute-done), channel_id=1, source_target_pairs={{1,2},{2,1},{5,6},{6,5},{9,10},{10,9},{13,14},{14,13},{17,18},{18,... | collective-permute-start | bytes 1179656 | tf_op jit(solution)/shard_map/ppermute | solution.py:259
  44.7 12.1 %copy-start = (f32[256,256]{1,0:T(8,128)S(1)}, f32[256,256]{1,0:T(8,128)}, u32[]{:S(2)}) copy-start(f32[256,256]{1,0:T(8,128)} %constant.35.clone.refs_1_.basis_ref.refs_4_) | copy-start | bytes 786436
  44.7 12.1 %copy-start.1 = (bf16[512,128]{1,0:T(8,128)(2,1)S(1)}, bf16[512,128]{1,0:T(8,128)(2,1)}, u32[]{:S(2)}) copy-start(bf16[512,128]{1,0:T(8,128)(2,1)} %constant.34.clone.refs_0_.fold_ref.refs_3_) | copy-start | bytes 393220
  59.4 4.2 %collective-permute-start.6 = (f32[64,128]{1,0:T(8,128)S(1)}, f32[64,128]{1,0:T(8,128)S(1)}, u32[]{:S(2)}, u32[]{:S(2)}) collective-permute-start(f32[64,128]{1,0:T(8,128)S(1)} %get-tuple-element.60), channel_id=1, source_target_pairs={{0,1},{1,0},{2,3},{3,2},{4,5},{5,4},{6,7},{7,6},{8,9},{9,8},{10,11... | collective-permute-start | bytes 98312 | tf_op jit(solution)/shard_map/ppermute | solution.py:259
  61.3 8.9 %collective-permute-start.11 = (s16[272,512]{1,0:T(8,128)(2,1)S(1)}, s16[272,512]{1,0:T(8,128)(2,1)S(1)}, u32[]{:S(2)}, u32[]{:S(2)}) collective-permute-start(s16[272,512]{1,0:T(8,128)(2,1)S(1)} %get-tuple-element.70), channel_id=1, source_target_pairs={{1,0},{2,3},{5,4},{6,7},{9,8},{10,11},{13,12},{14,15},{17,16},{18,... | collective-permute-start | bytes 835592 | tf_op jit(solution)/shard_map/ppermute | solution.py:259
  63.7 2.7 %collective-permute-start.7 = (f32[64,128]{1,0:T(8,128)S(1)}, f32[64,128]{1,0:T(8,128)S(1)}, u32[]{:S(2)}, u32[]{:S(2)}) collective-permute-start(f32[64,128]{1,0:T(8,128)S(1)} %select_add_fusion.bands_ref), channel_id=1, source_target_pairs={{0,4},{4,0},{8,12},{12,8},{16,20},{20,16},{24,28},{28,24},{1,5},{5... | collective-permute-start | bytes 98312 | tf_op jit(solution)/shard_map/ppermute | solution.py:224
  63.7 4.0 %collective-permute-start.8 = (f32[64,128]{1,0:T(8,128)S(1)}, f32[64,128]{1,0:T(8,128)S(1)}, u32[]{:S(2)}, u32[]{:S(2)}) collective-permute-start(f32[64,128]{1,0:T(8,128)S(1)} %select_add_fusion.bands_ref), channel_id=1, source_target_pairs={{0,8},{4,12},{8,0},{12,4},{16,24},{20,28},{24,16},{28,20},{1,9},{5... | collective-permute-start | bytes 98312 | tf_op jit(solution)/shard_map/ppermute | solution.py:224
  65.2 3.4 %collective-permute-start.9 = (f32[64,128]{1,0:T(8,128)S(1)}, f32[64,128]{1,0:T(8,128)S(1)}, u32[]{:S(2)}, u32[]{:S(2)}) collective-permute-start(f32[64,128]{1,0:T(8,128)S(1)} %select_add_fusion.bands_ref), channel_id=1, source_target_pairs={{0,12},{4,8},{8,4},{12,0},{16,28},{20,24},{24,20},{28,16},{1,13},{... | collective-permute-start | bytes 98312 | tf_op jit(solution)/shard_map/ppermute | solution.py:224
  68.6 4.0 %collective-permute-start.10 = (f32[64,128]{1,0:T(8,128)S(1)}, f32[64,128]{1,0:T(8,128)S(1)}, u32[]{:S(2)}, u32[]{:S(2)}) collective-permute-start(f32[64,128]{1,0:T(8,128)S(1)} %add_add_fusion.1.refs_0_), channel_id=1, source_target_pairs={{0,16},{4,20},{8,24},{12,28},{16,0},{20,4},{24,8},{28,12},{1,17},{... | collective-permute-start | bytes 98312 | tf_op jit(solution)/shard_map/ppermute | solution.py:224

commit v22 on v21

--- a/solution.py
+++ b/solution.py
@@ -141,16 +141,14 @@
 
 def swapped_kernel(m_ref, hidden_ref, cross_hidden_ref, cross_ref, far_ref, swapped_ref, places_ref, *refs):
     *matrix_refs, out_ref, helped_ref, own_turned_ref, end_turned_ref, end_places_ref, bands_ref = refs
-    handed, side = far_ref.shape[0], out_ref.shape[0]
+    handed, side = swapped_ref.shape[0] - place_rows, out_ref.shape[0]
     alone = cross_ref.shape[0] - handed
     out_ref[...] = m_ref[...] + dot(cross_hidden_ref[...], swapped_ref[:handed], ((0,), (0,)))
-    helped_ref[...] = (
-        dot(swapped_ref[:alone, :side], cross_ref[handed:], ((0,), (0,)))
-        + dot(swapped_ref[alone:handed, :side], far_ref[: handed - alone], ((0,), (0,)))
-        + dot(swapped_ref[:alone, side:], far_ref[handed - alone :], ((0,), (0,)))
+    helped_ref[...] = dot(swapped_ref[:alone, :side], cross_ref[handed:], ((0,), (0,))) + dot(
+        swapped_ref[alone:handed, :side], far_ref[...], ((0,), (0,))
     )
     own_turned_ref[...] = hidden_ref[...].T
-    end_turned_ref[...] = swapped_ref[alone:handed, side:].T
+    end_turned_ref[...] = swapped_ref[:handed, side:].T
     end_places_ref[...] = swapped_ref[handed:].astype(jnp.float32)
     bands_ref[...] = bands_of(out_ref[...], places_ref[...], *matrix_refs)
 
@@ -264,7 +262,7 @@
 
     cross_grad = send(out_grad, across)
     m = carried + product(rows_of(me), out_grad)
-    pair_parts = [send(out_grad[:handed], both_ways), send(out_grad[handed:], both_ways)]
+    pair_parts = [send(out_grad[:alone], both_ways), send(out_grad[alone:], both_ways)]
     far_hidden = rows_of(far)
     helped_hidden = jnp.concatenate(
         [
@@ -280,27 +278,27 @@
         (pair_parts[0], helped_hidden, cross_hidden, m)
     )
     far_head = send(pair_head, across)
-    m = m + product(rows_of(me ^ 1, 0, handed), pair_head)
+    m = m + product(rows_of(me ^ 1, 0, alone), pair_head)
     cross_grad, matrices, places = after((cross_grad, matrices, places), pair_head, m)
     to_swap = jnp.where(end, helped_hidden, cross_grad[: handed + place_rows])
     swapped = send(to_swap, both_ways)
     pair_rest, m, to_swap = lax.optimization_barrier((pair_parts[1], m, to_swap))
     far_parts = [far_head, send(pair_rest, across)]
     far_parts[0], pair_rest, cross_grad = lax.optimization_barrier((far_parts[0], pair_rest, cross_grad))
-    m = m + product(rows_of(me ^ 1, handed), pair_rest)
-    m = m + product(rows_of(cross), cross_grad) + product(far_hidden[:handed], far_parts[0])
+    m = m + product(rows_of(me ^ 1, alone), pair_rest)
+    m = m + product(rows_of(cross), cross_grad) + product(far_hidden[:alone], far_parts[0])
     m, swapped = lax.optimization_barrier((m, swapped))
 
     height, width = m.shape[0] // steps, m.shape[1] // steps
     full = jax.ShapeDtypeStruct(m.shape, jnp.float32)
-    turned = jax.ShapeDtypeStruct((m.shape[0], alone), hidden.dtype)
+    turned = jax.ShapeDtypeStruct((m.shape[0], handed), hidden.dtype)
     table = jax.ShapeDtypeStruct((place_rows, m.shape[1]), jnp.float32)
     folded = jax.ShapeDtypeStruct((height, width), jnp.float32)
     m, helped, own_turned, end_turned, end_places, own_bands = call(
         swapped_kernel,
         (full, full, turned, turned, table, folded),
         m,
-        far_hidden[handed:],
+        far_hidden[alone:],
         cross_hidden,
         cross_grad,
         far_parts[0],

time: 74.6 us -> 72.9 us (0.977)
  starting transfers between devices: 18.7 us -> 31.5 us
  waiting for transfers between devices: 33.9 us -> 24.5 us
  other arithmetic: 3.25 us -> 0.32 us
  matrix products: 6.46 us -> 4.36 us
    ppermute x8, starting transfers between devices: 15.3 us -> 28.1 us  [send(): return lax.ppermute(x, 'tp', perm)]
    ppermute x8, waiting for transfers between devices: 30.2 us -> 21 us  [send(): return lax.ppermute(x, 'tp', perm)]
    dot_general x6, matrix products: 6.46 us -> 4.36 us  [dot(): lax.dot_general(a, b, (dims, ((), ())), preferred_element_type=jnp.float32)]
    concatenate x1, other arithmetic: 1.87 us -> 0.05 us  [lined(): helped_hidden = jnp.concatenate([helped_hidden, place_part], axis=0)]
    slice x3 -> x2, local copies, waits for them, and re-layouts: 5.03 us -> 3.88 us  [the longest x1 2.11 us: lined(): out_grad[alone:]]
    select_n x1, other arithmetic: 1.19 us -> 0.08 us  [lined(): cross_hidden = jnp.where(end, rows_of(cross, 0, handed), 0)]
    unnamed x12 -> x16, local copies, waits for them, and re-layouts: 0.03 us -> 1.13 us
  transfers between devices with their start and end apart: 12 -> 12, of which waited for: 7 -> 8; matrix products, arithmetic and copies ran while one was open for 20% -> 12% of each run, Pallas kernels for 4% -> 4%
where the time goes in v22:
time: 72.9 us; the launch traced here: 72.5 us
  starting transfers between devices  31.5 us (43%)
  waiting for transfers between devices  24.5 us (34%)
  Pallas kernels  5.81 us (8%)
  local copies, waits for them, and re-layouts  5.04 us (7%)
  matrix products  4.36 us (6%)
  between operations  0.91 us (1%)
    ppermute x8, starting transfers between devices, send(): return lax.ppermute(x, 'tp', perm)  28.1 us
    ppermute x8, waiting for transfers between devices, send(): return lax.ppermute(x, 'tp', perm)  21 us
    pallas_call x6, Pallas kernels, call(): pl.pallas_call(kernel, out_shape=out_shapes, in_specs=[pl.BlockSpec(memor...  5.81 us
    dot_general x6, matrix products, dot(): lax.dot_general(a, b, (dims, ((), ())), preferred_element_type=jnp.float32)  4.36 us
    ppermute x4, waiting for transfers between devices, spread_sum(): lax.ppermute(x, axis, [(i, i ^ stride * k) for i in range(size)])  3.5 us
    ppermute x4, starting transfers between devices, spread_sum(): lax.ppermute(x, axis, [(i, i ^ stride * k) for i in range(size)])  3.44 us
    slice x1, local copies, waits for them, and re-layouts, lined(): out_grad[alone:]  2.11 us
    slice x1, local copies, waits for them, and re-layouts, lined(): out_grad[:alone]  1.77 us
  transfers between devices with their start and end apart: 12, of which 8 were waited for; matrix products, arithmetic and copies ran while one was open for 12% of the time, Pallas kernels for 4%

profile of v22, /device:TPU:0, one launch (start us, length us, event | category | flops | bytes accessed | tf_op | source)
XLA Modules:
  0.0 72.5 jit_solution(9365185986601193443)
XLA Ops:
  0.6 0.9 %collective-permute-start.2 = (bf16[1152,512]{1,0:T(8,128)(2,1)}, bf16[1152,512]{1,0:T(8,128)(2,1)S(1)}, u32[]{:S(2)}, u32[]{:S(2)}) collective-permute-start(bf16[1152,512]{1,0:T(8,128)(2,1)} %param.9), channel_id=1, source_target_pairs={{1,2},{2,1},{5,6},{6,5},{9,10},{10,9},{13,14},{14,13},{17,18},{18,... | collective-permute-start | bytes 3538952 | tf_op jit(solution)/shard_map/ppermute | solution.py:257
  1.5 1.8 %slice.18 = bf16[384,512]{1,0:T(8,128)(2,1)} slice(bf16[1152,512]{1,0:T(8,128)(2,1)} %param.9), slice={[0:384], [0:512]} | slice | bytes 786432 | tf_op jit(solution)/shard_map/slice | solution.py:265
  3.3 5.8 %collective-permute-start.1 = (bf16[384,512]{1,0:T(8,128)(2,1)}, bf16[384,512]{1,0:T(8,128)(2,1)}, u32[]{:S(2)}, u32[]{:S(2)}) collective-permute-start(bf16[384,512]{1,0:T(8,128)(2,1)} %slice.18), channel_id=1, source_target_pairs={{0,1},{1,0},{2,3},{3,2},{4,5},{5,4},{6,7},{7,6},{8,9},{9,8},{10,11... | collective-permute-start | bytes 1179656 | tf_op jit(solution)/shard_map/ppermute | solution.py:257
  9.1 2.1 %slice.17 = bf16[768,512]{1,0:T(8,128)(2,1)} slice(bf16[1152,512]{1,0:T(8,128)(2,1)} %param.9), slice={[384:1152], [0:512]} | slice | bytes 1572864 | tf_op jit(solution)/shard_map/slice | solution.py:265
  11.2 0.0 collective-permute-start
  11.3 0.0 copy-start.2
  11.3 0.0 copy-start.4
  11.3 0.1 dynamic-slice_select_fusion
  11.4 0.5 copy-done.5
  11.9 0.0 copy-done.7
  11.9 0.1 fusion.17
  12.0 0.1 fusion.1
  12.1 0.5 copy-done.2
  12.6 0.1 copy-done.4
  12.7 0.5 convolution_add_fusion
  13.2 6.1 %collective-permute-done.1 = bf16[384,512]{1,0:T(8,128)(2,1)} collective-permute-done((bf16[384,512]{1,0:T(8,128)(2,1)}, bf16[384,512]{1,0:T(8,128)(2,1)}, u32[]{:S(2)}, u32[]{:S(2)}) %collective-permute-start.1) | collective-permute-done | bytes 393248 | tf_op jit(solution)/shard_map/ppermute | solution.py:257
  19.4 0.7 collective-permute-start.3
  20.0 1.3 %fusion.7 = f32[256,512]{1,0:T(8,128)S(1)} fusion(bf16[384,512]{1,0:T(8,128)(2,1)} %collective-permute-done.1, bf16[4608,256]{1,0:T(8,128)(2,1)S(1)} %copy-done.3, s32[]{:T(128)S(6)} %select_n.58), kind=kOutput, calls=%fused_computation.12 | convolution fusion | flops 100663296 | bytes 1114116 | tf_op jit(solution)/shard_map/dot_general | solution.py:45
  21.4 0.1 add.65
  21.5 0.0 collective-permute-done.2.cross_ref
  21.5 0.1 slice_select_fusion
  21.6 13.3 %collective-permute-start.4 = (bf16[784,512]{1,0:T(8,128)(2,1)S(1)}, bf16[784,512]{1,0:T(8,128)(2,1)S(1)}, u32[]{:S(2)}, u32[]{:S(2)}) collective-permute-start(bf16[784,512]{1,0:T(8,128)(2,1)S(1)} %slice_select_fusion), channel_id=1, source_target_pairs={{0,1},{1,0},{2,3},{3,2},{4,5},{5,4},{6,7},{7,6},{8,9},{9,8},{10,11... | collective-permute-start | bytes 2408456 | tf_op jit(solution)/shard_map/ppermute | solution.py:257
  34.9 1.3 %collective-permute-done = bf16[768,512]{1,0:T(8,128)(2,1)} collective-permute-done((bf16[768,512]{1,0:T(8,128)(2,1)}, bf16[768,512]{1,0:T(8,128)(2,1)}, u32[]{:S(2)}, u32[]{:S(2)}) %collective-permute-start) | collective-permute-done | bytes 786464 | tf_op jit(solution)/shard_map/ppermute | solution.py:257
  36.2 0.7 collective-permute-start.5
  36.9 0.0 collective-permute-done.3.far_ref
  36.9 1.5 %fusion.5 = f32[256,512]{1,0:T(8,128)S(1)} fusion(bf16[768,512]{1,0:T(8,128)(2,1)} %collective-permute-done, bf16[4608,256]{1,0:T(8,128)(2,1)S(1)} %copy-done.3, s32[]{:T(128)S(6)} %select_n.61), kind=kOutput, calls=%fused_computation.9 | convolution fusion | flops 201326592 | bytes 1703940 | tf_op jit(solution)/shard_map/dot_general | solution.py:45
  38.5 0.5 fusion.2
  39.0 0.0 copy-start
  39.0 0.0 copy-start.1
  39.0 0.3 add_add_fusion.m_ref
  39.4 12.8 %collective-permute-done.4.swapped_ref = bf16[784,512]{1,0:T(8,128)(2,1)S(1)} collective-permute-done((bf16[784,512]{1,0:T(8,128)(2,1)S(1)}, bf16[784,512]{1,0:T(8,128)(2,1)S(1)}, u32[]{:S(2)}, u32[]{:S(2)}) %collective-permute-start.4) | collective-permute-done | bytes 802848 | tf_op jit(solution)/shard_map/ppermute | solution.py:257
  52.2 1.3 %shard_map.95 = (f32[256,512]{1,0:T(8,128)S(1)}, f32[256,512]{1,0:T(8,128)S(1)}, bf16[256,768]{1,0:T(8,128)(2,1)S(1)}, bf16[256,768]{1,0:T(8,128)(2,1)S(1)}, f32...) custom-call(f32[256,512]{1,0:T(8,128)S(1)} %add_add_fusion.m_ref, bf16[768,256]{1,0:T(8,128)(2,1)S(1)} %get-tuple-element.75.hidden_ref, ...), custom_call_target="tpu_custom_call" | custom-call | flops 400000000 | bytes 4000000 | tf_op jit(solution)/shard_map/pallas_call | solution.py:204
  53.5 0.0 collective-permute-done.5.far_ref
  53.5 1.2 %shard_map.96 = (s16[272,512]{1,0:T(8,128)(2,1)S(1)}, f32[64,128]{1,0:T(8,128)S(1)}) custom-call(f32[256,512]{1,0:T(8,128)S(1)} %get-tuple-element.54.helped_ref, bf16[256,768]{1,0:T(8,128)(2,1)S(1)} %get-tuple-element.55.turned_ref, bf16[768,512]{1,0:T(8,128)(2,1)S(1)} %collective-permute-done.5.far_ref, f32[16,512]{1,0:T(8,128)S(1)} %get-tuple-element.57.places_ref, ...), custom_call_target="tpu_custom_call" | custom-call | flops 400000000 | bytes 4000000 | tf_op jit(solution)/shard_map/pallas_call | solution.py:204
  54.7 5.4 %collective-permute-start.6 = (f32[64,128]{1,0:T(8,128)S(1)}, f32[64,128]{1,0:T(8,128)S(1)}, u32[]{:S(2)}, u32[]{:S(2)}) collective-permute-start(f32[64,128]{1,0:T(8,128)S(1)} %get-tuple-element.60), channel_id=1, source_target_pairs={{0,1},{1,0},{2,3},{3,2},{4,5},{5,4},{6,7},{7,6},{8,9},{9,8},{10,11... | collective-permute-start | bytes 98312 | tf_op jit(solution)/shard_map/ppermute | solution.py:257
  60.2 1.3 %collective-permute-start.11 = (s16[272,512]{1,0:T(8,128)(2,1)S(1)}, s16[272,512]{1,0:T(8,128)(2,1)S(1)}, u32[]{:S(2)}, u32[]{:S(2)}) collective-permute-start(s16[272,512]{1,0:T(8,128)(2,1)S(1)} %get-tuple-element.70), channel_id=1, source_target_pairs={{1,0},{2,3},{5,4},{6,7},{9,8},{10,11},{13,12},{14,15},{17,16},{18,... | collective-permute-start | bytes 835592 | tf_op jit(solution)/shard_map/ppermute | solution.py:257
  61.5 0.5 collective-permute-done.6
  62.0 0.0 collective-permute-start.7
  62.0 1.6 %collective-permute-start.8 = (f32[64,128]{1,0:T(8,128)S(1)}, f32[64,128]{1,0:T(8,128)S(1)}, u32[]{:S(2)}, u32[]{:S(2)}) collective-permute-start(f32[64,128]{1,0:T(8,128)S(1)} %select_add_fusion.bands_ref), channel_id=1, source_target_pairs={{0,8},{4,12},{8,0},{12,4},{16,24},{20,28},{24,16},{28,20},{1,9},{5... | collective-permute-start | bytes 98312 | tf_op jit(solution)/shard_map/ppermute | solution.py:222
  63.6 0.3 collective-permute-start.9
  63.9 0.8 %shard_map.98.x_ref = f32[256,512]{1,0:T(8,128)S(1)} custom-call(f32[256,512]{1,0:T(8,128)S(1)} %get-tuple-element.69.m_ref, f32[64,128]{1,0:T(8,128)S(1)} %select_add_fusion.bands_ref, f32[8,512]{1,0:T(8,128)S(1)} %get-tuple-element.50.places_ref.refs_2_, bf16[512,128]{1,0:T(8,128)(2,1)S(1)} %copy-done.1, f32[256,256]{1,0:T(8,128)S(1)} %copy-done), custom_call_target="tpu_custom_call" | custom-call | flops 400000000 | bytes 4000000 | tf_op jit(solution)/shard_map/pallas_call | solution.py:204
  64.8 1.3 %collective-permute-done.8 = f32[64,128]{1,0:T(8,128)S(1)} collective-permute-done((f32[64,128]{1,0:T(8,128)S(1)}, f32[64,128]{1,0:T(8,128)S(1)}, u32[]{:S(2)}, u32[]{:S(2)}) %collective-permute-start.8) | collective-permute-done | bytes 32800 | tf_op jit(solution)/shard_map/ppermute | solution.py:222
  66.0 0.9 %collective-permute-done.9 = f32[64,128]{1,0:T(8,128)S(1)} collective-permute-done((f32[64,128]{1,0:T(8,128)S(1)}, f32[64,128]{1,0:T(8,128)S(1)}, u32[]{:S(2)}, u32[]{:S(2)}) %collective-permute-start.9) | collective-permute-done | bytes 32800 | tf_op jit(solution)/shard_map/ppermute | solution.py:222
  67.0 1.6 %collective-permute-start.10 = (f32[64,128]{1,0:T(8,128)S(1)}, f32[64,128]{1,0:T(8,128)S(1)}, u32[]{:S(2)}, u32[]{:S(2)}) collective-permute-start(f32[64,128]{1,0:T(8,128)S(1)} %add_add_fusion.1.refs_0_), channel_id=1, source_target_pairs={{0,16},{4,20},{8,24},{12,28},{16,0},{20,4},{24,8},{28,12},{1,17},{... | collective-permute-start | bytes 98312 | tf_op jit(solution)/shard_map/ppermute | solution.py:222
  68.5 0.2 collective-permute-done.11.code_ref
  68.8 0.9 %shard_map.99 = f32[256,512]{1,0:T(8,128)} custom-call(f32[256,512]{1,0:T(8,128)S(1)} %shard_map.98.x_ref, s16[272,512]{1,0:T(8,128)(2,1)S(1)} %collective-permute-done.11.code_ref), custom_call_target="tpu_custom_call" | custom-call | flops 400000000 | bytes 4000000 | tf_op jit(solution)/shard_map/pallas_call | solution.py:204
  69.6 1.3 %collective-permute-done.10.refs_1_ = f32[64,128]{1,0:T(8,128)S(1)} collective-permute-done((f32[64,128]{1,0:T(8,128)S(1)}, f32[64,128]{1,0:T(8,128)S(1)}, u32[]{:S(2)}, u32[]{:S(2)}) %collective-permute-start.10) | collective-permute-done | bytes 32800 | tf_op jit(solution)/shard_map/ppermute | solution.py:222
  70.9 1.6 %shard_map.100 = bf16[256,512]{1,0:T(8,128)(2,1)} custom-call(f32[64,128]{1,0:T(8,128)S(1)} %add_add_fusion.1.refs_0_, f32[64,128]{1,0:T(8,128)S(1)} %collective-permute-done.10.refs_1_, f32[8,512]{1,0:T(8,128)S(1)} %get-tuple-element.50.places_ref.refs_2_, bf16[512,128]{1,0:T(8,128)(2,1)S(1)} %copy-done.1, f32[256,256]{1,0:T(8,128)S(1)} %copy-done), custom_call_target="tpu_custom_call" | custom-call | flops 400000000 | bytes 4000000 | tf_op jit(solution)/shard_map/pallas_call | solution.py:204
  (13 shorter events, 0.1 us)
Async XLA Ops:
  0.6 10.6 %copy-start.3 = (bf16[4608,256]{1,0:T(8,128)(2,1)S(1)}, bf16[4608,256]{1,0:T(8,128)(2,1)}, u32[]{:S(2)}) copy-start(bf16[4608,256]{1,0:T(8,128)(2,1)} %param.8) | copy-start | bytes 7077892
  0.6 20.8 %collective-permute-start.2 = (bf16[1152,512]{1,0:T(8,128)(2,1)}, bf16[1152,512]{1,0:T(8,128)(2,1)S(1)}, u32[]{:S(2)}, u32[]{:S(2)}) collective-permute-start(bf16[1152,512]{1,0:T(8,128)(2,1)} %param.9), channel_id=1, source_target_pairs={{1,2},{2,1},{5,6},{6,5},{9,10},{10,9},{13,14},{14,13},{17,18},{18,... | collective-permute-start | bytes 3538952 | tf_op jit(solution)/shard_map/ppermute | solution.py:257
  3.3 16.1 %collective-permute-start.1 = (bf16[384,512]{1,0:T(8,128)(2,1)}, bf16[384,512]{1,0:T(8,128)(2,1)}, u32[]{:S(2)}, u32[]{:S(2)}) collective-permute-start(bf16[384,512]{1,0:T(8,128)(2,1)} %slice.18), channel_id=1, source_target_pairs={{0,1},{1,0},{2,3},{3,2},{4,5},{5,4},{6,7},{7,6},{8,9},{9,8},{10,11... | collective-permute-start | bytes 1179656 | tf_op jit(solution)/shard_map/ppermute | solution.py:257
  11.2 0.7 copy-start.5
  11.2 0.7 copy-start.6
  11.2 0.7 copy-start.7
  11.2 25.0 %collective-permute-start = (bf16[768,512]{1,0:T(8,128)(2,1)}, bf16[768,512]{1,0:T(8,128)(2,1)}, u32[]{:S(2)}, u32[]{:S(2)}) collective-permute-start(bf16[768,512]{1,0:T(8,128)(2,1)} %slice.17), channel_id=1, source_target_pairs={{0,1},{1,0},{2,3},{3,2},{4,5},{5,4},{6,7},{7,6},{8,9},{9,8},{10,11... | collective-permute-start | bytes 2359304 | tf_op jit(solution)/shard_map/ppermute | solution.py:257
  11.3 1.3 %copy-start.2 = (bf16[1152,512]{1,0:T(8,128)(2,1)S(1)}, bf16[1152,512]{1,0:T(8,128)(2,1)}, u32[]{:S(2)}) copy-start(bf16[1152,512]{1,0:T(8,128)(2,1)} %param.9) | copy-start | bytes 3538948
  11.3 1.4 %copy-start.4 = (f32[1,256,512]{2,1,0:T(8,128)S(1)}, f32[1,256,512]{2,1,0:T(8,128)}, u32[]{:S(2)}) copy-start(f32[1,256,512]{2,1,0:T(8,128)} %param.10) | copy-start | bytes 1572868
  19.4 17.6 %collective-permute-start.3 = (bf16[384,512]{1,0:T(8,128)(2,1)}, bf16[384,512]{1,0:T(8,128)(2,1)S(1)}, u32[]{:S(2)}, u32[]{:S(2)}) collective-permute-start(bf16[384,512]{1,0:T(8,128)(2,1)} %collective-permute-done.1), channel_id=1, source_target_pairs={{1,2},{2,1},{5,6},{6,5},{9,10},{10,9},{13,14},{14,13},{17,18},{18,... | collective-permute-start | bytes 1179656 | tf_op jit(solution)/shard_map/ppermute | solution.py:257
  21.6 30.6 %collective-permute-start.4 = (bf16[784,512]{1,0:T(8,128)(2,1)S(1)}, bf16[784,512]{1,0:T(8,128)(2,1)S(1)}, u32[]{:S(2)}, u32[]{:S(2)}) collective-permute-start(bf16[784,512]{1,0:T(8,128)(2,1)S(1)} %slice_select_fusion), channel_id=1, source_target_pairs={{0,1},{1,0},{2,3},{3,2},{4,5},{5,4},{6,7},{7,6},{8,9},{9,8},{10,11... | collective-permute-start | bytes 2408456 | tf_op jit(solution)/shard_map/ppermute | solution.py:257
  36.2 17.3 %collective-permute-start.5 = (bf16[768,512]{1,0:T(8,128)(2,1)}, bf16[768,512]{1,0:T(8,128)(2,1)S(1)}, u32[]{:S(2)}, u32[]{:S(2)}) collective-permute-start(bf16[768,512]{1,0:T(8,128)(2,1)} %collective-permute-done), channel_id=1, source_target_pairs={{1,2},{2,1},{5,6},{6,5},{9,10},{10,9},{13,14},{14,13},{17,18},{18,... | collective-permute-start | bytes 2359304 | tf_op jit(solution)/shard_map/ppermute | solution.py:257
  39.0 13.2 %copy-start = (f32[256,256]{1,0:T(8,128)S(1)}, f32[256,256]{1,0:T(8,128)}, u32[]{:S(2)}) copy-start(f32[256,256]{1,0:T(8,128)} %constant.38.clone.refs_1_.basis_ref.refs_4_) | copy-start | bytes 786436
  39.0 13.2 %copy-start.1 = (bf16[512,128]{1,0:T(8,128)(2,1)S(1)}, bf16[512,128]{1,0:T(8,128)(2,1)}, u32[]{:S(2)}) copy-start(bf16[512,128]{1,0:T(8,128)(2,1)} %constant.37.clone.refs_0_.fold_ref.refs_3_) | copy-start | bytes 393220
  54.7 7.3 %collective-permute-start.6 = (f32[64,128]{1,0:T(8,128)S(1)}, f32[64,128]{1,0:T(8,128)S(1)}, u32[]{:S(2)}, u32[]{:S(2)}) collective-permute-start(f32[64,128]{1,0:T(8,128)S(1)} %get-tuple-element.60), channel_id=1, source_target_pairs={{0,1},{1,0},{2,3},{3,2},{4,5},{5,4},{6,7},{7,6},{8,9},{9,8},{10,11... | collective-permute-start | bytes 98312 | tf_op jit(solution)/shard_map/ppermute | solution.py:257
  60.2 8.6 %collective-permute-start.11 = (s16[272,512]{1,0:T(8,128)(2,1)S(1)}, s16[272,512]{1,0:T(8,128)(2,1)S(1)}, u32[]{:S(2)}, u32[]{:S(2)}) collective-permute-start(s16[272,512]{1,0:T(8,128)(2,1)S(1)} %get-tuple-element.70), channel_id=1, source_target_pairs={{1,0},{2,3},{5,4},{6,7},{9,8},{10,11},{13,12},{14,15},{17,16},{18,... | collective-permute-start | bytes 835592 | tf_op jit(solution)/shard_map/ppermute | solution.py:257
  62.0 2.7 %collective-permute-start.7 = (f32[64,128]{1,0:T(8,128)S(1)}, f32[64,128]{1,0:T(8,128)S(1)}, u32[]{:S(2)}, u32[]{:S(2)}) collective-permute-start(f32[64,128]{1,0:T(8,128)S(1)} %select_add_fusion.bands_ref), channel_id=1, source_target_pairs={{0,4},{4,0},{8,12},{12,8},{16,20},{20,16},{24,28},{28,24},{1,5},{5... | collective-permute-start | bytes 98312 | tf_op jit(solution)/shard_map/ppermute | solution.py:222
  62.0 4.0 %collective-permute-start.8 = (f32[64,128]{1,0:T(8,128)S(1)}, f32[64,128]{1,0:T(8,128)S(1)}, u32[]{:S(2)}, u32[]{:S(2)}) collective-permute-start(f32[64,128]{1,0:T(8,128)S(1)} %select_add_fusion.bands_ref), channel_id=1, source_target_pairs={{0,8},{4,12},{8,0},{12,4},{16,24},{20,28},{24,16},{28,20},{1,9},{5... | collective-permute-start | bytes 98312 | tf_op jit(solution)/shard_map/ppermute | solution.py:222
  63.6 3.4 %collective-permute-start.9 = (f32[64,128]{1,0:T(8,128)S(1)}, f32[64,128]{1,0:T(8,128)S(1)}, u32[]{:S(2)}, u32[]{:S(2)}) collective-permute-start(f32[64,128]{1,0:T(8,128)S(1)} %select_add_fusion.bands_ref), channel_id=1, source_target_pairs={{0,12},{4,8},{8,4},{12,0},{16,28},{20,24},{24,20},{28,16},{1,13},{... | collective-permute-start | bytes 98312 | tf_op jit(solution)/shard_map/ppermute | solution.py:222
  67.0 4.0 %collective-permute-start.10 = (f32[64,128]{1,0:T(8,128)S(1)}, f32[64,128]{1,0:T(8,128)S(1)}, u32[]{:S(2)}, u32[]{:S(2)}) collective-permute-start(f32[64,128]{1,0:T(8,128)S(1)} %add_add_fusion.1.refs_0_), channel_id=1, source_target_pairs={{0,16},{4,20},{8,24},{12,28},{16,0},{20,4},{24,8},{28,12},{1,17},{... | collective-permute-start | bytes 98312 | tf_op jit(solution)/shard_map/ppermute | solution.py:222

commit v23 on v22

--- a/solution.py
+++ b/solution.py
@@ -33,12 +33,6 @@
 def split2(x):
     high = x.astype(jnp.bfloat16)
     return high, (x - high.astype(jnp.float32)).astype(jnp.bfloat16)
-
-
-def split3(x):
-    high, low = split2(x)
-    rest = x - high.astype(jnp.float32) - low.astype(jnp.float32)
-    return high, low, rest.astype(jnp.bfloat16)
 
 
 def dot(a, b, dims=((1,), (0,))):
@@ -112,11 +106,11 @@
 
 
 def folded(x, fold):
-    return dot(jnp.concatenate(split3(x), axis=1), jnp.concatenate([fold] * 3, axis=0))
+    return dot(jnp.concatenate(split2(x), axis=1), jnp.concatenate([fold] * 2, axis=0))
 
 
 def spread(x, fold):
-    return dot(jnp.concatenate(split3(x), axis=1), jnp.concatenate([fold] * 3, axis=1), ((1,), (1,)))
+    return dot(jnp.concatenate(split2(x), axis=1), jnp.concatenate([fold] * 2, axis=1), ((1,), (1,)))
 
 
 def bands_kernel(m_ref, places_ref, *refs):

time: 72.9 us -> 72.8 us (level)
  no operation moved by 1% of the time
where the time goes in v23:
time: 72.8 us; the launch traced here: 72.4 us
  starting transfers between devices  31.6 us (43%)
  waiting for transfers between devices  24.5 us (34%)
  Pallas kernels  5.68 us (8%)
  local copies, waits for them, and re-layouts  5.04 us (7%)
  matrix products  4.36 us (6%)
  between operations  0.9 us (1%)
    ppermute x8, starting transfers between devices, send(): return lax.ppermute(x, 'tp', perm)  28.1 us
    ppermute x8, waiting for transfers between devices, send(): return lax.ppermute(x, 'tp', perm)  21 us
    pallas_call x6, Pallas kernels, call(): pl.pallas_call(kernel, out_shape=out_shapes, in_specs=[pl.BlockSpec(memor...  5.68 us
    dot_general x6, matrix products, dot(): lax.dot_general(a, b, (dims, ((), ())), preferred_element_type=jnp.float32)  4.36 us
    ppermute x4, waiting for transfers between devices, spread_sum(): lax.ppermute(x, axis, [(i, i ^ stride * k) for i in range(size)])  3.54 us
    ppermute x4, starting transfers between devices, spread_sum(): lax.ppermute(x, axis, [(i, i ^ stride * k) for i in range(size)])  3.44 us
    slice x1, local copies, waits for them, and re-layouts, lined(): out_grad[alone:]  2.11 us
    slice x1, local copies, waits for them, and re-layouts, lined(): out_grad[:alone]  1.77 us
  transfers between devices with their start and end apart: 12, of which 8 were waited for; matrix products, arithmetic and copies ran while one was open for 12% of the time, Pallas kernels for 4%

profile of v23, /device:TPU:0, one launch (start us, length us, event | category | flops | bytes accessed | tf_op | source)
XLA Modules:
  0.0 72.4 jit_solution(681694030524210659)
XLA Ops:
  0.6 0.9 %collective-permute-start.2 = (bf16[1152,512]{1,0:T(8,128)(2,1)}, bf16[1152,512]{1,0:T(8,128)(2,1)S(1)}, u32[]{:S(2)}, u32[]{:S(2)}) collective-permute-start(bf16[1152,512]{1,0:T(8,128)(2,1)} %param.9), channel_id=1, source_target_pairs={{1,2},{2,1},{5,6},{6,5},{9,10},{10,9},{13,14},{14,13},{17,18},{18,... | collective-permute-start | bytes 3538952 | tf_op jit(solution)/shard_map/ppermute | solution.py:251
  1.5 1.8 %slice.18 = bf16[384,512]{1,0:T(8,128)(2,1)} slice(bf16[1152,512]{1,0:T(8,128)(2,1)} %param.9), slice={[0:384], [0:512]} | slice | bytes 786432 | tf_op jit(solution)/shard_map/slice | solution.py:259
  3.3 5.8 %collective-permute-start.1 = (bf16[384,512]{1,0:T(8,128)(2,1)}, bf16[384,512]{1,0:T(8,128)(2,1)}, u32[]{:S(2)}, u32[]{:S(2)}) collective-permute-start(bf16[384,512]{1,0:T(8,128)(2,1)} %slice.18), channel_id=1, source_target_pairs={{0,1},{1,0},{2,3},{3,2},{4,5},{5,4},{6,7},{7,6},{8,9},{9,8},{10,11... | collective-permute-start | bytes 1179656 | tf_op jit(solution)/shard_map/ppermute | solution.py:251
  9.1 2.1 %slice.17 = bf16[768,512]{1,0:T(8,128)(2,1)} slice(bf16[1152,512]{1,0:T(8,128)(2,1)} %param.9), slice={[384:1152], [0:512]} | slice | bytes 1572864 | tf_op jit(solution)/shard_map/slice | solution.py:259
  11.2 0.0 collective-permute-start
  11.3 0.0 copy-start.2
  11.3 0.0 copy-start.4
  11.3 0.1 dynamic-slice_select_fusion
  11.4 0.5 copy-done.5
  11.9 0.0 copy-done.7
  11.9 0.1 fusion.17
  12.0 0.1 fusion.1
  12.1 0.5 copy-done.2
  12.6 0.1 copy-done.4
  12.7 0.5 convolution_add_fusion
  13.2 6.1 %collective-permute-done.1 = bf16[384,512]{1,0:T(8,128)(2,1)} collective-permute-done((bf16[384,512]{1,0:T(8,128)(2,1)}, bf16[384,512]{1,0:T(8,128)(2,1)}, u32[]{:S(2)}, u32[]{:S(2)}) %collective-permute-start.1) | collective-permute-done | bytes 393248 | tf_op jit(solution)/shard_map/ppermute | solution.py:251
  19.4 0.7 collective-permute-start.3
  20.0 1.3 %fusion.7 = f32[256,512]{1,0:T(8,128)S(1)} fusion(bf16[384,512]{1,0:T(8,128)(2,1)} %collective-permute-done.1, bf16[4608,256]{1,0:T(8,128)(2,1)S(1)} %copy-done.3, s32[]{:T(128)S(6)} %select_n.58), kind=kOutput, calls=%fused_computation.12 | convolution fusion | flops 100663296 | bytes 1114116 | tf_op jit(solution)/shard_map/dot_general | solution.py:39
  21.4 0.1 add.65
  21.5 0.0 collective-permute-done.2.cross_ref
  21.5 0.1 slice_select_fusion
  21.6 13.3 %collective-permute-start.4 = (bf16[784,512]{1,0:T(8,128)(2,1)S(1)}, bf16[784,512]{1,0:T(8,128)(2,1)S(1)}, u32[]{:S(2)}, u32[]{:S(2)}) collective-permute-start(bf16[784,512]{1,0:T(8,128)(2,1)S(1)} %slice_select_fusion), channel_id=1, source_target_pairs={{0,1},{1,0},{2,3},{3,2},{4,5},{5,4},{6,7},{7,6},{8,9},{9,8},{10,11... | collective-permute-start | bytes 2408456 | tf_op jit(solution)/shard_map/ppermute | solution.py:251
  34.9 1.3 %collective-permute-done = bf16[768,512]{1,0:T(8,128)(2,1)} collective-permute-done((bf16[768,512]{1,0:T(8,128)(2,1)}, bf16[768,512]{1,0:T(8,128)(2,1)}, u32[]{:S(2)}, u32[]{:S(2)}) %collective-permute-start) | collective-permute-done | bytes 786464 | tf_op jit(solution)/shard_map/ppermute | solution.py:251
  36.2 0.7 collective-permute-start.5
  36.9 1.5 %fusion.5 = f32[256,512]{1,0:T(8,128)S(1)} fusion(bf16[768,512]{1,0:T(8,128)(2,1)} %collective-permute-done, bf16[4608,256]{1,0:T(8,128)(2,1)S(1)} %copy-done.3, s32[]{:T(128)S(6)} %select_n.61), kind=kOutput, calls=%fused_computation.9 | convolution fusion | flops 201326592 | bytes 1703940 | tf_op jit(solution)/shard_map/dot_general | solution.py:39
  38.5 0.5 fusion.2
  39.0 0.0 copy-start
  39.0 0.0 copy-start.1
  39.0 0.3 add_add_fusion.m_ref
  39.4 12.8 %collective-permute-done.4.swapped_ref = bf16[784,512]{1,0:T(8,128)(2,1)S(1)} collective-permute-done((bf16[784,512]{1,0:T(8,128)(2,1)S(1)}, bf16[784,512]{1,0:T(8,128)(2,1)S(1)}, u32[]{:S(2)}, u32[]{:S(2)}) %collective-permute-start.4) | collective-permute-done | bytes 802848 | tf_op jit(solution)/shard_map/ppermute | solution.py:251
  52.2 1.3 %shard_map.95 = (f32[256,512]{1,0:T(8,128)S(1)}, f32[256,512]{1,0:T(8,128)S(1)}, bf16[256,768]{1,0:T(8,128)(2,1)S(1)}, bf16[256,768]{1,0:T(8,128)(2,1)S(1)}, f32...) custom-call(f32[256,512]{1,0:T(8,128)S(1)} %add_add_fusion.m_ref, bf16[768,256]{1,0:T(8,128)(2,1)S(1)} %get-tuple-element.75.hidden_ref, ...), custom_call_target="tpu_custom_call" | custom-call | flops 400000000 | bytes 4000000 | tf_op jit(solution)/shard_map/pallas_call | solution.py:198
  53.5 0.0 collective-permute-done.5.far_ref
  53.5 1.1 %shard_map.96 = (s16[272,512]{1,0:T(8,128)(2,1)S(1)}, f32[64,128]{1,0:T(8,128)S(1)}) custom-call(f32[256,512]{1,0:T(8,128)S(1)} %get-tuple-element.54.helped_ref, bf16[256,768]{1,0:T(8,128)(2,1)S(1)} %get-tuple-element.55.turned_ref, bf16[768,512]{1,0:T(8,128)(2,1)S(1)} %collective-permute-done.5.far_ref, f32[16,512]{1,0:T(8,128)S(1)} %get-tuple-element.57.places_ref, ...), custom_call_target="tpu_custom_call" | custom-call | flops 400000000 | bytes 4000000 | tf_op jit(solution)/shard_map/pallas_call | solution.py:198
  54.6 5.5 %collective-permute-start.6 = (f32[64,128]{1,0:T(8,128)S(1)}, f32[64,128]{1,0:T(8,128)S(1)}, u32[]{:S(2)}, u32[]{:S(2)}) collective-permute-start(f32[64,128]{1,0:T(8,128)S(1)} %get-tuple-element.60), channel_id=1, source_target_pairs={{0,1},{1,0},{2,3},{3,2},{4,5},{5,4},{6,7},{7,6},{8,9},{9,8},{10,11... | collective-permute-start | bytes 98312 | tf_op jit(solution)/shard_map/ppermute | solution.py:251
  60.1 1.3 %collective-permute-start.11 = (s16[272,512]{1,0:T(8,128)(2,1)S(1)}, s16[272,512]{1,0:T(8,128)(2,1)S(1)}, u32[]{:S(2)}, u32[]{:S(2)}) collective-permute-start(s16[272,512]{1,0:T(8,128)(2,1)S(1)} %get-tuple-element.70), channel_id=1, source_target_pairs={{1,0},{2,3},{5,4},{6,7},{9,8},{10,11},{13,12},{14,15},{17,16},{18,... | collective-permute-start | bytes 835592 | tf_op jit(solution)/shard_map/ppermute | solution.py:251
  61.4 0.5 collective-permute-done.6
  62.0 0.0 collective-permute-start.7
  62.0 1.6 %collective-permute-start.8 = (f32[64,128]{1,0:T(8,128)S(1)}, f32[64,128]{1,0:T(8,128)S(1)}, u32[]{:S(2)}, u32[]{:S(2)}) collective-permute-start(f32[64,128]{1,0:T(8,128)S(1)} %select_add_fusion.bands_ref), channel_id=1, source_target_pairs={{0,8},{4,12},{8,0},{12,4},{16,24},{20,28},{24,16},{28,20},{1,9},{5... | collective-permute-start | bytes 98312 | tf_op jit(solution)/shard_map/ppermute | solution.py:216
  63.6 0.3 collective-permute-start.9
  63.9 0.8 %shard_map.98.x_ref = f32[256,512]{1,0:T(8,128)S(1)} custom-call(f32[256,512]{1,0:T(8,128)S(1)} %get-tuple-element.69.m_ref, f32[64,128]{1,0:T(8,128)S(1)} %select_add_fusion.bands_ref, f32[8,512]{1,0:T(8,128)S(1)} %get-tuple-element.50.places_ref.refs_2_, bf16[512,128]{1,0:T(8,128)(2,1)S(1)} %copy-done.1, f32[256,256]{1,0:T(8,128)S(1)} %copy-done), custom_call_target="tpu_custom_call" | custom-call | flops 400000000 | bytes 4000000 | tf_op jit(solution)/shard_map/pallas_call | solution.py:198
  64.7 0.0 collective-permute-done.7
  64.7 1.3 %collective-permute-done.8 = f32[64,128]{1,0:T(8,128)S(1)} collective-permute-done((f32[64,128]{1,0:T(8,128)S(1)}, f32[64,128]{1,0:T(8,128)S(1)}, u32[]{:S(2)}, u32[]{:S(2)}) %collective-permute-start.8) | collective-permute-done | bytes 32800 | tf_op jit(solution)/shard_map/ppermute | solution.py:216
  66.0 0.9 %collective-permute-done.9 = f32[64,128]{1,0:T(8,128)S(1)} collective-permute-done((f32[64,128]{1,0:T(8,128)S(1)}, f32[64,128]{1,0:T(8,128)S(1)}, u32[]{:S(2)}, u32[]{:S(2)}) %collective-permute-start.9) | collective-permute-done | bytes 32800 | tf_op jit(solution)/shard_map/ppermute | solution.py:216
  66.9 1.6 %collective-permute-start.10 = (f32[64,128]{1,0:T(8,128)S(1)}, f32[64,128]{1,0:T(8,128)S(1)}, u32[]{:S(2)}, u32[]{:S(2)}) collective-permute-start(f32[64,128]{1,0:T(8,128)S(1)} %add_add_fusion.1.refs_0_), channel_id=1, source_target_pairs={{0,16},{4,20},{8,24},{12,28},{16,0},{20,4},{24,8},{28,12},{1,17},{... | collective-permute-start | bytes 98312 | tf_op jit(solution)/shard_map/ppermute | solution.py:216
  68.5 0.2 collective-permute-done.11.code_ref
  68.7 0.9 %shard_map.99 = f32[256,512]{1,0:T(8,128)} custom-call(f32[256,512]{1,0:T(8,128)S(1)} %shard_map.98.x_ref, s16[272,512]{1,0:T(8,128)(2,1)S(1)} %collective-permute-done.11.code_ref), custom_call_target="tpu_custom_call" | custom-call | flops 400000000 | bytes 4000000 | tf_op jit(solution)/shard_map/pallas_call | solution.py:198
  69.6 1.3 %collective-permute-done.10.refs_1_ = f32[64,128]{1,0:T(8,128)S(1)} collective-permute-done((f32[64,128]{1,0:T(8,128)S(1)}, f32[64,128]{1,0:T(8,128)S(1)}, u32[]{:S(2)}, u32[]{:S(2)}) %collective-permute-start.10) | collective-permute-done | bytes 32800 | tf_op jit(solution)/shard_map/ppermute | solution.py:216
  70.9 1.5 %shard_map.100 = bf16[256,512]{1,0:T(8,128)(2,1)} custom-call(f32[64,128]{1,0:T(8,128)S(1)} %add_add_fusion.1.refs_0_, f32[64,128]{1,0:T(8,128)S(1)} %collective-permute-done.10.refs_1_, f32[8,512]{1,0:T(8,128)S(1)} %get-tuple-element.50.places_ref.refs_2_, bf16[512,128]{1,0:T(8,128)(2,1)S(1)} %copy-done.1, f32[256,256]{1,0:T(8,128)S(1)} %copy-done), custom_call_target="tpu_custom_call" | custom-call | flops 400000000 | bytes 4000000 | tf_op jit(solution)/shard_map/pallas_call | solution.py:198
  (13 shorter events, 0.1 us)
Async XLA Ops:
  0.6 10.6 %copy-start.3 = (bf16[4608,256]{1,0:T(8,128)(2,1)S(1)}, bf16[4608,256]{1,0:T(8,128)(2,1)}, u32[]{:S(2)}) copy-start(bf16[4608,256]{1,0:T(8,128)(2,1)} %param.8) | copy-start | bytes 7077892
  0.6 20.8 %collective-permute-start.2 = (bf16[1152,512]{1,0:T(8,128)(2,1)}, bf16[1152,512]{1,0:T(8,128)(2,1)S(1)}, u32[]{:S(2)}, u32[]{:S(2)}) collective-permute-start(bf16[1152,512]{1,0:T(8,128)(2,1)} %param.9), channel_id=1, source_target_pairs={{1,2},{2,1},{5,6},{6,5},{9,10},{10,9},{13,14},{14,13},{17,18},{18,... | collective-permute-start | bytes 3538952 | tf_op jit(solution)/shard_map/ppermute | solution.py:251
  3.3 16.1 %collective-permute-start.1 = (bf16[384,512]{1,0:T(8,128)(2,1)}, bf16[384,512]{1,0:T(8,128)(2,1)}, u32[]{:S(2)}, u32[]{:S(2)}) collective-permute-start(bf16[384,512]{1,0:T(8,128)(2,1)} %slice.18), channel_id=1, source_target_pairs={{0,1},{1,0},{2,3},{3,2},{4,5},{5,4},{6,7},{7,6},{8,9},{9,8},{10,11... | collective-permute-start | bytes 1179656 | tf_op jit(solution)/shard_map/ppermute | solution.py:251
  11.2 0.7 copy-start.5
  11.2 0.7 copy-start.6
  11.2 0.7 copy-start.7
  11.2 25.0 %collective-permute-start = (bf16[768,512]{1,0:T(8,128)(2,1)}, bf16[768,512]{1,0:T(8,128)(2,1)}, u32[]{:S(2)}, u32[]{:S(2)}) collective-permute-start(bf16[768,512]{1,0:T(8,128)(2,1)} %slice.17), channel_id=1, source_target_pairs={{0,1},{1,0},{2,3},{3,2},{4,5},{5,4},{6,7},{7,6},{8,9},{9,8},{10,11... | collective-permute-start | bytes 2359304 | tf_op jit(solution)/shard_map/ppermute | solution.py:251
  11.3 1.3 %copy-start.2 = (bf16[1152,512]{1,0:T(8,128)(2,1)S(1)}, bf16[1152,512]{1,0:T(8,128)(2,1)}, u32[]{:S(2)}) copy-start(bf16[1152,512]{1,0:T(8,128)(2,1)} %param.9) | copy-start | bytes 3538948
  11.3 1.4 %copy-start.4 = (f32[1,256,512]{2,1,0:T(8,128)S(1)}, f32[1,256,512]{2,1,0:T(8,128)}, u32[]{:S(2)}) copy-start(f32[1,256,512]{2,1,0:T(8,128)} %param.10) | copy-start | bytes 1572868
  19.4 17.6 %collective-permute-start.3 = (bf16[384,512]{1,0:T(8,128)(2,1)}, bf16[384,512]{1,0:T(8,128)(2,1)S(1)}, u32[]{:S(2)}, u32[]{:S(2)}) collective-permute-start(bf16[384,512]{1,0:T(8,128)(2,1)} %collective-permute-done.1), channel_id=1, source_target_pairs={{1,2},{2,1},{5,6},{6,5},{9,10},{10,9},{13,14},{14,13},{17,18},{18,... | collective-permute-start | bytes 1179656 | tf_op jit(solution)/shard_map/ppermute | solution.py:251
  21.6 30.6 %collective-permute-start.4 = (bf16[784,512]{1,0:T(8,128)(2,1)S(1)}, bf16[784,512]{1,0:T(8,128)(2,1)S(1)}, u32[]{:S(2)}, u32[]{:S(2)}) collective-permute-start(bf16[784,512]{1,0:T(8,128)(2,1)S(1)} %slice_select_fusion), channel_id=1, source_target_pairs={{0,1},{1,0},{2,3},{3,2},{4,5},{5,4},{6,7},{7,6},{8,9},{9,8},{10,11... | collective-permute-start | bytes 2408456 | tf_op jit(solution)/shard_map/ppermute | solution.py:251
  36.2 17.3 %collective-permute-start.5 = (bf16[768,512]{1,0:T(8,128)(2,1)}, bf16[768,512]{1,0:T(8,128)(2,1)S(1)}, u32[]{:S(2)}, u32[]{:S(2)}) collective-permute-start(bf16[768,512]{1,0:T(8,128)(2,1)} %collective-permute-done), channel_id=1, source_target_pairs={{1,2},{2,1},{5,6},{6,5},{9,10},{10,9},{13,14},{14,13},{17,18},{18,... | collective-permute-start | bytes 2359304 | tf_op jit(solution)/shard_map/ppermute | solution.py:251
  39.0 13.2 %copy-start = (f32[256,256]{1,0:T(8,128)S(1)}, f32[256,256]{1,0:T(8,128)}, u32[]{:S(2)}) copy-start(f32[256,256]{1,0:T(8,128)} %constant.38.clone.refs_1_.basis_ref.refs_4_) | copy-start | bytes 786436
  39.0 13.2 %copy-start.1 = (bf16[512,128]{1,0:T(8,128)(2,1)S(1)}, bf16[512,128]{1,0:T(8,128)(2,1)}, u32[]{:S(2)}) copy-start(bf16[512,128]{1,0:T(8,128)(2,1)} %constant.37.clone.refs_0_.fold_ref.refs_3_) | copy-start | bytes 393220
  54.6 7.4 %collective-permute-start.6 = (f32[64,128]{1,0:T(8,128)S(1)}, f32[64,128]{1,0:T(8,128)S(1)}, u32[]{:S(2)}, u32[]{:S(2)}) collective-permute-start(f32[64,128]{1,0:T(8,128)S(1)} %get-tuple-element.60), channel_id=1, source_target_pairs={{0,1},{1,0},{2,3},{3,2},{4,5},{5,4},{6,7},{7,6},{8,9},{9,8},{10,11... | collective-permute-start | bytes 98312 | tf_op jit(solution)/shard_map/ppermute | solution.py:251
  60.1 8.6 %collective-permute-start.11 = (s16[272,512]{1,0:T(8,128)(2,1)S(1)}, s16[272,512]{1,0:T(8,128)(2,1)S(1)}, u32[]{:S(2)}, u32[]{:S(2)}) collective-permute-start(s16[272,512]{1,0:T(8,128)(2,1)S(1)} %get-tuple-element.70), channel_id=1, source_target_pairs={{1,0},{2,3},{5,4},{6,7},{9,8},{10,11},{13,12},{14,15},{17,16},{18,... | collective-permute-start | bytes 835592 | tf_op jit(solution)/shard_map/ppermute | solution.py:251
  62.0 2.7 %collective-permute-start.7 = (f32[64,128]{1,0:T(8,128)S(1)}, f32[64,128]{1,0:T(8,128)S(1)}, u32[]{:S(2)}, u32[]{:S(2)}) collective-permute-start(f32[64,128]{1,0:T(8,128)S(1)} %select_add_fusion.bands_ref), channel_id=1, source_target_pairs={{0,4},{4,0},{8,12},{12,8},{16,20},{20,16},{24,28},{28,24},{1,5},{5... | collective-permute-start | bytes 98312 | tf_op jit(solution)/shard_map/ppermute | solution.py:216
  62.0 4.0 %collective-permute-start.8 = (f32[64,128]{1,0:T(8,128)S(1)}, f32[64,128]{1,0:T(8,128)S(1)}, u32[]{:S(2)}, u32[]{:S(2)}) collective-permute-start(f32[64,128]{1,0:T(8,128)S(1)} %select_add_fusion.bands_ref), channel_id=1, source_target_pairs={{0,8},{4,12},{8,0},{12,4},{16,24},{20,28},{24,16},{28,20},{1,9},{5... | collective-permute-start | bytes 98312 | tf_op jit(solution)/shard_map/ppermute | solution.py:216
  63.6 3.4 %collective-permute-start.9 = (f32[64,128]{1,0:T(8,128)S(1)}, f32[64,128]{1,0:T(8,128)S(1)}, u32[]{:S(2)}, u32[]{:S(2)}) collective-permute-start(f32[64,128]{1,0:T(8,128)S(1)} %select_add_fusion.bands_ref), channel_id=1, source_target_pairs={{0,12},{4,8},{8,4},{12,0},{16,28},{20,24},{24,20},{28,16},{1,13},{... | collective-permute-start | bytes 98312 | tf_op jit(solution)/shard_map/ppermute | solution.py:216
  66.9 4.0 %collective-permute-start.10 = (f32[64,128]{1,0:T(8,128)S(1)}, f32[64,128]{1,0:T(8,128)S(1)}, u32[]{:S(2)}, u32[]{:S(2)}) collective-permute-start(f32[64,128]{1,0:T(8,128)S(1)} %add_add_fusion.1.refs_0_), channel_id=1, source_target_pairs={{0,16},{4,20},{8,24},{12,28},{16,0},{20,4},{24,8},{28,12},{1,17},{... | collective-permute-start | bytes 98312 | tf_op jit(solution)/shard_map/ppermute | solution.py:216
